TPU v7x, 1024 devices: a whole 4x8x16 slice. The times are simulated.
1024 devices in a mesh: gx: 8 (over z_lo), gy: 32 (over y, x), gz: 4 (over z_hi, core).
Axes of the slice: x: 4, y: 8, z: 16 (z_hi: 2, z_lo: 8; z = z_hi * 8 + z_lo), core: 2. Of those that a mesh axis runs over, the one named last changes fastest.
Arguments:
- old_field: float32 [64, 128, 4096], P('gx', 'gz', 'gy'), may hold values from -6 to 6
- new_home: int32 [8, 4, 128], P('gx', 'gz', 'gy'), may hold values from 0 to 127, as said below
- conduct: float32 [64, 128, 4096], P('gx', 'gz', 'gy'), may hold values from 0.2 to 4
- reaction: float32 [64, 128, 4096], P('gx', 'gz', 'gy'), may hold values from 0.05 to 2
- source: float32 [64, 128, 4096], P('gx', 'gz', 'gy'), may hold values from -6 to 6
- coarse: float32 [32, 64, 2048], P('gx', 'gz', 'gy'), may hold values from -12 to 12
Outputs:
- relaxed: float32 [64, 128, 4096], P('gx', 'gz', 'gy')
Inputs may be any that keep to these rules, and one draw needn't show every extreme that they name: In each line of box positions along the second direction (fixed a and c), new_home is a permutation of 0 to 127. Of the 4 positions i * 4 to i * 4 + 3 of each block i, exactly one has a new home outside the block, and it is the position in its target block whose own box leaves; every other position is its own new home.
All inputs are finite; a program needn't handle non-finite values.
Results may differ from a plain program's by a relative error of at most 0.00002.
Values sent between devices are 32-bit elements; how exact they have to be, the bound alone decides.
No kernel may reach another device: no remote copies, remote signals or barrier semaphores. Data moves between devices by JAX's collectives and lax.ppermute only.
A program may use at most 32 MiB of HBM per device.

v0:
```python
import jax
import jax.numpy as jnp
from jax import lax
from jax.sharding import PartitionSpec as P


def padded_2(block, sides, width):
    for axis, dim in sides:
        count = lax.axis_size(axis)
        forward = [(i, i + 1) for i in range(count - 1)]
        backward = [(target, source) for source, target in forward]
        low = lax.ppermute(
            lax.slice_in_dim(block, block.shape[dim] - width, None, axis=dim), axis, forward
        )
        high = lax.ppermute(lax.slice_in_dim(block, 0, width, axis=dim), axis, backward)
        block = jnp.concatenate([low, block, high], axis=dim)
    return block


def fill_ghosts(values, ghosts, thickness, low_edge, high_edge):
    for direction in range(3):
        extent = values.shape[direction]
        layer_source = values if ghosts is None else ghosts
        edge_low = lax.slice_in_dim(layer_source, thickness, thickness + 1, axis=direction)
        edge_high = lax.slice_in_dim(
            layer_source, extent - thickness - 1, extent - thickness, axis=direction
        )
        layer_ids = lax.broadcasted_iota(jnp.int32, values.shape, direction)
        values = jnp.where(low_edge[direction] & (layer_ids < thickness), edge_low, values)
        values = jnp.where(
            high_edge[direction] & (layer_ids >= extent - thickness), edge_high, values
        )
    return values


def relax(padded_phi, padded_kappa, start_field, source, reaction):
    kappa_mid = padded_kappa[1:-1, 1:-1, 1:-1]
    numerator = start_field + source
    denominator = 1.0 + reaction
    for direction in range(3):
        for offset in (0, 2):
            window = [slice(1, -1), slice(1, -1), slice(1, -1)]
            extent = padded_phi.shape[direction] - 2
            window[direction] = slice(offset, offset + extent)
            beside_phi = padded_phi[tuple(window)]
            beside_kappa = padded_kappa[tuple(window)]
            weight = 0.5 * (kappa_mid + beside_kappa)
            numerator = numerator + weight * beside_phi
            denominator = denominator + weight
    return numerator / denominator


def rims(stacked):
    return padded_2(stacked, (("gx", 1), ("gz", 2), ("gy", 3)), 1)


def on_device(old_field, new_home, conduct, reaction, source, coarse):
    position = lax.axis_index("gy")
    slot_count = new_home.shape[2]
    box_width = old_field.shape[2] // slot_count
    home_list = new_home[0, 0, :]
    slot_ids = jnp.arange(slot_count, dtype=jnp.int32)
    leaving = home_list != position * slot_count + slot_ids
    move_slot = jnp.sum(jnp.where(leaving, slot_ids, 0))
    target = jnp.sum(jnp.where(leaving, home_list, 0))
    moved_box = lax.dynamic_slice_in_dim(old_field, move_slot * box_width, box_width, 2)
    vacated = position * slot_count + move_slot
    box_list = lax.all_gather(moved_box[None], "gy", axis=0, tiled=True)
    tag_list = lax.all_gather(target.astype(jnp.float32)[None], "gy", axis=0, tiled=True)
    chosen = tag_list == vacated.astype(jnp.float32)
    arrived = jnp.sum(jnp.where(chosen[:, None, None, None], box_list, 0.0), axis=0)
    start_field = lax.dynamic_update_slice_in_dim(old_field, arrived, move_slot * box_width, 2)
    upsampled = jnp.repeat(jnp.repeat(jnp.repeat(coarse, 2, axis=0), 2, axis=1), 2, axis=2)
    low_edge = [lax.axis_index("gx") == 0, lax.axis_index("gz") == 0, lax.axis_index("gy") == 0]
    high_edge = [
        lax.axis_index("gx") == lax.axis_size("gx") - 1,
        lax.axis_index("gz") == lax.axis_size("gz") - 1,
        lax.axis_index("gy") == lax.axis_size("gy") - 1,
    ]
    ghost_coarse = jnp.pad(upsampled, 1, mode="edge")
    padded = rims(jnp.stack([start_field, conduct]))
    padded_kappa = fill_ghosts(padded[1], None, 1, low_edge, high_edge)
    first = relax(
        fill_ghosts(padded[0], ghost_coarse, 1, low_edge, high_edge),
        padded_kappa,
        start_field,
        source,
        reaction,
    )
    second = rims(first[None])
    relaxed = relax(
        fill_ghosts(second[0], ghost_coarse, 1, low_edge, high_edge),
        padded_kappa,
        start_field,
        source,
        reaction,
    )
    return relaxed


def solution(mesh):
    return jax.shard_map(
        on_device,
        mesh=mesh,
        in_specs=(
            P("gx", "gz", "gy"),
            P("gx", "gz", "gy"),
            P("gx", "gz", "gy"),
            P("gx", "gz", "gy"),
            P("gx", "gz", "gy"),
            P("gx", "gz", "gy"),
        ),
        out_specs=P("gx", "gz", "gy"),
        check_vma=False,
    )
```

profile of v0, /device:TPU:7, one launch (start us, length us, event | category | flops | bytes accessed | tf_op | source)
XLA Modules:
  0.0 218.4 jit_solution(3150965548884843274)
XLA Ops:
  6.5 0.0 all-gather.3.cloned.1.call-start
  6.5 0.9 copy.68
  7.4 1.3 fusion.37
  9.4 0.8 constant_dynamic-slice_fusion
  10.2 0.0 all-gather.3.cloned.1.call-update
  11.5 0.8 copy.39
  12.3 0.1 copy.40
  12.4 0.1 copy.43
  12.5 0.1 copy.42
  12.6 0.1 copy.45
  12.7 0.2 copy.41
  12.9 0.2 copy.44
  13.2 0.0 copy-start
  13.2 0.1 fusion.42
  13.5 1.3 dynamic-slice
  14.8 0.7 dynamic-update-slice
  15.5 53.9 %all-reduce = f32[32]{0:T(128)S(1)} all-reduce(f32[32]{0:T(128)S(1)} %dynamic-update-slice), channel_id=1, replica_groups=mesh['gx'=8,'gy'=32,'gz'=4] {'gy'}, use_global_device_ids=true, to_apply=%add | all-reduce | flops 32 | bytes 256
  69.5 0.1 maximum_bitcast_fusion.2
  69.6 0.3 pad_maximum_fusion.5
  69.9 43.1 %all-gather.3.cloned.1.call-done = f32[256,32,32]{2,1,0:T(8,128)} async-done(((f32[8,32,32]{2,1,0:T(8,128)}), f32[256,32,32]{2,1,0:T(8,128)}) %all-gather.3.cloned.1.call-update) | async-done | bytes 1048592 | tf_op jit(solution)/shard_map/all_gather | solution.py:68
  112.9 2.8 %select_reduce_fusion = f32[8,32,32]{2,1,0:T(8,128)S(1)} fusion(f32[32,8,32,32]{3,2,1,0:T(8,128)} %bitcast.77, pred[32]{0:T(512)(128)(4,1)S(1)} %broadcast_compare_fusion), kind=kLoop, calls=%fused_computation | loop fusion | flops 516096 | bytes 1081376 | tf_op jit(solution)/shard_map/reduce_sum | solution.py:71
  115.7 0.3 dynamic_update_slice.3
  116.1 0.0 copy-done
  116.1 4.4 %collective-permute-start = (f32[2,1,32,128]{3,2,1,0:T(8,128)S(1)}, f32[2,1,32,128]{3,2,1,0:T(8,128)S(1)}, u32[]{:S(2)}, u32[]{:S(2)}) collective-permute-start(f32[2,1,32,128]{3,2,1,0:T(8,128)S(1)} %get-tuple-element.25), channel_id=1, source_target_pairs={{0,128},{128,256},{256,384},{384,512},{512,640},{640,768},{768,896... | collective-permute-start | bytes 98312 | tf_op jit(solution)/shard_map/ppermute | solution.py:12
  120.5 1.3 collective-permute-start.1
  121.8 0.0 collective-permute-done
  121.8 3.3 %collective-permute-done.1 = f32[2,1,32,128]{3,2,1,0:T(8,128)S(1)} collective-permute-done((f32[2,1,32,128]{3,2,1,0:T(8,128)S(1)}, f32[2,1,32,128]{3,2,1,0:T(8,128)S(1)}, u32[]{:S(2)}, u32[]{:S(2)}) %collective-permute-start.1) | collective-permute-done | bytes 32800 | tf_op jit(solution)/shard_map/ppermute | solution.py:15
  125.1 17.0 %collective-permute-start.2 = (f32[2,10,1,128]{3,2,1,0:T(1,128)S(1)}, f32[2,10,1,128]{3,2,1,0:T(1,128)S(1)}, u32[]{:S(2)}, u32[]{:S(2)}) collective-permute-start(f32[2,10,1,128]{3,2,1,0:T(1,128)S(1)} %get-tuple-element.23), channel_id=1, source_target_pairs={{0,1},{1,2},{2,3},{4,5},{5,6},{6,7},{8,9},{9,10},{10,11},{12,13},{... | collective-permute-start | bytes 30728 | tf_op jit(solution)/shard_map/ppermute | solution.py:12
  142.1 1.9 collective-permute-start.3
  144.1 0.0 collective-permute-done.2
  144.1 11.7 %collective-permute-done.3 = f32[2,10,1,128]{3,2,1,0:T(1,128)S(1)} collective-permute-done((f32[2,10,1,128]{3,2,1,0:T(1,128)S(1)}, f32[2,10,1,128]{3,2,1,0:T(1,128)S(1)}, u32[]{:S(2)}, u32[]{:S(2)}) %collective-permute-start.3) | collective-permute-done | bytes 10272 | tf_op jit(solution)/shard_map/ppermute | solution.py:15
  155.8 0.1 pad_maximum_fusion.1
  155.9 0.0 copy-start.1
  155.9 0.0 copy-start.2
  155.9 0.2 fusion.40
  156.1 5.3 %collective-permute-start.4 = (f32[2,10,34,1]{3,2,1,0:T(8,128)S(1)}, f32[2,10,34,1]{3,2,1,0:T(8,128)S(1)}, u32[]{:S(2)}, u32[]{:S(2)}) collective-permute-start(f32[2,10,34,1]{3,2,1,0:T(8,128)S(1)} %get-tuple-element.21), channel_id=1, source_target_pairs={{0,4},{4,8},{8,12},{12,16},{16,20},{20,24},{24,28},{28,32},{32,36}... | collective-permute-start | bytes 8168 | tf_op jit(solution)/shard_map/ppermute | solution.py:12
  161.3 1.9 collective-permute-start.5
  163.3 0.2 copy.56
  163.5 0.2 copy.55
  163.7 2.6 %collective-permute-done.4 = f32[2,10,34,1]{3,2,1,0:T(8,128)S(1)} collective-permute-done((f32[2,10,34,1]{3,2,1,0:T(8,128)S(1)}, f32[2,10,34,1]{3,2,1,0:T(8,128)S(1)}, u32[]{:S(2)}, u32[]{:S(2)}) %collective-permute-start.4) | collective-permute-done | bytes 2752 | tf_op jit(solution)/shard_map/ppermute | solution.py:12
  166.2 5.9 %collective-permute-done.5 = f32[2,10,34,1]{3,2,1,0:T(8,128)S(1)} collective-permute-done((f32[2,10,34,1]{3,2,1,0:T(8,128)S(1)}, f32[2,10,34,1]{3,2,1,0:T(8,128)S(1)}, u32[]{:S(2)}, u32[]{:S(2)}) %collective-permute-start.5) | collective-permute-done | bytes 2752 | tf_op jit(solution)/shard_map/ppermute | solution.py:15
  172.1 0.5 pad_maximum_fusion
  172.6 0.3 fusion.7
  172.9 0.1 select_select_fusion.1
  173.1 0.2 slice_reduce_fusion.1
  173.3 0.2 select_select_fusion
  173.5 0.0 copy-done.1
  173.5 0.0 copy-done.2
  173.5 0.4 fusion.25
  174.0 2.4 %collective-permute-start.6 = (f32[1,1,32,128]{3,2,1,0:T(8,128)S(1)}, f32[1,1,32,128]{3,2,1,0:T(8,128)S(1)}, u32[]{:S(2)}, u32[]{:S(2)}) collective-permute-start(f32[1,1,32,128]{3,2,1,0:T(8,128)S(1)} %get-tuple-element.33), channel_id=1, source_target_pairs={{0,128},{128,256},{256,384},{384,512},{512,640},{640,768},{768,896... | collective-permute-start | bytes 49160 | tf_op jit(solution)/shard_map/ppermute | solution.py:12
  176.4 1.3 collective-permute-start.7
  177.7 0.0 collective-permute-done.6
  177.7 3.2 %collective-permute-done.7 = f32[1,1,32,128]{3,2,1,0:T(8,128)S(1)} collective-permute-done((f32[1,1,32,128]{3,2,1,0:T(8,128)S(1)}, f32[1,1,32,128]{3,2,1,0:T(8,128)S(1)}, u32[]{:S(2)}, u32[]{:S(2)}) %collective-permute-start.7) | collective-permute-done | bytes 16416 | tf_op jit(solution)/shard_map/ppermute | solution.py:15
  180.9 4.8 %collective-permute-start.8 = (f32[1,10,1,128]{3,2,1,0:T(1,128)S(1)}, f32[1,10,1,128]{3,2,1,0:T(1,128)S(1)}, u32[]{:S(2)}, u32[]{:S(2)}) collective-permute-start(f32[1,10,1,128]{3,2,1,0:T(1,128)S(1)} %get-tuple-element.31), channel_id=1, source_target_pairs={{0,1},{1,2},{2,3},{4,5},{5,6},{6,7},{8,9},{9,10},{10,11},{12,13},{... | collective-permute-start | bytes 15368 | tf_op jit(solution)/shard_map/ppermute | solution.py:12
  185.7 1.9 collective-permute-start.9
  187.6 0.0 collective-permute-done.8
  187.6 11.7 %collective-permute-done.9 = f32[1,10,1,128]{3,2,1,0:T(1,128)S(1)} collective-permute-done((f32[1,10,1,128]{3,2,1,0:T(1,128)S(1)}, f32[1,10,1,128]{3,2,1,0:T(1,128)S(1)}, u32[]{:S(2)}, u32[]{:S(2)}) %collective-permute-start.9) | collective-permute-done | bytes 5152 | tf_op jit(solution)/shard_map/ppermute | solution.py:15
  199.4 0.1 fusion.41
  199.5 1.9 collective-permute-start.10
  201.4 3.4 %collective-permute-start.11 = (f32[1,10,34,1]{3,2,1,0:T(8,128)S(1)}, f32[1,10,34,1]{3,2,1,0:T(8,128)S(1)}, u32[]{:S(2)}, u32[]{:S(2)}) collective-permute-start(f32[1,10,34,1]{3,2,1,0:T(8,128)S(1)} %get-tuple-element.28), channel_id=1, source_target_pairs={{4,0},{8,4},{12,8},{16,12},{20,16},{24,20},{28,24},{32,28},{36,32}... | collective-permute-start | bytes 4088 | tf_op jit(solution)/shard_map/ppermute | solution.py:15
  204.8 1.2 collective-permute-done.10
  206.0 4.0 %collective-permute-done.11 = f32[1,10,34,1]{3,2,1,0:T(8,128)S(1)} collective-permute-done((f32[1,10,34,1]{3,2,1,0:T(8,128)S(1)}, f32[1,10,34,1]{3,2,1,0:T(8,128)S(1)}, u32[]{:S(2)}, u32[]{:S(2)}) %collective-permute-start.11) | collective-permute-done | bytes 1392 | tf_op jit(solution)/shard_map/ppermute | solution.py:15
  210.0 0.4 fusion.13
  210.5 1.1 fusion.17
  (30 shorter events, 0.5 us)
Async XLA Ops:
  6.5 106.4 %all-gather.3.cloned.1.call-start = ((), (), s32[]{:S(2)}) async-start(), calls=%async_computation | async-start | bytes 4325376 | tf_op jit(solution)/shard_map/all_gather | solution.py:68
  13.2 102.9 %copy-start = (f32[8,32,128]{2,1,0:T(8,128)S(1)}, f32[8,32,128]{2,1,0:T(8,128)}, u32[]{:S(2)}) copy-start(f32[8,32,128]{2,1,0:T(8,128)} %param.8) | copy-start | bytes 393220
  116.1 5.7 %collective-permute-start = (f32[2,1,32,128]{3,2,1,0:T(8,128)S(1)}, f32[2,1,32,128]{3,2,1,0:T(8,128)S(1)}, u32[]{:S(2)}, u32[]{:S(2)}) collective-permute-start(f32[2,1,32,128]{3,2,1,0:T(8,128)S(1)} %get-tuple-element.25), channel_id=1, source_target_pairs={{0,128},{128,256},{256,384},{384,512},{512,640},{640,768},{768,896... | collective-permute-start | bytes 98312 | tf_op jit(solution)/shard_map/ppermute | solution.py:12
  120.5 4.7 %collective-permute-start.1 = (f32[2,1,32,128]{3,2,1,0:T(8,128)S(1)}, f32[2,1,32,128]{3,2,1,0:T(8,128)S(1)}, u32[]{:S(2)}, u32[]{:S(2)}) collective-permute-start(f32[2,1,32,128]{3,2,1,0:T(8,128)S(1)} %get-tuple-element.26), channel_id=1, source_target_pairs={{128,0},{256,128},{384,256},{512,384},{640,512},{768,640},{896,768... | collective-permute-start | bytes 98312 | tf_op jit(solution)/shard_map/ppermute | solution.py:15
  125.1 18.9 %collective-permute-start.2 = (f32[2,10,1,128]{3,2,1,0:T(1,128)S(1)}, f32[2,10,1,128]{3,2,1,0:T(1,128)S(1)}, u32[]{:S(2)}, u32[]{:S(2)}) collective-permute-start(f32[2,10,1,128]{3,2,1,0:T(1,128)S(1)} %get-tuple-element.23), channel_id=1, source_target_pairs={{0,1},{1,2},{2,3},{4,5},{5,6},{6,7},{8,9},{9,10},{10,11},{12,13},{... | collective-permute-start | bytes 30728 | tf_op jit(solution)/shard_map/ppermute | solution.py:12
  142.1 13.7 %collective-permute-start.3 = (f32[2,10,1,128]{3,2,1,0:T(1,128)S(1)}, f32[2,10,1,128]{3,2,1,0:T(1,128)S(1)}, u32[]{:S(2)}, u32[]{:S(2)}) collective-permute-start(f32[2,10,1,128]{3,2,1,0:T(1,128)S(1)} %get-tuple-element.24), channel_id=1, source_target_pairs={{1,0},{2,1},{3,2},{5,4},{6,5},{7,6},{9,8},{10,9},{11,10},{13,12},{... | collective-permute-start | bytes 30728 | tf_op jit(solution)/shard_map/ppermute | solution.py:15
  155.9 17.7 %copy-start.1 = (f32[8,32,128]{2,1,0:T(8,128)S(1)}, f32[8,32,128]{2,1,0:T(8,128)}, u32[]{:S(2)}) copy-start(f32[8,32,128]{2,1,0:T(8,128)} %param.9) | copy-start | bytes 393220
  155.9 17.7 %copy-start.2 = (f32[8,32,128]{2,1,0:T(8,128)S(1)}, f32[8,32,128]{2,1,0:T(8,128)}, u32[]{:S(2)}) copy-start(f32[8,32,128]{2,1,0:T(8,128)} %param.10) | copy-start | bytes 393220
  156.1 10.1 %collective-permute-start.4 = (f32[2,10,34,1]{3,2,1,0:T(8,128)S(1)}, f32[2,10,34,1]{3,2,1,0:T(8,128)S(1)}, u32[]{:S(2)}, u32[]{:S(2)}) collective-permute-start(f32[2,10,34,1]{3,2,1,0:T(8,128)S(1)} %get-tuple-element.21), channel_id=1, source_target_pairs={{0,4},{4,8},{8,12},{12,16},{16,20},{20,24},{24,28},{28,32},{32,36}... | collective-permute-start | bytes 8168 | tf_op jit(solution)/shard_map/ppermute | solution.py:12
  161.3 10.8 %collective-permute-start.5 = (f32[2,10,34,1]{3,2,1,0:T(8,128)S(1)}, f32[2,10,34,1]{3,2,1,0:T(8,128)S(1)}, u32[]{:S(2)}, u32[]{:S(2)}) collective-permute-start(f32[2,10,34,1]{3,2,1,0:T(8,128)S(1)} %get-tuple-element.22), channel_id=1, source_target_pairs={{4,0},{8,4},{12,8},{16,12},{20,16},{24,20},{28,24},{32,28},{36,32}... | collective-permute-start | bytes 8168 | tf_op jit(solution)/shard_map/ppermute | solution.py:15
  174.0 3.7 %collective-permute-start.6 = (f32[1,1,32,128]{3,2,1,0:T(8,128)S(1)}, f32[1,1,32,128]{3,2,1,0:T(8,128)S(1)}, u32[]{:S(2)}, u32[]{:S(2)}) collective-permute-start(f32[1,1,32,128]{3,2,1,0:T(8,128)S(1)} %get-tuple-element.33), channel_id=1, source_target_pairs={{0,128},{128,256},{256,384},{384,512},{512,640},{640,768},{768,896... | collective-permute-start | bytes 49160 | tf_op jit(solution)/shard_map/ppermute | solution.py:12
  176.4 4.5 %collective-permute-start.7 = (f32[1,1,32,128]{3,2,1,0:T(8,128)S(1)}, f32[1,1,32,128]{3,2,1,0:T(8,128)S(1)}, u32[]{:S(2)}, u32[]{:S(2)}) collective-permute-start(f32[1,1,32,128]{3,2,1,0:T(8,128)S(1)} %get-tuple-element.34), channel_id=1, source_target_pairs={{128,0},{256,128},{384,256},{512,384},{640,512},{768,640},{896,768... | collective-permute-start | bytes 49160 | tf_op jit(solution)/shard_map/ppermute | solution.py:15
  180.9 6.7 %collective-permute-start.8 = (f32[1,10,1,128]{3,2,1,0:T(1,128)S(1)}, f32[1,10,1,128]{3,2,1,0:T(1,128)S(1)}, u32[]{:S(2)}, u32[]{:S(2)}) collective-permute-start(f32[1,10,1,128]{3,2,1,0:T(1,128)S(1)} %get-tuple-element.31), channel_id=1, source_target_pairs={{0,1},{1,2},{2,3},{4,5},{5,6},{6,7},{8,9},{9,10},{10,11},{12,13},{... | collective-permute-start | bytes 15368 | tf_op jit(solution)/shard_map/ppermute | solution.py:12
  185.7 13.7 %collective-permute-start.9 = (f32[1,10,1,128]{3,2,1,0:T(1,128)S(1)}, f32[1,10,1,128]{3,2,1,0:T(1,128)S(1)}, u32[]{:S(2)}, u32[]{:S(2)}) collective-permute-start(f32[1,10,1,128]{3,2,1,0:T(1,128)S(1)} %get-tuple-element.32), channel_id=1, source_target_pairs={{1,0},{2,1},{3,2},{5,4},{6,5},{7,6},{9,8},{10,9},{11,10},{13,12},{... | collective-permute-start | bytes 15368 | tf_op jit(solution)/shard_map/ppermute | solution.py:15
  199.5 6.5 %collective-permute-start.10 = (f32[1,10,34,1]{3,2,1,0:T(8,128)S(1)}, f32[1,10,34,1]{3,2,1,0:T(8,128)S(1)}, u32[]{:S(2)}, u32[]{:S(2)}) collective-permute-start(f32[1,10,34,1]{3,2,1,0:T(8,128)S(1)} %get-tuple-element.27), channel_id=1, source_target_pairs={{0,4},{4,8},{8,12},{12,16},{16,20},{20,24},{24,28},{28,32},{32,36}... | collective-permute-start | bytes 4088 | tf_op jit(solution)/shard_map/ppermute | solution.py:12
  201.4 8.6 %collective-permute-start.11 = (f32[1,10,34,1]{3,2,1,0:T(8,128)S(1)}, f32[1,10,34,1]{3,2,1,0:T(8,128)S(1)}, u32[]{:S(2)}, u32[]{:S(2)}) collective-permute-start(f32[1,10,34,1]{3,2,1,0:T(8,128)S(1)} %get-tuple-element.28), channel_id=1, source_target_pairs={{4,0},{8,4},{12,8},{16,12},{20,16},{24,20},{28,24},{32,28},{36,32}... | collective-permute-start | bytes 4088 | tf_op jit(solution)/shard_map/ppermute | solution.py:15
Sparse Core Ops, SparseCore 0:
  11.7 101.2 all-gather.2
where the time goes:
time: 219 us; the launch traced here: 218 us
  waiting for transfers between devices  86.8 us (40%)
  blocking collectives  53.9 us (25%)
  starting transfers between devices  47.4 us (22%)
  between operations  15.8 us (7%)
  other arithmetic  7.7 us (4%)
  local copies, waits for them, and re-layouts  6.84 us (3%)
    unnamed x1, blocking collectives  53.9 us
    all_gather x1, waiting for transfers between devices, on_device(): box_list = lax.all_gather(moved_box[None], 'gy', axis=0, tiled=True)  43.1 us
    ppermute x6, waiting for transfers between devices, padded_2(): lax.ppermute(lax.slice_in_dim(block, 0, width, axis=dim), axis, backward)  39.9 us
    ppermute x6, starting transfers between devices, padded_2(): lax.ppermute(lax.slice_in_dim(block, block.shape[dim] - width, None, axis...  35.7 us
    ppermute x6, starting transfers between devices, padded_2(): lax.ppermute(lax.slice_in_dim(block, 0, width, axis=dim), axis, backward)  11.7 us
  transfers between devices with their start and end apart: 13, of which 9 were waited for; matrix products, arithmetic and copies ran while one was open for 2% of the time, Pallas kernels for 0%

commit v1 on v0

v1 whole, which is shorter than its diff:
```python
import jax
import jax.numpy as jnp
from jax import lax
from jax.experimental import pallas as pl
from jax.experimental.pallas import tpu as pltpu
from jax.sharding import PartitionSpec as P

LANES = 128
VMEM = pl.BlockSpec(memory_space=pltpu.VMEM)
SMEM = pl.BlockSpec(memory_space=pltpu.SMEM)
PARAMS = pltpu.CompilerParams(vmem_limit_bytes=24 * 1024 * 1024)
F32 = jnp.float32


def lane_of(shape):
    return lax.broadcasted_iota(jnp.int32, shape, len(shape) - 1)


def moved_slot(home_ref, slots):
    position = lax.axis_index("gy")
    slot = jnp.int32(0)
    target = jnp.int32(0)
    for j in range(slots):
        home = home_ref[j]
        leaves = home != position * slots + j
        slot = jnp.where(leaves, j, slot)
        target = jnp.where(leaves, home, target)
    return slot, target


def pack_kernel(home_ref, old_ref, send_ref):
    slots = home_ref.shape[0]
    width = LANES // slots
    rows = old_ref.shape[1] // slots
    slot, target = moved_slot(home_ref, slots)
    shape = (old_ref.shape[0], rows, LANES)
    group = lax.div(lane_of(shape), width)
    box = jnp.zeros(shape, F32)
    for g in range(slots):
        shift = lax.rem(width * (g - slot) + LANES, LANES)
        rolled = pltpu.roll(old_ref[:, g * rows : (g + 1) * rows, :], shift, 2)
        box = jnp.where(group == g, rolled, box)
    send_ref[...] = jnp.zeros(send_ref.shape, F32)
    send_ref[lax.div(target, slots)] = box


def write_y_faces(planes, low_ref, high_ref):
    low = high = jnp.zeros(low_ref.shape, F32)
    lane = lane_of(low_ref.shape)
    for i, plane in enumerate(planes):
        low = jnp.where(lane == i, pltpu.roll(plane, i, 1) if i else plane, low)
        high = jnp.where(lane == i, pltpu.roll(plane, i + 1, 1), high)
    low_ref[...] = low
    high_ref[...] = high


def place_kernel(
    home_ref, recv_ref, old_ref, conduct_ref, start_ref, xl_ref, xh_ref, zl_ref, zh_ref, yl_ref, yh_ref
):
    slots = home_ref.shape[0]
    width = LANES // slots
    nx, nz, _ = old_ref.shape
    rows = nz // slots
    slot, _ = moved_slot(home_ref, slots)
    arrived = recv_ref[0]
    for i in range(1, recv_ref.shape[0]):
        arrived = arrived + recv_ref[i]
    here = lax.div(lane_of(arrived.shape), width) == slot
    for g in range(slots):
        shift = lax.rem(width * (slot - g) + LANES, LANES)
        part = pl.ds(g * rows, rows)
        start_ref[:, part, :] = jnp.where(here, pltpu.roll(arrived, shift, 2), old_ref[:, part, :])
    for f, ref in enumerate((start_ref, conduct_ref)):
        xl_ref[f] = ref[0]
        xh_ref[f] = ref[nx - 1]
        zl_ref[f] = ref[:, 0, :]
        zh_ref[f] = ref[:, nz - 1, :]
    planes = [start_ref[x] for x in range(nx)] + [conduct_ref[x] for x in range(nx)]
    write_y_faces(planes, yl_ref, yh_ref)


def edges():
    flags = []
    for axis in ("gx", "gz", "gy"):
        index = lax.axis_index(axis)
        flags.append((index == 0, index == lax.axis_size(axis) - 1))
    return flags


def refine(coarse_ref):
    _, cz, cy = coarse_ref.shape
    left = lax.div(lax.broadcasted_iota(jnp.int32, (2 * cz, cz), 0), 2)
    left = (left == lax.broadcasted_iota(jnp.int32, (2 * cz, cz), 1)).astype(F32)
    right = lax.div(lax.broadcasted_iota(jnp.int32, (cy, 2 * cy), 1), 2)
    right = (right == lax.broadcasted_iota(jnp.int32, (cy, 2 * cy), 0)).astype(F32)
    planes = []
    for x in range(coarse_ref.shape[0]):
        wide = jnp.dot(
            coarse_ref[x], right, precision=lax.Precision.HIGHEST, preferred_element_type=F32
        )
        planes.append(
            jnp.dot(left, wide, precision=lax.Precision.HIGHEST, preferred_element_type=F32)
        )
    return planes


def beside(values, ghosts, x, nx, halo, flags):
    (x_first, x_last), (z_first, z_last), (y_first, y_last) = flags
    plane = values[x]
    ghost = ghosts[x]
    nz = plane.shape[0]
    row = lax.broadcasted_iota(jnp.int32, plane.shape, 0)
    lane = lane_of(plane.shape)
    xl, xh, zl, zh, yl, yh = halo
    below = values[x - 1] if x else jnp.where(x_first, ghost, xl)
    above = values[x + 1] if x < nx - 1 else jnp.where(x_last, ghost, xh)
    front = jnp.where(row == 0, jnp.where(z_first, ghost, zl[x : x + 1]), pltpu.roll(plane, 1, 0))
    back = jnp.where(
        row == nz - 1, jnp.where(z_last, ghost, zh[x : x + 1]), pltpu.roll(plane, nz - 1, 0)
    )
    left = jnp.where(lane == 0, jnp.where(y_first, ghost, yl(x)), pltpu.roll(plane, 1, 1))
    right = jnp.where(
        lane == LANES - 1, jnp.where(y_last, ghost, yh(x)), pltpu.roll(plane, LANES - 1, 1)
    )
    return below, above, front, back, left, right


def to_lane(packed, index, lane):
    shift = (lane - index) % LANES
    return pltpu.roll(packed, shift, 1) if shift else packed


def sweep_planes(refs, phi_planes, phi_halo):
    (start_ref, conduct_ref, source_ref, reaction_ref, coarse_ref, kappa_halo) = refs
    nx = start_ref.shape[0]
    flags = edges()
    refined = refine(coarse_ref)
    ghosts = [refined[x // 2] for x in range(nx)]
    kappas = [conduct_ref[x] for x in range(nx)]
    results = []
    for x in range(nx):
        numerator = start_ref[x] + source_ref[x]
        denominator = 1.0 + reaction_ref[x]
        phis = beside(phi_planes, ghosts, x, nx, phi_halo, flags)
        beside_kappas = beside(kappas, kappas, x, nx, kappa_halo, flags)
        for phi, kappa in zip(phis, beside_kappas):
            weight = 0.5 * (kappas[x] + kappa)
            numerator = numerator + weight * phi
            denominator = denominator + weight
        results.append(numerator / denominator)
    return results


def halo_of(xl, xh, zl, zh, yl, yh, offset):
    return (
        xl,
        xh,
        zl,
        zh,
        lambda x: to_lane(yl, offset + x, 0),
        lambda x: to_lane(yh, offset + x, LANES - 1),
    )


def first_kernel(
    start_ref, conduct_ref, source_ref, reaction_ref, coarse_ref,
    hxl, hxh, hzl, hzh, hyl, hyh,
    out_ref, xl_ref, xh_ref, zl_ref, zh_ref, yl_ref, yh_ref,
):
    nx, nz, _ = start_ref.shape
    ylow, yhigh = hyl[...], hyh[...]
    phi_halo = halo_of(hxl[0], hxh[0], hzl[0], hzh[0], ylow, yhigh, 0)
    kappa_halo = halo_of(hxl[1], hxh[1], hzl[1], hzh[1], ylow, yhigh, nx)
    refs = (start_ref, conduct_ref, source_ref, reaction_ref, coarse_ref, kappa_halo)
    planes = sweep_planes(refs, [start_ref[x] for x in range(nx)], phi_halo)
    for x, plane in enumerate(planes):
        out_ref[x] = plane
        zl_ref[x : x + 1] = plane[0:1]
        zh_ref[x : x + 1] = plane[nz - 1 : nz]
    xl_ref[...] = planes[0]
    xh_ref[...] = planes[nx - 1]
    write_y_faces(planes, yl_ref, yh_ref)


def second_kernel(
    first_ref, start_ref, conduct_ref, source_ref, reaction_ref, coarse_ref,
    kxl, kxh, kzl, kzh, kyl, kyh,
    hxl, hxh, hzl, hzh, hyl, hyh,
    out_ref,
):
    nx = start_ref.shape[0]
    phi_halo = halo_of(hxl[...], hxh[...], hzl[...], hzh[...], hyl[...], hyh[...], 0)
    kappa_halo = halo_of(kxl[1], kxh[1], kzl[1], kzh[1], kyl[...], kyh[...], nx)
    refs = (start_ref, conduct_ref, source_ref, reaction_ref, coarse_ref, kappa_halo)
    planes = sweep_planes(refs, [first_ref[x] for x in range(nx)], phi_halo)
    for x, plane in enumerate(planes):
        out_ref[x] = plane


def swap_faces(faces):
    halos = []
    for axis, low, high in (
        ("gx", faces[0], faces[1]),
        ("gz", faces[2], faces[3]),
        ("gy", faces[4], faces[5]),
    ):
        count = lax.axis_size(axis)
        forward = [(i, i + 1) for i in range(count - 1)]
        backward = [(b, a) for a, b in forward]
        halos.append(lax.ppermute(high, axis, forward))
        halos.append(lax.ppermute(low, axis, backward))
    return halos


def call(kernel, operands, outs, smem=0):
    specs = [SMEM] * smem + [VMEM] * (len(operands) - smem)
    return pl.pallas_call(
        kernel,
        out_shape=[jax.ShapeDtypeStruct(shape, F32) for shape in outs],
        in_specs=specs,
        out_specs=[VMEM] * len(outs),
        compiler_params=PARAMS,
    )(*operands)


def on_device(old_field, new_home, conduct, reaction, source, coarse):
    nx, nz, ny = old_field.shape
    home = new_home[0, 0]
    slots = home.shape[0]
    line = lax.axis_size("gy")
    (send,) = call(
        pack_kernel, (home, old_field), [(line, nx, nz // slots, ny)], smem=1
    )
    recv = lax.all_to_all(send, "gy", 0, 0, tiled=True)
    start, *faces = call(
        place_kernel,
        (home, recv, old_field, conduct),
        [old_field.shape]
        + [(2, nz, ny)] * 2
        + [(2, nx, ny)] * 2
        + [(nz, ny)] * 2,
        smem=1,
    )
    halos = swap_faces(faces)
    first, *faces = call(
        first_kernel,
        (start, conduct, source, reaction, coarse, *halos),
        [old_field.shape] + [(nz, ny)] * 2 + [(nx, ny)] * 2 + [(nz, ny)] * 2,
    )
    first_halos = swap_faces(faces)
    (relaxed,) = call(
        second_kernel,
        (first, start, conduct, source, reaction, coarse, *halos, *first_halos),
        [old_field.shape],
    )
    return relaxed


def solution(mesh):
    return jax.shard_map(
        on_device,
        mesh=mesh,
        in_specs=(P("gx", "gz", "gy"),) * 6,
        out_specs=P("gx", "gz", "gy"),
        check_vma=False,
    )
```

time: 219 us -> 121 us (0.55)
  the two profiles are of different devices: /device:TPU:7 before, /device:TPU:81 now
where the time goes in v1:
time: 121 us; the launch traced here: 120 us
  starting transfers between devices  53.3 us (44%)
  blocking collectives  36.4 us (30%)
  waiting for transfers between devices  24.8 us (20%)
  Pallas kernels  4.23 us (3%)
  local copies, waits for them, and re-layouts  1.57 us (1%)
    all_to_all x1, blocking collectives, on_device(): recv = lax.all_to_all(send, 'gy', 0, 0, tiled=True)  36.4 us
    ppermute x6, starting transfers between devices, swap_faces(): halos.append(lax.ppermute(high, axis, forward))  34.4 us
    ppermute x6, waiting for transfers between devices, swap_faces(): halos.append(lax.ppermute(low, axis, backward))  24 us
    ppermute x6, starting transfers between devices, swap_faces(): halos.append(lax.ppermute(low, axis, backward))  18.9 us
    pallas_call x4, Pallas kernels, call(): pl.pallas_call(kernel, out_shape=[jax.ShapeDtypeStruct(shape, F32) for sh...  4.23 us
  transfers between devices with their start and end apart: 12, of which 3 were waited for; matrix products, arithmetic and copies ran while one was open for 0% of the time, Pallas kernels for 0%

profile of v1, /device:TPU:81, one launch (start us, length us, event | category | flops | bytes accessed | tf_op | source)
XLA Modules:
  0.0 120.4 jit_solution(16434517110768096917)
XLA Ops:
  0.0 0.0 copy-start.5
  0.0 0.7 copy-done.5
  0.7 0.0 copy-start.1
  0.7 0.9 copy-done.1
  1.6 0.7 shard_map.64
  2.2 0.0 copy-start
  2.2 36.4 %all_to_all.5.recv_ref = f32[32,8,8,128]{3,2,1,0:T(8,128)S(1)} all-to-all(f32[32,8,8,128]{3,2,1,0:T(8,128)S(1)} %shard_map.64), channel_id=1, replica_groups=mesh['gx'=8,'gy'=32,'gz'=4] {'gy'}, dimensions={0} | all-to-all | bytes 2097152 | tf_op jit(solution)/shard_map/all_to_all | solution.py:234
  38.6 0.0 copy-done
  38.6 0.0 copy-start.2
  38.6 0.0 copy-start.3
  38.6 0.0 copy-start.4
  38.6 0.9 shard_map.65
  39.5 4.0 %collective-permute-start = (f32[2,32,128]{2,1,0:T(8,128)S(1)}, f32[2,32,128]{2,1,0:T(8,128)S(1)}, u32[]{:S(2)}, u32[]{:S(2)}) collective-permute-start(f32[2,32,128]{2,1,0:T(8,128)S(1)} %get-tuple-element.20), channel_id=1, source_target_pairs={{0,128},{128,256},{256,384},{384,512},{512,640},{640,768},{768,896... | collective-permute-start | bytes 98312 | tf_op jit(solution)/shard_map/ppermute | solution.py:210
  43.5 1.9 %collective-permute-start.1 = (f32[2,32,128]{2,1,0:T(8,128)S(1)}, f32[2,32,128]{2,1,0:T(8,128)S(1)}, u32[]{:S(2)}, u32[]{:S(2)}) collective-permute-start(f32[2,32,128]{2,1,0:T(8,128)S(1)} %get-tuple-element.21), channel_id=1, source_target_pairs={{128,0},{256,128},{384,256},{512,384},{640,512},{768,640},{896,768... | collective-permute-start | bytes 98312 | tf_op jit(solution)/shard_map/ppermute | solution.py:211
  45.5 20.4 %collective-permute-start.2 = (f32[2,8,128]{2,1,0:T(8,128)S(1)}, f32[2,8,128]{2,1,0:T(8,128)S(1)}, u32[]{:S(2)}, u32[]{:S(2)}) collective-permute-start(f32[2,8,128]{2,1,0:T(8,128)S(1)} %get-tuple-element.22), channel_id=1, source_target_pairs={{0,1},{1,2},{2,3},{4,5},{5,6},{6,7},{8,9},{9,10},{10,11},{12,13},{... | collective-permute-start | bytes 24584 | tf_op jit(solution)/shard_map/ppermute | solution.py:210
  65.9 1.9 %collective-permute-start.4 = (f32[32,128]{1,0:T(8,128)S(1)}, f32[32,128]{1,0:T(8,128)S(1)}, u32[]{:S(2)}, u32[]{:S(2)}) collective-permute-start(f32[32,128]{1,0:T(8,128)S(1)} %get-tuple-element.24), channel_id=1, source_target_pairs={{0,4},{4,8},{8,12},{12,16},{16,20},{20,24},{24,28},{28,32},{32,36}... | collective-permute-start | bytes 49160 | tf_op jit(solution)/shard_map/ppermute | solution.py:210
  67.8 5.5 %collective-permute-start.5 = (f32[32,128]{1,0:T(8,128)S(1)}, f32[32,128]{1,0:T(8,128)S(1)}, u32[]{:S(2)}, u32[]{:S(2)}) collective-permute-start(f32[32,128]{1,0:T(8,128)S(1)} %get-tuple-element.25), channel_id=1, source_target_pairs={{4,0},{8,4},{12,8},{16,12},{20,16},{24,20},{28,24},{32,28},{36,32}... | collective-permute-start | bytes 49160 | tf_op jit(solution)/shard_map/ppermute | solution.py:211
  73.3 0.0 collective-permute-done.2.hzl.kzl
  73.3 1.9 %collective-permute-start.3 = (f32[2,8,128]{2,1,0:T(8,128)S(1)}, f32[2,8,128]{2,1,0:T(8,128)S(1)}, u32[]{:S(2)}, u32[]{:S(2)}) collective-permute-start(f32[2,8,128]{2,1,0:T(8,128)S(1)} %get-tuple-element.23), channel_id=1, source_target_pairs={{1,0},{2,1},{3,2},{5,4},{6,5},{7,6},{9,8},{10,9},{11,10},{13,12},{... | collective-permute-start | bytes 24584 | tf_op jit(solution)/shard_map/ppermute | solution.py:211
  75.2 11.8 %collective-permute-done.3.hzh.kzh = f32[2,8,128]{2,1,0:T(8,128)S(1)} collective-permute-done((f32[2,8,128]{2,1,0:T(8,128)S(1)}, f32[2,8,128]{2,1,0:T(8,128)S(1)}, u32[]{:S(2)}, u32[]{:S(2)}) %collective-permute-start.3) | collective-permute-done | bytes 8224 | tf_op jit(solution)/shard_map/ppermute | solution.py:211
  87.0 0.0 collective-permute-done.4.hyl.kyl
  87.0 0.0 collective-permute-done.5.hyh.kyh
  87.0 0.0 collective-permute-done.hxl.kxl
  87.0 0.0 collective-permute-done.1.hxh.kxh
  87.0 0.0 copy-done.2
  87.0 0.0 copy-done.3
  87.0 0.0 copy-done.4
  87.0 1.1 shard_map.66
  88.1 3.1 %collective-permute-start.6 = (f32[32,128]{1,0:T(8,128)S(1)}, f32[32,128]{1,0:T(8,128)S(1)}, u32[]{:S(2)}, u32[]{:S(2)}) collective-permute-start(f32[32,128]{1,0:T(8,128)S(1)} %get-tuple-element.27), channel_id=1, source_target_pairs={{0,128},{128,256},{256,384},{384,512},{512,640},{640,768},{768,896... | collective-permute-start | bytes 49160 | tf_op jit(solution)/shard_map/ppermute | solution.py:210
  91.2 2.2 %collective-permute-start.7 = (f32[32,128]{1,0:T(8,128)S(1)}, f32[32,128]{1,0:T(8,128)S(1)}, u32[]{:S(2)}, u32[]{:S(2)}) collective-permute-start(f32[32,128]{1,0:T(8,128)S(1)} %get-tuple-element.28), channel_id=1, source_target_pairs={{128,0},{256,128},{384,256},{512,384},{640,512},{768,640},{896,768... | collective-permute-start | bytes 49160 | tf_op jit(solution)/shard_map/ppermute | solution.py:211
  93.4 1.9 %collective-permute-start.10 = (f32[32,128]{1,0:T(8,128)S(1)}, f32[32,128]{1,0:T(8,128)S(1)}, u32[]{:S(2)}, u32[]{:S(2)}) collective-permute-start(f32[32,128]{1,0:T(8,128)S(1)} %get-tuple-element.31), channel_id=1, source_target_pairs={{0,4},{4,8},{8,12},{12,16},{16,20},{20,24},{24,28},{28,32},{32,36}... | collective-permute-start | bytes 49160 | tf_op jit(solution)/shard_map/ppermute | solution.py:210
  95.3 5.5 %collective-permute-start.11 = (f32[32,128]{1,0:T(8,128)S(1)}, f32[32,128]{1,0:T(8,128)S(1)}, u32[]{:S(2)}, u32[]{:S(2)}) collective-permute-start(f32[32,128]{1,0:T(8,128)S(1)} %get-tuple-element.32), channel_id=1, source_target_pairs={{4,0},{8,4},{12,8},{16,12},{20,16},{24,20},{28,24},{32,28},{36,32}... | collective-permute-start | bytes 49160 | tf_op jit(solution)/shard_map/ppermute | solution.py:211
  100.8 3.1 %collective-permute-start.8 = (f32[8,128]{1,0:T(8,128)S(1)}, f32[8,128]{1,0:T(8,128)S(1)}, u32[]{:S(2)}, u32[]{:S(2)}) collective-permute-start(f32[8,128]{1,0:T(8,128)S(1)} %get-tuple-element.29), channel_id=1, source_target_pairs={{0,1},{1,2},{2,3},{4,5},{5,6},{6,7},{8,9},{9,10},{10,11},{12,13},{... | collective-permute-start | bytes 12296 | tf_op jit(solution)/shard_map/ppermute | solution.py:210
  103.9 0.7 collective-permute-done.8.hzl
  104.6 1.9 %collective-permute-start.9 = (f32[8,128]{1,0:T(8,128)S(1)}, f32[8,128]{1,0:T(8,128)S(1)}, u32[]{:S(2)}, u32[]{:S(2)}) collective-permute-start(f32[8,128]{1,0:T(8,128)S(1)} %get-tuple-element.30), channel_id=1, source_target_pairs={{1,0},{2,1},{3,2},{5,4},{6,5},{7,6},{9,8},{10,9},{11,10},{13,12},{... | collective-permute-start | bytes 12296 | tf_op jit(solution)/shard_map/ppermute | solution.py:211
  106.5 12.3 %collective-permute-done.9.hzh = f32[8,128]{1,0:T(8,128)S(1)} collective-permute-done((f32[8,128]{1,0:T(8,128)S(1)}, f32[8,128]{1,0:T(8,128)S(1)}, u32[]{:S(2)}, u32[]{:S(2)}) %collective-permute-start.9) | collective-permute-done | bytes 4128 | tf_op jit(solution)/shard_map/ppermute | solution.py:211
  118.8 0.0 collective-permute-done.6.hxl
  118.8 0.0 collective-permute-done.7.hxh
  118.8 0.0 collective-permute-done.10.hyl
  118.8 0.0 collective-permute-done.11.hyh
  118.8 1.6 %shard_map.67 = f32[8,32,128]{2,1,0:T(8,128)} custom-call(f32[8,32,128]{2,1,0:T(8,128)S(1)} %get-tuple-element.26.first_ref, f32[8,32,128]{2,1,0:T(8,128)S(1)} %get-tuple-element.19.start_ref, f32[8,32,128]{2,1,0:T(8,128)S(1)} %copy-done, f32[8,32,128]{2,1,0:T(8,128)S(1)} %copy-done.2, f32[8,32,128]{2,1,0:T(8,128)S(1)} %copy-done.3, ...), custom_call_target="tpu_custom_call" | custom-call | tf_op jit(solution)/shard_map/pallas_call | solution.py:217
Async XLA Ops:
  0.0 0.7 copy-start.5
  0.7 0.9 copy-start.1
  2.2 36.4 %copy-start = (f32[8,32,128]{2,1,0:T(8,128)S(1)}, f32[8,32,128]{2,1,0:T(8,128)}, u32[]{:S(2)}) copy-start(f32[8,32,128]{2,1,0:T(8,128)} %conduct_ref.5) | copy-start | bytes 393220
  38.6 48.4 %copy-start.2 = (f32[8,32,128]{2,1,0:T(8,128)S(1)}, f32[8,32,128]{2,1,0:T(8,128)}, u32[]{:S(2)}) copy-start(f32[8,32,128]{2,1,0:T(8,128)} %source_ref.3) | copy-start | bytes 393220
  38.6 48.4 %copy-start.3 = (f32[8,32,128]{2,1,0:T(8,128)S(1)}, f32[8,32,128]{2,1,0:T(8,128)}, u32[]{:S(2)}) copy-start(f32[8,32,128]{2,1,0:T(8,128)} %reaction_ref.3) | copy-start | bytes 393220
  38.6 48.4 %copy-start.4 = (f32[4,16,64]{2,1,0:T(8,128)S(1)}, f32[4,16,64]{2,1,0:T(8,128)}, u32[]{:S(2)}) copy-start(f32[4,16,64]{2,1,0:T(8,128)} %coarse_ref.3) | copy-start | bytes 49156
  39.5 47.5 %collective-permute-start = (f32[2,32,128]{2,1,0:T(8,128)S(1)}, f32[2,32,128]{2,1,0:T(8,128)S(1)}, u32[]{:S(2)}, u32[]{:S(2)}) collective-permute-start(f32[2,32,128]{2,1,0:T(8,128)S(1)} %get-tuple-element.20), channel_id=1, source_target_pairs={{0,128},{128,256},{256,384},{384,512},{512,640},{640,768},{768,896... | collective-permute-start | bytes 98312 | tf_op jit(solution)/shard_map/ppermute | solution.py:210
  43.5 43.5 %collective-permute-start.1 = (f32[2,32,128]{2,1,0:T(8,128)S(1)}, f32[2,32,128]{2,1,0:T(8,128)S(1)}, u32[]{:S(2)}, u32[]{:S(2)}) collective-permute-start(f32[2,32,128]{2,1,0:T(8,128)S(1)} %get-tuple-element.21), channel_id=1, source_target_pairs={{128,0},{256,128},{384,256},{512,384},{640,512},{768,640},{896,768... | collective-permute-start | bytes 98312 | tf_op jit(solution)/shard_map/ppermute | solution.py:211
  45.5 27.8 %collective-permute-start.2 = (f32[2,8,128]{2,1,0:T(8,128)S(1)}, f32[2,8,128]{2,1,0:T(8,128)S(1)}, u32[]{:S(2)}, u32[]{:S(2)}) collective-permute-start(f32[2,8,128]{2,1,0:T(8,128)S(1)} %get-tuple-element.22), channel_id=1, source_target_pairs={{0,1},{1,2},{2,3},{4,5},{5,6},{6,7},{8,9},{9,10},{10,11},{12,13},{... | collective-permute-start | bytes 24584 | tf_op jit(solution)/shard_map/ppermute | solution.py:210
  65.9 21.1 %collective-permute-start.4 = (f32[32,128]{1,0:T(8,128)S(1)}, f32[32,128]{1,0:T(8,128)S(1)}, u32[]{:S(2)}, u32[]{:S(2)}) collective-permute-start(f32[32,128]{1,0:T(8,128)S(1)} %get-tuple-element.24), channel_id=1, source_target_pairs={{0,4},{4,8},{8,12},{12,16},{16,20},{20,24},{24,28},{28,32},{32,36}... | collective-permute-start | bytes 49160 | tf_op jit(solution)/shard_map/ppermute | solution.py:210
  67.8 19.2 %collective-permute-start.5 = (f32[32,128]{1,0:T(8,128)S(1)}, f32[32,128]{1,0:T(8,128)S(1)}, u32[]{:S(2)}, u32[]{:S(2)}) collective-permute-start(f32[32,128]{1,0:T(8,128)S(1)} %get-tuple-element.25), channel_id=1, source_target_pairs={{4,0},{8,4},{12,8},{16,12},{20,16},{24,20},{28,24},{32,28},{36,32}... | collective-permute-start | bytes 49160 | tf_op jit(solution)/shard_map/ppermute | solution.py:211
  73.3 13.7 %collective-permute-start.3 = (f32[2,8,128]{2,1,0:T(8,128)S(1)}, f32[2,8,128]{2,1,0:T(8,128)S(1)}, u32[]{:S(2)}, u32[]{:S(2)}) collective-permute-start(f32[2,8,128]{2,1,0:T(8,128)S(1)} %get-tuple-element.23), channel_id=1, source_target_pairs={{1,0},{2,1},{3,2},{5,4},{6,5},{7,6},{9,8},{10,9},{11,10},{13,12},{... | collective-permute-start | bytes 24584 | tf_op jit(solution)/shard_map/ppermute | solution.py:211
  88.1 30.7 %collective-permute-start.6 = (f32[32,128]{1,0:T(8,128)S(1)}, f32[32,128]{1,0:T(8,128)S(1)}, u32[]{:S(2)}, u32[]{:S(2)}) collective-permute-start(f32[32,128]{1,0:T(8,128)S(1)} %get-tuple-element.27), channel_id=1, source_target_pairs={{0,128},{128,256},{256,384},{384,512},{512,640},{640,768},{768,896... | collective-permute-start | bytes 49160 | tf_op jit(solution)/shard_map/ppermute | solution.py:210
  91.2 27.6 %collective-permute-start.7 = (f32[32,128]{1,0:T(8,128)S(1)}, f32[32,128]{1,0:T(8,128)S(1)}, u32[]{:S(2)}, u32[]{:S(2)}) collective-permute-start(f32[32,128]{1,0:T(8,128)S(1)} %get-tuple-element.28), channel_id=1, source_target_pairs={{128,0},{256,128},{384,256},{512,384},{640,512},{768,640},{896,768... | collective-permute-start | bytes 49160 | tf_op jit(solution)/shard_map/ppermute | solution.py:211
  93.4 25.4 %collective-permute-start.10 = (f32[32,128]{1,0:T(8,128)S(1)}, f32[32,128]{1,0:T(8,128)S(1)}, u32[]{:S(2)}, u32[]{:S(2)}) collective-permute-start(f32[32,128]{1,0:T(8,128)S(1)} %get-tuple-element.31), channel_id=1, source_target_pairs={{0,4},{4,8},{8,12},{12,16},{16,20},{20,24},{24,28},{28,32},{32,36}... | collective-permute-start | bytes 49160 | tf_op jit(solution)/shard_map/ppermute | solution.py:210
  95.3 23.5 %collective-permute-start.11 = (f32[32,128]{1,0:T(8,128)S(1)}, f32[32,128]{1,0:T(8,128)S(1)}, u32[]{:S(2)}, u32[]{:S(2)}) collective-permute-start(f32[32,128]{1,0:T(8,128)S(1)} %get-tuple-element.32), channel_id=1, source_target_pairs={{4,0},{8,4},{12,8},{16,12},{20,16},{24,20},{28,24},{32,28},{36,32}... | collective-permute-start | bytes 49160 | tf_op jit(solution)/shard_map/ppermute | solution.py:211
  100.8 3.8 %collective-permute-start.8 = (f32[8,128]{1,0:T(8,128)S(1)}, f32[8,128]{1,0:T(8,128)S(1)}, u32[]{:S(2)}, u32[]{:S(2)}) collective-permute-start(f32[8,128]{1,0:T(8,128)S(1)} %get-tuple-element.29), channel_id=1, source_target_pairs={{0,1},{1,2},{2,3},{4,5},{5,6},{6,7},{8,9},{9,10},{10,11},{12,13},{... | collective-permute-start | bytes 12296 | tf_op jit(solution)/shard_map/ppermute | solution.py:210
  104.6 14.2 %collective-permute-start.9 = (f32[8,128]{1,0:T(8,128)S(1)}, f32[8,128]{1,0:T(8,128)S(1)}, u32[]{:S(2)}, u32[]{:S(2)}) collective-permute-start(f32[8,128]{1,0:T(8,128)S(1)} %get-tuple-element.30), channel_id=1, source_target_pairs={{1,0},{2,1},{3,2},{5,4},{6,5},{7,6},{9,8},{10,9},{11,10},{13,12},{... | collective-permute-start | bytes 12296 | tf_op jit(solution)/shard_map/ppermute | solution.py:211

commit v2 on v1

--- a/solution.py
+++ b/solution.py
@@ -6,6 +6,7 @@
 from jax.sharding import PartitionSpec as P
 
 LANES = 128
+RUN = 4
 VMEM = pl.BlockSpec(memory_space=pltpu.VMEM)
 SMEM = pl.BlockSpec(memory_space=pltpu.SMEM)
 PARAMS = pltpu.CompilerParams(vmem_limit_bytes=24 * 1024 * 1024)
@@ -28,11 +29,12 @@
     return slot, target
 
 
-def pack_kernel(home_ref, old_ref, send_ref):
+def split_kernel(home_ref, old_ref, parts_ref):
     slots = home_ref.shape[0]
     width = LANES // slots
     rows = old_ref.shape[1] // slots
     slot, target = moved_slot(home_ref, slots)
+    count, planes = parts_ref.shape[0], parts_ref.shape[1] - 1
     shape = (old_ref.shape[0], rows, LANES)
     group = lax.div(lane_of(shape), width)
     box = jnp.zeros(shape, F32)
@@ -40,43 +42,72 @@
         shift = lax.rem(width * (g - slot) + LANES, LANES)
         rolled = pltpu.roll(old_ref[:, g * rows : (g + 1) * rows, :], shift, 2)
         box = jnp.where(group == g, rolled, box)
-    send_ref[...] = jnp.zeros(send_ref.shape, F32)
-    send_ref[lax.div(target, slots)] = box
-
-
-def write_y_faces(planes, low_ref, high_ref):
-    low = high = jnp.zeros(low_ref.shape, F32)
-    lane = lane_of(low_ref.shape)
+    tag = jnp.full((rows, LANES), lax.div(target, slots), jnp.int32).astype(F32)
+    for k in range(count):
+        parts_ref[k, :planes] = box[k * planes : (k + 1) * planes]
+        parts_ref[k, planes] = tag
+
+
+def address_kernel(parts_ref, send_ref):
+    planes = send_ref.shape[1]
+    for device in range(send_ref.shape[0]):
+        for i in range(planes):
+            value = jnp.zeros(send_ref.shape[2:], F32)
+            for k in range(parts_ref.shape[0]):
+                value = jnp.where(parts_ref[k, planes] == device, parts_ref[k, i], value)
+            send_ref[device, i] = value
+
+
+def is_even(axis):
+    return lax.rem(lax.axis_index(axis), 2) == 0
+
+
+def write_pair(axis, first_ref, second_ref, index, low, high):
+    even = is_even(axis)
+    first_ref[index] = jnp.where(even, high, low)
+    second_ref[index] = jnp.where(even, low, high)
+
+
+def read_pair(axis, first, second):
+    even = is_even(axis)
+    return jnp.where(even, second, first), jnp.where(even, first, second)
+
+
+def write_y_pair(planes, first_ref, second_ref):
+    low = high = jnp.zeros(first_ref.shape, F32)
+    lane = lane_of(first_ref.shape)
     for i, plane in enumerate(planes):
         low = jnp.where(lane == i, pltpu.roll(plane, i, 1) if i else plane, low)
         high = jnp.where(lane == i, pltpu.roll(plane, i + 1, 1), high)
-    low_ref[...] = low
-    high_ref[...] = high
+    write_pair("gy", first_ref, second_ref, Ellipsis, low, high)
 
 
 def place_kernel(
-    home_ref, recv_ref, old_ref, conduct_ref, start_ref, xl_ref, xh_ref, zl_ref, zh_ref, yl_ref, yh_ref
+    home_ref, recv_ref, old_ref, conduct_ref, start_ref, xa_ref, xb_ref, za_ref, zb_ref, ya_ref, yb_ref
 ):
     slots = home_ref.shape[0]
     width = LANES // slots
     nx, nz, _ = old_ref.shape
     rows = nz // slots
     slot, _ = moved_slot(home_ref, slots)
-    arrived = recv_ref[0]
-    for i in range(1, recv_ref.shape[0]):
-        arrived = arrived + recv_ref[i]
-    here = lax.div(lane_of(arrived.shape), width) == slot
-    for g in range(slots):
-        shift = lax.rem(width * (slot - g) + LANES, LANES)
-        part = pl.ds(g * rows, rows)
-        start_ref[:, part, :] = jnp.where(here, pltpu.roll(arrived, shift, 2), old_ref[:, part, :])
+    planes = recv_ref.shape[1]
+    run = nx // planes
+    here = lax.div(lane_of((rows, LANES)), width) == slot
+    for k in range(run):
+        for i in range(planes):
+            x = k * planes + i
+            arrived = recv_ref[k, i]
+            for source in range(k + run, recv_ref.shape[0], run):
+                arrived = arrived + recv_ref[source, i]
+            for g in range(slots):
+                shift = lax.rem(width * (slot - g) + LANES, LANES)
+                part = pl.ds(g * rows, rows)
+                start_ref[x, part, :] = jnp.where(here, pltpu.roll(arrived, shift, 1), old_ref[x, part, :])
     for f, ref in enumerate((start_ref, conduct_ref)):
-        xl_ref[f] = ref[0]
-        xh_ref[f] = ref[nx - 1]
-        zl_ref[f] = ref[:, 0, :]
-        zh_ref[f] = ref[:, nz - 1, :]
+        write_pair("gx", xa_ref, xb_ref, f, ref[0], ref[nx - 1])
+        write_pair("gz", za_ref, zb_ref, f, ref[:, 0, :], ref[:, nz - 1, :])
     planes = [start_ref[x] for x in range(nx)] + [conduct_ref[x] for x in range(nx)]
-    write_y_faces(planes, yl_ref, yh_ref)
+    write_y_pair(planes, ya_ref, yb_ref)
 
 
 def edges():
@@ -151,7 +182,11 @@
     return results
 
 
-def halo_of(xl, xh, zl, zh, yl, yh, offset):
+def halo_of(halos, offset, index=Ellipsis):
+    xa, xb, za, zb, ya, yb = halos
+    xl, xh = read_pair("gx", xa[index], xb[index])
+    zl, zh = read_pair("gz", za[index], zb[index])
+    yl, yh = read_pair("gy", ya[...], yb[...])
     return (
         xl,
         xh,
@@ -163,34 +198,28 @@
 
 
 def first_kernel(
-    start_ref, conduct_ref, source_ref, reaction_ref, coarse_ref,
-    hxl, hxh, hzl, hzh, hyl, hyh,
-    out_ref, xl_ref, xh_ref, zl_ref, zh_ref, yl_ref, yh_ref,
+    start_ref, conduct_ref, source_ref, reaction_ref, coarse_ref, *rest
 ):
+    halos, out_ref, (xa_ref, xb_ref, za_ref, zb_ref, ya_ref, yb_ref) = rest[:6], rest[6], rest[7:]
     nx, nz, _ = start_ref.shape
-    ylow, yhigh = hyl[...], hyh[...]
-    phi_halo = halo_of(hxl[0], hxh[0], hzl[0], hzh[0], ylow, yhigh, 0)
-    kappa_halo = halo_of(hxl[1], hxh[1], hzl[1], hzh[1], ylow, yhigh, nx)
+    phi_halo = halo_of(halos, 0, 0)
+    kappa_halo = halo_of(halos, nx, 1)
     refs = (start_ref, conduct_ref, source_ref, reaction_ref, coarse_ref, kappa_halo)
     planes = sweep_planes(refs, [start_ref[x] for x in range(nx)], phi_halo)
     for x, plane in enumerate(planes):
         out_ref[x] = plane
-        zl_ref[x : x + 1] = plane[0:1]
-        zh_ref[x : x + 1] = plane[nz - 1 : nz]
-    xl_ref[...] = planes[0]
-    xh_ref[...] = planes[nx - 1]
-    write_y_faces(planes, yl_ref, yh_ref)
+        write_pair("gz", za_ref, zb_ref, slice(x, x + 1), plane[0:1], plane[nz - 1 : nz])
+    write_pair("gx", xa_ref, xb_ref, Ellipsis, planes[0], planes[nx - 1])
+    write_y_pair(planes, ya_ref, yb_ref)
 
 
 def second_kernel(
-    first_ref, start_ref, conduct_ref, source_ref, reaction_ref, coarse_ref,
-    kxl, kxh, kzl, kzh, kyl, kyh,
-    hxl, hxh, hzl, hzh, hyl, hyh,
-    out_ref,
+    first_ref, start_ref, conduct_ref, source_ref, reaction_ref, coarse_ref, *rest
 ):
+    halos, first_halos, out_ref = rest[:6], rest[6:12], rest[12]
     nx = start_ref.shape[0]
-    phi_halo = halo_of(hxl[...], hxh[...], hzl[...], hzh[...], hyl[...], hyh[...], 0)
-    kappa_halo = halo_of(kxl[1], kxh[1], kzl[1], kzh[1], kyl[...], kyh[...], nx)
+    phi_halo = halo_of(first_halos, 0)
+    kappa_halo = halo_of(halos, nx, 1)
     refs = (start_ref, conduct_ref, source_ref, reaction_ref, coarse_ref, kappa_halo)
     planes = sweep_planes(refs, [first_ref[x] for x in range(nx)], phi_halo)
     for x, plane in enumerate(planes):
@@ -199,16 +228,13 @@
 
 def swap_faces(faces):
     halos = []
-    for axis, low, high in (
-        ("gx", faces[0], faces[1]),
-        ("gz", faces[2], faces[3]),
-        ("gy", faces[4], faces[5]),
-    ):
+    for i, axis in enumerate(("gx", "gz", "gy")):
         count = lax.axis_size(axis)
-        forward = [(i, i + 1) for i in range(count - 1)]
-        backward = [(b, a) for a, b in forward]
-        halos.append(lax.ppermute(high, axis, forward))
-        halos.append(lax.ppermute(low, axis, backward))
+        for j in range(2):
+            pairs = []
+            for low in range(j, count - 1, 2):
+                pairs += [(low, low + 1), (low + 1, low)]
+            halos.append(lax.ppermute(faces[2 * i + j], axis, pairs))
     return halos
 
 
@@ -228,9 +254,14 @@
     home = new_home[0, 0]
     slots = home.shape[0]
     line = lax.axis_size("gy")
-    (send,) = call(
-        pack_kernel, (home, old_field), [(line, nx, nz // slots, ny)], smem=1
-    )
+    run = RUN
+    part = nx // run
+    (parts,) = call(
+        split_kernel, (home, old_field), [(run, part + 1, nz // slots, ny)], smem=1
+    )
+    groups = [[i * run + k for k in range(run)] for i in range(line // run)]
+    parts = lax.all_to_all(parts, "gy", 0, 0, tiled=True, axis_index_groups=groups)
+    (send,) = call(address_kernel, (parts,), [(line, part, nz // slots, ny)])
     recv = lax.all_to_all(send, "gy", 0, 0, tiled=True)
     start, *faces = call(
         place_kernel,

time: 121 us -> 101 us (0.83)
  the two profiles are of different devices: /device:TPU:81 before, /device:TPU:73 now
where the time goes in v2:
time: 101 us; the launch traced here: 100 us
  starting transfers between devices  64.2 us (64%)
  blocking collectives  26 us (26%)
  Pallas kernels  4.23 us (4%)
  waiting for transfers between devices  3.86 us (4%)
  local copies, waits for them, and re-layouts  1.58 us (2%)
    ppermute x12, starting transfers between devices, swap_faces(): halos.append(lax.ppermute(faces[2 * i + j], axis, pairs))  64.2 us
    all_to_all x1, blocking collectives, on_device(): recv = lax.all_to_all(send, 'gy', 0, 0, tiled=True)  17.8 us
    all_to_all x1, blocking collectives, on_device(): lax.all_to_all(parts, 'gy', 0, 0, tiled=True, axis_index_groups=groups)  8.2 us
    pallas_call x5, Pallas kernels, call(): pl.pallas_call(kernel, out_shape=[jax.ShapeDtypeStruct(shape, F32) for sh...  4.23 us
    ppermute x12, waiting for transfers between devices, swap_faces(): halos.append(lax.ppermute(faces[2 * i + j], axis, pairs))  3.86 us
  transfers between devices with their start and end apart: 12, of which 3 were waited for; matrix products, arithmetic and copies ran while one was open for 0% of the time, Pallas kernels for 0%

profile of v2, /device:TPU:73, one launch (start us, length us, event | category | flops | bytes accessed | tf_op | source)
XLA Modules:
  0.0 100.1 jit_solution(11813448186929505225)
XLA Ops:
  0.0 0.0 copy-start.6
  0.0 0.7 copy-done.6
  0.7 0.0 copy-start.1
  0.7 0.9 copy-done.1
  1.6 0.6 shard_map.64
  2.2 8.2 %all_to_all.10.parts_ref = f32[4,3,8,128]{3,2,1,0:T(8,128)S(1)} all-to-all(f32[4,3,8,128]{3,2,1,0:T(8,128)S(1)} %shard_map.64), channel_id=1, replica_groups={{0,4,8,12},{16,20,24,28},{32,36,40,44},{48,52,56,60},{64,68,72,76},{80,..., dimensions={0} | all-to-all | bytes 98304 | tf_op jit(solution)/shard_map/all_to_all | solution.py:263
  10.4 0.1 shard_map.65
  10.5 0.0 copy-start
  10.5 0.0 copy-start.2
  10.5 17.8 %all_to_all.11.recv_ref = f32[32,2,8,128]{3,2,1,0:T(8,128)S(1)} all-to-all(f32[32,2,8,128]{3,2,1,0:T(8,128)S(1)} %shard_map.65), channel_id=1, replica_groups=mesh['gx'=8,'gy'=32,'gz'=4] {'gy'}, dimensions={0} | all-to-all | bytes 524288 | tf_op jit(solution)/shard_map/all_to_all | solution.py:265
  28.3 0.0 copy-done
  28.3 0.0 copy-done.2
  28.3 0.0 copy-start.3
  28.3 0.0 copy-start.4
  28.3 0.0 copy-start.5
  28.3 0.8 shard_map.66
  29.2 1.9 %collective-permute-start = (f32[2,32,128]{2,1,0:T(8,128)S(1)}, f32[2,32,128]{2,1,0:T(8,128)S(1)}, u32[]{:S(2)}, u32[]{:S(2)}) collective-permute-start(f32[2,32,128]{2,1,0:T(8,128)S(1)} %get-tuple-element.20), channel_id=1, source_target_pairs={{0,128},{128,0},{256,384},{384,256},{512,640},{640,512},{768,896},... | collective-permute-start | bytes 98312 | tf_op jit(solution)/shard_map/ppermute | solution.py:237
  31.1 6.1 %collective-permute-start.1 = (f32[2,32,128]{2,1,0:T(8,128)S(1)}, f32[2,32,128]{2,1,0:T(8,128)S(1)}, u32[]{:S(2)}, u32[]{:S(2)}) collective-permute-start(f32[2,32,128]{2,1,0:T(8,128)S(1)} %get-tuple-element.21), channel_id=1, source_target_pairs={{128,256},{256,128},{384,512},{512,384},{640,768},{768,640},{129,2... | collective-permute-start | bytes 98312 | tf_op jit(solution)/shard_map/ppermute | solution.py:237
  37.2 6.6 %collective-permute-start.2 = (f32[2,8,128]{2,1,0:T(8,128)S(1)}, f32[2,8,128]{2,1,0:T(8,128)S(1)}, u32[]{:S(2)}, u32[]{:S(2)}) collective-permute-start(f32[2,8,128]{2,1,0:T(8,128)S(1)} %get-tuple-element.22), channel_id=1, source_target_pairs={{0,1},{1,0},{2,3},{3,2},{4,5},{5,4},{6,7},{7,6},{8,9},{9,8},{10,11... | collective-permute-start | bytes 24584 | tf_op jit(solution)/shard_map/ppermute | solution.py:237
  43.9 2.1 %collective-permute-start.4 = (f32[32,128]{1,0:T(8,128)S(1)}, f32[32,128]{1,0:T(8,128)S(1)}, u32[]{:S(2)}, u32[]{:S(2)}) collective-permute-start(f32[32,128]{1,0:T(8,128)S(1)} %get-tuple-element.24), channel_id=1, source_target_pairs={{0,4},{4,0},{8,12},{12,8},{16,20},{20,16},{24,28},{28,24},{32,36},... | collective-permute-start | bytes 49160 | tf_op jit(solution)/shard_map/ppermute | solution.py:237
  46.0 3.7 %collective-permute-start.5 = (f32[32,128]{1,0:T(8,128)S(1)}, f32[32,128]{1,0:T(8,128)S(1)}, u32[]{:S(2)}, u32[]{:S(2)}) collective-permute-start(f32[32,128]{1,0:T(8,128)S(1)} %get-tuple-element.25), channel_id=1, source_target_pairs={{4,8},{8,4},{12,16},{16,12},{20,24},{24,20},{28,32},{32,28},{36,40... | collective-permute-start | bytes 49160 | tf_op jit(solution)/shard_map/ppermute | solution.py:237
  49.7 0.0 collective-permute-done.2.rest_2_
  49.7 16.1 %collective-permute-start.3 = (f32[2,8,128]{2,1,0:T(8,128)S(1)}, f32[2,8,128]{2,1,0:T(8,128)S(1)}, u32[]{:S(2)}, u32[]{:S(2)}) collective-permute-start(f32[2,8,128]{2,1,0:T(8,128)S(1)} %get-tuple-element.23), channel_id=1, source_target_pairs={{1,2},{2,1},{5,6},{6,5},{9,10},{10,9},{13,14},{14,13},{17,18},{18,... | collective-permute-start | bytes 24584 | tf_op jit(solution)/shard_map/ppermute | solution.py:237
  65.8 1.4 %collective-permute-done.3.rest_3_ = f32[2,8,128]{2,1,0:T(8,128)S(1)} collective-permute-done((f32[2,8,128]{2,1,0:T(8,128)S(1)}, f32[2,8,128]{2,1,0:T(8,128)S(1)}, u32[]{:S(2)}, u32[]{:S(2)}) %collective-permute-start.3) | collective-permute-done | bytes 8224 | tf_op jit(solution)/shard_map/ppermute | solution.py:237
  67.3 0.0 collective-permute-done.4.rest_4_
  67.3 0.0 collective-permute-done.5.rest_5_
  67.3 0.0 collective-permute-done.rest_0_
  67.3 0.0 collective-permute-done.1.rest_1_
  67.3 0.0 copy-done.3
  67.3 0.0 copy-done.4
  67.3 0.0 copy-done.5
  67.3 1.1 %shard_map.67 = (f32[8,32,128]{2,1,0:T(8,128)S(1)}, f32[32,128]{1,0:T(8,128)S(1)}, f32[32,128]{1,0:T(8,128)S(1)}, f32[8,128]{1,0:T(8,128)S(1)}, f32[8,128]{1,0:T...) custom-call(f32[8,32,128]{2,1,0:T(8,128)S(1)} %get-tuple-element.19.start_ref, f32[8,32,128]{2,1,0:T(8,128)S(1)} %copy-done, ...), custom_call_target="tpu_custom_call" | custom-call | tf_op jit(solution)/shard_map/pallas_call | solution.py:243
  68.4 1.9 %collective-permute-start.6 = (f32[32,128]{1,0:T(8,128)S(1)}, f32[32,128]{1,0:T(8,128)S(1)}, u32[]{:S(2)}, u32[]{:S(2)}) collective-permute-start(f32[32,128]{1,0:T(8,128)S(1)} %get-tuple-element.27), channel_id=1, source_target_pairs={{0,128},{128,0},{256,384},{384,256},{512,640},{640,512},{768,896},... | collective-permute-start | bytes 49160 | tf_op jit(solution)/shard_map/ppermute | solution.py:237
  70.3 4.3 %collective-permute-start.7 = (f32[32,128]{1,0:T(8,128)S(1)}, f32[32,128]{1,0:T(8,128)S(1)}, u32[]{:S(2)}, u32[]{:S(2)}) collective-permute-start(f32[32,128]{1,0:T(8,128)S(1)} %get-tuple-element.28), channel_id=1, source_target_pairs={{128,256},{256,128},{384,512},{512,384},{640,768},{768,640},{129,2... | collective-permute-start | bytes 49160 | tf_op jit(solution)/shard_map/ppermute | solution.py:237
  74.6 1.9 %collective-permute-start.10 = (f32[32,128]{1,0:T(8,128)S(1)}, f32[32,128]{1,0:T(8,128)S(1)}, u32[]{:S(2)}, u32[]{:S(2)}) collective-permute-start(f32[32,128]{1,0:T(8,128)S(1)} %get-tuple-element.31), channel_id=1, source_target_pairs={{0,4},{4,0},{8,12},{12,8},{16,20},{20,16},{24,28},{28,24},{32,36},... | collective-permute-start | bytes 49160 | tf_op jit(solution)/shard_map/ppermute | solution.py:237
  76.5 4.1 %collective-permute-start.11 = (f32[32,128]{1,0:T(8,128)S(1)}, f32[32,128]{1,0:T(8,128)S(1)}, u32[]{:S(2)}, u32[]{:S(2)}) collective-permute-start(f32[32,128]{1,0:T(8,128)S(1)} %get-tuple-element.32), channel_id=1, source_target_pairs={{4,8},{8,4},{12,16},{16,12},{20,24},{24,20},{28,32},{32,28},{36,40... | collective-permute-start | bytes 49160 | tf_op jit(solution)/shard_map/ppermute | solution.py:237
  80.6 1.9 %collective-permute-start.8 = (f32[8,128]{1,0:T(8,128)S(1)}, f32[8,128]{1,0:T(8,128)S(1)}, u32[]{:S(2)}, u32[]{:S(2)}) collective-permute-start(f32[8,128]{1,0:T(8,128)S(1)} %get-tuple-element.29), channel_id=1, source_target_pairs={{0,1},{1,0},{2,3},{3,2},{4,5},{5,4},{6,7},{7,6},{8,9},{9,8},{10,11... | collective-permute-start | bytes 12296 | tf_op jit(solution)/shard_map/ppermute | solution.py:237
  82.6 1.1 %collective-permute-done.8.rest_8_ = f32[8,128]{1,0:T(8,128)S(1)} collective-permute-done((f32[8,128]{1,0:T(8,128)S(1)}, f32[8,128]{1,0:T(8,128)S(1)}, u32[]{:S(2)}, u32[]{:S(2)}) %collective-permute-start.8) | collective-permute-done | bytes 4128 | tf_op jit(solution)/shard_map/ppermute | solution.py:237
  83.7 13.4 %collective-permute-start.9 = (f32[8,128]{1,0:T(8,128)S(1)}, f32[8,128]{1,0:T(8,128)S(1)}, u32[]{:S(2)}, u32[]{:S(2)}) collective-permute-start(f32[8,128]{1,0:T(8,128)S(1)} %get-tuple-element.30), channel_id=1, source_target_pairs={{1,2},{2,1},{5,6},{6,5},{9,10},{10,9},{13,14},{14,13},{17,18},{18,... | collective-permute-start | bytes 12296 | tf_op jit(solution)/shard_map/ppermute | solution.py:237
  97.2 1.3 %collective-permute-done.9.rest_9_ = f32[8,128]{1,0:T(8,128)S(1)} collective-permute-done((f32[8,128]{1,0:T(8,128)S(1)}, f32[8,128]{1,0:T(8,128)S(1)}, u32[]{:S(2)}, u32[]{:S(2)}) %collective-permute-start.9) | collective-permute-done | bytes 4128 | tf_op jit(solution)/shard_map/ppermute | solution.py:237
  98.4 0.0 collective-permute-done.6.rest_6_
  98.4 0.0 collective-permute-done.7.rest_7_
  98.4 0.0 collective-permute-done.10.rest_10_
  98.5 0.0 collective-permute-done.11.rest_11_
  98.5 1.6 %shard_map.68 = f32[8,32,128]{2,1,0:T(8,128)} custom-call(f32[8,32,128]{2,1,0:T(8,128)S(1)} %get-tuple-element.26.first_ref, f32[8,32,128]{2,1,0:T(8,128)S(1)} %get-tuple-element.19.start_ref, f32[8,32,128]{2,1,0:T(8,128)S(1)} %copy-done, f32[8,32,128]{2,1,0:T(8,128)S(1)} %copy-done.3, f32[8,32,128]{2,1,0:T(8,128)S(1)} %copy-done.4, ...), custom_call_target="tpu_custom_call" | custom-call | tf_op jit(solution)/shard_map/pallas_call | solution.py:243
Async XLA Ops:
  0.0 0.7 copy-start.6
  0.7 0.9 copy-start.1
  10.5 17.8 %copy-start = (f32[8,32,128]{2,1,0:T(8,128)S(1)}, f32[8,32,128]{2,1,0:T(8,128)}, u32[]{:S(2)}) copy-start(f32[8,32,128]{2,1,0:T(8,128)} %conduct_ref.5) | copy-start | bytes 393220
  10.5 17.8 %copy-start.2 = (f32[8,32,128]{2,1,0:T(8,128)S(1)}, f32[8,32,128]{2,1,0:T(8,128)}, u32[]{:S(2)}) copy-start(f32[8,32,128]{2,1,0:T(8,128)} %old_ref.3) | copy-start | bytes 393220
  28.3 39.0 %copy-start.3 = (f32[8,32,128]{2,1,0:T(8,128)S(1)}, f32[8,32,128]{2,1,0:T(8,128)}, u32[]{:S(2)}) copy-start(f32[8,32,128]{2,1,0:T(8,128)} %source_ref.3) | copy-start | bytes 393220
  28.3 39.0 %copy-start.4 = (f32[8,32,128]{2,1,0:T(8,128)S(1)}, f32[8,32,128]{2,1,0:T(8,128)}, u32[]{:S(2)}) copy-start(f32[8,32,128]{2,1,0:T(8,128)} %reaction_ref.3) | copy-start | bytes 393220
  28.3 39.0 %copy-start.5 = (f32[4,16,64]{2,1,0:T(8,128)S(1)}, f32[4,16,64]{2,1,0:T(8,128)}, u32[]{:S(2)}) copy-start(f32[4,16,64]{2,1,0:T(8,128)} %coarse_ref.3) | copy-start | bytes 49156
  29.2 38.1 %collective-permute-start = (f32[2,32,128]{2,1,0:T(8,128)S(1)}, f32[2,32,128]{2,1,0:T(8,128)S(1)}, u32[]{:S(2)}, u32[]{:S(2)}) collective-permute-start(f32[2,32,128]{2,1,0:T(8,128)S(1)} %get-tuple-element.20), channel_id=1, source_target_pairs={{0,128},{128,0},{256,384},{384,256},{512,640},{640,512},{768,896},... | collective-permute-start | bytes 98312 | tf_op jit(solution)/shard_map/ppermute | solution.py:237
  31.1 36.2 %collective-permute-start.1 = (f32[2,32,128]{2,1,0:T(8,128)S(1)}, f32[2,32,128]{2,1,0:T(8,128)S(1)}, u32[]{:S(2)}, u32[]{:S(2)}) collective-permute-start(f32[2,32,128]{2,1,0:T(8,128)S(1)} %get-tuple-element.21), channel_id=1, source_target_pairs={{128,256},{256,128},{384,512},{512,384},{640,768},{768,640},{129,2... | collective-permute-start | bytes 98312 | tf_op jit(solution)/shard_map/ppermute | solution.py:237
  37.2 12.5 %collective-permute-start.2 = (f32[2,8,128]{2,1,0:T(8,128)S(1)}, f32[2,8,128]{2,1,0:T(8,128)S(1)}, u32[]{:S(2)}, u32[]{:S(2)}) collective-permute-start(f32[2,8,128]{2,1,0:T(8,128)S(1)} %get-tuple-element.22), channel_id=1, source_target_pairs={{0,1},{1,0},{2,3},{3,2},{4,5},{5,4},{6,7},{7,6},{8,9},{9,8},{10,11... | collective-permute-start | bytes 24584 | tf_op jit(solution)/shard_map/ppermute | solution.py:237
  43.9 23.4 %collective-permute-start.4 = (f32[32,128]{1,0:T(8,128)S(1)}, f32[32,128]{1,0:T(8,128)S(1)}, u32[]{:S(2)}, u32[]{:S(2)}) collective-permute-start(f32[32,128]{1,0:T(8,128)S(1)} %get-tuple-element.24), channel_id=1, source_target_pairs={{0,4},{4,0},{8,12},{12,8},{16,20},{20,16},{24,28},{28,24},{32,36},... | collective-permute-start | bytes 49160 | tf_op jit(solution)/shard_map/ppermute | solution.py:237
  46.0 21.3 %collective-permute-start.5 = (f32[32,128]{1,0:T(8,128)S(1)}, f32[32,128]{1,0:T(8,128)S(1)}, u32[]{:S(2)}, u32[]{:S(2)}) collective-permute-start(f32[32,128]{1,0:T(8,128)S(1)} %get-tuple-element.25), channel_id=1, source_target_pairs={{4,8},{8,4},{12,16},{16,12},{20,24},{24,20},{28,32},{32,28},{36,40... | collective-permute-start | bytes 49160 | tf_op jit(solution)/shard_map/ppermute | solution.py:237
  49.7 17.5 %collective-permute-start.3 = (f32[2,8,128]{2,1,0:T(8,128)S(1)}, f32[2,8,128]{2,1,0:T(8,128)S(1)}, u32[]{:S(2)}, u32[]{:S(2)}) collective-permute-start(f32[2,8,128]{2,1,0:T(8,128)S(1)} %get-tuple-element.23), channel_id=1, source_target_pairs={{1,2},{2,1},{5,6},{6,5},{9,10},{10,9},{13,14},{14,13},{17,18},{18,... | collective-permute-start | bytes 24584 | tf_op jit(solution)/shard_map/ppermute | solution.py:237
  68.4 30.1 %collective-permute-start.6 = (f32[32,128]{1,0:T(8,128)S(1)}, f32[32,128]{1,0:T(8,128)S(1)}, u32[]{:S(2)}, u32[]{:S(2)}) collective-permute-start(f32[32,128]{1,0:T(8,128)S(1)} %get-tuple-element.27), channel_id=1, source_target_pairs={{0,128},{128,0},{256,384},{384,256},{512,640},{640,512},{768,896},... | collective-permute-start | bytes 49160 | tf_op jit(solution)/shard_map/ppermute | solution.py:237
  70.3 28.1 %collective-permute-start.7 = (f32[32,128]{1,0:T(8,128)S(1)}, f32[32,128]{1,0:T(8,128)S(1)}, u32[]{:S(2)}, u32[]{:S(2)}) collective-permute-start(f32[32,128]{1,0:T(8,128)S(1)} %get-tuple-element.28), channel_id=1, source_target_pairs={{128,256},{256,128},{384,512},{512,384},{640,768},{768,640},{129,2... | collective-permute-start | bytes 49160 | tf_op jit(solution)/shard_map/ppermute | solution.py:237
  74.6 23.9 %collective-permute-start.10 = (f32[32,128]{1,0:T(8,128)S(1)}, f32[32,128]{1,0:T(8,128)S(1)}, u32[]{:S(2)}, u32[]{:S(2)}) collective-permute-start(f32[32,128]{1,0:T(8,128)S(1)} %get-tuple-element.31), channel_id=1, source_target_pairs={{0,4},{4,0},{8,12},{12,8},{16,20},{20,16},{24,28},{28,24},{32,36},... | collective-permute-start | bytes 49160 | tf_op jit(solution)/shard_map/ppermute | solution.py:237
  76.5 22.0 %collective-permute-start.11 = (f32[32,128]{1,0:T(8,128)S(1)}, f32[32,128]{1,0:T(8,128)S(1)}, u32[]{:S(2)}, u32[]{:S(2)}) collective-permute-start(f32[32,128]{1,0:T(8,128)S(1)} %get-tuple-element.32), channel_id=1, source_target_pairs={{4,8},{8,4},{12,16},{16,12},{20,24},{24,20},{28,32},{32,28},{36,40... | collective-permute-start | bytes 49160 | tf_op jit(solution)/shard_map/ppermute | solution.py:237
  80.6 3.1 %collective-permute-start.8 = (f32[8,128]{1,0:T(8,128)S(1)}, f32[8,128]{1,0:T(8,128)S(1)}, u32[]{:S(2)}, u32[]{:S(2)}) collective-permute-start(f32[8,128]{1,0:T(8,128)S(1)} %get-tuple-element.29), channel_id=1, source_target_pairs={{0,1},{1,0},{2,3},{3,2},{4,5},{5,4},{6,7},{7,6},{8,9},{9,8},{10,11... | collective-permute-start | bytes 12296 | tf_op jit(solution)/shard_map/ppermute | solution.py:237
  83.7 14.7 %collective-permute-start.9 = (f32[8,128]{1,0:T(8,128)S(1)}, f32[8,128]{1,0:T(8,128)S(1)}, u32[]{:S(2)}, u32[]{:S(2)}) collective-permute-start(f32[8,128]{1,0:T(8,128)S(1)} %get-tuple-element.30), channel_id=1, source_target_pairs={{1,2},{2,1},{5,6},{6,5},{9,10},{10,9},{13,14},{14,13},{17,18},{18,... | collective-permute-start | bytes 12296 | tf_op jit(solution)/shard_map/ppermute | solution.py:237

commit v3 on v0

v3 whole, which is shorter than its diff:
```python
import jax
import jax.numpy as jnp
from jax import lax
from jax.experimental import pallas as pl
from jax.experimental.pallas import tpu as pltpu
from jax.sharding import PartitionSpec as P

LANES = 128
RUN = 4
VMEM = pl.BlockSpec(memory_space=pltpu.VMEM)
SMEM = pl.BlockSpec(memory_space=pltpu.SMEM)
PARAMS = pltpu.CompilerParams(vmem_limit_bytes=24 * 1024 * 1024)
F32 = jnp.float32

PHI1, PHI2, KAP1, KAP2, SRC, REA, RIM = range(7)


def lane_of(shape):
    return lax.broadcasted_iota(jnp.int32, shape, len(shape) - 1)


def row_of(shape):
    return lax.broadcasted_iota(jnp.int32, shape, len(shape) - 2)


def roll_lanes(value, shift):
    shift = shift % LANES
    return pltpu.roll(value, shift, value.ndim - 1) if shift else value


def roll_rows(value, shift):
    return pltpu.roll(value, shift % value.shape[0], 0)


def moved_slot(home_ref, slots):
    position = lax.axis_index("gy")
    slot = jnp.int32(0)
    target = jnp.int32(0)
    for j in range(slots):
        home = home_ref[j]
        leaves = home != position * slots + j
        slot = jnp.where(leaves, j, slot)
        target = jnp.where(leaves, home, target)
    return slot, target


def edges():
    flags = []
    for axis in ("gx", "gz", "gy"):
        index = lax.axis_index(axis)
        flags.append((index == 0, index == lax.axis_size(axis) - 1))
    return flags


def is_even(axis):
    return lax.rem(lax.axis_index(axis), 2) == 0


def write_pair(axis, first_ref, second_ref, index, low, high):
    even = is_even(axis)
    first_ref[index] = jnp.where(even, high, low)
    second_ref[index] = jnp.where(even, low, high)


def received(axis, first, second):
    even = is_even(axis)
    return jnp.where(even, second, first), jnp.where(even, first, second)


def sent(axis, first, second):
    even = is_even(axis)
    return jnp.where(even, second, first), jnp.where(even, first, second)


def refine(coarse_ref):
    _, cz, cy = coarse_ref.shape
    left = lax.div(lax.broadcasted_iota(jnp.int32, (2 * cz, cz), 0), 2)
    left = (left == lax.broadcasted_iota(jnp.int32, (2 * cz, cz), 1)).astype(F32)
    right = lax.div(lax.broadcasted_iota(jnp.int32, (cy, 2 * cy), 1), 2)
    right = (right == lax.broadcasted_iota(jnp.int32, (cy, 2 * cy), 0)).astype(F32)
    planes = []
    for x in range(coarse_ref.shape[0]):
        wide = jnp.dot(
            coarse_ref[x], right, precision=lax.Precision.HIGHEST, preferred_element_type=F32
        )
        planes.append(
            jnp.dot(left, wide, precision=lax.Precision.HIGHEST, preferred_element_type=F32)
        )
    return planes


def prepare_kernel(
    home_ref, old_ref, conduct_ref, source_ref, reaction_ref, coarse_ref,
    parts_ref, src_ref, rea_ref, za_ref, zb_ref,
):
    slots = home_ref.shape[0]
    width = LANES // slots
    nx, nz, _ = old_ref.shape
    rows = nz // slots
    slot, target = moved_slot(home_ref, slots)
    device = lax.div(target, slots)
    back = LANES - width * slot

    count, planes = parts_ref.shape[0], parts_ref.shape[1] - 1
    shape = (nx, rows, LANES)
    group = lax.div(lane_of(shape), width)
    box = jnp.zeros(shape, F32)
    for g in range(slots):
        shift = lax.rem(back + width * g, LANES)
        rolled = pltpu.roll(old_ref[:, g * rows : (g + 1) * rows, :], shift, 2)
        box = jnp.where(group == g, rolled, box)
    for k in range(count):
        parts_ref[k, :planes] = box[k * planes : (k + 1) * planes]
        parts_ref[k, planes] = jnp.full((rows, LANES), device, jnp.int32).astype(F32)

    (x_first, x_last), (z_first, z_last), (y_first, y_last) = edges()
    refined = refine(coarse_ref)
    row, lane = row_of((nz, LANES)), lane_of((nz, LANES))
    inner = (
        ((row == 0) & z_first).astype(F32)
        + ((row == nz - 1) & z_last).astype(F32)
        + ((lane == 0) & y_first).astype(F32)
        + ((lane == LANES - 1) & y_last).astype(F32)
    )
    for x in range(nx):
        faces = inner
        if x == 0:
            faces = faces + jnp.where(x_first, 1.0, 0.0)
        if x == nx - 1:
            faces = faces + jnp.where(x_last, 1.0, 0.0)
        weight = faces * conduct_ref[x]
        src_ref[x] = source_ref[x] + weight * refined[x // 2]
        rea_ref[x] = 1.0 + reaction_ref[x] + weight

    lane = lane_of((nx, LANES))
    note = jnp.where(lane < 3 * width, device, slot).astype(F32)

    def rims(first, second):
        near = pltpu.roll(first, lax.rem(back, LANES), 1)
        far = pltpu.roll(second, lax.rem(back + width, LANES), 1)
        return jnp.where(lane < width, near, jnp.where(lane < 2 * width, far, note))

    low = [old_ref[:, 0, :], old_ref[:, 1, :], conduct_ref[:, 0, :], conduct_ref[:, 1, :]]
    low += [src_ref[:, 0, :], rea_ref[:, 0, :], rims(low[0], low[1])]
    high = [old_ref[:, nz - 1, :], old_ref[:, nz - 2, :]]
    high += [conduct_ref[:, nz - 1, :], conduct_ref[:, nz - 2, :]]
    high += [src_ref[:, nz - 1, :], rea_ref[:, nz - 1, :], rims(high[0], high[1])]
    for i in range(7):
        write_pair("gz", za_ref, zb_ref, i, low[i], high[i])


def address_kernel(parts_ref, za_ref, zb_ref, send_ref, *, width):
    planes = send_ref.shape[1] - 1
    low, high = received("gz", za_ref[RIM], zb_ref[RIM])
    shape = low.shape
    lane = lane_of(shape)
    low_tag = jnp.broadcast_to(low[:, 2 * width : 2 * width + 1], shape)
    high_tag = jnp.broadcast_to(high[:, 2 * width : 2 * width + 1], shape)
    high = roll_lanes(high, 2 * width)
    lower = lane < 2 * width
    rims = jnp.where(lower, low, high)
    tag = jnp.where(lower, low_tag, high_tag)
    for device in range(send_ref.shape[0]):
        for i in range(planes):
            value = jnp.zeros(shape, F32)
            for k in range(parts_ref.shape[0]):
                value = jnp.where(parts_ref[k, planes] == device, parts_ref[k, i], value)
            send_ref[device, i] = value
        send_ref[device, planes] = jnp.where(tag == device, rims, 0.0)


def spread(tile, offset, width):
    piece = jnp.where(lane_of(tile.shape) < width, roll_lanes(tile, -offset), 0.0)
    result = piece
    for shift in range(width, LANES, width):
        result = result + roll_lanes(piece, shift)
    return result


def place_kernel(
    home_ref, recv_ref, old_ref, conduct_ref, src_ref, rea_ref, za_ref, zb_ref,
    start_ref, zhalo_ref, ya_ref, yb_ref,
):
    slots = home_ref.shape[0]
    width = LANES // slots
    nx, nz, _ = old_ref.shape
    rows = nz // slots
    slot, _ = moved_slot(home_ref, slots)
    planes = recv_ref.shape[1] - 1
    run = nx // planes
    count = recv_ref.shape[0]
    here = lax.div(lane_of((rows, LANES)), width) == slot
    for k in range(run):
        for i in range(planes):
            x = k * planes + i
            arrived = recv_ref[k, i]
            for source in range(k + run, count, run):
                arrived = arrived + recv_ref[source, i]
            for g in range(slots):
                shift = lax.rem(width * (slot - g) + LANES, LANES)
                part = pl.ds(g * rows, rows)
                start_ref[x, part, :] = jnp.where(
                    here, pltpu.roll(arrived, shift, 1), old_ref[x, part, :]
                )

    rims = recv_ref[0, planes]
    for source in range(1, count):
        rims = rims + recv_ref[source, planes]
    faces = [received("gz", za_ref[i], zb_ref[i]) for i in range(7)]
    group = lax.div(lane_of((nx, LANES)), width).astype(F32)
    for side in range(2):
        note = faces[RIM][side]
        there = jnp.broadcast_to(note[:, 3 * width : 3 * width + 1], note.shape) == group
        for depth in range(2):
            moved = spread(rims, (2 * side + depth) * width, width)
            zhalo_ref[side, depth] = jnp.where(there, moved, faces[depth][side])

    lane = lane_of((nz, LANES))
    low = high = jnp.zeros((nz, LANES), F32)
    for f, (ref, depth) in enumerate(
        ((start_ref, 0), (start_ref, 1), (conduct_ref, 0), (conduct_ref, 1), (src_ref, 0), (rea_ref, 0))
    ):
        for x in range(nx):
            spot = f * nx + x
            low = jnp.where(lane == spot, roll_lanes(ref[x], spot - depth), low)
            high = jnp.where(lane == spot, roll_lanes(ref[x], spot + 1 + depth), high)
    write_pair("gy", ya_ref, yb_ref, slice(0, nz), low, high)
    lane = lane_of((nx, LANES))
    low = high = jnp.zeros((nx, LANES), F32)
    for side in range(2):
        for f, tile in enumerate((zhalo_ref[side, 0], faces[KAP1][side])):
            spot = 2 * side + f
            low = jnp.where(lane == spot, roll_lanes(tile, spot), low)
            high = jnp.where(lane == spot, roll_lanes(tile, spot + 1), high)
    write_pair("gy", ya_ref, yb_ref, slice(nz, nz + nx), low, high)


def edge_kernel(
    start_ref, conduct_ref, src_ref, rea_ref, zhalo_ref, za_ref, zb_ref, ya_ref, yb_ref,
    xa_ref, xb_ref,
):
    nx, nz, _ = start_ref.shape
    for f, (ref, depth) in enumerate(
        ((start_ref, 0), (start_ref, 1), (conduct_ref, 0), (conduct_ref, 1), (src_ref, 0), (rea_ref, 0))
    ):
        write_pair(
            "gx", xa_ref, xb_ref, slice(f * nz, (f + 1) * nz), ref[depth], ref[nx - 1 - depth]
        )
    base = 6 * nz
    kappas = received("gz", za_ref[KAP1], zb_ref[KAP1])
    xa_ref[base : base + 8] = jnp.zeros((8, LANES), F32)
    xb_ref[base : base + 8] = jnp.zeros((8, LANES), F32)
    for side in range(2):
        for f, tile in enumerate((zhalo_ref[side, 0], kappas[side])):
            spot = base + 2 * side + f
            write_pair(
                "gx", xa_ref, xb_ref, slice(spot, spot + 1), tile[0:1], tile[nx - 1 : nx]
            )
    lane = lane_of((nz, LANES))
    low = high = jnp.zeros((nz, LANES), F32)
    for side, halo in enumerate(received("gy", ya_ref[:nz], yb_ref[:nz])):
        for f, offset in enumerate((PHI1 * nx, KAP1 * nx)):
            spot = 2 * side + f
            low = jnp.where(lane == spot, roll_lanes(halo, spot - offset), low)
            high = jnp.where(lane == spot, roll_lanes(halo, spot - offset - nx + 1), high)
    write_pair("gx", xa_ref, xb_ref, slice(base + 8, base + 8 + nz), low, high)


def step(numerator, denominator, kappa, sides):
    for phi, beside, outside in sides:
        weight = 0.5 * (kappa + beside)
        if outside is not None:
            weight = jnp.where(outside, 0.0, weight)
        numerator = numerator + weight * phi
        denominator = denominator + weight
    return numerator / denominator


def along_rows(phi, kappa, low, high, flags):
    row = row_of(phi.shape)
    last = phi.shape[0] - 1
    low_edge, high_edge = row == 0, row == last
    return [
        (
            jnp.where(low_edge, low[0], roll_rows(phi, 1)),
            jnp.where(low_edge, low[1], roll_rows(kappa, 1)),
            low_edge & flags[0],
        ),
        (
            jnp.where(high_edge, high[0], roll_rows(phi, last)),
            jnp.where(high_edge, high[1], roll_rows(kappa, last)),
            high_edge & flags[1],
        ),
    ]


def along_lanes(phi, kappa, low, high, flags, last=LANES - 1):
    lane = lane_of(phi.shape)
    low_edge, high_edge = lane == 0, lane == last
    return [
        (
            jnp.where(low_edge, low[0], roll_lanes(phi, 1)),
            jnp.where(low_edge, low[1], roll_lanes(kappa, 1)),
            low_edge & flags[0],
        ),
        (
            jnp.where(high_edge, high[0], roll_lanes(phi, -1)),
            jnp.where(high_edge, high[1], roll_lanes(kappa, -1)),
            high_edge & flags[1],
        ),
    ]


def to_row(tile, spot):
    column = jnp.broadcast_to(tile[:, spot : spot + 1], tile.shape)
    return jnp.sum(
        jnp.where(lane_of(tile.shape) == row_of(tile.shape), column, 0.0), axis=0, keepdims=True
    )


def sweeps_kernel(
    start_ref, conduct_ref, src_ref, rea_ref, zhalo_ref,
    za_ref, zb_ref, sya_ref, syb_ref, ya_ref, yb_ref, xa_ref, xb_ref,
    out_ref,
):
    nx, nz, _ = start_ref.shape
    flags_x, flags_z, flags_y = edges()
    start = [start_ref[x] for x in range(nx)]
    conduct = [conduct_ref[x] for x in range(nx)]
    base = 6 * nz

    def part(axis, a_ref, b_ref, begin, size):
        return received(axis, a_ref[begin : begin + size], b_ref[begin : begin + size])

    xf = [part("gx", xa_ref, xb_ref, f * nz, nz) for f in range(6)]
    xrows = part("gx", xa_ref, xb_ref, base, 8)
    xcols = part("gx", xa_ref, xb_ref, base + 8, nz)
    zf = [received("gz", za_ref[i], zb_ref[i]) for i in range(6)]
    yf = part("gy", ya_ref, yb_ref, 0, nz)
    yt = part("gy", ya_ref, yb_ref, nz, nx)
    sf = sent("gy", sya_ref[:nz], syb_ref[:nz])

    def columns(tile, phi_spot, kappa_spot, lane):
        return roll_lanes(tile, lane - phi_spot), roll_lanes(tile, lane - kappa_spot)

    x_first_sweep = []
    for side in range(2):
        phi, kappa = xf[PHI1][side], xf[KAP1][side]
        me = 0 if side == 0 else nx - 1
        rows = xrows[side]
        sides = [(xf[PHI2][side], xf[KAP2][side], None), (start[me], conduct[me], None)]
        sides += along_rows(phi, kappa, (rows[0:1], rows[1:2]), (rows[2:3], rows[3:4]), flags_z)
        tile = xcols[side]
        sides += along_lanes(
            phi, kappa, columns(tile, 0, 1, 0), columns(tile, 2, 3, LANES - 1), flags_y
        )
        x_first_sweep.append(step(phi + xf[SRC][side], xf[REA][side], kappa, sides))

    z_first_sweep = []
    for side in range(2):
        phi, kappa = zhalo_ref[side, 0], zf[KAP1][side]
        me = 0 if side == 0 else nz - 1
        at = 2 * side
        sides = [
            (zhalo_ref[side, 1], zf[KAP2][side], None),
            (start_ref[:, me, :], conduct_ref[:, me, :], None),
        ]
        sides += along_rows(
            phi,
            kappa,
            (xrows[0][at : at + 1], xrows[0][at + 1 : at + 2]),
            (xrows[1][at : at + 1], xrows[1][at + 1 : at + 2]),
            flags_x,
        )
        sides += along_lanes(
            phi,
            kappa,
            columns(yt[0], at, at + 1, 0),
            columns(yt[1], at, at + 1, LANES - 1),
            flags_y,
        )
        z_first_sweep.append(step(phi + zf[SRC][side], zf[REA][side], kappa, sides))

    y_first_sweep = []
    for side in range(2):
        phi, phi2, kappa, kappa2, src, rea = [roll_lanes(yf[side], -f * nx) for f in range(6)]
        at = 2 * side
        sides = [(phi2, kappa2, None), (sf[side], roll_lanes(sf[side], -KAP1 * nx), None)]
        sides += along_rows(
            phi,
            kappa,
            (to_row(yt[side], 0), to_row(yt[side], 1)),
            (to_row(yt[side], 2), to_row(yt[side], 3)),
            flags_z,
        )
        sides += along_lanes(
            phi,
            kappa,
            columns(xcols[0], at, at + 1, 0),
            columns(xcols[1], at, at + 1, nx - 1),
            flags_x,
            nx - 1,
        )
        y_first_sweep.append(step(phi + src, rea, kappa, sides))

    def sweep(phis, x_phi, z_phi, y_phi):
        results = []
        for x in range(nx):
            phi, kappa = phis[x], conduct[x]
            sides = []
            if x:
                sides.append((phis[x - 1], conduct[x - 1], None))
            else:
                sides.append((x_phi[0], xf[KAP1][0], flags_x[0]))
            if x < nx - 1:
                sides.append((phis[x + 1], conduct[x + 1], None))
            else:
                sides.append((x_phi[1], xf[KAP1][1], flags_x[1]))
            sides += along_rows(
                phi,
                kappa,
                (z_phi[0][x : x + 1], zf[KAP1][0][x : x + 1]),
                (z_phi[1][x : x + 1], zf[KAP1][1][x : x + 1]),
                flags_z,
            )
            spot = KAP1 * nx + x
            sides += along_lanes(
                phi,
                kappa,
                (roll_lanes(y_phi[0], -x), roll_lanes(yf[0], -spot)),
                (roll_lanes(y_phi[1], LANES - 1 - x), roll_lanes(yf[1], LANES - 1 - spot)),
                flags_y,
            )
            results.append(step(start[x] + src_ref[x], rea_ref[x], kappa, sides))
        return results

    first = sweep(start, xf[PHI1], (zhalo_ref[0, 0], zhalo_ref[1, 0]), yf)
    second = sweep(first, x_first_sweep, z_first_sweep, y_first_sweep)
    for x in range(nx):
        out_ref[x] = second[x]


def swap(axis, first, second):
    count = lax.axis_size(axis)
    results = []
    for j, value in enumerate((first, second)):
        pairs = []
        for low in range(j, count - 1, 2):
            pairs += [(low, low + 1), (low + 1, low)]
        results.append(lax.ppermute(value, axis, pairs))
    return results


def call(kernel, operands, outs, smem=0):
    specs = [SMEM] * smem + [VMEM] * (len(operands) - smem)
    return pl.pallas_call(
        kernel,
        out_shape=[jax.ShapeDtypeStruct(shape, F32) for shape in outs],
        in_specs=specs,
        out_specs=[VMEM] * len(outs),
        compiler_params=PARAMS,
    )(*operands)


def on_device(old_field, new_home, conduct, reaction, source, coarse):
    nx, nz, ny = block = old_field.shape
    home = new_home[0, 0]
    slots = home.shape[0]
    rows, width = nz // slots, ny // slots
    line = lax.axis_size("gy")
    part = nx // RUN

    parts, src, rea, za, zb = call(
        prepare_kernel,
        (home, old_field, conduct, source, reaction, coarse),
        [(RUN, part + 1, rows, ny), block, block, (7, nx, ny), (7, nx, ny)],
        smem=1,
    )
    za, zb = swap("gz", za, zb)
    groups = [[i * RUN + k for k in range(RUN)] for i in range(line // RUN)]
    parts = lax.all_to_all(parts, "gy", 0, 0, tiled=True, axis_index_groups=groups)

    def address(*refs):
        address_kernel(*refs, width=width)

    (send,) = call(address, (parts, za, zb), [(line, part + 1, rows, ny)])
    recv = lax.all_to_all(send, "gy", 0, 0, tiled=True)
    start, zhalo, sya, syb = call(
        place_kernel,
        (home, recv, old_field, conduct, src, rea, za, zb),
        [block, (2, 2, nx, ny), (nz + nx, ny), (nz + nx, ny)],
        smem=1,
    )
    ya, yb = swap("gy", sya, syb)
    xa, xb = call(
        edge_kernel,
        (start, conduct, src, rea, zhalo, za, zb, ya, yb),
        [(7 * nz + 8, ny)] * 2,
    )
    xa, xb = swap("gx", xa, xb)
    (relaxed,) = call(
        sweeps_kernel,
        (start, conduct, src, rea, zhalo, za, zb, sya, syb, ya, yb, xa, xb),
        [block],
    )
    return relaxed


def solution(mesh):
    return jax.shard_map(
        on_device,
        mesh=mesh,
        in_specs=(P("gx", "gz", "gy"),) * 6,
        out_specs=P("gx", "gz", "gy"),
        check_vma=False,
    )
```

time: 219 us -> 75.1 us (0.34)
  the two profiles are of different devices: /device:TPU:7 before, /device:TPU:73 now
where the time goes in v3:
time: 75.1 us; the launch traced here: 74.6 us
  starting transfers between devices  37.3 us (50%)
  blocking collectives  21.1 us (28%)
  waiting for transfers between devices  6.32 us (8%)
  local copies, waits for them, and re-layouts  5.04 us (7%)
  Pallas kernels  4.8 us (6%)
    ppermute x6, starting transfers between devices, swap(): results.append(lax.ppermute(value, axis, pairs))  33.3 us
    all_to_all x1, blocking collectives, on_device(): recv = lax.all_to_all(send, 'gy', 0, 0, tiled=True)  21.1 us
    ppermute x6, waiting for transfers between devices, swap(): results.append(lax.ppermute(value, axis, pairs))  6.31 us
    unnamed x16, local copies, waits for them, and re-layouts  5.04 us
    pallas_call x5, Pallas kernels, call(): pl.pallas_call(kernel, out_shape=[jax.ShapeDtypeStruct(shape, F32) for sh...  4.8 us
    all_to_all x1, starting transfers between devices, on_device(): lax.all_to_all(parts, 'gy', 0, 0, tiled=True, axis_index_groups=groups)  4.01 us
  transfers between devices with their start and end apart: 7, of which 3 were waited for; matrix products, arithmetic and copies ran while one was open for 0% of the time, Pallas kernels for 0%

profile of v3, /device:TPU:73, one launch (start us, length us, event | category | flops | bytes accessed | tf_op | source)
XLA Modules:
  0.0 74.6 jit_solution(1838999640732222226)
XLA Ops:
  0.0 0.0 copy-start.7
  0.0 0.7 copy-done.7
  0.7 0.0 copy-start
  0.7 0.9 %copy-done = f32[8,32,128]{2,1,0:T(8,128)S(1)} copy-done((f32[8,32,128]{2,1,0:T(8,128)S(1)}, f32[8,32,128]{2,1,0:T(8,128)}, u32[]{:S(2)}) %copy-start) | copy-done | bytes 131096
  1.6 0.0 copy-start.2
  1.6 0.9 %copy-done.2 = f32[8,32,128]{2,1,0:T(8,128)S(1)} copy-done((f32[8,32,128]{2,1,0:T(8,128)S(1)}, f32[8,32,128]{2,1,0:T(8,128)}, u32[]{:S(2)}) %copy-start.2) | copy-done | bytes 131096
  2.5 0.0 copy-start.4
  2.5 0.9 %copy-done.4 = f32[8,32,128]{2,1,0:T(8,128)S(1)} copy-done((f32[8,32,128]{2,1,0:T(8,128)S(1)}, f32[8,32,128]{2,1,0:T(8,128)}, u32[]{:S(2)}) %copy-start.4) | copy-done | bytes 131096
  3.4 0.0 copy-start.5
  3.4 0.9 %copy-done.5 = f32[8,32,128]{2,1,0:T(8,128)S(1)} copy-done((f32[8,32,128]{2,1,0:T(8,128)S(1)}, f32[8,32,128]{2,1,0:T(8,128)}, u32[]{:S(2)}) %copy-start.5) | copy-done | bytes 131096
  4.3 0.0 copy-start.6
  4.3 0.8 %copy-done.6 = f32[4,16,64]{2,1,0:T(8,128)S(1)} copy-done((f32[4,16,64]{2,1,0:T(8,128)S(1)}, f32[4,16,64]{2,1,0:T(8,128)}, u32[]{:S(2)}) %copy-start.6) | copy-done | bytes 16408
  5.0 2.0 %shard_map.64 = (f32[4,3,8,128]{3,2,1,0:T(8,128)}, f32[8,32,128]{2,1,0:T(8,128)S(1)}, f32[8,32,128]{2,1,0:T(8,128)S(1)}, f32[7,8,128]{2,1,0:T(8,128)S(1)}, f32[7,8,128]{2,1,0:T(8,128)S(1)}) custom-call(s32[4]{0:T(128)S(1)} %bitcast.1, f32[8,32,128]{2,1,0:T(8,128)S(1)} %copy-done.2, f32[8,32,128]{2,1,0:T(8,128)S(1)} %copy-done, f32[8,32,128]{2,1,0:T(8,128)S(1)} %copy-done.4, ...), custom_call_target="tpu_custom_call" | custom-call | tf_op jit(solution)/shard_map/pallas_call | solution.py:456
  7.1 4.0 %all-to-all-start = ((f32[4,3,8,128]{3,2,1,0:T(8,128)}), f32[4,3,8,128]{3,2,1,0:T(8,128)S(1)}, u32[]{:S(2)}, u32[]{:S(2)}) async-start(f32[4,3,8,128]{3,2,1,0:T(8,128)} %get-tuple-element.16), calls=%async_computation | async-start | bytes 98304 | tf_op jit(solution)/shard_map/all_to_all | solution.py:481
  11.1 2.9 %collective-permute-start = (f32[7,8,128]{2,1,0:T(8,128)S(1)}, f32[7,8,128]{2,1,0:T(8,128)S(1)}, u32[]{:S(2)}, u32[]{:S(2)}) collective-permute-start(f32[7,8,128]{2,1,0:T(8,128)S(1)} %get-tuple-element.17), channel_id=1, source_target_pairs={{0,1},{1,0},{2,3},{3,2},{4,5},{5,4},{6,7},{7,6},{8,9},{9,8},{10,11... | collective-permute-start | bytes 86024 | tf_op jit(solution)/shard_map/ppermute | solution.py:450
  13.9 18.1 %collective-permute-start.1 = (f32[7,8,128]{2,1,0:T(8,128)S(1)}, f32[7,8,128]{2,1,0:T(8,128)S(1)}, u32[]{:S(2)}, u32[]{:S(2)}) collective-permute-start(f32[7,8,128]{2,1,0:T(8,128)S(1)} %get-tuple-element.18), channel_id=1, source_target_pairs={{1,2},{2,1},{5,6},{6,5},{9,10},{10,9},{13,14},{14,13},{17,18},{18,... | collective-permute-start | bytes 86024 | tf_op jit(solution)/shard_map/ppermute | solution.py:450
  32.0 0.0 collective-permute-done.refs_1_.za_ref
  32.0 1.5 %collective-permute-done.1.refs_2_.zb_ref = f32[7,8,128]{2,1,0:T(8,128)S(1)} collective-permute-done((f32[7,8,128]{2,1,0:T(8,128)S(1)}, f32[7,8,128]{2,1,0:T(8,128)S(1)}, u32[]{:S(2)}, u32[]{:S(2)}) %collective-permute-start.1) | collective-permute-done | bytes 28704 | tf_op jit(solution)/shard_map/ppermute | solution.py:450
  33.6 0.0 all-to-all-done.refs_0_
  33.6 0.1 shard_map.65
  33.7 0.0 copy-start.1
  33.7 0.0 copy-start.3
  33.7 21.1 %all_to_all.10.recv_ref = f32[32,3,8,128]{3,2,1,0:T(8,128)S(1)} all-to-all(f32[32,3,8,128]{3,2,1,0:T(8,128)S(1)} %shard_map.65), channel_id=1, replica_groups=mesh['gx'=8,'gy'=32,'gz'=4] {'gy'}, dimensions={0} | all-to-all | bytes 786432 | tf_op jit(solution)/shard_map/all_to_all | solution.py:487
  54.7 0.0 copy-done.1
  54.7 0.0 copy-done.3
  54.8 1.1 %shard_map.66 = (f32[8,32,128]{2,1,0:T(8,128)S(1)}, f32[2,2,8,128]{3,2,1,0:T(8,128)S(1)}, f32[40,128]{1,0:T(8,128)S(1)}, f32[40,128]{1,0:T(8,128)S(1)}) custom-call(s32[4]{0:T(128)S(1)} %bitcast.2, f32[32,3,8,128]{3,2,1,0:T(8,128)S(1)} %all_to_all.10.recv_ref, f32[8,32,128]{2,1,0:T(8,128)S(1)} %copy-done.3, f32[8,32,128]{2,1,0:T(8,128)S(1)} %copy-done.1, ...), custom_call_target="tpu_custom_call" | custom-call | tf_op jit(solution)/shard_map/pallas_call | solution.py:456
  55.9 2.1 %collective-permute-start.2 = (f32[40,128]{1,0:T(8,128)S(1)}, f32[40,128]{1,0:T(8,128)S(1)}, u32[]{:S(2)}, u32[]{:S(2)}) collective-permute-start(f32[40,128]{1,0:T(8,128)S(1)} %get-tuple-element.23.sya_ref), channel_id=1, source_target_pairs={{0,4},{4,0},{8,12},{12,8},{16,20},{20,16},{24,28},{28,24},{32,36},... | collective-permute-start | bytes 61448 | tf_op jit(solution)/shard_map/ppermute | solution.py:450
  58.0 4.0 %collective-permute-start.3 = (f32[40,128]{1,0:T(8,128)S(1)}, f32[40,128]{1,0:T(8,128)S(1)}, u32[]{:S(2)}, u32[]{:S(2)}) collective-permute-start(f32[40,128]{1,0:T(8,128)S(1)} %get-tuple-element.24.syb_ref), channel_id=1, source_target_pairs={{4,8},{8,4},{12,16},{16,12},{20,24},{24,20},{28,32},{32,28},{36,40... | collective-permute-start | bytes 61448 | tf_op jit(solution)/shard_map/ppermute | solution.py:450
  62.0 0.0 collective-permute-done.2.ya_ref
  62.0 2.6 %collective-permute-done.3.yb_ref = f32[40,128]{1,0:T(8,128)S(1)} collective-permute-done((f32[40,128]{1,0:T(8,128)S(1)}, f32[40,128]{1,0:T(8,128)S(1)}, u32[]{:S(2)}, u32[]{:S(2)}) %collective-permute-start.3) | collective-permute-done | bytes 20512 | tf_op jit(solution)/shard_map/ppermute | solution.py:450
  64.6 0.1 shard_map.67
  64.7 2.2 %collective-permute-start.4 = (f32[232,128]{1,0:T(8,128)S(1)}, f32[232,128]{1,0:T(8,128)S(1)}, u32[]{:S(2)}, u32[]{:S(2)}) collective-permute-start(f32[232,128]{1,0:T(8,128)S(1)} %get-tuple-element.25), channel_id=1, source_target_pairs={{0,128},{128,0},{256,384},{384,256},{512,640},{640,512},{768,896},... | collective-permute-start | bytes 356360 | tf_op jit(solution)/shard_map/ppermute | solution.py:450
  66.9 4.0 %collective-permute-start.5 = (f32[232,128]{1,0:T(8,128)S(1)}, f32[232,128]{1,0:T(8,128)S(1)}, u32[]{:S(2)}, u32[]{:S(2)}) collective-permute-start(f32[232,128]{1,0:T(8,128)S(1)} %get-tuple-element.26), channel_id=1, source_target_pairs={{128,256},{256,128},{384,512},{512,384},{640,768},{768,640},{129,2... | collective-permute-start | bytes 356360 | tf_op jit(solution)/shard_map/ppermute | solution.py:450
  70.9 0.0 collective-permute-done.4.xa_ref
  71.0 2.2 %collective-permute-done.5.xb_ref = f32[232,128]{1,0:T(8,128)S(1)} collective-permute-done((f32[232,128]{1,0:T(8,128)S(1)}, f32[232,128]{1,0:T(8,128)S(1)}, u32[]{:S(2)}, u32[]{:S(2)}) %collective-permute-start.5) | collective-permute-done | bytes 118816 | tf_op jit(solution)/shard_map/ppermute | solution.py:450
  73.2 1.4 %shard_map.68 = f32[8,32,128]{2,1,0:T(8,128)} custom-call(f32[8,32,128]{2,1,0:T(8,128)S(1)} %get-tuple-element.21.start_ref, f32[8,32,128]{2,1,0:T(8,128)S(1)} %copy-done.1, f32[8,32,128]{2,1,0:T(8,128)S(1)} %get-tuple-element.19.src_ref, f32[8,32,128]{2,1,0:T(8,128)S(1)} %get-tuple-element.20.rea_ref, f32[2,2,8,128]{3,2,1,0:T(8,128)S(1)} %get-tuple-element.22.zhalo_ref, ...), custom_call_target="tpu_custom_call" | custom-call | tf_op jit(solution)/shard_map/pallas_call | solution.py:456
Async XLA Ops:
  0.0 0.7 copy-start.7
  0.7 0.9 %copy-start = (f32[8,32,128]{2,1,0:T(8,128)S(1)}, f32[8,32,128]{2,1,0:T(8,128)}, u32[]{:S(2)}) copy-start(f32[8,32,128]{2,1,0:T(8,128)} %conduct_ref.7) | copy-start | bytes 393220
  1.6 0.9 %copy-start.2 = (f32[8,32,128]{2,1,0:T(8,128)S(1)}, f32[8,32,128]{2,1,0:T(8,128)}, u32[]{:S(2)}) copy-start(f32[8,32,128]{2,1,0:T(8,128)} %old_ref.3) | copy-start | bytes 393220
  2.5 0.9 %copy-start.4 = (f32[8,32,128]{2,1,0:T(8,128)S(1)}, f32[8,32,128]{2,1,0:T(8,128)}, u32[]{:S(2)}) copy-start(f32[8,32,128]{2,1,0:T(8,128)} %source_ref.1) | copy-start | bytes 393220
  3.4 0.9 %copy-start.5 = (f32[8,32,128]{2,1,0:T(8,128)S(1)}, f32[8,32,128]{2,1,0:T(8,128)}, u32[]{:S(2)}) copy-start(f32[8,32,128]{2,1,0:T(8,128)} %reaction_ref.1) | copy-start | bytes 393220
  4.3 0.8 %copy-start.6 = (f32[4,16,64]{2,1,0:T(8,128)S(1)}, f32[4,16,64]{2,1,0:T(8,128)}, u32[]{:S(2)}) copy-start(f32[4,16,64]{2,1,0:T(8,128)} %coarse_ref.1) | copy-start | bytes 49156
  7.1 26.5 %all-to-all-start = ((f32[4,3,8,128]{3,2,1,0:T(8,128)}), f32[4,3,8,128]{3,2,1,0:T(8,128)S(1)}, u32[]{:S(2)}, u32[]{:S(2)}) async-start(f32[4,3,8,128]{3,2,1,0:T(8,128)} %get-tuple-element.16), calls=%async_computation | async-start | bytes 98304 | tf_op jit(solution)/shard_map/all_to_all | solution.py:481
  11.1 20.9 %collective-permute-start = (f32[7,8,128]{2,1,0:T(8,128)S(1)}, f32[7,8,128]{2,1,0:T(8,128)S(1)}, u32[]{:S(2)}, u32[]{:S(2)}) collective-permute-start(f32[7,8,128]{2,1,0:T(8,128)S(1)} %get-tuple-element.17), channel_id=1, source_target_pairs={{0,1},{1,0},{2,3},{3,2},{4,5},{5,4},{6,7},{7,6},{8,9},{9,8},{10,11... | collective-permute-start | bytes 86024 | tf_op jit(solution)/shard_map/ppermute | solution.py:450
  13.9 19.6 %collective-permute-start.1 = (f32[7,8,128]{2,1,0:T(8,128)S(1)}, f32[7,8,128]{2,1,0:T(8,128)S(1)}, u32[]{:S(2)}, u32[]{:S(2)}) collective-permute-start(f32[7,8,128]{2,1,0:T(8,128)S(1)} %get-tuple-element.18), channel_id=1, source_target_pairs={{1,2},{2,1},{5,6},{6,5},{9,10},{10,9},{13,14},{14,13},{17,18},{18,... | collective-permute-start | bytes 86024 | tf_op jit(solution)/shard_map/ppermute | solution.py:450
  33.7 21.1 %copy-start.1 = (f32[8,32,128]{2,1,0:T(8,128)S(1)}, f32[8,32,128]{2,1,0:T(8,128)}, u32[]{:S(2)}) copy-start(f32[8,32,128]{2,1,0:T(8,128)} %conduct_ref.7) | copy-start | bytes 393220
  33.7 21.1 %copy-start.3 = (f32[8,32,128]{2,1,0:T(8,128)S(1)}, f32[8,32,128]{2,1,0:T(8,128)}, u32[]{:S(2)}) copy-start(f32[8,32,128]{2,1,0:T(8,128)} %old_ref.3) | copy-start | bytes 393220
  55.9 6.1 %collective-permute-start.2 = (f32[40,128]{1,0:T(8,128)S(1)}, f32[40,128]{1,0:T(8,128)S(1)}, u32[]{:S(2)}, u32[]{:S(2)}) collective-permute-start(f32[40,128]{1,0:T(8,128)S(1)} %get-tuple-element.23.sya_ref), channel_id=1, source_target_pairs={{0,4},{4,0},{8,12},{12,8},{16,20},{20,16},{24,28},{28,24},{32,36},... | collective-permute-start | bytes 61448 | tf_op jit(solution)/shard_map/ppermute | solution.py:450
  58.0 6.6 %collective-permute-start.3 = (f32[40,128]{1,0:T(8,128)S(1)}, f32[40,128]{1,0:T(8,128)S(1)}, u32[]{:S(2)}, u32[]{:S(2)}) collective-permute-start(f32[40,128]{1,0:T(8,128)S(1)} %get-tuple-element.24.syb_ref), channel_id=1, source_target_pairs={{4,8},{8,4},{12,16},{16,12},{20,24},{24,20},{28,32},{32,28},{36,40... | collective-permute-start | bytes 61448 | tf_op jit(solution)/shard_map/ppermute | solution.py:450
  64.7 6.2 %collective-permute-start.4 = (f32[232,128]{1,0:T(8,128)S(1)}, f32[232,128]{1,0:T(8,128)S(1)}, u32[]{:S(2)}, u32[]{:S(2)}) collective-permute-start(f32[232,128]{1,0:T(8,128)S(1)} %get-tuple-element.25), channel_id=1, source_target_pairs={{0,128},{128,0},{256,384},{384,256},{512,640},{640,512},{768,896},... | collective-permute-start | bytes 356360 | tf_op jit(solution)/shard_map/ppermute | solution.py:450
  66.9 6.2 %collective-permute-start.5 = (f32[232,128]{1,0:T(8,128)S(1)}, f32[232,128]{1,0:T(8,128)S(1)}, u32[]{:S(2)}, u32[]{:S(2)}) collective-permute-start(f32[232,128]{1,0:T(8,128)S(1)} %get-tuple-element.26), channel_id=1, source_target_pairs={{128,256},{256,128},{384,512},{512,384},{640,768},{768,640},{129,2... | collective-permute-start | bytes 356360 | tf_op jit(solution)/shard_map/ppermute | solution.py:450

commit v4 on v3

--- a/solution.py
+++ b/solution.py
@@ -9,6 +9,7 @@
 RUN = 4
 VMEM = pl.BlockSpec(memory_space=pltpu.VMEM)
 SMEM = pl.BlockSpec(memory_space=pltpu.SMEM)
+HBM = pl.BlockSpec(memory_space=pltpu.HBM)
 PARAMS = pltpu.CompilerParams(vmem_limit_bytes=24 * 1024 * 1024)
 F32 = jnp.float32
 
@@ -72,47 +73,108 @@
     return jnp.where(even, second, first), jnp.where(even, first, second)
 
 
+def doubler(count):
+    half = lax.div(lax.broadcasted_iota(jnp.int32, (count, 2 * count), 1), 2)
+    return (half == lax.broadcasted_iota(jnp.int32, (count, 2 * count), 0)).astype(F32)
+
+
+def exact_dot(left, right):
+    return jnp.dot(left, right, precision=lax.Precision.HIGHEST, preferred_element_type=F32)
+
+
 def refine(coarse_ref):
-    _, cz, cy = coarse_ref.shape
-    left = lax.div(lax.broadcasted_iota(jnp.int32, (2 * cz, cz), 0), 2)
-    left = (left == lax.broadcasted_iota(jnp.int32, (2 * cz, cz), 1)).astype(F32)
-    right = lax.div(lax.broadcasted_iota(jnp.int32, (cy, 2 * cy), 1), 2)
-    right = (right == lax.broadcasted_iota(jnp.int32, (cy, 2 * cy), 0)).astype(F32)
-    planes = []
-    for x in range(coarse_ref.shape[0]):
-        wide = jnp.dot(
-            coarse_ref[x], right, precision=lax.Precision.HIGHEST, preferred_element_type=F32
-        )
-        planes.append(
-            jnp.dot(left, wide, precision=lax.Precision.HIGHEST, preferred_element_type=F32)
-        )
-    return planes
-
-
-def prepare_kernel(
-    home_ref, old_ref, conduct_ref, source_ref, reaction_ref, coarse_ref,
-    parts_ref, src_ref, rea_ref, za_ref, zb_ref,
+    cx, cz, cy = coarse_ref.shape
+    left, right = doubler(cz).T, doubler(cy)
+    return [exact_dot(left, exact_dot(coarse_ref[x], right)) for x in range(cx)]
+
+
+def face_kernel(
+    home_ref, old_hbm, conduct_hbm, source_hbm, reaction_hbm, coarse_hbm,
+    za_ref, zb_ref, rows_ref, coarse_ref, sems, coarse_sem,
 ):
     slots = home_ref.shape[0]
     width = LANES // slots
+    nx, nz, _ = old_hbm.shape
+    size = rows_ref.shape[3]
+    copies = [pltpu.make_async_copy(coarse_hbm, coarse_ref, coarse_sem)]
+    for i, ref in enumerate((old_hbm, conduct_hbm, source_hbm, reaction_hbm)):
+        for side, begin in enumerate((0, nz - size)):
+            copies.append(
+                pltpu.make_async_copy(
+                    ref.at[:, pl.ds(begin, size), :], rows_ref.at[i, side], sems.at[i, side]
+                )
+            )
+    for copy in copies:
+        copy.start()
+
+    slot, target = moved_slot(home_ref, slots)
+    device = lax.div(target, slots)
+    back = LANES - width * slot
+    (x_first, x_last), (z_first, z_last), (y_first, y_last) = edges()
+    row, lane = row_of((nx, LANES)), lane_of((nx, LANES))
+    note = jnp.where(lane < 3 * width, device, slot).astype(F32)
+    inner = (
+        ((row == 0) & x_first).astype(F32)
+        + ((row == nx - 1) & x_last).astype(F32)
+        + ((lane == 0) & y_first).astype(F32)
+        + ((lane == LANES - 1) & y_last).astype(F32)
+    )
+    for copy in copies:
+        copy.wait()
+    cx, cz, cy = coarse_ref.shape
+    left, right = doubler(cx).T, doubler(cy)
+
+    def rims(first, second):
+        near = pltpu.roll(first, lax.rem(back, LANES), 1)
+        far = pltpu.roll(second, lax.rem(back + width, LANES), 1)
+        return jnp.where(lane < width, near, jnp.where(lane < 2 * width, far, note))
+
+    faces = []
+    for side, first, second, end, edge in ((0, 0, 1, 0, z_first), (1, size - 1, size - 2, cz - 1, z_last)):
+        refined = exact_dot(left, exact_dot(coarse_ref[:, end, :], right))
+        old, old2 = rows_ref[0, side, :, first, :], rows_ref[0, side, :, second, :]
+        kappa, kappa2 = rows_ref[1, side, :, first, :], rows_ref[1, side, :, second, :]
+        weight = (inner + jnp.where(edge, 1.0, 0.0)) * kappa
+        src = rows_ref[2, side, :, first, :] + weight * refined
+        rea = 1.0 + rows_ref[3, side, :, first, :] + weight
+        faces.append([old, old2, kappa, kappa2, src, rea, rims(old, old2)])
+    for i in range(7):
+        write_pair("gz", za_ref, zb_ref, i, faces[0][i], faces[1][i])
+
+
+def split_kernel(home_ref, old_hbm, after_ref, *rest):
+    del after_ref
+    parts, (box_ref, old_ref, sems) = rest[:RUN], rest[RUN:]
+    slots = home_ref.shape[0]
+    width = LANES // slots
     nx, nz, _ = old_ref.shape
+    copies = [
+        pltpu.make_async_copy(old_hbm.at[x], old_ref.at[x], sems.at[x]) for x in range(nx)
+    ]
+    for copy in copies:
+        copy.start()
     rows = nz // slots
     slot, target = moved_slot(home_ref, slots)
     device = lax.div(target, slots)
-    back = LANES - width * slot
-
-    count, planes = parts_ref.shape[0], parts_ref.shape[1] - 1
-    shape = (nx, rows, LANES)
-    group = lax.div(lane_of(shape), width)
-    box = jnp.zeros(shape, F32)
-    for g in range(slots):
-        shift = lax.rem(back + width * g, LANES)
-        rolled = pltpu.roll(old_ref[:, g * rows : (g + 1) * rows, :], shift, 2)
-        box = jnp.where(group == g, rolled, box)
-    for k in range(count):
-        parts_ref[k, :planes] = box[k * planes : (k + 1) * planes]
-        parts_ref[k, planes] = jnp.full((rows, LANES), device, jnp.int32).astype(F32)
-
+    planes = parts[0].shape[0] - 1
+    group = lax.div(lane_of((rows, LANES)), width)
+    for x in range(nx):
+        copies[x].wait()
+        box = jnp.zeros((rows, LANES), F32)
+        for g in range(slots):
+            shift = lax.rem(width * (g - slot) + LANES, LANES)
+            rolled = pltpu.roll(old_ref[x, g * rows : (g + 1) * rows, :], shift, 1)
+            box = jnp.where(group == g, rolled, box)
+        box_ref[x // planes, x % planes] = box
+    place = lax.rem(lax.axis_index("gy"), RUN)
+    for j in range(RUN):
+        parts[j][:planes] = box_ref[jnp.bitwise_xor(place, j)]
+        parts[j][planes] = jnp.full((rows, LANES), device, jnp.int32).astype(F32)
+
+
+def fold_kernel(conduct_ref, source_ref, reaction_ref, coarse_ref, after_ref, src_ref, rea_ref):
+    del after_ref
+    nx, nz, _ = conduct_ref.shape
     (x_first, x_last), (z_first, z_last), (y_first, y_last) = edges()
     refined = refine(coarse_ref)
     row, lane = row_of((nz, LANES)), lane_of((nz, LANES))
@@ -132,24 +194,9 @@
         src_ref[x] = source_ref[x] + weight * refined[x // 2]
         rea_ref[x] = 1.0 + reaction_ref[x] + weight
 
-    lane = lane_of((nx, LANES))
-    note = jnp.where(lane < 3 * width, device, slot).astype(F32)
-
-    def rims(first, second):
-        near = pltpu.roll(first, lax.rem(back, LANES), 1)
-        far = pltpu.roll(second, lax.rem(back + width, LANES), 1)
-        return jnp.where(lane < width, near, jnp.where(lane < 2 * width, far, note))
-
-    low = [old_ref[:, 0, :], old_ref[:, 1, :], conduct_ref[:, 0, :], conduct_ref[:, 1, :]]
-    low += [src_ref[:, 0, :], rea_ref[:, 0, :], rims(low[0], low[1])]
-    high = [old_ref[:, nz - 1, :], old_ref[:, nz - 2, :]]
-    high += [conduct_ref[:, nz - 1, :], conduct_ref[:, nz - 2, :]]
-    high += [src_ref[:, nz - 1, :], rea_ref[:, nz - 1, :], rims(high[0], high[1])]
-    for i in range(7):
-        write_pair("gz", za_ref, zb_ref, i, low[i], high[i])
-
-
-def address_kernel(parts_ref, za_ref, zb_ref, send_ref, *, width):
+
+def address_kernel(*refs, width):
+    parts, (za_ref, zb_ref, send_ref) = refs[:RUN], refs[RUN:]
     planes = send_ref.shape[1] - 1
     low, high = received("gz", za_ref[RIM], zb_ref[RIM])
     shape = low.shape
@@ -163,8 +210,8 @@
     for device in range(send_ref.shape[0]):
         for i in range(planes):
             value = jnp.zeros(shape, F32)
-            for k in range(parts_ref.shape[0]):
-                value = jnp.where(parts_ref[k, planes] == device, parts_ref[k, i], value)
+            for part in parts:
+                value = jnp.where(part[planes] == device, part[i], value)
             send_ref[device, i] = value
         send_ref[device, planes] = jnp.where(tag == device, rims, 0.0)
 
@@ -443,21 +490,26 @@
 def swap(axis, first, second):
     count = lax.axis_size(axis)
     results = []
-    for j, value in enumerate((first, second)):
+    for j, value in ((1, second), (0, first)):
         pairs = []
         for low in range(j, count - 1, 2):
             pairs += [(low, low + 1), (low + 1, low)]
         results.append(lax.ppermute(value, axis, pairs))
-    return results
-
-
-def call(kernel, operands, outs, smem=0):
+    return results[::-1]
+
+
+def call(kernel, operands, outs, smem=0, hbm=(), scratch=()):
     specs = [SMEM] * smem + [VMEM] * (len(operands) - smem)
+    operands = list(operands)
+    for i in hbm:
+        specs[i] = HBM
+        operands[i] = pltpu.with_memory_space_constraint(operands[i], pltpu.HBM)
     return pl.pallas_call(
         kernel,
         out_shape=[jax.ShapeDtypeStruct(shape, F32) for shape in outs],
         in_specs=specs,
         out_specs=[VMEM] * len(outs),
+        scratch_shapes=scratch,
         compiler_params=PARAMS,
     )(*operands)
 
@@ -470,20 +522,41 @@
     line = lax.axis_size("gy")
     part = nx // RUN
 
-    parts, src, rea, za, zb = call(
-        prepare_kernel,
+    sza, szb = call(
+        face_kernel,
         (home, old_field, conduct, source, reaction, coarse),
-        [(RUN, part + 1, rows, ny), block, block, (7, nx, ny), (7, nx, ny)],
+        [(7, nx, ny), (7, nx, ny)],
         smem=1,
-    )
-    za, zb = swap("gz", za, zb)
-    groups = [[i * RUN + k for k in range(RUN)] for i in range(line // RUN)]
-    parts = lax.all_to_all(parts, "gy", 0, 0, tiled=True, axis_index_groups=groups)
+        hbm=(1, 2, 3, 4, 5),
+        scratch=[
+            pltpu.VMEM((4, 2, nx, 8, ny), F32),
+            pltpu.VMEM(coarse.shape, F32),
+            pltpu.SemaphoreType.DMA((4, 2)),
+            pltpu.SemaphoreType.DMA,
+        ],
+    )
+    za, zb = swap("gz", sza, szb)
+    kept, *parts = call(
+        split_kernel,
+        (home, old_field, sza),
+        [(part + 1, rows, ny)] * RUN,
+        smem=1,
+        hbm=(1,),
+        scratch=[
+            pltpu.VMEM((RUN, part, rows, ny), F32),
+            pltpu.VMEM(block, F32),
+            pltpu.SemaphoreType.DMA((nx,)),
+        ],
+    )
+    src, rea = call(fold_kernel, (conduct, source, reaction, coarse, kept), [block, block])
+    for j in range(1, RUN):
+        pairs = [(i, i ^ j) for i in range(line)]
+        parts[j - 1] = lax.ppermute(parts[j - 1], "gy", pairs)
 
     def address(*refs):
         address_kernel(*refs, width=width)
 
-    (send,) = call(address, (parts, za, zb), [(line, part + 1, rows, ny)])
+    (send,) = call(address, (kept, *parts, za, zb), [(line, part + 1, rows, ny)])
     recv = lax.all_to_all(send, "gy", 0, 0, tiled=True)
     start, zhalo, sya, syb = call(
         place_kernel,

time: 75.1 us -> 78.3 us (1.043)
  blocking collectives: 21.1 us -> 0 us
  starting transfers between devices: 37.3 us -> 49.9 us
  waiting for transfers between devices: 6.32 us -> 18.6 us
  local copies, waits for them, and re-layouts: 5.04 us -> 0.68 us
  Pallas kernels: 4.8 us -> 8.36 us
    all_to_all x1 -> x0, blocking collectives: 21.1 us -> none  [on_device(): recv = lax.all_to_all(send, 'gy', 0, 0, tiled=True)]
    all_to_all x1, waiting for transfers between devices: 0.01 us -> 10 us  [on_device(): recv = lax.all_to_all(send, 'gy', 0, 0, tiled=True)]
    ppermute x0 -> x3, starting transfers between devices: none -> 9.58 us  [on_device(): parts[j - 1] = lax.ppermute(parts[j - 1], 'gy', pairs)]
    unnamed x16 -> x12, local copies, waits for them, and re-layouts: 5.04 us -> 0.68 us
    ppermute x0 -> x3, waiting for transfers between devices: none -> 3.82 us  [on_device(): parts[j - 1] = lax.ppermute(parts[j - 1], 'gy', pairs)]
    all_to_all x1, starting transfers between devices: 4.01 us -> 7.61 us  [on_device(): recv = lax.all_to_all(send, 'gy', 0, 0, tiled=True)]
    pallas_call x5 -> x7, Pallas kernels: 4.8 us -> 8.36 us  [call(): pl.pallas_call(kernel, out_shape=[jax.ShapeDtypeStruct(shape, F32) for sh...]
    ppermute x6, waiting for transfers between devices: 6.31 us -> 4.79 us  [swap(): results.append(lax.ppermute(value, axis, pairs))]
  transfers between devices with their start and end apart: 7 -> 10, of which waited for: 3 -> 4; matrix products, arithmetic and copies ran while one was open for 0% -> 0% of each run, Pallas kernels for 0% -> 4%
where the time goes in v4:
time: 78.3 us; the launch traced here: 77.7 us
  starting transfers between devices  49.9 us (64%)
  waiting for transfers between devices  18.6 us (24%)
  Pallas kernels  8.36 us (11%)
    ppermute x6, starting transfers between devices, swap(): results.append(lax.ppermute(value, axis, pairs))  32.7 us
    all_to_all x1, waiting for transfers between devices, on_device(): recv = lax.all_to_all(send, 'gy', 0, 0, tiled=True)  10 us
    ppermute x3, starting transfers between devices, on_device(): parts[j - 1] = lax.ppermute(parts[j - 1], 'gy', pairs)  9.58 us
    pallas_call x7, Pallas kernels, call(): pl.pallas_call(kernel, out_shape=[jax.ShapeDtypeStruct(shape, F32) for sh...  8.36 us
    all_to_all x1, starting transfers between devices, on_device(): recv = lax.all_to_all(send, 'gy', 0, 0, tiled=True)  7.61 us
    ppermute x6, waiting for transfers between devices, swap(): results.append(lax.ppermute(value, axis, pairs))  4.79 us
    ppermute x3, waiting for transfers between devices, on_device(): parts[j - 1] = lax.ppermute(parts[j - 1], 'gy', pairs)  3.82 us
  transfers between devices with their start and end apart: 10, of which 4 were waited for; matrix products, arithmetic and copies ran while one was open for 0% of the time, Pallas kernels for 4%

profile of v4, /device:TPU:73, one launch (start us, length us, event | category | flops | bytes accessed | tf_op | source)
XLA Modules:
  0.0 77.7 jit_solution(12359049980666447202)
XLA Ops:
  0.0 0.0 copy-start.5
  0.0 0.7 copy-done.5
  0.7 2.0 %shard_map.64 = (f32[7,8,128]{2,1,0:T(8,128)S(1)}, f32[7,8,128]{2,1,0:T(8,128)S(1)}) custom-call(s32[4]{0:T(128)S(1)} %bitcast.1, f32[8,32,128]{2,1,0:T(8,128)} %old_ref.1, f32[8,32,128]{2,1,0:T(8,128)} %conduct_ref.7, f32[8,32,128]{2,1,0:T(8,128)} %source_ref.1, f32[8,32,128]{2,1,0:T(8,128)} %reaction_ref.1, f32[4,16,64]{2,1,0:T(8,128)} %coarse_ref.1), custom_call_target="tpu_custom_call" | custom-call | tf_op jit(solution)/shard_map/pallas_call | solution.py:507
  2.7 2.6 %collective-permute-start.3 = (f32[7,8,128]{2,1,0:T(8,128)S(1)}, f32[7,8,128]{2,1,0:T(8,128)S(1)}, u32[]{:S(2)}, u32[]{:S(2)}) collective-permute-start(f32[7,8,128]{2,1,0:T(8,128)S(1)} %get-tuple-element.19.after_ref), channel_id=1, source_target_pairs={{0,1},{1,0},{2,3},{3,2},{4,5},{5,4},{6,7},{7,6},{8,9},{9,8},{10,11... | collective-permute-start | bytes 86024 | tf_op jit(solution)/shard_map/ppermute | solution.py:497
  5.3 18.1 %collective-permute-start.4 = (f32[7,8,128]{2,1,0:T(8,128)S(1)}, f32[7,8,128]{2,1,0:T(8,128)S(1)}, u32[]{:S(2)}, u32[]{:S(2)}) collective-permute-start(f32[7,8,128]{2,1,0:T(8,128)S(1)} %get-tuple-element.24), channel_id=1, source_target_pairs={{1,2},{2,1},{5,6},{6,5},{9,10},{10,9},{13,14},{14,13},{17,18},{18,... | collective-permute-start | bytes 86024 | tf_op jit(solution)/shard_map/ppermute | solution.py:497
  23.3 1.9 %shard_map.65 = (f32[3,8,128]{2,1,0:T(8,128)S(1)}, f32[3,8,128]{2,1,0:T(8,128)S(1)}, f32[3,8,128]{2,1,0:T(8,128)S(1)}, f32[3,8,128]{2,1,0:T(8,128)S(1)}) custom-call(s32[4]{0:T(128)S(1)} %bitcast.2, f32[8,32,128]{2,1,0:T(8,128)} %old_ref.1, f32[7,8,128]{2,1,0:T(8,128)S(1)} %get-tuple-element.19.after_ref), custom_call_target="tpu_custom_call" | custom-call | tf_op jit(solution)/shard_map/pallas_call | solution.py:507
  25.3 3.1 %collective-permute-start = (f32[3,8,128]{2,1,0:T(8,128)S(1)}, f32[3,8,128]{2,1,0:T(8,128)S(1)}, u32[]{:S(2)}, u32[]{:S(2)}) collective-permute-start(f32[3,8,128]{2,1,0:T(8,128)S(1)} %get-tuple-element.21), channel_id=1, source_target_pairs={{0,4},{4,0},{8,12},{12,8},{16,20},{20,16},{24,28},{28,24},{32,36},... | collective-permute-start | bytes 36872 | tf_op jit(solution)/shard_map/ppermute | solution.py:554
  28.4 4.4 %collective-permute-start.1 = (f32[3,8,128]{2,1,0:T(8,128)S(1)}, f32[3,8,128]{2,1,0:T(8,128)S(1)}, u32[]{:S(2)}, u32[]{:S(2)}) collective-permute-start(f32[3,8,128]{2,1,0:T(8,128)S(1)} %get-tuple-element.22), channel_id=1, source_target_pairs={{0,8},{4,12},{8,0},{12,4},{16,24},{20,28},{24,16},{28,20},{32,40},... | collective-permute-start | bytes 36872 | tf_op jit(solution)/shard_map/ppermute | solution.py:554
  32.8 2.1 %collective-permute-start.2 = (f32[3,8,128]{2,1,0:T(8,128)S(1)}, f32[3,8,128]{2,1,0:T(8,128)S(1)}, u32[]{:S(2)}, u32[]{:S(2)}) collective-permute-start(f32[3,8,128]{2,1,0:T(8,128)S(1)} %get-tuple-element.23), channel_id=1, source_target_pairs={{0,12},{4,8},{8,4},{12,0},{16,28},{20,24},{24,20},{28,16},{32,44},... | collective-permute-start | bytes 36872 | tf_op jit(solution)/shard_map/ppermute | solution.py:554
  34.9 0.0 collective-permute-done.refs_1_
  34.9 0.0 collective-permute-done.1.refs_2_
  34.9 3.8 %collective-permute-done.2.refs_3_ = f32[3,8,128]{2,1,0:T(8,128)S(1)} collective-permute-done((f32[3,8,128]{2,1,0:T(8,128)S(1)}, f32[3,8,128]{2,1,0:T(8,128)S(1)}, u32[]{:S(2)}, u32[]{:S(2)}) %collective-permute-start.2) | collective-permute-done | bytes 12320 | tf_op jit(solution)/shard_map/ppermute | solution.py:554
  38.7 0.0 collective-permute-done.3.refs_4_.za_ref
  38.7 0.0 collective-permute-done.4.refs_5_.zb_ref
  38.7 0.8 %shard_map.66 = f32[32,3,8,128]{3,2,1,0:T(8,128)} custom-call(f32[3,8,128]{2,1,0:T(8,128)S(1)} %get-tuple-element.20.refs_0_.after_ref, f32[3,8,128]{2,1,0:T(8,128)S(1)} %collective-permute-done.refs_1_, f32[3,8,128]{2,1,0:T(8,128)S(1)} %collective-permute-done.1.refs_2_, f32[3,8,128]{2,1,0:T(8,128)S(1)} %collective-permute-done.2.refs_3_, ...), custom_call_target="tpu_custom_call" | custom-call | tf_op jit(solution)/shard_map/pallas_call | solution.py:507
  39.6 0.0 copy-start
  39.6 0.0 copy-start.2
  39.6 0.0 copy-start.3
  39.6 0.0 copy-start.4
  39.6 7.6 %all-to-all-start = ((f32[32,3,8,128]{3,2,1,0:T(8,128)}), f32[32,3,8,128]{3,2,1,0:T(8,128)S(1)}, u32[]{:S(2)}, u32[]{:S(2)}) async-start(f32[32,3,8,128]{3,2,1,0:T(8,128)} %shard_map.66), calls=%async_computation | async-start | bytes 786432 | tf_op jit(solution)/shard_map/all_to_all | solution.py:560
  47.2 0.0 copy-done
  47.2 0.0 copy-done.2
  47.2 0.0 copy-done.3
  47.2 0.0 copy-done.4
  47.2 0.0 copy-start.1
  47.2 0.9 %shard_map.67 = (f32[8,32,128]{2,1,0:T(8,128)S(1)}, f32[8,32,128]{2,1,0:T(8,128)S(1)}) custom-call(f32[8,32,128]{2,1,0:T(8,128)S(1)} %copy-done, f32[8,32,128]{2,1,0:T(8,128)S(1)} %copy-done.2, f32[8,32,128]{2,1,0:T(8,128)S(1)} %copy-done.3, f32[4,16,64]{2,1,0:T(8,128)S(1)} %copy-done.4, f32[3,8,128]{2,1,0:T(8,128)S(1)} %get-tuple-element.20.refs_0_.after_ref), custom_call_target="tpu_custom_call" | custom-call | tf_op jit(solution)/shard_map/pallas_call | solution.py:507
  48.2 10.0 %all-to-all-done.recv_ref = f32[32,3,8,128]{3,2,1,0:T(8,128)S(1)} async-done(((f32[32,3,8,128]{3,2,1,0:T(8,128)}), f32[32,3,8,128]{3,2,1,0:T(8,128)S(1)}, u32[]{:S(2)}, u32[]{:S(2)}) %all-to-all-start) | async-done | bytes 393248 | tf_op jit(solution)/shard_map/all_to_all | solution.py:560
  58.2 0.0 copy-done.1
  58.2 1.1 %shard_map.68 = (f32[8,32,128]{2,1,0:T(8,128)S(1)}, f32[2,2,8,128]{3,2,1,0:T(8,128)S(1)}, f32[40,128]{1,0:T(8,128)S(1)}, f32[40,128]{1,0:T(8,128)S(1)}) custom-call(s32[4]{0:T(128)S(1)} %bitcast.3, f32[32,3,8,128]{3,2,1,0:T(8,128)S(1)} %all-to-all-done.recv_ref, f32[8,32,128]{2,1,0:T(8,128)S(1)} %copy-done.1, f32[8,32,128]{2,1,0:T(8,128)S(1)} %copy-done, ...), custom_call_target="tpu_custom_call" | custom-call | tf_op jit(solution)/shard_map/pallas_call | solution.py:507
  59.3 2.1 %collective-permute-start.5 = (f32[40,128]{1,0:T(8,128)S(1)}, f32[40,128]{1,0:T(8,128)S(1)}, u32[]{:S(2)}, u32[]{:S(2)}) collective-permute-start(f32[40,128]{1,0:T(8,128)S(1)} %get-tuple-element.29.sya_ref), channel_id=1, source_target_pairs={{0,4},{4,0},{8,12},{12,8},{16,20},{20,16},{24,28},{28,24},{32,36},... | collective-permute-start | bytes 61448 | tf_op jit(solution)/shard_map/ppermute | solution.py:497
  61.4 4.0 %collective-permute-start.6 = (f32[40,128]{1,0:T(8,128)S(1)}, f32[40,128]{1,0:T(8,128)S(1)}, u32[]{:S(2)}, u32[]{:S(2)}) collective-permute-start(f32[40,128]{1,0:T(8,128)S(1)} %get-tuple-element.30.syb_ref), channel_id=1, source_target_pairs={{4,8},{8,4},{12,16},{16,12},{20,24},{24,20},{28,32},{32,28},{36,40... | collective-permute-start | bytes 61448 | tf_op jit(solution)/shard_map/ppermute | solution.py:497
  65.5 0.0 collective-permute-done.5.ya_ref
  65.5 2.6 %collective-permute-done.6.yb_ref = f32[40,128]{1,0:T(8,128)S(1)} collective-permute-done((f32[40,128]{1,0:T(8,128)S(1)}, f32[40,128]{1,0:T(8,128)S(1)}, u32[]{:S(2)}, u32[]{:S(2)}) %collective-permute-start.6) | collective-permute-done | bytes 20512 | tf_op jit(solution)/shard_map/ppermute | solution.py:497
  68.1 0.1 shard_map.69
  68.2 1.9 %collective-permute-start.7 = (f32[232,128]{1,0:T(8,128)S(1)}, f32[232,128]{1,0:T(8,128)S(1)}, u32[]{:S(2)}, u32[]{:S(2)}) collective-permute-start(f32[232,128]{1,0:T(8,128)S(1)} %get-tuple-element.31), channel_id=1, source_target_pairs={{0,128},{128,0},{256,384},{384,256},{512,640},{640,512},{768,896},... | collective-permute-start | bytes 356360 | tf_op jit(solution)/shard_map/ppermute | solution.py:497
  70.1 4.0 %collective-permute-start.8 = (f32[232,128]{1,0:T(8,128)S(1)}, f32[232,128]{1,0:T(8,128)S(1)}, u32[]{:S(2)}, u32[]{:S(2)}) collective-permute-start(f32[232,128]{1,0:T(8,128)S(1)} %get-tuple-element.32), channel_id=1, source_target_pairs={{128,256},{256,128},{384,512},{512,384},{640,768},{768,640},{129,2... | collective-permute-start | bytes 356360 | tf_op jit(solution)/shard_map/ppermute | solution.py:497
  74.1 0.0 collective-permute-done.7.xa_ref
  74.1 2.2 %collective-permute-done.8.xb_ref = f32[232,128]{1,0:T(8,128)S(1)} collective-permute-done((f32[232,128]{1,0:T(8,128)S(1)}, f32[232,128]{1,0:T(8,128)S(1)}, u32[]{:S(2)}, u32[]{:S(2)}) %collective-permute-start.8) | collective-permute-done | bytes 118816 | tf_op jit(solution)/shard_map/ppermute | solution.py:497
  76.3 1.4 %shard_map.70 = f32[8,32,128]{2,1,0:T(8,128)} custom-call(f32[8,32,128]{2,1,0:T(8,128)S(1)} %get-tuple-element.27.start_ref, f32[8,32,128]{2,1,0:T(8,128)S(1)} %copy-done, f32[8,32,128]{2,1,0:T(8,128)S(1)} %get-tuple-element.25.src_ref, f32[8,32,128]{2,1,0:T(8,128)S(1)} %get-tuple-element.26.rea_ref, f32[2,2,8,128]{3,2,1,0:T(8,128)S(1)} %get-tuple-element.28.zhalo_ref, ...), custom_call_target="tpu_custom_call" | custom-call | tf_op jit(solution)/shard_map/pallas_call | solution.py:507
Async XLA Ops:
  0.0 0.7 copy-start.5
  2.7 36.1 %collective-permute-start.3 = (f32[7,8,128]{2,1,0:T(8,128)S(1)}, f32[7,8,128]{2,1,0:T(8,128)S(1)}, u32[]{:S(2)}, u32[]{:S(2)}) collective-permute-start(f32[7,8,128]{2,1,0:T(8,128)S(1)} %get-tuple-element.19.after_ref), channel_id=1, source_target_pairs={{0,1},{1,0},{2,3},{3,2},{4,5},{5,4},{6,7},{7,6},{8,9},{9,8},{10,11... | collective-permute-start | bytes 86024 | tf_op jit(solution)/shard_map/ppermute | solution.py:497
  5.3 33.5 %collective-permute-start.4 = (f32[7,8,128]{2,1,0:T(8,128)S(1)}, f32[7,8,128]{2,1,0:T(8,128)S(1)}, u32[]{:S(2)}, u32[]{:S(2)}) collective-permute-start(f32[7,8,128]{2,1,0:T(8,128)S(1)} %get-tuple-element.24), channel_id=1, source_target_pairs={{1,2},{2,1},{5,6},{6,5},{9,10},{10,9},{13,14},{14,13},{17,18},{18,... | collective-permute-start | bytes 86024 | tf_op jit(solution)/shard_map/ppermute | solution.py:497
  25.3 9.6 %collective-permute-start = (f32[3,8,128]{2,1,0:T(8,128)S(1)}, f32[3,8,128]{2,1,0:T(8,128)S(1)}, u32[]{:S(2)}, u32[]{:S(2)}) collective-permute-start(f32[3,8,128]{2,1,0:T(8,128)S(1)} %get-tuple-element.21), channel_id=1, source_target_pairs={{0,4},{4,0},{8,12},{12,8},{16,20},{20,16},{24,28},{28,24},{32,36},... | collective-permute-start | bytes 36872 | tf_op jit(solution)/shard_map/ppermute | solution.py:554
  28.4 6.5 %collective-permute-start.1 = (f32[3,8,128]{2,1,0:T(8,128)S(1)}, f32[3,8,128]{2,1,0:T(8,128)S(1)}, u32[]{:S(2)}, u32[]{:S(2)}) collective-permute-start(f32[3,8,128]{2,1,0:T(8,128)S(1)} %get-tuple-element.22), channel_id=1, source_target_pairs={{0,8},{4,12},{8,0},{12,4},{16,24},{20,28},{24,16},{28,20},{32,40},... | collective-permute-start | bytes 36872 | tf_op jit(solution)/shard_map/ppermute | solution.py:554
  32.8 5.9 %collective-permute-start.2 = (f32[3,8,128]{2,1,0:T(8,128)S(1)}, f32[3,8,128]{2,1,0:T(8,128)S(1)}, u32[]{:S(2)}, u32[]{:S(2)}) collective-permute-start(f32[3,8,128]{2,1,0:T(8,128)S(1)} %get-tuple-element.23), channel_id=1, source_target_pairs={{0,12},{4,8},{8,4},{12,0},{16,28},{20,24},{24,20},{28,16},{32,44},... | collective-permute-start | bytes 36872 | tf_op jit(solution)/shard_map/ppermute | solution.py:554
  39.6 7.6 %copy-start = (f32[8,32,128]{2,1,0:T(8,128)S(1)}, f32[8,32,128]{2,1,0:T(8,128)}, u32[]{:S(2)}) copy-start(f32[8,32,128]{2,1,0:T(8,128)} %conduct_ref.7) | copy-start | bytes 393220
  39.6 7.6 %copy-start.2 = (f32[8,32,128]{2,1,0:T(8,128)S(1)}, f32[8,32,128]{2,1,0:T(8,128)}, u32[]{:S(2)}) copy-start(f32[8,32,128]{2,1,0:T(8,128)} %source_ref.1) | copy-start | bytes 393220
  39.6 7.6 %copy-start.3 = (f32[8,32,128]{2,1,0:T(8,128)S(1)}, f32[8,32,128]{2,1,0:T(8,128)}, u32[]{:S(2)}) copy-start(f32[8,32,128]{2,1,0:T(8,128)} %reaction_ref.1) | copy-start | bytes 393220
  39.6 7.7 %copy-start.4 = (f32[4,16,64]{2,1,0:T(8,128)S(1)}, f32[4,16,64]{2,1,0:T(8,128)}, u32[]{:S(2)}) copy-start(f32[4,16,64]{2,1,0:T(8,128)} %coarse_ref.1) | copy-start | bytes 49156
  39.6 18.6 %all-to-all-start = ((f32[32,3,8,128]{3,2,1,0:T(8,128)}), f32[32,3,8,128]{3,2,1,0:T(8,128)S(1)}, u32[]{:S(2)}, u32[]{:S(2)}) async-start(f32[32,3,8,128]{3,2,1,0:T(8,128)} %shard_map.66), calls=%async_computation | async-start | bytes 786432 | tf_op jit(solution)/shard_map/all_to_all | solution.py:560
  47.2 11.0 %copy-start.1 = (f32[8,32,128]{2,1,0:T(8,128)S(1)}, f32[8,32,128]{2,1,0:T(8,128)}, u32[]{:S(2)}) copy-start(f32[8,32,128]{2,1,0:T(8,128)} %old_ref.1) | copy-start | bytes 393220
  59.3 6.1 %collective-permute-start.5 = (f32[40,128]{1,0:T(8,128)S(1)}, f32[40,128]{1,0:T(8,128)S(1)}, u32[]{:S(2)}, u32[]{:S(2)}) collective-permute-start(f32[40,128]{1,0:T(8,128)S(1)} %get-tuple-element.29.sya_ref), channel_id=1, source_target_pairs={{0,4},{4,0},{8,12},{12,8},{16,20},{20,16},{24,28},{28,24},{32,36},... | collective-permute-start | bytes 61448 | tf_op jit(solution)/shard_map/ppermute | solution.py:497
  61.4 6.6 %collective-permute-start.6 = (f32[40,128]{1,0:T(8,128)S(1)}, f32[40,128]{1,0:T(8,128)S(1)}, u32[]{:S(2)}, u32[]{:S(2)}) collective-permute-start(f32[40,128]{1,0:T(8,128)S(1)} %get-tuple-element.30.syb_ref), channel_id=1, source_target_pairs={{4,8},{8,4},{12,16},{16,12},{20,24},{24,20},{28,32},{32,28},{36,40... | collective-permute-start | bytes 61448 | tf_op jit(solution)/shard_map/ppermute | solution.py:497
  68.2 5.9 %collective-permute-start.7 = (f32[232,128]{1,0:T(8,128)S(1)}, f32[232,128]{1,0:T(8,128)S(1)}, u32[]{:S(2)}, u32[]{:S(2)}) collective-permute-start(f32[232,128]{1,0:T(8,128)S(1)} %get-tuple-element.31), channel_id=1, source_target_pairs={{0,128},{128,0},{256,384},{384,256},{512,640},{640,512},{768,896},... | collective-permute-start | bytes 356360 | tf_op jit(solution)/shard_map/ppermute | solution.py:497
  70.1 6.2 %collective-permute-start.8 = (f32[232,128]{1,0:T(8,128)S(1)}, f32[232,128]{1,0:T(8,128)S(1)}, u32[]{:S(2)}, u32[]{:S(2)}) collective-permute-start(f32[232,128]{1,0:T(8,128)S(1)} %get-tuple-element.32), channel_id=1, source_target_pairs={{128,256},{256,128},{384,512},{512,384},{640,768},{768,640},{129,2... | collective-permute-start | bytes 356360 | tf_op jit(solution)/shard_map/ppermute | solution.py:497

commit v5 on v4

--- a/solution.py
+++ b/solution.py
@@ -88,23 +88,24 @@
     return [exact_dot(left, exact_dot(coarse_ref[x], right)) for x in range(cx)]
 
 
-def face_kernel(
+def first_kernel(
     home_ref, old_hbm, conduct_hbm, source_hbm, reaction_hbm, coarse_hbm,
-    za_ref, zb_ref, rows_ref, coarse_ref, sems, coarse_sem,
+    zb_ref, za_ref, parts_ref, old_ref, rows_ref, coarse_ref, old_sems, sems, coarse_sem,
 ):
     slots = home_ref.shape[0]
     width = LANES // slots
     nx, nz, _ = old_hbm.shape
     size = rows_ref.shape[3]
     copies = [pltpu.make_async_copy(coarse_hbm, coarse_ref, coarse_sem)]
-    for i, ref in enumerate((old_hbm, conduct_hbm, source_hbm, reaction_hbm)):
+    loads = [pltpu.make_async_copy(old_hbm.at[x], old_ref.at[x], old_sems.at[x]) for x in range(nx)]
+    for i, ref in enumerate((conduct_hbm, source_hbm, reaction_hbm)):
         for side, begin in enumerate((0, nz - size)):
             copies.append(
                 pltpu.make_async_copy(
                     ref.at[:, pl.ds(begin, size), :], rows_ref.at[i, side], sems.at[i, side]
                 )
             )
-    for copy in copies:
+    for copy in loads + copies:
         copy.start()
 
     slot, target = moved_slot(home_ref, slots)
@@ -119,57 +120,41 @@
         + ((lane == 0) & y_first).astype(F32)
         + ((lane == LANES - 1) & y_last).astype(F32)
     )
-    for copy in copies:
-        copy.wait()
-    cx, cz, cy = coarse_ref.shape
-    left, right = doubler(cx).T, doubler(cy)
-
-    def rims(first, second):
-        near = pltpu.roll(first, lax.rem(back, LANES), 1)
-        far = pltpu.roll(second, lax.rem(back + width, LANES), 1)
-        return jnp.where(lane < width, near, jnp.where(lane < 2 * width, far, note))
-
-    faces = []
-    for side, first, second, end, edge in ((0, 0, 1, 0, z_first), (1, size - 1, size - 2, cz - 1, z_last)):
-        refined = exact_dot(left, exact_dot(coarse_ref[:, end, :], right))
-        old, old2 = rows_ref[0, side, :, first, :], rows_ref[0, side, :, second, :]
-        kappa, kappa2 = rows_ref[1, side, :, first, :], rows_ref[1, side, :, second, :]
-        weight = (inner + jnp.where(edge, 1.0, 0.0)) * kappa
-        src = rows_ref[2, side, :, first, :] + weight * refined
-        rea = 1.0 + rows_ref[3, side, :, first, :] + weight
-        faces.append([old, old2, kappa, kappa2, src, rea, rims(old, old2)])
-    for i in range(7):
-        write_pair("gz", za_ref, zb_ref, i, faces[0][i], faces[1][i])
-
-
-def split_kernel(home_ref, old_hbm, after_ref, *rest):
-    del after_ref
-    parts, (box_ref, old_ref, sems) = rest[:RUN], rest[RUN:]
-    slots = home_ref.shape[0]
-    width = LANES // slots
-    nx, nz, _ = old_ref.shape
-    copies = [
-        pltpu.make_async_copy(old_hbm.at[x], old_ref.at[x], sems.at[x]) for x in range(nx)
-    ]
-    for copy in copies:
-        copy.start()
     rows = nz // slots
-    slot, target = moved_slot(home_ref, slots)
-    device = lax.div(target, slots)
-    planes = parts[0].shape[0] - 1
+    count, planes = parts_ref.shape[0], parts_ref.shape[1] - 1
     group = lax.div(lane_of((rows, LANES)), width)
     for x in range(nx):
-        copies[x].wait()
+        loads[x].wait()
         box = jnp.zeros((rows, LANES), F32)
         for g in range(slots):
             shift = lax.rem(width * (g - slot) + LANES, LANES)
             rolled = pltpu.roll(old_ref[x, g * rows : (g + 1) * rows, :], shift, 1)
             box = jnp.where(group == g, rolled, box)
-        box_ref[x // planes, x % planes] = box
-    place = lax.rem(lax.axis_index("gy"), RUN)
-    for j in range(RUN):
-        parts[j][:planes] = box_ref[jnp.bitwise_xor(place, j)]
-        parts[j][planes] = jnp.full((rows, LANES), device, jnp.int32).astype(F32)
+        parts_ref[x // planes, x % planes] = box
+    for k in range(count):
+        parts_ref[k, planes] = jnp.full((rows, LANES), device, jnp.int32).astype(F32)
+    for copy in copies:
+        copy.wait()
+    cx, cz, cy = coarse_ref.shape
+    left, right = doubler(cx).T, doubler(cy)
+
+    def rims(first, second):
+        near = pltpu.roll(first, lax.rem(back, LANES), 1)
+        far = pltpu.roll(second, lax.rem(back + width, LANES), 1)
+        return jnp.where(lane < width, near, jnp.where(lane < 2 * width, far, note))
+
+    faces = []
+    for side, first, second, end, edge in ((0, 0, 1, 0, z_first), (1, size - 1, size - 2, cz - 1, z_last)):
+        refined = exact_dot(left, exact_dot(coarse_ref[:, end, :], right))
+        top = side * (nz - size)
+        old, old2 = old_ref[:, top + first, :], old_ref[:, top + second, :]
+        kappa, kappa2 = rows_ref[0, side, :, first, :], rows_ref[0, side, :, second, :]
+        weight = (inner + jnp.where(edge, 1.0, 0.0)) * kappa
+        src = rows_ref[1, side, :, first, :] + weight * refined
+        rea = 1.0 + rows_ref[2, side, :, first, :] + weight
+        faces.append([old, old2, kappa, kappa2, src, rea, rims(old, old2)])
+    for i in range(7):
+        write_pair("gz", za_ref, zb_ref, i, faces[0][i], faces[1][i])
 
 
 def fold_kernel(conduct_ref, source_ref, reaction_ref, coarse_ref, after_ref, src_ref, rea_ref):
@@ -195,8 +180,7 @@
         rea_ref[x] = 1.0 + reaction_ref[x] + weight
 
 
-def address_kernel(*refs, width):
-    parts, (za_ref, zb_ref, send_ref) = refs[:RUN], refs[RUN:]
+def address_kernel(parts_ref, zb_ref, za_ref, send_ref, *, width):
     planes = send_ref.shape[1] - 1
     low, high = received("gz", za_ref[RIM], zb_ref[RIM])
     shape = low.shape
@@ -210,8 +194,8 @@
     for device in range(send_ref.shape[0]):
         for i in range(planes):
             value = jnp.zeros(shape, F32)
-            for part in parts:
-                value = jnp.where(part[planes] == device, part[i], value)
+            for k in range(parts_ref.shape[0]):
+                value = jnp.where(parts_ref[k, planes] == device, parts_ref[k, i], value)
             send_ref[device, i] = value
         send_ref[device, planes] = jnp.where(tag == device, rims, 0.0)
 
@@ -522,41 +506,30 @@
     line = lax.axis_size("gy")
     part = nx // RUN
 
-    sza, szb = call(
-        face_kernel,
+    szb, sza, parts = call(
+        first_kernel,
         (home, old_field, conduct, source, reaction, coarse),
-        [(7, nx, ny), (7, nx, ny)],
+        [(7, nx, ny), (7, nx, ny), (RUN, part + 1, rows, ny)],
         smem=1,
         hbm=(1, 2, 3, 4, 5),
         scratch=[
-            pltpu.VMEM((4, 2, nx, 8, ny), F32),
+            pltpu.VMEM(block, F32),
+            pltpu.VMEM((3, 2, nx, 8, ny), F32),
             pltpu.VMEM(coarse.shape, F32),
-            pltpu.SemaphoreType.DMA((4, 2)),
+            pltpu.SemaphoreType.DMA((nx,)),
+            pltpu.SemaphoreType.DMA((3, 2)),
             pltpu.SemaphoreType.DMA,
         ],
     )
     za, zb = swap("gz", sza, szb)
-    kept, *parts = call(
-        split_kernel,
-        (home, old_field, sza),
-        [(part + 1, rows, ny)] * RUN,
-        smem=1,
-        hbm=(1,),
-        scratch=[
-            pltpu.VMEM((RUN, part, rows, ny), F32),
-            pltpu.VMEM(block, F32),
-            pltpu.SemaphoreType.DMA((nx,)),
-        ],
-    )
-    src, rea = call(fold_kernel, (conduct, source, reaction, coarse, kept), [block, block])
-    for j in range(1, RUN):
-        pairs = [(i, i ^ j) for i in range(line)]
-        parts[j - 1] = lax.ppermute(parts[j - 1], "gy", pairs)
+    groups = [[i * RUN + k for k in range(RUN)] for i in range(line // RUN)]
+    parts = lax.all_to_all(parts, "gy", 0, 0, tiled=True, axis_index_groups=groups)
+    src, rea = call(fold_kernel, (conduct, source, reaction, coarse, szb), [block, block])
 
     def address(*refs):
         address_kernel(*refs, width=width)
 
-    (send,) = call(address, (kept, *parts, za, zb), [(line, part + 1, rows, ny)])
+    (send,) = call(address, (parts, zb, za), [(line, part + 1, rows, ny)])
     recv = lax.all_to_all(send, "gy", 0, 0, tiled=True)
     start, zhalo, sya, syb = call(
         place_kernel,

time: 78.3 us -> 78.7 us (level)
  the two profiles are of different devices: /device:TPU:73 before, /device:TPU:72 now
where the time goes in v5:
time: 78.7 us; the launch traced here: 78.1 us
  starting transfers between devices  49.1 us (62%)
  waiting for transfers between devices  21.2 us (27%)
  Pallas kernels  7.04 us (9%)
    ppermute x6, starting transfers between devices, swap(): results.append(lax.ppermute(value, axis, pairs))  34 us
    all_to_all x1, waiting for transfers between devices, on_device(): recv = lax.all_to_all(send, 'gy', 0, 0, tiled=True)  14.1 us
    all_to_all x1, starting transfers between devices, on_device(): recv = lax.all_to_all(send, 'gy', 0, 0, tiled=True)  10.8 us
    pallas_call x6, Pallas kernels, call(): pl.pallas_call(kernel, out_shape=[jax.ShapeDtypeStruct(shape, F32) for sh...  7.04 us
    ppermute x6, waiting for transfers between devices, swap(): results.append(lax.ppermute(value, axis, pairs))  7.03 us
    all_to_all x1, starting transfers between devices, on_device(): lax.all_to_all(parts, 'gy', 0, 0, tiled=True, axis_index_groups=groups)  4.3 us
  transfers between devices with their start and end apart: 8, of which 4 were waited for; matrix products, arithmetic and copies ran while one was open for 0% of the time, Pallas kernels for 1%

profile of v5, /device:TPU:72, one launch (start us, length us, event | category | flops | bytes accessed | tf_op | source)
XLA Modules:
  0.0 78.1 jit_solution(862397140755771118)
XLA Ops:
  0.0 0.0 copy-start.5
  0.0 0.7 copy-done.5
  0.7 2.6 %shard_map.64 = (f32[7,8,128]{2,1,0:T(8,128)S(1)}, f32[7,8,128]{2,1,0:T(8,128)S(1)}, f32[4,3,8,128]{3,2,1,0:T(8,128)}) custom-call(s32[4]{0:T(128)S(1)} %bitcast.1, f32[8,32,128]{2,1,0:T(8,128)} %old_ref.1, f32[8,32,128]{2,1,0:T(8,128)} %conduct_ref.7, f32[8,32,128]{2,1,0:T(8,128)} %source_ref.1, f32[8,32,128]{2,1,0:T(8,128)} %reaction_ref.1, ...), custom_call_target="tpu_custom_call" | custom-call | tf_op jit(solution)/shard_map/pallas_call | solution.py:491
  3.3 4.3 %all-to-all-start = ((f32[4,3,8,128]{3,2,1,0:T(8,128)}), f32[4,3,8,128]{3,2,1,0:T(8,128)S(1)}, u32[]{:S(2)}, u32[]{:S(2)}) async-start(f32[4,3,8,128]{3,2,1,0:T(8,128)} %get-tuple-element.16), calls=%async_computation | async-start | bytes 98304 | tf_op jit(solution)/shard_map/all_to_all | solution.py:526
  7.6 0.7 collective-permute-start
  8.2 19.8 %collective-permute-start.1 = (f32[7,8,128]{2,1,0:T(8,128)S(1)}, f32[7,8,128]{2,1,0:T(8,128)S(1)}, u32[]{:S(2)}, u32[]{:S(2)}) collective-permute-start(f32[7,8,128]{2,1,0:T(8,128)S(1)} %get-tuple-element.18), channel_id=1, source_target_pairs={{0,1},{1,0},{2,3},{3,2},{4,5},{5,4},{6,7},{7,6},{8,9},{9,8},{10,11... | collective-permute-start | bytes 86024 | tf_op jit(solution)/shard_map/ppermute | solution.py:481
  28.1 0.0 collective-permute-done.refs_1_.zb_ref
  28.1 0.8 %collective-permute-done.1.refs_2_.za_ref = f32[7,8,128]{2,1,0:T(8,128)S(1)} collective-permute-done((f32[7,8,128]{2,1,0:T(8,128)S(1)}, f32[7,8,128]{2,1,0:T(8,128)S(1)}, u32[]{:S(2)}, u32[]{:S(2)}) %collective-permute-start.1) | collective-permute-done | bytes 28704 | tf_op jit(solution)/shard_map/ppermute | solution.py:481
  28.9 0.0 all-to-all-done.refs_0_
  28.9 0.8 %shard_map.65 = f32[32,3,8,128]{3,2,1,0:T(8,128)} custom-call(f32[4,3,8,128]{3,2,1,0:T(8,128)S(1)} %all-to-all-done.refs_0_, f32[7,8,128]{2,1,0:T(8,128)S(1)} %collective-permute-done.refs_1_.zb_ref, f32[7,8,128]{2,1,0:T(8,128)S(1)} %collective-permute-done.1.refs_2_.za_ref), custom_call_target="tpu_custom_call" | custom-call | tf_op jit(solution)/shard_map/pallas_call | solution.py:491
  29.7 0.0 copy-start
  29.7 0.0 copy-start.1
  29.8 0.0 copy-start.2
  29.8 0.0 copy-start.4
  29.8 10.8 %all-to-all-start.1 = ((f32[32,3,8,128]{3,2,1,0:T(8,128)}), f32[32,3,8,128]{3,2,1,0:T(8,128)S(1)}, u32[]{:S(2)}, u32[]{:S(2)}) async-start(f32[32,3,8,128]{3,2,1,0:T(8,128)} %shard_map.65), calls=%async_computation.1 | async-start | bytes 786432 | tf_op jit(solution)/shard_map/all_to_all | solution.py:533
  40.6 0.0 copy-done
  40.6 0.0 copy-done.1
  40.6 0.0 copy-done.2
  40.6 0.0 copy-done.4
  40.6 0.0 copy-start.3
  40.6 0.9 %shard_map.66 = (f32[8,32,128]{2,1,0:T(8,128)S(1)}, f32[8,32,128]{2,1,0:T(8,128)S(1)}) custom-call(f32[8,32,128]{2,1,0:T(8,128)S(1)} %copy-done, f32[8,32,128]{2,1,0:T(8,128)S(1)} %copy-done.1, f32[8,32,128]{2,1,0:T(8,128)S(1)} %copy-done.2, f32[4,16,64]{2,1,0:T(8,128)S(1)} %copy-done.4, f32[7,8,128]{2,1,0:T(8,128)S(1)} %get-tuple-element.17.after_ref), custom_call_target="tpu_custom_call" | custom-call | tf_op jit(solution)/shard_map/pallas_call | solution.py:491
  41.6 14.1 %all-to-all-done.1.recv_ref = f32[32,3,8,128]{3,2,1,0:T(8,128)S(1)} async-done(((f32[32,3,8,128]{3,2,1,0:T(8,128)}), f32[32,3,8,128]{3,2,1,0:T(8,128)S(1)}, u32[]{:S(2)}, u32[]{:S(2)}) %all-to-all-start.1) | async-done | bytes 393248 | tf_op jit(solution)/shard_map/all_to_all | solution.py:533
  55.7 0.0 copy-done.3
  55.7 1.1 %shard_map.67 = (f32[8,32,128]{2,1,0:T(8,128)S(1)}, f32[2,2,8,128]{3,2,1,0:T(8,128)S(1)}, f32[40,128]{1,0:T(8,128)S(1)}, f32[40,128]{1,0:T(8,128)S(1)}) custom-call(s32[4]{0:T(128)S(1)} %bitcast.2, f32[32,3,8,128]{3,2,1,0:T(8,128)S(1)} %all-to-all-done.1.recv_ref, f32[8,32,128]{2,1,0:T(8,128)S(1)} %copy-done.3, f32[8,32,128]{2,1,0:T(8,128)S(1)} %copy-done, ...), custom_call_target="tpu_custom_call" | custom-call | tf_op jit(solution)/shard_map/pallas_call | solution.py:491
  56.8 2.4 %collective-permute-start.2 = (f32[40,128]{1,0:T(8,128)S(1)}, f32[40,128]{1,0:T(8,128)S(1)}, u32[]{:S(2)}, u32[]{:S(2)}) collective-permute-start(f32[40,128]{1,0:T(8,128)S(1)} %get-tuple-element.23.sya_ref), channel_id=1, source_target_pairs={{0,4},{4,0},{8,12},{12,8},{16,20},{20,16},{24,28},{28,24},{32,36},... | collective-permute-start | bytes 61448 | tf_op jit(solution)/shard_map/ppermute | solution.py:481
  59.2 4.4 %collective-permute-start.3 = (f32[40,128]{1,0:T(8,128)S(1)}, f32[40,128]{1,0:T(8,128)S(1)}, u32[]{:S(2)}, u32[]{:S(2)}) collective-permute-start(f32[40,128]{1,0:T(8,128)S(1)} %get-tuple-element.24.syb_ref), channel_id=1, source_target_pairs={{4,8},{8,4},{12,16},{16,12},{20,24},{24,20},{28,32},{32,28},{36,40... | collective-permute-start | bytes 61448 | tf_op jit(solution)/shard_map/ppermute | solution.py:481
  63.6 0.0 collective-permute-done.2.ya_ref
  63.6 3.4 %collective-permute-done.3.yb_ref = f32[40,128]{1,0:T(8,128)S(1)} collective-permute-done((f32[40,128]{1,0:T(8,128)S(1)}, f32[40,128]{1,0:T(8,128)S(1)}, u32[]{:S(2)}, u32[]{:S(2)}) %collective-permute-start.3) | collective-permute-done | bytes 20512 | tf_op jit(solution)/shard_map/ppermute | solution.py:481
  67.0 0.1 shard_map.68
  67.1 2.5 %collective-permute-start.4 = (f32[232,128]{1,0:T(8,128)S(1)}, f32[232,128]{1,0:T(8,128)S(1)}, u32[]{:S(2)}, u32[]{:S(2)}) collective-permute-start(f32[232,128]{1,0:T(8,128)S(1)} %get-tuple-element.25), channel_id=1, source_target_pairs={{0,128},{128,0},{256,384},{384,256},{512,640},{640,512},{768,896},... | collective-permute-start | bytes 356360 | tf_op jit(solution)/shard_map/ppermute | solution.py:481
  69.6 4.3 %collective-permute-start.5 = (f32[232,128]{1,0:T(8,128)S(1)}, f32[232,128]{1,0:T(8,128)S(1)}, u32[]{:S(2)}, u32[]{:S(2)}) collective-permute-start(f32[232,128]{1,0:T(8,128)S(1)} %get-tuple-element.26), channel_id=1, source_target_pairs={{128,256},{256,128},{384,512},{512,384},{640,768},{768,640},{129,2... | collective-permute-start | bytes 356360 | tf_op jit(solution)/shard_map/ppermute | solution.py:481
  73.9 0.0 collective-permute-done.4.xa_ref
  73.9 2.8 %collective-permute-done.5.xb_ref = f32[232,128]{1,0:T(8,128)S(1)} collective-permute-done((f32[232,128]{1,0:T(8,128)S(1)}, f32[232,128]{1,0:T(8,128)S(1)}, u32[]{:S(2)}, u32[]{:S(2)}) %collective-permute-start.5) | collective-permute-done | bytes 118816 | tf_op jit(solution)/shard_map/ppermute | solution.py:481
  76.7 1.4 %shard_map.69 = f32[8,32,128]{2,1,0:T(8,128)} custom-call(f32[8,32,128]{2,1,0:T(8,128)S(1)} %get-tuple-element.21.start_ref, f32[8,32,128]{2,1,0:T(8,128)S(1)} %copy-done, f32[8,32,128]{2,1,0:T(8,128)S(1)} %get-tuple-element.19.src_ref, f32[8,32,128]{2,1,0:T(8,128)S(1)} %get-tuple-element.20.rea_ref, f32[2,2,8,128]{3,2,1,0:T(8,128)S(1)} %get-tuple-element.22.zhalo_ref, ...), custom_call_target="tpu_custom_call" | custom-call | tf_op jit(solution)/shard_map/pallas_call | solution.py:491
Async XLA Ops:
  0.0 0.7 copy-start.5
  3.3 25.6 %all-to-all-start = ((f32[4,3,8,128]{3,2,1,0:T(8,128)}), f32[4,3,8,128]{3,2,1,0:T(8,128)S(1)}, u32[]{:S(2)}, u32[]{:S(2)}) async-start(f32[4,3,8,128]{3,2,1,0:T(8,128)} %get-tuple-element.16), calls=%async_computation | async-start | bytes 98304 | tf_op jit(solution)/shard_map/all_to_all | solution.py:526
  7.6 20.5 %collective-permute-start = (f32[7,8,128]{2,1,0:T(8,128)S(1)}, f32[7,8,128]{2,1,0:T(8,128)S(1)}, u32[]{:S(2)}, u32[]{:S(2)}) collective-permute-start(f32[7,8,128]{2,1,0:T(8,128)S(1)} %get-tuple-element.17.after_ref), channel_id=1, source_target_pairs={{1,2},{2,1},{5,6},{6,5},{9,10},{10,9},{13,14},{14,13},{17,18},{18,... | collective-permute-start | bytes 86024 | tf_op jit(solution)/shard_map/ppermute | solution.py:481
  8.2 20.7 %collective-permute-start.1 = (f32[7,8,128]{2,1,0:T(8,128)S(1)}, f32[7,8,128]{2,1,0:T(8,128)S(1)}, u32[]{:S(2)}, u32[]{:S(2)}) collective-permute-start(f32[7,8,128]{2,1,0:T(8,128)S(1)} %get-tuple-element.18), channel_id=1, source_target_pairs={{0,1},{1,0},{2,3},{3,2},{4,5},{5,4},{6,7},{7,6},{8,9},{9,8},{10,11... | collective-permute-start | bytes 86024 | tf_op jit(solution)/shard_map/ppermute | solution.py:481
  29.7 10.8 %copy-start = (f32[8,32,128]{2,1,0:T(8,128)S(1)}, f32[8,32,128]{2,1,0:T(8,128)}, u32[]{:S(2)}) copy-start(f32[8,32,128]{2,1,0:T(8,128)} %conduct_ref.7) | copy-start | bytes 393220
  29.7 10.8 %copy-start.1 = (f32[8,32,128]{2,1,0:T(8,128)S(1)}, f32[8,32,128]{2,1,0:T(8,128)}, u32[]{:S(2)}) copy-start(f32[8,32,128]{2,1,0:T(8,128)} %source_ref.1) | copy-start | bytes 393220
  29.8 10.9 %copy-start.2 = (f32[8,32,128]{2,1,0:T(8,128)S(1)}, f32[8,32,128]{2,1,0:T(8,128)}, u32[]{:S(2)}) copy-start(f32[8,32,128]{2,1,0:T(8,128)} %reaction_ref.1) | copy-start | bytes 393220
  29.8 10.9 %copy-start.4 = (f32[4,16,64]{2,1,0:T(8,128)S(1)}, f32[4,16,64]{2,1,0:T(8,128)}, u32[]{:S(2)}) copy-start(f32[4,16,64]{2,1,0:T(8,128)} %coarse_ref.1) | copy-start | bytes 49156
  29.8 25.9 %all-to-all-start.1 = ((f32[32,3,8,128]{3,2,1,0:T(8,128)}), f32[32,3,8,128]{3,2,1,0:T(8,128)S(1)}, u32[]{:S(2)}, u32[]{:S(2)}) async-start(f32[32,3,8,128]{3,2,1,0:T(8,128)} %shard_map.65), calls=%async_computation.1 | async-start | bytes 786432 | tf_op jit(solution)/shard_map/all_to_all | solution.py:533
  40.6 15.1 %copy-start.3 = (f32[8,32,128]{2,1,0:T(8,128)S(1)}, f32[8,32,128]{2,1,0:T(8,128)}, u32[]{:S(2)}) copy-start(f32[8,32,128]{2,1,0:T(8,128)} %old_ref.1) | copy-start | bytes 393220
  56.8 6.8 %collective-permute-start.2 = (f32[40,128]{1,0:T(8,128)S(1)}, f32[40,128]{1,0:T(8,128)S(1)}, u32[]{:S(2)}, u32[]{:S(2)}) collective-permute-start(f32[40,128]{1,0:T(8,128)S(1)} %get-tuple-element.23.sya_ref), channel_id=1, source_target_pairs={{0,4},{4,0},{8,12},{12,8},{16,20},{20,16},{24,28},{28,24},{32,36},... | collective-permute-start | bytes 61448 | tf_op jit(solution)/shard_map/ppermute | solution.py:481
  59.2 7.8 %collective-permute-start.3 = (f32[40,128]{1,0:T(8,128)S(1)}, f32[40,128]{1,0:T(8,128)S(1)}, u32[]{:S(2)}, u32[]{:S(2)}) collective-permute-start(f32[40,128]{1,0:T(8,128)S(1)} %get-tuple-element.24.syb_ref), channel_id=1, source_target_pairs={{4,8},{8,4},{12,16},{16,12},{20,24},{24,20},{28,32},{32,28},{36,40... | collective-permute-start | bytes 61448 | tf_op jit(solution)/shard_map/ppermute | solution.py:481
  67.1 6.8 %collective-permute-start.4 = (f32[232,128]{1,0:T(8,128)S(1)}, f32[232,128]{1,0:T(8,128)S(1)}, u32[]{:S(2)}, u32[]{:S(2)}) collective-permute-start(f32[232,128]{1,0:T(8,128)S(1)} %get-tuple-element.25), channel_id=1, source_target_pairs={{0,128},{128,0},{256,384},{384,256},{512,640},{640,512},{768,896},... | collective-permute-start | bytes 356360 | tf_op jit(solution)/shard_map/ppermute | solution.py:481
  69.6 7.1 %collective-permute-start.5 = (f32[232,128]{1,0:T(8,128)S(1)}, f32[232,128]{1,0:T(8,128)S(1)}, u32[]{:S(2)}, u32[]{:S(2)}) collective-permute-start(f32[232,128]{1,0:T(8,128)S(1)} %get-tuple-element.26), channel_id=1, source_target_pairs={{128,256},{256,128},{384,512},{512,384},{640,768},{768,640},{129,2... | collective-permute-start | bytes 356360 | tf_op jit(solution)/shard_map/ppermute | solution.py:481

commit v6 on v5

--- a/solution.py
+++ b/solution.py
@@ -90,7 +90,7 @@
 
 def first_kernel(
     home_ref, old_hbm, conduct_hbm, source_hbm, reaction_hbm, coarse_hbm,
-    zb_ref, za_ref, parts_ref, old_ref, rows_ref, coarse_ref, old_sems, sems, coarse_sem,
+    za_ref, zb_ref, parts_ref, old_ref, rows_ref, coarse_ref, old_sems, sems, coarse_sem,
 ):
     slots = home_ref.shape[0]
     width = LANES // slots
@@ -157,8 +157,12 @@
         write_pair("gz", za_ref, zb_ref, i, faces[0][i], faces[1][i])
 
 
-def fold_kernel(conduct_ref, source_ref, reaction_ref, coarse_ref, after_ref, src_ref, rea_ref):
-    del after_ref
+def fold_kernel(
+    home_ref, old_ref, conduct_ref, source_ref, reaction_ref, coarse_ref, za_ref, zb_ref,
+    src_ref, rea_ref, ya_ref, yb_ref,
+):
+    slots = home_ref.shape[0]
+    width = LANES // slots
     nx, nz, _ = conduct_ref.shape
     (x_first, x_last), (z_first, z_last), (y_first, y_last) = edges()
     refined = refine(coarse_ref)
@@ -179,9 +183,34 @@
         src_ref[x] = source_ref[x] + weight * refined[x // 2]
         rea_ref[x] = 1.0 + reaction_ref[x] + weight
 
-
-def address_kernel(parts_ref, zb_ref, za_ref, send_ref, *, width):
-    planes = send_ref.shape[1] - 1
+    low = high = jnp.zeros((nz, LANES), F32)
+    for f, (ref, depth) in enumerate(
+        ((old_ref, 0), (old_ref, 1), (conduct_ref, 0), (conduct_ref, 1), (src_ref, 0), (rea_ref, 0))
+    ):
+        for x in range(nx):
+            spot = f * nx + x
+            low = jnp.where(lane == spot, roll_lanes(ref[x], spot - depth), low)
+            high = jnp.where(lane == spot, roll_lanes(ref[x], spot + 1 + depth), high)
+    write_pair("gy", ya_ref, yb_ref, slice(0, nz), low, high)
+
+    lane = lane_of((nx, LANES))
+    slot, _ = moved_slot(home_ref, slots)
+    low = high = jnp.where(lane == 4, slot, 0).astype(F32)
+    notes = received("gz", za_ref[RIM], zb_ref[RIM])
+    for side in range(2):
+        note = jnp.broadcast_to(notes[side][:, 3 * width : 3 * width + 1], (nx, LANES))
+        low = jnp.where(lane == 5 + side, note, low)
+        high = jnp.where(lane == 5 + side, note, high)
+        for f, tile in enumerate((PHI1, KAP1)):
+            value = received("gz", za_ref[tile], zb_ref[tile])[side]
+            spot = 2 * side + f
+            low = jnp.where(lane == spot, roll_lanes(value, spot), low)
+            high = jnp.where(lane == spot, roll_lanes(value, spot + 1), high)
+    write_pair("gy", ya_ref, yb_ref, slice(nz, nz + nx), low, high)
+
+
+def address_kernel(parts_ref, za_ref, zb_ref, send_ref, *, width):
+    planes = send_ref.shape[1] - 2
     low, high = received("gz", za_ref[RIM], zb_ref[RIM])
     shape = low.shape
     lane = lane_of(shape)
@@ -191,13 +220,27 @@
     lower = lane < 2 * width
     rims = jnp.where(lower, low, high)
     tag = jnp.where(lower, low_tag, high_tag)
+    column = lax.rem(lane, width)
+    beside = jnp.where(column < 2, -1.0, jnp.where(column >= width - 2, 1.0, -4096.0))
+    edge = jnp.where(column == 0, -1.0, jnp.where(column == width - 1, 1.0, -4096.0))
+    count = parts_ref.shape[0]
+    columns = [
+        (roll_lanes(parts_ref[k, planes] + beside, 4 * i), roll_lanes(parts_ref[k, i], 4 * i))
+        for k in range(count)
+        for i in range(planes)
+    ]
+    columns.append((roll_lanes(tag + edge, 4 * planes), roll_lanes(rims, 4 * planes)))
     for device in range(send_ref.shape[0]):
         for i in range(planes):
             value = jnp.zeros(shape, F32)
-            for k in range(parts_ref.shape[0]):
+            for k in range(count):
                 value = jnp.where(parts_ref[k, planes] == device, parts_ref[k, i], value)
             send_ref[device, i] = value
         send_ref[device, planes] = jnp.where(tag == device, rims, 0.0)
+        value = jnp.zeros(shape, F32)
+        for spot, source in columns:
+            value = jnp.where(spot == device, source, value)
+        send_ref[device, planes + 1] = value
 
 
 def spread(tile, offset, width):
@@ -209,24 +252,29 @@
 
 
 def place_kernel(
-    home_ref, recv_ref, old_ref, conduct_ref, src_ref, rea_ref, za_ref, zb_ref,
-    start_ref, zhalo_ref, ya_ref, yb_ref,
+    home_ref, recv_ref, old_ref, za_ref, zb_ref, ya_ref, yb_ref,
+    start_ref, zhalo_ref, yhalo_ref, own_ref,
 ):
     slots = home_ref.shape[0]
     width = LANES // slots
     nx, nz, _ = old_ref.shape
     rows = nz // slots
     slot, _ = moved_slot(home_ref, slots)
-    planes = recv_ref.shape[1] - 1
+    planes = recv_ref.shape[1] - 2
     run = nx // planes
     count = recv_ref.shape[0]
     here = lax.div(lane_of((rows, LANES)), width) == slot
+
+    def total(first, stride, tile):
+        value = recv_ref[first, tile]
+        for source in range(first + stride, count, stride):
+            value = value + recv_ref[source, tile]
+        return value
+
     for k in range(run):
         for i in range(planes):
             x = k * planes + i
-            arrived = recv_ref[k, i]
-            for source in range(k + run, count, run):
-                arrived = arrived + recv_ref[source, i]
+            arrived = total(k, run, i)
             for g in range(slots):
                 shift = lax.rem(width * (slot - g) + LANES, LANES)
                 part = pl.ds(g * rows, rows)
@@ -234,9 +282,7 @@
                     here, pltpu.roll(arrived, shift, 1), old_ref[x, part, :]
                 )
 
-    rims = recv_ref[0, planes]
-    for source in range(1, count):
-        rims = rims + recv_ref[source, planes]
+    rims = total(0, 1, planes)
     faces = [received("gz", za_ref[i], zb_ref[i]) for i in range(7)]
     group = lax.div(lane_of((nx, LANES)), width).astype(F32)
     for side in range(2):
@@ -246,28 +292,52 @@
             moved = spread(rims, (2 * side + depth) * width, width)
             zhalo_ref[side, depth] = jnp.where(there, moved, faces[depth][side])
 
+    beside = [total(k, run, planes + 1) for k in range(run)]
+    every = beside[0]
+    for k in range(1, run):
+        every = every + beside[k]
+    lane = lane_of((rows, LANES))
+    corner_lane = lane_of((nx, LANES))
+    halos = received("gy", ya_ref[:nz], yb_ref[:nz])
+    corners = received("gy", ya_ref[nz : nz + nx], yb_ref[nz : nz + nx])
+    for side in range(2):
+        outer = width - 1 if side == 0 else 0
+        inward = -1 if side == 0 else 1
+        touched = float(slots - 1 if side == 0 else 0)
+        note = jnp.broadcast_to(corners[side][0:1, 4:5], (rows, LANES)) == touched
+        for g in range(slots):
+            value = jnp.zeros((rows, LANES), F32)
+            for x in range(nx):
+                source = beside[x // planes]
+                for depth in range(2):
+                    at = g * width + outer + inward * depth + 4 * (x % planes)
+                    spot = depth * nx + x
+                    value = jnp.where(lane == spot, roll_lanes(source, spot - at), value)
+            held = halos[side][g * rows : (g + 1) * rows]
+            yhalo_ref[side, g * rows : (g + 1) * rows] = jnp.where(
+                note & (lane < 2 * nx), value, held
+            )
+        corner = corners[side]
+        for z_side in range(2):
+            note = jnp.broadcast_to(corner[:, 5 + z_side : 6 + z_side], (nx, LANES)) == touched
+            at = 2 * width * z_side + outer + 4 * planes
+            spot = 2 * z_side
+            corner = jnp.where(
+                note & (corner_lane == spot), roll_lanes(every, spot - at), corner
+            )
+        yhalo_ref[side, nz : nz + nx] = corner
+
     lane = lane_of((nz, LANES))
     low = high = jnp.zeros((nz, LANES), F32)
-    for f, (ref, depth) in enumerate(
-        ((start_ref, 0), (start_ref, 1), (conduct_ref, 0), (conduct_ref, 1), (src_ref, 0), (rea_ref, 0))
-    ):
-        for x in range(nx):
-            spot = f * nx + x
-            low = jnp.where(lane == spot, roll_lanes(ref[x], spot - depth), low)
-            high = jnp.where(lane == spot, roll_lanes(ref[x], spot + 1 + depth), high)
-    write_pair("gy", ya_ref, yb_ref, slice(0, nz), low, high)
-    lane = lane_of((nx, LANES))
-    low = high = jnp.zeros((nx, LANES), F32)
-    for side in range(2):
-        for f, tile in enumerate((zhalo_ref[side, 0], faces[KAP1][side])):
-            spot = 2 * side + f
-            low = jnp.where(lane == spot, roll_lanes(tile, spot), low)
-            high = jnp.where(lane == spot, roll_lanes(tile, spot + 1), high)
-    write_pair("gy", ya_ref, yb_ref, slice(nz, nz + nx), low, high)
+    for x in range(nx):
+        low = jnp.where(lane == x, roll_lanes(start_ref[x], x), low)
+        high = jnp.where(lane == x, roll_lanes(start_ref[x], x + 1), high)
+    own_ref[0] = low
+    own_ref[1] = high
 
 
 def edge_kernel(
-    start_ref, conduct_ref, src_ref, rea_ref, zhalo_ref, za_ref, zb_ref, ya_ref, yb_ref,
+    start_ref, conduct_ref, src_ref, rea_ref, zhalo_ref, yhalo_ref, za_ref, zb_ref,
     xa_ref, xb_ref,
 ):
     nx, nz, _ = start_ref.shape
@@ -289,7 +359,8 @@
             )
     lane = lane_of((nz, LANES))
     low = high = jnp.zeros((nz, LANES), F32)
-    for side, halo in enumerate(received("gy", ya_ref[:nz], yb_ref[:nz])):
+    for side in range(2):
+        halo = yhalo_ref[side, :nz]
         for f, offset in enumerate((PHI1 * nx, KAP1 * nx)):
             spot = 2 * side + f
             low = jnp.where(lane == spot, roll_lanes(halo, spot - offset), low)
@@ -350,8 +421,8 @@
 
 
 def sweeps_kernel(
-    start_ref, conduct_ref, src_ref, rea_ref, zhalo_ref,
-    za_ref, zb_ref, sya_ref, syb_ref, ya_ref, yb_ref, xa_ref, xb_ref,
+    start_ref, conduct_ref, src_ref, rea_ref, zhalo_ref, yhalo_ref, own_ref,
+    za_ref, zb_ref, sya_ref, syb_ref, xa_ref, xb_ref,
     out_ref,
 ):
     nx, nz, _ = start_ref.shape
@@ -367,8 +438,8 @@
     xrows = part("gx", xa_ref, xb_ref, base, 8)
     xcols = part("gx", xa_ref, xb_ref, base + 8, nz)
     zf = [received("gz", za_ref[i], zb_ref[i]) for i in range(6)]
-    yf = part("gy", ya_ref, yb_ref, 0, nz)
-    yt = part("gy", ya_ref, yb_ref, nz, nx)
+    yf = [yhalo_ref[side, :nz] for side in range(2)]
+    yt = [yhalo_ref[side, nz : nz + nx] for side in range(2)]
     sf = sent("gy", sya_ref[:nz], syb_ref[:nz])
 
     def columns(tile, phi_spot, kappa_spot, lane):
@@ -416,7 +487,7 @@
     for side in range(2):
         phi, phi2, kappa, kappa2, src, rea = [roll_lanes(yf[side], -f * nx) for f in range(6)]
         at = 2 * side
-        sides = [(phi2, kappa2, None), (sf[side], roll_lanes(sf[side], -KAP1 * nx), None)]
+        sides = [(phi2, kappa2, None), (own_ref[side], roll_lanes(sf[side], -KAP1 * nx), None)]
         sides += along_rows(
             phi,
             kappa,
@@ -506,7 +577,7 @@
     line = lax.axis_size("gy")
     part = nx // RUN
 
-    szb, sza, parts = call(
+    sza, szb, parts = call(
         first_kernel,
         (home, old_field, conduct, source, reaction, coarse),
         [(7, nx, ny), (7, nx, ny), (RUN, part + 1, rows, ny)],
@@ -524,29 +595,34 @@
     za, zb = swap("gz", sza, szb)
     groups = [[i * RUN + k for k in range(RUN)] for i in range(line // RUN)]
     parts = lax.all_to_all(parts, "gy", 0, 0, tiled=True, axis_index_groups=groups)
-    src, rea = call(fold_kernel, (conduct, source, reaction, coarse, szb), [block, block])
 
     def address(*refs):
         address_kernel(*refs, width=width)
 
-    (send,) = call(address, (parts, zb, za), [(line, part + 1, rows, ny)])
+    (send,) = call(address, (parts, za, zb), [(line, part + 2, rows, ny)])
     recv = lax.all_to_all(send, "gy", 0, 0, tiled=True)
-    start, zhalo, sya, syb = call(
+    src, rea, sya, syb = call(
+        fold_kernel,
+        (home, old_field, conduct, source, reaction, coarse, za, zb),
+        [block, block, (nz + nx, ny), (nz + nx, ny)],
+        smem=1,
+    )
+    ya, yb = swap("gy", sya, syb)
+    start, zhalo, yhalo, own = call(
         place_kernel,
-        (home, recv, old_field, conduct, src, rea, za, zb),
-        [block, (2, 2, nx, ny), (nz + nx, ny), (nz + nx, ny)],
+        (home, recv, old_field, za, zb, ya, yb),
+        [block, (2, 2, nx, ny), (2, nz + nx, ny), (2, nz, ny)],
         smem=1,
     )
-    ya, yb = swap("gy", sya, syb)
     xa, xb = call(
         edge_kernel,
-        (start, conduct, src, rea, zhalo, za, zb, ya, yb),
+        (start, conduct, src, rea, zhalo, yhalo, za, zb),
         [(7 * nz + 8, ny)] * 2,
     )
     xa, xb = swap("gx", xa, xb)
     (relaxed,) = call(
         sweeps_kernel,
-        (start, conduct, src, rea, zhalo, za, zb, sya, syb, ya, yb, xa, xb),
+        (start, conduct, src, rea, zhalo, yhalo, own, za, zb, sya, syb, xa, xb),
         [block],
     )
     return relaxed

time: 78.7 us -> 65.4 us (0.83)
  the two profiles are of different devices: /device:TPU:72 before, /device:TPU:65 now
where the time goes in v6:
time: 65.4 us; the launch traced here: 64.8 us
  starting transfers between devices  45.3 us (69%)
  waiting for transfers between devices  11 us (17%)
  Pallas kernels  7.76 us (12%)
  local copies, waits for them, and re-layouts  0.68 us (1%)
    ppermute x6, starting transfers between devices, swap(): results.append(lax.ppermute(value, axis, pairs))  30.9 us
    all_to_all x1, starting transfers between devices, on_device(): recv = lax.all_to_all(send, 'gy', 0, 0, tiled=True)  10.3 us
    pallas_call x6, Pallas kernels, call(): pl.pallas_call(kernel, out_shape=[jax.ShapeDtypeStruct(shape, F32) for sh...  7.76 us
    all_to_all x1, waiting for transfers between devices, on_device(): recv = lax.all_to_all(send, 'gy', 0, 0, tiled=True)  6.53 us
    ppermute x6, waiting for transfers between devices, swap(): results.append(lax.ppermute(value, axis, pairs))  4.45 us
    all_to_all x1, starting transfers between devices, on_device(): lax.all_to_all(parts, 'gy', 0, 0, tiled=True, axis_index_groups=groups)  4.02 us
  transfers between devices with their start and end apart: 8, of which 4 were waited for; matrix products, arithmetic and copies ran while one was open for 0% of the time, Pallas kernels for 2%

profile of v6, /device:TPU:65, one launch (start us, length us, event | category | flops | bytes accessed | tf_op | source)
XLA Modules:
  0.0 64.8 jit_solution(7264380410702464467)
XLA Ops:
  0.0 0.0 copy-start.5
  0.0 0.7 %copy-done.5 = s32[1,1,4]{2,1,0:T(1,128)S(1)} copy-done((s32[1,1,4]{2,1,0:T(1,128)S(1)}, s32[1,1,4]{2,1,0:T(1,128)}, u32[]{:S(2)}) %copy-start.5) | copy-done | bytes 40
  0.7 2.6 %shard_map.64 = (f32[7,8,128]{2,1,0:T(8,128)S(1)}, f32[7,8,128]{2,1,0:T(8,128)S(1)}, f32[4,3,8,128]{3,2,1,0:T(8,128)}) custom-call(s32[4]{0:T(128)S(1)} %bitcast.1, f32[8,32,128]{2,1,0:T(8,128)} %old_ref.3, f32[8,32,128]{2,1,0:T(8,128)} %conduct_ref.5, f32[8,32,128]{2,1,0:T(8,128)} %source_ref.1, f32[8,32,128]{2,1,0:T(8,128)} %reaction_ref.1, ...), custom_call_target="tpu_custom_call" | custom-call | tf_op jit(solution)/shard_map/pallas_call | solution.py:562
  3.3 4.0 %all-to-all-start = ((f32[4,3,8,128]{3,2,1,0:T(8,128)}), f32[4,3,8,128]{3,2,1,0:T(8,128)S(1)}, u32[]{:S(2)}, u32[]{:S(2)}) async-start(f32[4,3,8,128]{3,2,1,0:T(8,128)} %get-tuple-element.18), calls=%async_computation | async-start | bytes 98304 | tf_op jit(solution)/shard_map/all_to_all | solution.py:597
  7.3 2.9 %collective-permute-start = (f32[7,8,128]{2,1,0:T(8,128)S(1)}, f32[7,8,128]{2,1,0:T(8,128)S(1)}, u32[]{:S(2)}, u32[]{:S(2)}) collective-permute-start(f32[7,8,128]{2,1,0:T(8,128)S(1)} %get-tuple-element.19), channel_id=1, source_target_pairs={{0,1},{1,0},{2,3},{3,2},{4,5},{5,4},{6,7},{7,6},{8,9},{9,8},{10,11... | collective-permute-start | bytes 86024 | tf_op jit(solution)/shard_map/ppermute | solution.py:552
  10.2 18.1 %collective-permute-start.1 = (f32[7,8,128]{2,1,0:T(8,128)S(1)}, f32[7,8,128]{2,1,0:T(8,128)S(1)}, u32[]{:S(2)}, u32[]{:S(2)}) collective-permute-start(f32[7,8,128]{2,1,0:T(8,128)S(1)} %get-tuple-element.20), channel_id=1, source_target_pairs={{1,2},{2,1},{5,6},{6,5},{9,10},{10,9},{13,14},{14,13},{17,18},{18,... | collective-permute-start | bytes 86024 | tf_op jit(solution)/shard_map/ppermute | solution.py:552
  28.2 0.0 collective-permute-done.refs_1_.za_ref
  28.3 1.5 %collective-permute-done.1.refs_2_.zb_ref = f32[7,8,128]{2,1,0:T(8,128)S(1)} collective-permute-done((f32[7,8,128]{2,1,0:T(8,128)S(1)}, f32[7,8,128]{2,1,0:T(8,128)S(1)}, u32[]{:S(2)}, u32[]{:S(2)}) %collective-permute-start.1) | collective-permute-done | bytes 28704 | tf_op jit(solution)/shard_map/ppermute | solution.py:552
  29.8 0.0 all-to-all-done.refs_0_
  29.8 1.0 %shard_map.65 = f32[32,4,8,128]{3,2,1,0:T(8,128)} custom-call(f32[4,3,8,128]{3,2,1,0:T(8,128)S(1)} %all-to-all-done.refs_0_, f32[7,8,128]{2,1,0:T(8,128)S(1)} %collective-permute-done.refs_1_.za_ref, f32[7,8,128]{2,1,0:T(8,128)S(1)} %collective-permute-done.1.refs_2_.zb_ref), custom_call_target="tpu_custom_call" | custom-call | tf_op jit(solution)/shard_map/pallas_call | solution.py:562
  30.8 0.0 copy-start
  30.8 0.0 copy-start.1
  30.8 0.0 copy-start.2
  30.8 0.0 copy-start.3
  30.8 0.0 copy-start.4
  30.8 10.3 %all-to-all-start.1 = ((f32[32,4,8,128]{3,2,1,0:T(8,128)}), f32[32,4,8,128]{3,2,1,0:T(8,128)S(1)}, u32[]{:S(2)}, u32[]{:S(2)}) async-start(f32[32,4,8,128]{3,2,1,0:T(8,128)} %shard_map.65), calls=%async_computation.1 | async-start | bytes 1048576 | tf_op jit(solution)/shard_map/all_to_all | solution.py:603
  41.2 0.0 copy-done
  41.2 0.0 copy-done.1
  41.2 0.0 copy-done.2
  41.2 0.0 copy-done.3
  41.2 0.0 copy-done.4
  41.2 1.6 %shard_map.66 = (f32[8,32,128]{2,1,0:T(8,128)S(1)}, f32[8,32,128]{2,1,0:T(8,128)S(1)}, f32[40,128]{1,0:T(8,128)S(1)}, f32[40,128]{1,0:T(8,128)S(1)}) custom-call(s32[4]{0:T(128)S(1)} %bitcast.2, f32[8,32,128]{2,1,0:T(8,128)S(1)} %copy-done.1, f32[8,32,128]{2,1,0:T(8,128)S(1)} %copy-done, f32[8,32,128]{2,1,0:T(8,128)S(1)} %copy-done.2, ...), custom_call_target="tpu_custom_call" | custom-call | tf_op jit(solution)/shard_map/pallas_call | solution.py:562
  42.8 3.1 %collective-permute-start.2 = (f32[40,128]{1,0:T(8,128)S(1)}, f32[40,128]{1,0:T(8,128)S(1)}, u32[]{:S(2)}, u32[]{:S(2)}) collective-permute-start(f32[40,128]{1,0:T(8,128)S(1)} %get-tuple-element.21.sya_ref), channel_id=1, source_target_pairs={{0,4},{4,0},{8,12},{12,8},{16,20},{20,16},{24,28},{28,24},{32,36},... | collective-permute-start | bytes 61448 | tf_op jit(solution)/shard_map/ppermute | solution.py:552
  45.9 0.7 %collective-permute-start.3 = (f32[40,128]{1,0:T(8,128)S(1)}, f32[40,128]{1,0:T(8,128)S(1)}, u32[]{:S(2)}, u32[]{:S(2)}) collective-permute-start(f32[40,128]{1,0:T(8,128)S(1)} %get-tuple-element.22.syb_ref), channel_id=1, source_target_pairs={{4,8},{8,4},{12,16},{16,12},{20,24},{24,20},{28,32},{32,28},{36,40... | collective-permute-start | bytes 61448 | tf_op jit(solution)/shard_map/ppermute | solution.py:552
  46.6 0.7 %collective-permute-done.2.ya_ref = f32[40,128]{1,0:T(8,128)S(1)} collective-permute-done((f32[40,128]{1,0:T(8,128)S(1)}, f32[40,128]{1,0:T(8,128)S(1)}, u32[]{:S(2)}, u32[]{:S(2)}) %collective-permute-start.2) | collective-permute-done | bytes 20512 | tf_op jit(solution)/shard_map/ppermute | solution.py:552
  47.3 0.0 collective-permute-done.3.yb_ref
  47.3 6.5 %all-to-all-done.1.recv_ref = f32[32,4,8,128]{3,2,1,0:T(8,128)S(1)} async-done(((f32[32,4,8,128]{3,2,1,0:T(8,128)}), f32[32,4,8,128]{3,2,1,0:T(8,128)S(1)}, u32[]{:S(2)}, u32[]{:S(2)}) %all-to-all-start.1) | async-done | bytes 524320 | tf_op jit(solution)/shard_map/all_to_all | solution.py:603
  53.8 1.0 %shard_map.67 = (f32[8,32,128]{2,1,0:T(8,128)S(1)}, f32[2,2,8,128]{3,2,1,0:T(8,128)S(1)}, f32[2,40,128]{2,1,0:T(8,128)S(1)}, f32[2,32,128]{2,1,0:T(8,128)S(1)}) custom-call(s32[4]{0:T(128)S(1)} %bitcast.3, f32[32,4,8,128]{3,2,1,0:T(8,128)S(1)} %all-to-all-done.1.recv_ref, f32[8,32,128]{2,1,0:T(8,128)S(1)} %copy-done.1, ...), custom_call_target="tpu_custom_call" | custom-call | tf_op jit(solution)/shard_map/pallas_call | solution.py:562
  54.9 0.1 shard_map.68
  55.0 2.2 %collective-permute-start.4 = (f32[232,128]{1,0:T(8,128)S(1)}, f32[232,128]{1,0:T(8,128)S(1)}, u32[]{:S(2)}, u32[]{:S(2)}) collective-permute-start(f32[232,128]{1,0:T(8,128)S(1)} %get-tuple-element.29), channel_id=1, source_target_pairs={{0,128},{128,0},{256,384},{384,256},{512,640},{640,512},{768,896},... | collective-permute-start | bytes 356360 | tf_op jit(solution)/shard_map/ppermute | solution.py:552
  57.2 4.0 %collective-permute-start.5 = (f32[232,128]{1,0:T(8,128)S(1)}, f32[232,128]{1,0:T(8,128)S(1)}, u32[]{:S(2)}, u32[]{:S(2)}) collective-permute-start(f32[232,128]{1,0:T(8,128)S(1)} %get-tuple-element.30), channel_id=1, source_target_pairs={{128,256},{256,128},{384,512},{512,384},{640,768},{768,640},{129,2... | collective-permute-start | bytes 356360 | tf_op jit(solution)/shard_map/ppermute | solution.py:552
  61.2 0.0 collective-permute-done.4.xa_ref
  61.2 2.2 %collective-permute-done.5.xb_ref = f32[232,128]{1,0:T(8,128)S(1)} collective-permute-done((f32[232,128]{1,0:T(8,128)S(1)}, f32[232,128]{1,0:T(8,128)S(1)}, u32[]{:S(2)}, u32[]{:S(2)}) %collective-permute-start.5) | collective-permute-done | bytes 118816 | tf_op jit(solution)/shard_map/ppermute | solution.py:552
  63.4 1.4 %shard_map.69 = f32[8,32,128]{2,1,0:T(8,128)} custom-call(f32[8,32,128]{2,1,0:T(8,128)S(1)} %get-tuple-element.23.start_ref, f32[8,32,128]{2,1,0:T(8,128)S(1)} %copy-done, f32[8,32,128]{2,1,0:T(8,128)S(1)} %get-tuple-element.24.src_ref, f32[8,32,128]{2,1,0:T(8,128)S(1)} %get-tuple-element.25.rea_ref, f32[2,2,8,128]{3,2,1,0:T(8,128)S(1)} %get-tuple-element.26.zhalo_ref, ...), custom_call_target="tpu_custom_call" | custom-call | tf_op jit(solution)/shard_map/pallas_call | solution.py:562
Async XLA Ops:
  0.0 0.7 %copy-start.5 = (s32[1,1,4]{2,1,0:T(1,128)S(1)}, s32[1,1,4]{2,1,0:T(1,128)}, u32[]{:S(2)}) copy-start(s32[1,1,4]{2,1,0:T(1,128)} %param.7) | copy-start | bytes 52
  3.3 26.5 %all-to-all-start = ((f32[4,3,8,128]{3,2,1,0:T(8,128)}), f32[4,3,8,128]{3,2,1,0:T(8,128)S(1)}, u32[]{:S(2)}, u32[]{:S(2)}) async-start(f32[4,3,8,128]{3,2,1,0:T(8,128)} %get-tuple-element.18), calls=%async_computation | async-start | bytes 98304 | tf_op jit(solution)/shard_map/all_to_all | solution.py:597
  7.3 20.9 %collective-permute-start = (f32[7,8,128]{2,1,0:T(8,128)S(1)}, f32[7,8,128]{2,1,0:T(8,128)S(1)}, u32[]{:S(2)}, u32[]{:S(2)}) collective-permute-start(f32[7,8,128]{2,1,0:T(8,128)S(1)} %get-tuple-element.19), channel_id=1, source_target_pairs={{0,1},{1,0},{2,3},{3,2},{4,5},{5,4},{6,7},{7,6},{8,9},{9,8},{10,11... | collective-permute-start | bytes 86024 | tf_op jit(solution)/shard_map/ppermute | solution.py:552
  10.2 19.6 %collective-permute-start.1 = (f32[7,8,128]{2,1,0:T(8,128)S(1)}, f32[7,8,128]{2,1,0:T(8,128)S(1)}, u32[]{:S(2)}, u32[]{:S(2)}) collective-permute-start(f32[7,8,128]{2,1,0:T(8,128)S(1)} %get-tuple-element.20), channel_id=1, source_target_pairs={{1,2},{2,1},{5,6},{6,5},{9,10},{10,9},{13,14},{14,13},{17,18},{18,... | collective-permute-start | bytes 86024 | tf_op jit(solution)/shard_map/ppermute | solution.py:552
  30.8 10.3 %copy-start = (f32[8,32,128]{2,1,0:T(8,128)S(1)}, f32[8,32,128]{2,1,0:T(8,128)}, u32[]{:S(2)}) copy-start(f32[8,32,128]{2,1,0:T(8,128)} %conduct_ref.5) | copy-start | bytes 393220
  30.8 10.4 %copy-start.1 = (f32[8,32,128]{2,1,0:T(8,128)S(1)}, f32[8,32,128]{2,1,0:T(8,128)}, u32[]{:S(2)}) copy-start(f32[8,32,128]{2,1,0:T(8,128)} %old_ref.3) | copy-start | bytes 393220
  30.8 10.4 %copy-start.2 = (f32[8,32,128]{2,1,0:T(8,128)S(1)}, f32[8,32,128]{2,1,0:T(8,128)}, u32[]{:S(2)}) copy-start(f32[8,32,128]{2,1,0:T(8,128)} %source_ref.1) | copy-start | bytes 393220
  30.8 10.4 %copy-start.3 = (f32[8,32,128]{2,1,0:T(8,128)S(1)}, f32[8,32,128]{2,1,0:T(8,128)}, u32[]{:S(2)}) copy-start(f32[8,32,128]{2,1,0:T(8,128)} %reaction_ref.1) | copy-start | bytes 393220
  30.8 10.4 %copy-start.4 = (f32[4,16,64]{2,1,0:T(8,128)S(1)}, f32[4,16,64]{2,1,0:T(8,128)}, u32[]{:S(2)}) copy-start(f32[4,16,64]{2,1,0:T(8,128)} %coarse_ref.1) | copy-start | bytes 49156
  30.8 23.0 %all-to-all-start.1 = ((f32[32,4,8,128]{3,2,1,0:T(8,128)}), f32[32,4,8,128]{3,2,1,0:T(8,128)S(1)}, u32[]{:S(2)}, u32[]{:S(2)}) async-start(f32[32,4,8,128]{3,2,1,0:T(8,128)} %shard_map.65), calls=%async_computation.1 | async-start | bytes 1048576 | tf_op jit(solution)/shard_map/all_to_all | solution.py:603
  42.8 4.5 %collective-permute-start.2 = (f32[40,128]{1,0:T(8,128)S(1)}, f32[40,128]{1,0:T(8,128)S(1)}, u32[]{:S(2)}, u32[]{:S(2)}) collective-permute-start(f32[40,128]{1,0:T(8,128)S(1)} %get-tuple-element.21.sya_ref), channel_id=1, source_target_pairs={{0,4},{4,0},{8,12},{12,8},{16,20},{20,16},{24,28},{28,24},{32,36},... | collective-permute-start | bytes 61448 | tf_op jit(solution)/shard_map/ppermute | solution.py:552
  45.9 1.4 %collective-permute-start.3 = (f32[40,128]{1,0:T(8,128)S(1)}, f32[40,128]{1,0:T(8,128)S(1)}, u32[]{:S(2)}, u32[]{:S(2)}) collective-permute-start(f32[40,128]{1,0:T(8,128)S(1)} %get-tuple-element.22.syb_ref), channel_id=1, source_target_pairs={{4,8},{8,4},{12,16},{16,12},{20,24},{24,20},{28,32},{32,28},{36,40... | collective-permute-start | bytes 61448 | tf_op jit(solution)/shard_map/ppermute | solution.py:552
  55.0 6.2 %collective-permute-start.4 = (f32[232,128]{1,0:T(8,128)S(1)}, f32[232,128]{1,0:T(8,128)S(1)}, u32[]{:S(2)}, u32[]{:S(2)}) collective-permute-start(f32[232,128]{1,0:T(8,128)S(1)} %get-tuple-element.29), channel_id=1, source_target_pairs={{0,128},{128,0},{256,384},{384,256},{512,640},{640,512},{768,896},... | collective-permute-start | bytes 356360 | tf_op jit(solution)/shard_map/ppermute | solution.py:552
  57.2 6.2 %collective-permute-start.5 = (f32[232,128]{1,0:T(8,128)S(1)}, f32[232,128]{1,0:T(8,128)S(1)}, u32[]{:S(2)}, u32[]{:S(2)}) collective-permute-start(f32[232,128]{1,0:T(8,128)S(1)} %get-tuple-element.30), channel_id=1, source_target_pairs={{128,256},{256,128},{384,512},{512,384},{640,768},{768,640},{129,2... | collective-permute-start | bytes 356360 | tf_op jit(solution)/shard_map/ppermute | solution.py:552

commit v7 on v6

v7 whole, which is shorter than its diff:
```python
import jax
import jax.numpy as jnp
from jax import lax
from jax.experimental import pallas as pl
from jax.experimental.pallas import tpu as pltpu
from jax.sharding import PartitionSpec as P

LANES = 128
RUN = 4
VMEM = pl.BlockSpec(memory_space=pltpu.VMEM)
SMEM = pl.BlockSpec(memory_space=pltpu.SMEM)
HBM = pl.BlockSpec(memory_space=pltpu.HBM)
PARAMS = pltpu.CompilerParams(vmem_limit_bytes=24 * 1024 * 1024)
F32 = jnp.float32

PHI1, PHI2, KAP1, KAP2, SRC, REA, HALO = range(7)


def lane_of(shape):
    return lax.broadcasted_iota(jnp.int32, shape, len(shape) - 1)


def row_of(shape):
    return lax.broadcasted_iota(jnp.int32, shape, len(shape) - 2)


def roll_lanes(value, shift):
    shift = shift % LANES
    return pltpu.roll(value, shift, value.ndim - 1) if shift else value


def roll_rows(value, shift):
    return pltpu.roll(value, shift % value.shape[0], 0)


def moved_slot(home_of, slots):
    position = lax.axis_index("gy")
    slot = jnp.int32(0)
    target = jnp.int32(0)
    for j in range(slots):
        home = home_of(j)
        leaves = home != position * slots + j
        slot = jnp.where(leaves, j, slot)
        target = jnp.where(leaves, home, target)
    return slot, target


def edges():
    flags = []
    for axis in ("gx", "gz", "gy"):
        index = lax.axis_index(axis)
        flags.append((index == 0, index == lax.axis_size(axis) - 1))
    return flags


def is_even(axis):
    return lax.rem(lax.axis_index(axis), 2) == 0


def write_pair(axis, first_ref, second_ref, index, low, high):
    even = is_even(axis)
    first_ref[index] = jnp.where(even, high, low)
    second_ref[index] = jnp.where(even, low, high)


def received(axis, first, second):
    even = is_even(axis)
    return jnp.where(even, second, first), jnp.where(even, first, second)


def sent(axis, first, second):
    even = is_even(axis)
    return jnp.where(even, second, first), jnp.where(even, first, second)


def doubler(count):
    half = lax.div(lax.broadcasted_iota(jnp.int32, (count, 2 * count), 1), 2)
    return (half == lax.broadcasted_iota(jnp.int32, (count, 2 * count), 0)).astype(F32)


def exact_dot(left, right):
    return jnp.dot(left, right, precision=lax.Precision.HIGHEST, preferred_element_type=F32)


def refine(coarse_ref):
    cx, cz, cy = coarse_ref.shape
    left, right = doubler(cz).T, doubler(cy)
    return [exact_dot(left, exact_dot(coarse_ref[x], right)) for x in range(cx)]


def split_kernel(home_hbm, old_hbm, parts_ref, home_ref, old_ref, home_sem, sems):
    nx, nz, _ = old_ref.shape
    load_home = pltpu.make_async_copy(home_hbm, home_ref, home_sem)
    loads = [pltpu.make_async_copy(old_hbm.at[x], old_ref.at[x], sems.at[x]) for x in range(nx)]
    load_home.start()
    for load in loads:
        load.start()
    load_home.wait()
    slots = home_ref.shape[2]
    width = LANES // slots
    rows = nz // slots
    slot, target = moved_slot(lambda j: home_ref[0, 0, j], slots)
    device = lax.div(target, slots)
    count, planes = parts_ref.shape[0], parts_ref.shape[1] - 1
    group = lax.div(lane_of((rows, LANES)), width)
    for k in range(count):
        parts_ref[k, planes] = jnp.full((rows, LANES), device, jnp.int32).astype(F32)
    for x in range(nx):
        loads[x].wait()
        box = jnp.zeros((rows, LANES), F32)
        for g in range(slots):
            shift = lax.rem(width * (g - slot) + LANES, LANES)
            rolled = pltpu.roll(old_ref[x, g * rows : (g + 1) * rows, :], shift, 1)
            box = jnp.where(group == g, rolled, box)
        parts_ref[x // planes, x % planes] = box


def fold_kernel(
    home_ref, old_ref, conduct_ref, source_ref, reaction_ref, coarse_ref, after_ref,
    src_ref, rea_ref, ya_ref, yb_ref,
):
    del after_ref
    slots = home_ref.shape[0]
    nx, nz, _ = conduct_ref.shape
    (x_first, x_last), (z_first, z_last), (y_first, y_last) = edges()
    refined = refine(coarse_ref)
    row, lane = row_of((nz, LANES)), lane_of((nz, LANES))
    inner = (
        ((row == 0) & z_first).astype(F32)
        + ((row == nz - 1) & z_last).astype(F32)
        + ((lane == 0) & y_first).astype(F32)
        + ((lane == LANES - 1) & y_last).astype(F32)
    )
    for x in range(nx):
        faces = inner
        if x == 0:
            faces = faces + jnp.where(x_first, 1.0, 0.0)
        if x == nx - 1:
            faces = faces + jnp.where(x_last, 1.0, 0.0)
        weight = faces * conduct_ref[x]
        src_ref[x] = source_ref[x] + weight * refined[x // 2]
        rea_ref[x] = 1.0 + reaction_ref[x] + weight

    low = high = jnp.zeros((nz, LANES), F32)
    for f, (ref, depth) in enumerate(
        ((old_ref, 0), (old_ref, 1), (conduct_ref, 0), (conduct_ref, 1), (src_ref, 0), (rea_ref, 0))
    ):
        for x in range(nx):
            spot = f * nx + x
            low = jnp.where(lane == spot, roll_lanes(ref[x], spot - depth), low)
            high = jnp.where(lane == spot, roll_lanes(ref[x], spot + 1 + depth), high)
    slot, _ = moved_slot(lambda j: home_ref[j], slots)
    note = lane == 6 * nx
    low = jnp.where(note, slot.astype(F32), low)
    high = jnp.where(note, slot.astype(F32), high)
    write_pair("gy", ya_ref, yb_ref, Ellipsis, low, high)


def address_kernel(parts_ref, send_hbm, send_ref, sems, *, width):
    planes = send_ref.shape[1] - 1
    shape = parts_ref.shape[2:]
    column = lax.rem(lane_of(shape), width)
    beside = jnp.where(column < 2, -1.0, jnp.where(column >= width - 2, 1.0, -4096.0))
    count = parts_ref.shape[0]
    columns = [
        (roll_lanes(parts_ref[k, planes] + beside, 4 * i), roll_lanes(parts_ref[k, i], 4 * i))
        for k in range(count)
        for i in range(planes)
    ]
    chunks = sems.shape[0]
    size = send_ref.shape[0] // chunks
    copies = []
    for chunk in range(chunks):
        for device in range(chunk * size, (chunk + 1) * size):
            for i in range(planes):
                value = jnp.zeros(shape, F32)
                for k in range(count):
                    value = jnp.where(parts_ref[k, planes] == device, parts_ref[k, i], value)
                send_ref[device, i] = value
            value = jnp.zeros(shape, F32)
            for spot, source in columns:
                value = jnp.where(spot == device, source, value)
            send_ref[device, planes] = value
        part = pl.ds(chunk * size, size)
        copies.append(pltpu.make_async_copy(send_ref.at[part], send_hbm.at[part], sems.at[chunk]))
        copies[-1].start()
    for copy in copies:
        copy.wait()


def place_kernel(
    home_ref, recv_ref, old_ref, conduct_ref, src_ref, rea_ref, ya_ref, yb_ref,
    start_ref, yhalo_ref, own_ref, xa_ref, xb_ref,
):
    slots = home_ref.shape[0]
    width = LANES // slots
    nx, nz, _ = old_ref.shape
    rows = nz // slots
    slot, _ = moved_slot(lambda j: home_ref[j], slots)
    planes = recv_ref.shape[1] - 1
    run = nx // planes
    count = recv_ref.shape[0]
    here = lax.div(lane_of((rows, LANES)), width) == slot

    def total(first, tile):
        value = recv_ref[first, tile]
        for source in range(first + run, count, run):
            value = value + recv_ref[source, tile]
        return value

    for k in range(run):
        for i in range(planes):
            x = k * planes + i
            arrived = total(k, i)
            for g in range(slots):
                shift = lax.rem(width * (slot - g) + LANES, LANES)
                part = pl.ds(g * rows, rows)
                start_ref[x, part, :] = jnp.where(
                    here, pltpu.roll(arrived, shift, 1), old_ref[x, part, :]
                )

    beside = [total(k, planes) for k in range(run)]
    lane = lane_of((rows, LANES))
    halos = received("gy", ya_ref[...], yb_ref[...])
    for side in range(2):
        outer = width - 1 if side == 0 else 0
        inward = -1 if side == 0 else 1
        touched = float(slots - 1 if side == 0 else 0)
        note = jnp.broadcast_to(halos[side][0:1, 6 * nx : 6 * nx + 1], (rows, LANES)) == touched
        for g in range(slots):
            value = jnp.zeros((rows, LANES), F32)
            for x in range(nx):
                source = beside[x // planes]
                for depth in range(2):
                    at = g * width + outer + inward * depth + 4 * (x % planes)
                    spot = depth * nx + x
                    value = jnp.where(lane == spot, roll_lanes(source, spot - at), value)
            held = halos[side][g * rows : (g + 1) * rows]
            yhalo_ref[side, g * rows : (g + 1) * rows] = jnp.where(
                note & (lane < 2 * nx), value, held
            )

    lane = lane_of((nz, LANES))
    low = high = jnp.zeros((nz, LANES), F32)
    for x in range(nx):
        low = jnp.where(lane == x, roll_lanes(start_ref[x], x), low)
        high = jnp.where(lane == x, roll_lanes(start_ref[x], x + 1), high)
    own_ref[0] = low
    own_ref[1] = high

    for f, (ref, depth) in enumerate(
        ((start_ref, 0), (start_ref, 1), (conduct_ref, 0), (conduct_ref, 1), (src_ref, 0), (rea_ref, 0))
    ):
        write_pair(
            "gx", xa_ref, xb_ref, slice(f * nz, (f + 1) * nz), ref[depth], ref[nx - 1 - depth]
        )
    low = high = jnp.zeros((nz, LANES), F32)
    for side in range(2):
        halo = yhalo_ref[side]
        for f, offset in enumerate((PHI1 * nx, KAP1 * nx)):
            spot = 2 * side + f
            low = jnp.where(lane == spot, roll_lanes(halo, spot - offset), low)
            high = jnp.where(lane == spot, roll_lanes(halo, spot - offset - nx + 1), high)
    write_pair("gx", xa_ref, xb_ref, slice(6 * nz, 7 * nz), low, high)


def rows_kernel(
    start_ref, conduct_ref, src_ref, rea_ref, yhalo_ref, xa_ref, xb_ref,
    za_ref, zb_ref,
):
    _, nz, _ = start_ref.shape
    nx = start_ref.shape[0]
    last = nz - 1
    for f, (ref, depth) in enumerate(
        ((start_ref, 0), (start_ref, 1), (conduct_ref, 0), (conduct_ref, 1), (src_ref, 0), (rea_ref, 0))
    ):
        write_pair("gz", za_ref, zb_ref, f, ref[:, depth, :], ref[:, last - depth, :])
    for f, field in enumerate((PHI1, KAP1)):
        begin = field * nz
        halo = received("gx", xa_ref[begin : begin + nz], xb_ref[begin : begin + nz])
        for side in range(2):
            row = 2 * side + f
            write_pair(
                "gz", za_ref, zb_ref, (HALO, slice(row, row + 1)),
                halo[side][0:1], halo[side][last : last + 1],
            )
            row = 4 + 2 * side + f
            columns = roll_lanes(yhalo_ref[side], -field * nx)
            write_pair(
                "gz", za_ref, zb_ref, (HALO, slice(row, row + 1)),
                columns[0:1], columns[last : last + 1],
            )


def step(numerator, denominator, kappa, sides):
    for phi, beside, outside in sides:
        weight = 0.5 * (kappa + beside)
        if outside is not None:
            weight = jnp.where(outside, 0.0, weight)
        numerator = numerator + weight * phi
        denominator = denominator + weight
    return numerator / denominator


def along_rows(phi, kappa, low, high, flags):
    row = row_of(phi.shape)
    last = phi.shape[0] - 1
    low_edge, high_edge = row == 0, row == last
    return [
        (
            jnp.where(low_edge, low[0], roll_rows(phi, 1)),
            jnp.where(low_edge, low[1], roll_rows(kappa, 1)),
            low_edge & flags[0],
        ),
        (
            jnp.where(high_edge, high[0], roll_rows(phi, last)),
            jnp.where(high_edge, high[1], roll_rows(kappa, last)),
            high_edge & flags[1],
        ),
    ]


def along_lanes(phi, kappa, low, high, flags, last=LANES - 1):
    lane = lane_of(phi.shape)
    low_edge, high_edge = lane == 0, lane == last
    return [
        (
            jnp.where(low_edge, low[0], roll_lanes(phi, 1)),
            jnp.where(low_edge, low[1], roll_lanes(kappa, 1)),
            low_edge & flags[0],
        ),
        (
            jnp.where(high_edge, high[0], roll_lanes(phi, -1)),
            jnp.where(high_edge, high[1], roll_lanes(kappa, -1)),
            high_edge & flags[1],
        ),
    ]


def to_column(row, count):
    shape = (count, LANES)
    picked = jnp.where(lane_of(shape) == row_of(shape), jnp.broadcast_to(row, shape), 0.0)
    return jnp.broadcast_to(jnp.sum(picked, axis=1, keepdims=True), shape)


def sweeps_kernel(
    start_ref, conduct_ref, src_ref, rea_ref, yhalo_ref, own_ref,
    sya_ref, syb_ref, xa_ref, xb_ref, za_ref, zb_ref,
    out_hbm, out_ref, sems,
):
    nx, nz, _ = start_ref.shape
    flags_x, flags_z, flags_y = edges()
    start = [start_ref[x] for x in range(nx)]
    conduct = [conduct_ref[x] for x in range(nx)]

    def part(begin, size):
        return received("gx", xa_ref[begin : begin + size], xb_ref[begin : begin + size])

    xf = [part(f * nz, nz) for f in range(6)]
    xcols = part(6 * nz, nz)
    zf = [received("gz", za_ref[i], zb_ref[i]) for i in range(7)]
    around = zf[HALO]
    yf = [yhalo_ref[side] for side in range(2)]
    sf = sent("gy", sya_ref[...], syb_ref[...])

    def columns(tile, phi_spot, kappa_spot, lane):
        return roll_lanes(tile, lane - phi_spot), roll_lanes(tile, lane - kappa_spot)

    def two_rows(tile, at):
        return tile[at : at + 1], tile[at + 1 : at + 2]

    x_first_sweep = []
    for side in range(2):
        phi, kappa = xf[PHI1][side], xf[KAP1][side]
        me = 0 if side == 0 else nx - 1
        at = 2 * side
        sides = [(xf[PHI2][side], xf[KAP2][side], None), (start[me], conduct[me], None)]
        sides += along_rows(phi, kappa, two_rows(around[0], at), two_rows(around[1], at), flags_z)
        tile = xcols[side]
        sides += along_lanes(
            phi, kappa, columns(tile, 0, 1, 0), columns(tile, 2, 3, LANES - 1), flags_y
        )
        x_first_sweep.append(step(phi + xf[SRC][side], xf[REA][side], kappa, sides))

    z_first_sweep = []
    for side in range(2):
        phi, kappa = zf[PHI1][side], zf[KAP1][side]
        me = 0 if side == 0 else nz - 1
        tile = around[side]
        sides = [
            (zf[PHI2][side], zf[KAP2][side], None),
            (start_ref[:, me, :], conduct_ref[:, me, :], None),
        ]
        sides += along_rows(phi, kappa, two_rows(tile, 0), two_rows(tile, 2), flags_x)
        sides += along_lanes(
            phi,
            kappa,
            tuple(to_column(row, nx) for row in two_rows(tile, 4)),
            tuple(to_column(row, nx) for row in two_rows(tile, 6)),
            flags_y,
        )
        z_first_sweep.append(step(phi + zf[SRC][side], zf[REA][side], kappa, sides))

    y_first_sweep = []
    for side in range(2):
        phi, phi2, kappa, kappa2, src, rea = [roll_lanes(yf[side], -f * nx) for f in range(6)]
        at = 2 * side
        sides = [(phi2, kappa2, None), (own_ref[side], roll_lanes(sf[side], -KAP1 * nx), None)]
        sides += along_rows(
            phi,
            kappa,
            two_rows(around[0], 4 + at),
            two_rows(around[1], 4 + at),
            flags_z,
        )
        sides += along_lanes(
            phi,
            kappa,
            columns(xcols[0], at, at + 1, 0),
            columns(xcols[1], at, at + 1, nx - 1),
            flags_x,
            nx - 1,
        )
        y_first_sweep.append(step(phi + src, rea, kappa, sides))

    copies = []

    def sweep(phis, x_phi, z_phi, y_phi, store=False):
        results = []
        for x in range(nx):
            phi, kappa = phis[x], conduct[x]
            sides = []
            if x:
                sides.append((phis[x - 1], conduct[x - 1], None))
            else:
                sides.append((x_phi[0], xf[KAP1][0], flags_x[0]))
            if x < nx - 1:
                sides.append((phis[x + 1], conduct[x + 1], None))
            else:
                sides.append((x_phi[1], xf[KAP1][1], flags_x[1]))
            sides += along_rows(
                phi,
                kappa,
                (z_phi[0][x : x + 1], zf[KAP1][0][x : x + 1]),
                (z_phi[1][x : x + 1], zf[KAP1][1][x : x + 1]),
                flags_z,
            )
            spot = KAP1 * nx + x
            sides += along_lanes(
                phi,
                kappa,
                (roll_lanes(y_phi[0], -x), roll_lanes(yf[0], -spot)),
                (roll_lanes(y_phi[1], LANES - 1 - x), roll_lanes(yf[1], LANES - 1 - spot)),
                flags_y,
            )
            results.append(step(start[x] + src_ref[x], rea_ref[x], kappa, sides))
            if store:
                out_ref[x] = results[x]
                copies.append(pltpu.make_async_copy(out_ref.at[x], out_hbm.at[x], sems.at[x]))
                copies[x].start()
        return results

    first = sweep(start, xf[PHI1], zf[PHI1], yf)
    sweep(first, x_first_sweep, z_first_sweep, y_first_sweep, store=True)
    for copy in copies:
        copy.wait()


def swap(axis, first, second):
    count = lax.axis_size(axis)
    results = []
    for j, value in ((1, second), (0, first)):
        pairs = []
        for low in range(j, count - 1, 2):
            pairs += [(low, low + 1), (low + 1, low)]
        results.append(lax.ppermute(value, axis, pairs))
    return results[::-1]


def call(kernel, operands, outs, smem=0, hbm=(), out_space=VMEM, scratch=()):
    specs = [SMEM] * smem + [VMEM] * (len(operands) - smem)
    operands = list(operands)
    for i in hbm:
        specs[i] = HBM
        operands[i] = pltpu.with_memory_space_constraint(operands[i], pltpu.HBM)
    return pl.pallas_call(
        kernel,
        out_shape=[jax.ShapeDtypeStruct(shape, F32) for shape in outs],
        in_specs=specs,
        out_specs=[out_space] * len(outs),
        scratch_shapes=scratch,
        compiler_params=PARAMS,
    )(*operands)


def on_device(old_field, new_home, conduct, reaction, source, coarse):
    nx, nz, ny = block = old_field.shape
    home = new_home[0, 0]
    slots = home.shape[0]
    rows, width = nz // slots, ny // slots
    line = lax.axis_size("gy")
    part = nx // RUN

    (parts,) = call(
        split_kernel,
        (new_home, old_field),
        [(RUN, part + 1, rows, ny)],
        hbm=(0, 1),
        scratch=[
            pltpu.SMEM(new_home.shape, jnp.int32),
            pltpu.VMEM(block, F32),
            pltpu.SemaphoreType.DMA,
            pltpu.SemaphoreType.DMA((nx,)),
        ],
    )
    groups = [[i * RUN + k for k in range(RUN)] for i in range(line // RUN)]
    parts = lax.all_to_all(parts, "gy", 0, 0, tiled=True, axis_index_groups=groups)

    def address(*refs):
        address_kernel(*refs, width=width)

    slot_shape = (line, part + 1, rows, ny)
    (send,) = call(
        address,
        (parts,),
        [slot_shape],
        out_space=HBM,
        scratch=[pltpu.VMEM(slot_shape, F32), pltpu.SemaphoreType.DMA((4,))],
    )
    recv = lax.all_to_all(send, "gy", 0, 0, tiled=True)
    src, rea, sya, syb = call(
        fold_kernel,
        (home, old_field, conduct, source, reaction, coarse, parts),
        [block, block, (nz, ny), (nz, ny)],
        smem=1,
    )
    ya, yb = swap("gy", sya, syb)
    start, yhalo, own, xa, xb = call(
        place_kernel,
        (home, recv, old_field, conduct, src, rea, ya, yb),
        [block, (2, nz, ny), (2, nz, ny), (7 * nz, ny), (7 * nz, ny)],
        smem=1,
    )
    xa, xb = swap("gx", xa, xb)
    za, zb = call(
        rows_kernel,
        (start, conduct, src, rea, yhalo, xa, xb),
        [(7, nx, ny), (7, nx, ny)],
    )
    za, zb = swap("gz", za, zb)
    (relaxed,) = call(
        sweeps_kernel,
        (start, conduct, src, rea, yhalo, own, sya, syb, xa, xb, za, zb),
        [block],
        out_space=HBM,
        scratch=[pltpu.VMEM(block, F32), pltpu.SemaphoreType.DMA((nx,))],
    )
    return relaxed


def solution(mesh):
    return jax.shard_map(
        on_device,
        mesh=mesh,
        in_specs=(P("gx", "gz", "gy"),) * 6,
        out_specs=P("gx", "gz", "gy"),
        check_vma=False,
    )
```

time: 65.4 us -> 69.4 us (1.061)
  the two profiles are of different devices: /device:TPU:65 before, /device:TPU:97 now
where the time goes in v7:
time: 69.4 us; the launch traced here: 69 us
  starting transfers between devices  45.8 us (66%)
  blocking collectives  8.2 us (12%)
  waiting for transfers between devices  7.79 us (11%)
  Pallas kernels  6.39 us (9%)
    ppermute x6, starting transfers between devices, swap(): results.append(lax.ppermute(value, axis, pairs))  38 us
    all_to_all x1, blocking collectives, on_device(): lax.all_to_all(parts, 'gy', 0, 0, tiled=True, axis_index_groups=groups)  8.2 us
    ppermute x6, waiting for transfers between devices, swap(): results.append(lax.ppermute(value, axis, pairs))  7.78 us
    all_to_all x1, starting transfers between devices, on_device(): recv = lax.all_to_all(send, 'gy', 0, 0, tiled=True)  7.72 us
    pallas_call x6, Pallas kernels, call(): pl.pallas_call(kernel, out_shape=[jax.ShapeDtypeStruct(shape, F32) for sh...  6.39 us
  transfers between devices with their start and end apart: 7, of which 3 were waited for; matrix products, arithmetic and copies ran while one was open for 0% of the time, Pallas kernels for 2%

profile of v7, /device:TPU:97, one launch (start us, length us, event | category | flops | bytes accessed | tf_op | source)
XLA Modules:
  0.0 69.0 jit_solution(8979434152237761361)
XLA Ops:
  0.0 1.5 %shard_map.64 = f32[4,3,8,128]{3,2,1,0:T(8,128)S(1)} custom-call(s32[1,1,4]{2,1,0:T(1,128)} %home_hbm.1, f32[8,32,128]{2,1,0:T(8,128)} %old_ref.3), custom_call_target="tpu_custom_call" | custom-call | tf_op jit(solution)/shard_map/pallas_call | solution.py:486
  1.5 8.2 %all_to_all.10.refs_0_.after_ref = f32[4,3,8,128]{3,2,1,0:T(8,128)S(1)} all-to-all(f32[4,3,8,128]{3,2,1,0:T(8,128)S(1)} %shard_map.64), channel_id=1, replica_groups={{0,4,8,12},{16,20,24,28},{32,36,40,44},{48,52,56,60},{64,68,72,76},{80,..., dimensions={0} | all-to-all | bytes 98304 | tf_op jit(solution)/shard_map/all_to_all | solution.py:517
  9.7 0.9 %shard_map.65 = f32[32,3,8,128]{3,2,1,0:T(8,128)} custom-call(f32[4,3,8,128]{3,2,1,0:T(8,128)S(1)} %all_to_all.10.refs_0_.after_ref), custom_call_target="tpu_custom_call" | custom-call | tf_op jit(solution)/shard_map/pallas_call | solution.py:486
  10.6 0.0 copy-start
  10.6 0.0 copy-start.1
  10.6 0.0 copy-start.2
  10.6 0.0 copy-start.3
  10.6 0.0 copy-start.4
  10.6 7.7 %all-to-all-start.1 = ((f32[32,3,8,128]{3,2,1,0:T(8,128)}), f32[32,3,8,128]{3,2,1,0:T(8,128)S(1)}, u32[]{:S(2)}, u32[]{:S(2)}) async-start(f32[32,3,8,128]{3,2,1,0:T(8,128)} %shard_map.65), calls=%async_computation.1 | async-start | bytes 786432 | tf_op jit(solution)/shard_map/all_to_all | solution.py:530
  18.4 0.0 copy-start.5
  18.4 0.0 copy-done
  18.4 0.0 copy-done.1
  18.4 0.0 copy-done.2
  18.4 0.0 copy-done.3
  18.4 0.0 copy-done.4
  18.4 0.6 copy-done.5
  19.0 1.6 %shard_map.66 = (f32[8,32,128]{2,1,0:T(8,128)S(1)}, f32[8,32,128]{2,1,0:T(8,128)S(1)}, f32[32,128]{1,0:T(8,128)S(1)}, f32[32,128]{1,0:T(8,128)S(1)}) custom-call(s32[4]{0:T(128)S(1)} %bitcast.1, f32[8,32,128]{2,1,0:T(8,128)S(1)} %copy-done.1, f32[8,32,128]{2,1,0:T(8,128)S(1)} %copy-done, f32[8,32,128]{2,1,0:T(8,128)S(1)} %copy-done.2, ...), custom_call_target="tpu_custom_call" | custom-call | tf_op jit(solution)/shard_map/pallas_call | solution.py:486
  20.6 3.1 %collective-permute-start = (f32[32,128]{1,0:T(8,128)S(1)}, f32[32,128]{1,0:T(8,128)S(1)}, u32[]{:S(2)}, u32[]{:S(2)}) collective-permute-start(f32[32,128]{1,0:T(8,128)S(1)} %get-tuple-element.18.sya_ref), channel_id=1, source_target_pairs={{0,4},{4,0},{8,12},{12,8},{16,20},{20,16},{24,28},{28,24},{32,36},... | collective-permute-start | bytes 49160 | tf_op jit(solution)/shard_map/ppermute | solution.py:476
  23.7 3.7 %collective-permute-start.1 = (f32[32,128]{1,0:T(8,128)S(1)}, f32[32,128]{1,0:T(8,128)S(1)}, u32[]{:S(2)}, u32[]{:S(2)}) collective-permute-start(f32[32,128]{1,0:T(8,128)S(1)} %get-tuple-element.19.syb_ref), channel_id=1, source_target_pairs={{4,8},{8,4},{12,16},{16,12},{20,24},{24,20},{28,32},{32,28},{36,40... | collective-permute-start | bytes 49160 | tf_op jit(solution)/shard_map/ppermute | solution.py:476
  27.4 0.0 collective-permute-done.ya_ref
  27.4 4.1 %collective-permute-done.1.yb_ref = f32[32,128]{1,0:T(8,128)S(1)} collective-permute-done((f32[32,128]{1,0:T(8,128)S(1)}, f32[32,128]{1,0:T(8,128)S(1)}, u32[]{:S(2)}, u32[]{:S(2)}) %collective-permute-start.1) | collective-permute-done | bytes 16416 | tf_op jit(solution)/shard_map/ppermute | solution.py:476
  31.5 0.0 all-to-all-done.1.recv_ref
  31.5 0.9 %shard_map.67 = (f32[8,32,128]{2,1,0:T(8,128)S(1)}, f32[2,32,128]{2,1,0:T(8,128)S(1)}, f32[2,32,128]{2,1,0:T(8,128)S(1)}, f32[224,128]{1,0:T(8,128)S(1)}, f32[224,128]{1,0:T(8,128)S(1)}) custom-call(s32[4]{0:T(128)S(1)} %bitcast.2, f32[32,3,8,128]{3,2,1,0:T(8,128)S(1)} %all-to-all-done.1.recv_ref, f32[8,32,128]{2,1,0:T(8,128)S(1)} %copy-done.1, ...), custom_call_target="tpu_custom_call" | custom-call | tf_op jit(solution)/shard_map/pallas_call | solution.py:486
  32.4 2.3 %collective-permute-start.2 = (f32[224,128]{1,0:T(8,128)S(1)}, f32[224,128]{1,0:T(8,128)S(1)}, u32[]{:S(2)}, u32[]{:S(2)}) collective-permute-start(f32[224,128]{1,0:T(8,128)S(1)} %get-tuple-element.23), channel_id=1, source_target_pairs={{0,128},{128,0},{256,384},{384,256},{512,640},{640,512},{768,896},... | collective-permute-start | bytes 344072 | tf_op jit(solution)/shard_map/ppermute | solution.py:476
  34.7 5.7 %collective-permute-start.3 = (f32[224,128]{1,0:T(8,128)S(1)}, f32[224,128]{1,0:T(8,128)S(1)}, u32[]{:S(2)}, u32[]{:S(2)}) collective-permute-start(f32[224,128]{1,0:T(8,128)S(1)} %get-tuple-element.24), channel_id=1, source_target_pairs={{128,256},{256,128},{384,512},{512,384},{640,768},{768,640},{129,2... | collective-permute-start | bytes 344072 | tf_op jit(solution)/shard_map/ppermute | solution.py:476
  40.4 0.0 collective-permute-done.2.xa_ref
  40.4 2.2 %collective-permute-done.3.xb_ref = f32[224,128]{1,0:T(8,128)S(1)} collective-permute-done((f32[224,128]{1,0:T(8,128)S(1)}, f32[224,128]{1,0:T(8,128)S(1)}, u32[]{:S(2)}, u32[]{:S(2)}) %collective-permute-start.3) | collective-permute-done | bytes 114720 | tf_op jit(solution)/shard_map/ppermute | solution.py:476
  42.6 0.1 shard_map.68
  42.7 10.6 %collective-permute-start.4 = (f32[7,8,128]{2,1,0:T(8,128)S(1)}, f32[7,8,128]{2,1,0:T(8,128)S(1)}, u32[]{:S(2)}, u32[]{:S(2)}) collective-permute-start(f32[7,8,128]{2,1,0:T(8,128)S(1)} %get-tuple-element.25), channel_id=1, source_target_pairs={{0,1},{1,0},{2,3},{3,2},{4,5},{5,4},{6,7},{7,6},{8,9},{9,8},{10,11... | collective-permute-start | bytes 86024 | tf_op jit(solution)/shard_map/ppermute | solution.py:476
  53.3 12.7 %collective-permute-start.5 = (f32[7,8,128]{2,1,0:T(8,128)S(1)}, f32[7,8,128]{2,1,0:T(8,128)S(1)}, u32[]{:S(2)}, u32[]{:S(2)}) collective-permute-start(f32[7,8,128]{2,1,0:T(8,128)S(1)} %get-tuple-element.26), channel_id=1, source_target_pairs={{1,2},{2,1},{5,6},{6,5},{9,10},{10,9},{13,14},{14,13},{17,18},{18,... | collective-permute-start | bytes 86024 | tf_op jit(solution)/shard_map/ppermute | solution.py:476
  65.9 0.0 collective-permute-done.4.za_ref
  65.9 1.5 %collective-permute-done.5.zb_ref = f32[7,8,128]{2,1,0:T(8,128)S(1)} collective-permute-done((f32[7,8,128]{2,1,0:T(8,128)S(1)}, f32[7,8,128]{2,1,0:T(8,128)S(1)}, u32[]{:S(2)}, u32[]{:S(2)}) %collective-permute-start.5) | collective-permute-done | bytes 28704 | tf_op jit(solution)/shard_map/ppermute | solution.py:476
  67.5 1.5 %shard_map.69 = f32[8,32,128]{2,1,0:T(8,128)} custom-call(f32[8,32,128]{2,1,0:T(8,128)S(1)} %get-tuple-element.20.start_ref, f32[8,32,128]{2,1,0:T(8,128)S(1)} %copy-done, f32[8,32,128]{2,1,0:T(8,128)S(1)} %get-tuple-element.16.src_ref, f32[8,32,128]{2,1,0:T(8,128)S(1)} %get-tuple-element.17.rea_ref, f32[2,32,128]{2,1,0:T(8,128)S(1)} %get-tuple-element.21.yhalo_ref, ...), custom_call_target="tpu_custom_call" | custom-call | tf_op jit(solution)/shard_map/pallas_call | solution.py:486
Async XLA Ops:
  10.6 7.8 %copy-start = (f32[8,32,128]{2,1,0:T(8,128)S(1)}, f32[8,32,128]{2,1,0:T(8,128)}, u32[]{:S(2)}) copy-start(f32[8,32,128]{2,1,0:T(8,128)} %conduct_ref.7) | copy-start | bytes 393220
  10.6 7.8 %copy-start.1 = (f32[8,32,128]{2,1,0:T(8,128)S(1)}, f32[8,32,128]{2,1,0:T(8,128)}, u32[]{:S(2)}) copy-start(f32[8,32,128]{2,1,0:T(8,128)} %old_ref.3) | copy-start | bytes 393220
  10.6 7.8 %copy-start.2 = (f32[8,32,128]{2,1,0:T(8,128)S(1)}, f32[8,32,128]{2,1,0:T(8,128)}, u32[]{:S(2)}) copy-start(f32[8,32,128]{2,1,0:T(8,128)} %source_ref.1) | copy-start | bytes 393220
  10.6 7.8 %copy-start.3 = (f32[8,32,128]{2,1,0:T(8,128)S(1)}, f32[8,32,128]{2,1,0:T(8,128)}, u32[]{:S(2)}) copy-start(f32[8,32,128]{2,1,0:T(8,128)} %reaction_ref.1) | copy-start | bytes 393220
  10.6 7.8 %copy-start.4 = (f32[4,16,64]{2,1,0:T(8,128)S(1)}, f32[4,16,64]{2,1,0:T(8,128)}, u32[]{:S(2)}) copy-start(f32[4,16,64]{2,1,0:T(8,128)} %coarse_ref.1) | copy-start | bytes 49156
  10.6 20.9 %all-to-all-start.1 = ((f32[32,3,8,128]{3,2,1,0:T(8,128)}), f32[32,3,8,128]{3,2,1,0:T(8,128)S(1)}, u32[]{:S(2)}, u32[]{:S(2)}) async-start(f32[32,3,8,128]{3,2,1,0:T(8,128)} %shard_map.65), calls=%async_computation.1 | async-start | bytes 786432 | tf_op jit(solution)/shard_map/all_to_all | solution.py:530
  18.4 0.7 copy-start.5
  20.6 6.8 %collective-permute-start = (f32[32,128]{1,0:T(8,128)S(1)}, f32[32,128]{1,0:T(8,128)S(1)}, u32[]{:S(2)}, u32[]{:S(2)}) collective-permute-start(f32[32,128]{1,0:T(8,128)S(1)} %get-tuple-element.18.sya_ref), channel_id=1, source_target_pairs={{0,4},{4,0},{8,12},{12,8},{16,20},{20,16},{24,28},{28,24},{32,36},... | collective-permute-start | bytes 49160 | tf_op jit(solution)/shard_map/ppermute | solution.py:476
  23.7 7.8 %collective-permute-start.1 = (f32[32,128]{1,0:T(8,128)S(1)}, f32[32,128]{1,0:T(8,128)S(1)}, u32[]{:S(2)}, u32[]{:S(2)}) collective-permute-start(f32[32,128]{1,0:T(8,128)S(1)} %get-tuple-element.19.syb_ref), channel_id=1, source_target_pairs={{4,8},{8,4},{12,16},{16,12},{20,24},{24,20},{28,32},{32,28},{36,40... | collective-permute-start | bytes 49160 | tf_op jit(solution)/shard_map/ppermute | solution.py:476
  32.4 8.0 %collective-permute-start.2 = (f32[224,128]{1,0:T(8,128)S(1)}, f32[224,128]{1,0:T(8,128)S(1)}, u32[]{:S(2)}, u32[]{:S(2)}) collective-permute-start(f32[224,128]{1,0:T(8,128)S(1)} %get-tuple-element.23), channel_id=1, source_target_pairs={{0,128},{128,0},{256,384},{384,256},{512,640},{640,512},{768,896},... | collective-permute-start | bytes 344072 | tf_op jit(solution)/shard_map/ppermute | solution.py:476
  34.7 7.9 %collective-permute-start.3 = (f32[224,128]{1,0:T(8,128)S(1)}, f32[224,128]{1,0:T(8,128)S(1)}, u32[]{:S(2)}, u32[]{:S(2)}) collective-permute-start(f32[224,128]{1,0:T(8,128)S(1)} %get-tuple-element.24), channel_id=1, source_target_pairs={{128,256},{256,128},{384,512},{512,384},{640,768},{768,640},{129,2... | collective-permute-start | bytes 344072 | tf_op jit(solution)/shard_map/ppermute | solution.py:476
  42.7 23.3 %collective-permute-start.4 = (f32[7,8,128]{2,1,0:T(8,128)S(1)}, f32[7,8,128]{2,1,0:T(8,128)S(1)}, u32[]{:S(2)}, u32[]{:S(2)}) collective-permute-start(f32[7,8,128]{2,1,0:T(8,128)S(1)} %get-tuple-element.25), channel_id=1, source_target_pairs={{0,1},{1,0},{2,3},{3,2},{4,5},{5,4},{6,7},{7,6},{8,9},{9,8},{10,11... | collective-permute-start | bytes 86024 | tf_op jit(solution)/shard_map/ppermute | solution.py:476
  53.3 14.2 %collective-permute-start.5 = (f32[7,8,128]{2,1,0:T(8,128)S(1)}, f32[7,8,128]{2,1,0:T(8,128)S(1)}, u32[]{:S(2)}, u32[]{:S(2)}) collective-permute-start(f32[7,8,128]{2,1,0:T(8,128)S(1)} %get-tuple-element.26), channel_id=1, source_target_pairs={{1,2},{2,1},{5,6},{6,5},{9,10},{10,9},{13,14},{14,13},{17,18},{18,... | collective-permute-start | bytes 86024 | tf_op jit(solution)/shard_map/ppermute | solution.py:476

commit v8 on v6

--- a/solution.py
+++ b/solution.py
@@ -6,7 +6,7 @@
 from jax.sharding import PartitionSpec as P
 
 LANES = 128
-RUN = 4
+RUN = 8
 VMEM = pl.BlockSpec(memory_space=pltpu.VMEM)
 SMEM = pl.BlockSpec(memory_space=pltpu.SMEM)
 HBM = pl.BlockSpec(memory_space=pltpu.HBM)
@@ -33,12 +33,12 @@
     return pltpu.roll(value, shift % value.shape[0], 0)
 
 
-def moved_slot(home_ref, slots):
+def moved_slot(home_of, slots):
     position = lax.axis_index("gy")
     slot = jnp.int32(0)
     target = jnp.int32(0)
     for j in range(slots):
-        home = home_ref[j]
+        home = home_of(j)
         leaves = home != position * slots + j
         slot = jnp.where(leaves, j, slot)
         target = jnp.where(leaves, home, target)
@@ -89,10 +89,11 @@
 
 
 def first_kernel(
-    home_ref, old_hbm, conduct_hbm, source_hbm, reaction_hbm, coarse_hbm,
-    za_ref, zb_ref, parts_ref, old_ref, rows_ref, coarse_ref, old_sems, sems, coarse_sem,
+    home_hbm, old_hbm, conduct_hbm, source_hbm, reaction_hbm, coarse_hbm,
+    za_ref, zb_ref, parts_ref, home_ref, old_ref, rows_ref, coarse_ref,
+    home_sem, old_sems, sems, coarse_sem,
 ):
-    slots = home_ref.shape[0]
+    slots = home_ref.shape[2]
     width = LANES // slots
     nx, nz, _ = old_hbm.shape
     size = rows_ref.shape[3]
@@ -105,10 +106,12 @@
                     ref.at[:, pl.ds(begin, size), :], rows_ref.at[i, side], sems.at[i, side]
                 )
             )
-    for copy in loads + copies:
+    load_home = pltpu.make_async_copy(home_hbm, home_ref, home_sem)
+    for copy in [load_home] + loads + copies:
         copy.start()
-
-    slot, target = moved_slot(home_ref, slots)
+    load_home.wait()
+
+    slot, target = moved_slot(lambda j: home_ref[0, 0, j], slots)
     device = lax.div(target, slots)
     back = LANES - width * slot
     (x_first, x_last), (z_first, z_last), (y_first, y_last) = edges()
@@ -136,7 +139,8 @@
     for copy in copies:
         copy.wait()
     cx, cz, cy = coarse_ref.shape
-    left, right = doubler(cx).T, doubler(cy)
+    ends = jnp.concatenate([coarse_ref[:, 0, :], coarse_ref[:, cz - 1, :]], axis=0)
+    wide = exact_dot(ends, doubler(cy))
 
     def rims(first, second):
         near = pltpu.roll(first, lax.rem(back, LANES), 1)
@@ -144,8 +148,10 @@
         return jnp.where(lane < width, near, jnp.where(lane < 2 * width, far, note))
 
     faces = []
-    for side, first, second, end, edge in ((0, 0, 1, 0, z_first), (1, size - 1, size - 2, cz - 1, z_last)):
-        refined = exact_dot(left, exact_dot(coarse_ref[:, end, :], right))
+    for side, first, second, edge in ((0, 0, 1, z_first), (1, size - 1, size - 2, z_last)):
+        refined = jnp.zeros((nx, LANES), F32)
+        for x in range(cx):
+            refined = jnp.where(lax.div(row, 2) == x, wide[side * cx + x : side * cx + x + 1], refined)
         top = side * (nz - size)
         old, old2 = old_ref[:, top + first, :], old_ref[:, top + second, :]
         kappa, kappa2 = rows_ref[0, side, :, first, :], rows_ref[0, side, :, second, :]
@@ -194,7 +200,7 @@
     write_pair("gy", ya_ref, yb_ref, slice(0, nz), low, high)
 
     lane = lane_of((nx, LANES))
-    slot, _ = moved_slot(home_ref, slots)
+    slot, _ = moved_slot(lambda j: home_ref[j], slots)
     low = high = jnp.where(lane == 4, slot, 0).astype(F32)
     notes = received("gz", za_ref[RIM], zb_ref[RIM])
     for side in range(2):
@@ -259,7 +265,7 @@
     width = LANES // slots
     nx, nz, _ = old_ref.shape
     rows = nz // slots
-    slot, _ = moved_slot(home_ref, slots)
+    slot, _ = moved_slot(lambda j: home_ref[j], slots)
     planes = recv_ref.shape[1] - 2
     run = nx // planes
     count = recv_ref.shape[0]
@@ -579,14 +585,15 @@
 
     sza, szb, parts = call(
         first_kernel,
-        (home, old_field, conduct, source, reaction, coarse),
+        (new_home, old_field, conduct, source, reaction, coarse),
         [(7, nx, ny), (7, nx, ny), (RUN, part + 1, rows, ny)],
-        smem=1,
-        hbm=(1, 2, 3, 4, 5),
+        hbm=(0, 1, 2, 3, 4, 5),
         scratch=[
+            pltpu.SMEM(new_home.shape, jnp.int32),
             pltpu.VMEM(block, F32),
             pltpu.VMEM((3, 2, nx, 8, ny), F32),
             pltpu.VMEM(coarse.shape, F32),
+            pltpu.SemaphoreType.DMA,
             pltpu.SemaphoreType.DMA((nx,)),
             pltpu.SemaphoreType.DMA((3, 2)),
             pltpu.SemaphoreType.DMA,

time: 65.4 us -> 64.5 us (0.986)
  the two profiles are of different devices: /device:TPU:65 before, /device:TPU:97 now
where the time goes in v8:
time: 64.5 us; the launch traced here: 64 us
  starting transfers between devices  48 us (74%)
  waiting for transfers between devices  7.88 us (12%)
  Pallas kernels  7.33 us (11%)
    ppermute x6, starting transfers between devices, swap(): results.append(lax.ppermute(value, axis, pairs))  33.9 us
    all_to_all x1, starting transfers between devices, on_device(): recv = lax.all_to_all(send, 'gy', 0, 0, tiled=True)  9.92 us
    ppermute x6, waiting for transfers between devices, swap(): results.append(lax.ppermute(value, axis, pairs))  7.87 us
    pallas_call x6, Pallas kernels, call(): pl.pallas_call(kernel, out_shape=[jax.ShapeDtypeStruct(shape, F32) for sh...  7.33 us
    all_to_all x1, starting transfers between devices, on_device(): lax.all_to_all(parts, 'gy', 0, 0, tiled=True, axis_index_groups=groups)  4.15 us
  transfers between devices with their start and end apart: 8, of which 3 were waited for; matrix products, arithmetic and copies ran while one was open for 0% of the time, Pallas kernels for 2%

profile of v8, /device:TPU:97, one launch (start us, length us, event | category | flops | bytes accessed | tf_op | source)
XLA Modules:
  0.0 64.0 jit_solution(12718833925569555435)
XLA Ops:
  0.0 2.2 %shard_map.64 = (f32[7,8,128]{2,1,0:T(8,128)S(1)}, f32[7,8,128]{2,1,0:T(8,128)S(1)}, f32[8,2,8,128]{3,2,1,0:T(8,128)}) custom-call(s32[1,1,4]{2,1,0:T(1,128)} %home_hbm.1, f32[8,32,128]{2,1,0:T(8,128)} %old_ref.3, f32[8,32,128]{2,1,0:T(8,128)} %conduct_ref.5, f32[8,32,128]{2,1,0:T(8,128)} %source_ref.1, f32[8,32,128]{2,1,0:T(8,128)} %reaction_ref.1, ...), custom_call_target="tpu_custom_call" | custom-call | tf_op jit(solution)/shard_map/pallas_call | solution.py:568
  2.2 4.1 %all-to-all-start = ((f32[8,2,8,128]{3,2,1,0:T(8,128)}), f32[8,2,8,128]{3,2,1,0:T(8,128)S(1)}, u32[]{:S(2)}, u32[]{:S(2)}) async-start(f32[8,2,8,128]{3,2,1,0:T(8,128)} %get-tuple-element.18), calls=%async_computation | async-start | bytes 131072 | tf_op jit(solution)/shard_map/all_to_all | solution.py:604
  6.4 2.9 %collective-permute-start = (f32[7,8,128]{2,1,0:T(8,128)S(1)}, f32[7,8,128]{2,1,0:T(8,128)S(1)}, u32[]{:S(2)}, u32[]{:S(2)}) collective-permute-start(f32[7,8,128]{2,1,0:T(8,128)S(1)} %get-tuple-element.19), channel_id=1, source_target_pairs={{0,1},{1,0},{2,3},{3,2},{4,5},{5,4},{6,7},{7,6},{8,9},{9,8},{10,11... | collective-permute-start | bytes 86024 | tf_op jit(solution)/shard_map/ppermute | solution.py:558
  9.2 18.1 %collective-permute-start.1 = (f32[7,8,128]{2,1,0:T(8,128)S(1)}, f32[7,8,128]{2,1,0:T(8,128)S(1)}, u32[]{:S(2)}, u32[]{:S(2)}) collective-permute-start(f32[7,8,128]{2,1,0:T(8,128)S(1)} %get-tuple-element.20), channel_id=1, source_target_pairs={{1,2},{2,1},{5,6},{6,5},{9,10},{10,9},{13,14},{14,13},{17,18},{18,... | collective-permute-start | bytes 86024 | tf_op jit(solution)/shard_map/ppermute | solution.py:558
  27.3 0.0 collective-permute-done.refs_1_.za_ref
  27.3 1.5 %collective-permute-done.1.refs_2_.zb_ref = f32[7,8,128]{2,1,0:T(8,128)S(1)} collective-permute-done((f32[7,8,128]{2,1,0:T(8,128)S(1)}, f32[7,8,128]{2,1,0:T(8,128)S(1)}, u32[]{:S(2)}, u32[]{:S(2)}) %collective-permute-start.1) | collective-permute-done | bytes 28704 | tf_op jit(solution)/shard_map/ppermute | solution.py:558
  28.8 0.0 all-to-all-done.refs_0_
  28.9 1.0 %shard_map.65 = f32[32,3,8,128]{3,2,1,0:T(8,128)} custom-call(f32[8,2,8,128]{3,2,1,0:T(8,128)S(1)} %all-to-all-done.refs_0_, f32[7,8,128]{2,1,0:T(8,128)S(1)} %collective-permute-done.refs_1_.za_ref, f32[7,8,128]{2,1,0:T(8,128)S(1)} %collective-permute-done.1.refs_2_.zb_ref), custom_call_target="tpu_custom_call" | custom-call | tf_op jit(solution)/shard_map/pallas_call | solution.py:568
  29.8 0.0 copy-start
  29.8 0.0 copy-start.1
  29.8 0.0 copy-start.2
  29.8 0.0 copy-start.3
  29.8 0.0 copy-start.4
  29.9 9.9 %all-to-all-start.1 = ((f32[32,3,8,128]{3,2,1,0:T(8,128)}), f32[32,3,8,128]{3,2,1,0:T(8,128)S(1)}, u32[]{:S(2)}, u32[]{:S(2)}) async-start(f32[32,3,8,128]{3,2,1,0:T(8,128)} %shard_map.65), calls=%async_computation.1 | async-start | bytes 786432 | tf_op jit(solution)/shard_map/all_to_all | solution.py:610
  39.8 0.0 copy-start.5
  39.8 0.0 copy-done
  39.8 0.0 copy-done.1
  39.8 0.0 copy-done.2
  39.8 0.0 copy-done.3
  39.8 0.0 copy-done.4
  39.8 0.6 copy-done.5
  40.4 1.6 %shard_map.66 = (f32[8,32,128]{2,1,0:T(8,128)S(1)}, f32[8,32,128]{2,1,0:T(8,128)S(1)}, f32[40,128]{1,0:T(8,128)S(1)}, f32[40,128]{1,0:T(8,128)S(1)}) custom-call(s32[4]{0:T(128)S(1)} %bitcast.1, f32[8,32,128]{2,1,0:T(8,128)S(1)} %copy-done.1, f32[8,32,128]{2,1,0:T(8,128)S(1)} %copy-done, f32[8,32,128]{2,1,0:T(8,128)S(1)} %copy-done.2, ...), custom_call_target="tpu_custom_call" | custom-call | tf_op jit(solution)/shard_map/pallas_call | solution.py:568
  42.0 3.1 %collective-permute-start.2 = (f32[40,128]{1,0:T(8,128)S(1)}, f32[40,128]{1,0:T(8,128)S(1)}, u32[]{:S(2)}, u32[]{:S(2)}) collective-permute-start(f32[40,128]{1,0:T(8,128)S(1)} %get-tuple-element.21.sya_ref), channel_id=1, source_target_pairs={{0,4},{4,0},{8,12},{12,8},{16,20},{20,16},{24,28},{28,24},{32,36},... | collective-permute-start | bytes 61448 | tf_op jit(solution)/shard_map/ppermute | solution.py:558
  45.1 3.7 %collective-permute-start.3 = (f32[40,128]{1,0:T(8,128)S(1)}, f32[40,128]{1,0:T(8,128)S(1)}, u32[]{:S(2)}, u32[]{:S(2)}) collective-permute-start(f32[40,128]{1,0:T(8,128)S(1)} %get-tuple-element.22.syb_ref), channel_id=1, source_target_pairs={{4,8},{8,4},{12,16},{16,12},{20,24},{24,20},{28,32},{32,28},{36,40... | collective-permute-start | bytes 61448 | tf_op jit(solution)/shard_map/ppermute | solution.py:558
  48.8 0.0 collective-permute-done.2.ya_ref
  48.8 4.1 %collective-permute-done.3.yb_ref = f32[40,128]{1,0:T(8,128)S(1)} collective-permute-done((f32[40,128]{1,0:T(8,128)S(1)}, f32[40,128]{1,0:T(8,128)S(1)}, u32[]{:S(2)}, u32[]{:S(2)}) %collective-permute-start.3) | collective-permute-done | bytes 20512 | tf_op jit(solution)/shard_map/ppermute | solution.py:558
  53.0 0.0 all-to-all-done.1.recv_ref
  53.0 1.0 %shard_map.67 = (f32[8,32,128]{2,1,0:T(8,128)S(1)}, f32[2,2,8,128]{3,2,1,0:T(8,128)S(1)}, f32[2,40,128]{2,1,0:T(8,128)S(1)}, f32[2,32,128]{2,1,0:T(8,128)S(1)}) custom-call(s32[4]{0:T(128)S(1)} %bitcast.2, f32[32,3,8,128]{3,2,1,0:T(8,128)S(1)} %all-to-all-done.1.recv_ref, f32[8,32,128]{2,1,0:T(8,128)S(1)} %copy-done.1, ...), custom_call_target="tpu_custom_call" | custom-call | tf_op jit(solution)/shard_map/pallas_call | solution.py:568
  54.0 0.1 shard_map.68
  54.1 2.7 %collective-permute-start.4 = (f32[232,128]{1,0:T(8,128)S(1)}, f32[232,128]{1,0:T(8,128)S(1)}, u32[]{:S(2)}, u32[]{:S(2)}) collective-permute-start(f32[232,128]{1,0:T(8,128)S(1)} %get-tuple-element.29), channel_id=1, source_target_pairs={{0,128},{128,0},{256,384},{384,256},{512,640},{640,512},{768,896},... | collective-permute-start | bytes 356360 | tf_op jit(solution)/shard_map/ppermute | solution.py:558
  56.8 3.5 %collective-permute-start.5 = (f32[232,128]{1,0:T(8,128)S(1)}, f32[232,128]{1,0:T(8,128)S(1)}, u32[]{:S(2)}, u32[]{:S(2)}) collective-permute-start(f32[232,128]{1,0:T(8,128)S(1)} %get-tuple-element.30), channel_id=1, source_target_pairs={{128,256},{256,128},{384,512},{512,384},{640,768},{768,640},{129,2... | collective-permute-start | bytes 356360 | tf_op jit(solution)/shard_map/ppermute | solution.py:558
  60.3 0.0 collective-permute-done.4.xa_ref
  60.3 2.2 %collective-permute-done.5.xb_ref = f32[232,128]{1,0:T(8,128)S(1)} collective-permute-done((f32[232,128]{1,0:T(8,128)S(1)}, f32[232,128]{1,0:T(8,128)S(1)}, u32[]{:S(2)}, u32[]{:S(2)}) %collective-permute-start.5) | collective-permute-done | bytes 118816 | tf_op jit(solution)/shard_map/ppermute | solution.py:558
  62.5 1.4 %shard_map.69 = f32[8,32,128]{2,1,0:T(8,128)} custom-call(f32[8,32,128]{2,1,0:T(8,128)S(1)} %get-tuple-element.23.start_ref, f32[8,32,128]{2,1,0:T(8,128)S(1)} %copy-done, f32[8,32,128]{2,1,0:T(8,128)S(1)} %get-tuple-element.24.src_ref, f32[8,32,128]{2,1,0:T(8,128)S(1)} %get-tuple-element.25.rea_ref, f32[2,2,8,128]{3,2,1,0:T(8,128)S(1)} %get-tuple-element.26.zhalo_ref, ...), custom_call_target="tpu_custom_call" | custom-call | tf_op jit(solution)/shard_map/pallas_call | solution.py:568
Async XLA Ops:
  2.2 26.6 %all-to-all-start = ((f32[8,2,8,128]{3,2,1,0:T(8,128)}), f32[8,2,8,128]{3,2,1,0:T(8,128)S(1)}, u32[]{:S(2)}, u32[]{:S(2)}) async-start(f32[8,2,8,128]{3,2,1,0:T(8,128)} %get-tuple-element.18), calls=%async_computation | async-start | bytes 131072 | tf_op jit(solution)/shard_map/all_to_all | solution.py:604
  6.4 20.9 %collective-permute-start = (f32[7,8,128]{2,1,0:T(8,128)S(1)}, f32[7,8,128]{2,1,0:T(8,128)S(1)}, u32[]{:S(2)}, u32[]{:S(2)}) collective-permute-start(f32[7,8,128]{2,1,0:T(8,128)S(1)} %get-tuple-element.19), channel_id=1, source_target_pairs={{0,1},{1,0},{2,3},{3,2},{4,5},{5,4},{6,7},{7,6},{8,9},{9,8},{10,11... | collective-permute-start | bytes 86024 | tf_op jit(solution)/shard_map/ppermute | solution.py:558
  9.2 19.6 %collective-permute-start.1 = (f32[7,8,128]{2,1,0:T(8,128)S(1)}, f32[7,8,128]{2,1,0:T(8,128)S(1)}, u32[]{:S(2)}, u32[]{:S(2)}) collective-permute-start(f32[7,8,128]{2,1,0:T(8,128)S(1)} %get-tuple-element.20), channel_id=1, source_target_pairs={{1,2},{2,1},{5,6},{6,5},{9,10},{10,9},{13,14},{14,13},{17,18},{18,... | collective-permute-start | bytes 86024 | tf_op jit(solution)/shard_map/ppermute | solution.py:558
  29.8 10.0 %copy-start = (f32[8,32,128]{2,1,0:T(8,128)S(1)}, f32[8,32,128]{2,1,0:T(8,128)}, u32[]{:S(2)}) copy-start(f32[8,32,128]{2,1,0:T(8,128)} %conduct_ref.5) | copy-start | bytes 393220
  29.8 10.0 %copy-start.1 = (f32[8,32,128]{2,1,0:T(8,128)S(1)}, f32[8,32,128]{2,1,0:T(8,128)}, u32[]{:S(2)}) copy-start(f32[8,32,128]{2,1,0:T(8,128)} %old_ref.3) | copy-start | bytes 393220
  29.8 10.0 %copy-start.2 = (f32[8,32,128]{2,1,0:T(8,128)S(1)}, f32[8,32,128]{2,1,0:T(8,128)}, u32[]{:S(2)}) copy-start(f32[8,32,128]{2,1,0:T(8,128)} %source_ref.1) | copy-start | bytes 393220
  29.8 10.0 %copy-start.3 = (f32[8,32,128]{2,1,0:T(8,128)S(1)}, f32[8,32,128]{2,1,0:T(8,128)}, u32[]{:S(2)}) copy-start(f32[8,32,128]{2,1,0:T(8,128)} %reaction_ref.1) | copy-start | bytes 393220
  29.8 10.0 %copy-start.4 = (f32[4,16,64]{2,1,0:T(8,128)S(1)}, f32[4,16,64]{2,1,0:T(8,128)}, u32[]{:S(2)}) copy-start(f32[4,16,64]{2,1,0:T(8,128)} %coarse_ref.1) | copy-start | bytes 49156
  29.9 23.1 %all-to-all-start.1 = ((f32[32,3,8,128]{3,2,1,0:T(8,128)}), f32[32,3,8,128]{3,2,1,0:T(8,128)S(1)}, u32[]{:S(2)}, u32[]{:S(2)}) async-start(f32[32,3,8,128]{3,2,1,0:T(8,128)} %shard_map.65), calls=%async_computation.1 | async-start | bytes 786432 | tf_op jit(solution)/shard_map/all_to_all | solution.py:610
  39.8 0.7 %copy-start.5 = (s32[1,1,4]{2,1,0:T(1,128)S(1)}, s32[1,1,4]{2,1,0:T(1,128)}, u32[]{:S(2)}) copy-start(s32[1,1,4]{2,1,0:T(1,128)} %home_hbm.1) | copy-start | bytes 52
  42.0 6.8 %collective-permute-start.2 = (f32[40,128]{1,0:T(8,128)S(1)}, f32[40,128]{1,0:T(8,128)S(1)}, u32[]{:S(2)}, u32[]{:S(2)}) collective-permute-start(f32[40,128]{1,0:T(8,128)S(1)} %get-tuple-element.21.sya_ref), channel_id=1, source_target_pairs={{0,4},{4,0},{8,12},{12,8},{16,20},{20,16},{24,28},{28,24},{32,36},... | collective-permute-start | bytes 61448 | tf_op jit(solution)/shard_map/ppermute | solution.py:558
  45.1 7.8 %collective-permute-start.3 = (f32[40,128]{1,0:T(8,128)S(1)}, f32[40,128]{1,0:T(8,128)S(1)}, u32[]{:S(2)}, u32[]{:S(2)}) collective-permute-start(f32[40,128]{1,0:T(8,128)S(1)} %get-tuple-element.22.syb_ref), channel_id=1, source_target_pairs={{4,8},{8,4},{12,16},{16,12},{20,24},{24,20},{28,32},{32,28},{36,40... | collective-permute-start | bytes 61448 | tf_op jit(solution)/shard_map/ppermute | solution.py:558
  54.1 6.2 %collective-permute-start.4 = (f32[232,128]{1,0:T(8,128)S(1)}, f32[232,128]{1,0:T(8,128)S(1)}, u32[]{:S(2)}, u32[]{:S(2)}) collective-permute-start(f32[232,128]{1,0:T(8,128)S(1)} %get-tuple-element.29), channel_id=1, source_target_pairs={{0,128},{128,0},{256,384},{384,256},{512,640},{640,512},{768,896},... | collective-permute-start | bytes 356360 | tf_op jit(solution)/shard_map/ppermute | solution.py:558
  56.8 5.7 %collective-permute-start.5 = (f32[232,128]{1,0:T(8,128)S(1)}, f32[232,128]{1,0:T(8,128)S(1)}, u32[]{:S(2)}, u32[]{:S(2)}) collective-permute-start(f32[232,128]{1,0:T(8,128)S(1)} %get-tuple-element.30), channel_id=1, source_target_pairs={{128,256},{256,128},{384,512},{512,384},{640,768},{768,640},{129,2... | collective-permute-start | bytes 356360 | tf_op jit(solution)/shard_map/ppermute | solution.py:558

commit v9 on v8

--- a/solution.py
+++ b/solution.py
@@ -163,12 +163,65 @@
         write_pair("gz", za_ref, zb_ref, i, faces[0][i], faces[1][i])
 
 
-def fold_kernel(
-    home_ref, old_ref, conduct_ref, source_ref, reaction_ref, coarse_ref, za_ref, zb_ref,
-    src_ref, rea_ref, ya_ref, yb_ref,
+def columns_kernel(
+    sent_ref, old_ref, conduct_ref, source_ref, reaction_ref, coarse_ref, za_ref, zb_ref,
+    ya_ref, yb_ref, *, width,
 ):
-    slots = home_ref.shape[0]
-    width = LANES // slots
+    nx, nz, _ = conduct_ref.shape
+    cx, cz, cy = coarse_ref.shape
+    (x_first, x_last), (z_first, z_last), _ = edges()
+    lane = lane_of((cz, LANES))
+    ends = jnp.zeros((cz, LANES), F32)
+    for x in range(cx):
+        plane = coarse_ref[x]
+        for side, at in ((0, 0), (1, cy - 1)):
+            column = jnp.broadcast_to(plane[:, at : at + 1], (cz, LANES))
+            ends = jnp.where(lax.div(lane, 2) == side * cx + x, column, ends)
+    refined = exact_dot(doubler(cz).T, ends)
+
+    row, lane = row_of((nz, LANES)), lane_of((nz, LANES))
+    low = high = jnp.zeros((nz, LANES), F32)
+    for f, (ref, depth) in enumerate(
+        ((old_ref, 0), (old_ref, 1), (conduct_ref, 0), (conduct_ref, 1), (source_ref, 0), (reaction_ref, 0))
+    ):
+        for x in range(nx):
+            spot = f * nx + x
+            low = jnp.where(lane == spot, roll_lanes(ref[x], spot - depth), low)
+            high = jnp.where(lane == spot, roll_lanes(ref[x], spot + 1 + depth), high)
+    field, x_at = lax.div(lane, nx), lax.rem(lane, nx)
+    outside = (
+        ((row == 0) & z_first).astype(F32)
+        + ((row == nz - 1) & z_last).astype(F32)
+        + ((x_at == 0) & x_first).astype(F32)
+        + ((x_at == nx - 1) & x_last).astype(F32)
+    )
+
+    def fold(tile, at):
+        src = tile + outside * roll_lanes(tile, (SRC - KAP1) * nx) * roll_lanes(refined, SRC * nx - at)
+        rea = 1.0 + tile + outside * roll_lanes(tile, (REA - KAP1) * nx)
+        return jnp.where(field == SRC, src, jnp.where(field == REA, rea, tile))
+
+    write_pair("gy", ya_ref, yb_ref, slice(0, nz), fold(low, 0), fold(high, nx))
+
+    lane = lane_of((nx, LANES))
+    spot = slice(3 * width, 3 * width + 1)
+    own = jnp.broadcast_to(sent_ref[RIM][:, spot], (nx, LANES))
+    low = high = jnp.where(lane == 4, own, 0.0)
+    notes = received("gz", za_ref[RIM], zb_ref[RIM])
+    for side in range(2):
+        note = jnp.broadcast_to(notes[side][:, spot], (nx, LANES))
+        low = jnp.where(lane == 5 + side, note, low)
+        high = jnp.where(lane == 5 + side, note, high)
+        for f, tile in enumerate((PHI1, KAP1)):
+            value = received("gz", za_ref[tile], zb_ref[tile])[side]
+            at = 2 * side + f
+            low = jnp.where(lane == at, roll_lanes(value, at), low)
+            high = jnp.where(lane == at, roll_lanes(value, at + 1), high)
+    write_pair("gy", ya_ref, yb_ref, slice(nz, nz + nx), low, high)
+
+
+def fold_kernel(conduct_ref, source_ref, reaction_ref, coarse_ref, after_ref, src_ref, rea_ref):
+    del after_ref
     nx, nz, _ = conduct_ref.shape
     (x_first, x_last), (z_first, z_last), (y_first, y_last) = edges()
     refined = refine(coarse_ref)
@@ -188,31 +241,6 @@
         weight = faces * conduct_ref[x]
         src_ref[x] = source_ref[x] + weight * refined[x // 2]
         rea_ref[x] = 1.0 + reaction_ref[x] + weight
-
-    low = high = jnp.zeros((nz, LANES), F32)
-    for f, (ref, depth) in enumerate(
-        ((old_ref, 0), (old_ref, 1), (conduct_ref, 0), (conduct_ref, 1), (src_ref, 0), (rea_ref, 0))
-    ):
-        for x in range(nx):
-            spot = f * nx + x
-            low = jnp.where(lane == spot, roll_lanes(ref[x], spot - depth), low)
-            high = jnp.where(lane == spot, roll_lanes(ref[x], spot + 1 + depth), high)
-    write_pair("gy", ya_ref, yb_ref, slice(0, nz), low, high)
-
-    lane = lane_of((nx, LANES))
-    slot, _ = moved_slot(lambda j: home_ref[j], slots)
-    low = high = jnp.where(lane == 4, slot, 0).astype(F32)
-    notes = received("gz", za_ref[RIM], zb_ref[RIM])
-    for side in range(2):
-        note = jnp.broadcast_to(notes[side][:, 3 * width : 3 * width + 1], (nx, LANES))
-        low = jnp.where(lane == 5 + side, note, low)
-        high = jnp.where(lane == 5 + side, note, high)
-        for f, tile in enumerate((PHI1, KAP1)):
-            value = received("gz", za_ref[tile], zb_ref[tile])[side]
-            spot = 2 * side + f
-            low = jnp.where(lane == spot, roll_lanes(value, spot), low)
-            high = jnp.where(lane == spot, roll_lanes(value, spot + 1), high)
-    write_pair("gy", ya_ref, yb_ref, slice(nz, nz + nx), low, high)
 
 
 def address_kernel(parts_ref, za_ref, zb_ref, send_ref, *, width):
@@ -426,9 +454,48 @@
     )
 
 
+def sweep_plane(x, phi, kappa, numerator, denominator, sides, z_phi, z_kappa, y_phi, y_kappa, flags_z, flags_y):
+    sides = sides + along_rows(
+        phi,
+        kappa,
+        (z_phi[0][x : x + 1], z_kappa[0][x : x + 1]),
+        (z_phi[1][x : x + 1], z_kappa[1][x : x + 1]),
+        flags_z,
+    )
+    spot = KAP1 * z_phi[0].shape[0] + x
+    sides += along_lanes(
+        phi,
+        kappa,
+        (roll_lanes(y_phi[0], -x), roll_lanes(y_kappa[0], -spot)),
+        (roll_lanes(y_phi[1], LANES - 1 - x), roll_lanes(y_kappa[1], LANES - 1 - spot)),
+        flags_y,
+    )
+    return step(numerator, denominator, kappa, sides)
+
+
+def inner_kernel(
+    start_ref, conduct_ref, src_ref, rea_ref, zhalo_ref, yhalo_ref, za_ref, zb_ref, after_ref,
+    first_ref,
+):
+    del after_ref
+    nx, nz, _ = start_ref.shape
+    _, flags_z, flags_y = edges()
+    z_kappa = received("gz", za_ref[KAP1], zb_ref[KAP1])
+    z_phi = (zhalo_ref[0, 0], zhalo_ref[1, 0])
+    yf = [yhalo_ref[side, :nz] for side in range(2)]
+    first_ref[0] = start_ref[0]
+    first_ref[nx - 1] = start_ref[nx - 1]
+    for x in range(1, nx - 1):
+        sides = [(start_ref[i], conduct_ref[i], None) for i in (x - 1, x + 1)]
+        first_ref[x] = sweep_plane(
+            x, start_ref[x], conduct_ref[x], start_ref[x] + src_ref[x], rea_ref[x],
+            sides, z_phi, z_kappa, yf, yf, flags_z, flags_y,
+        )
+
+
 def sweeps_kernel(
     start_ref, conduct_ref, src_ref, rea_ref, zhalo_ref, yhalo_ref, own_ref,
-    za_ref, zb_ref, sya_ref, syb_ref, xa_ref, xb_ref,
+    za_ref, zb_ref, sya_ref, syb_ref, xa_ref, xb_ref, first_ref,
     out_ref,
 ):
     nx, nz, _ = start_ref.shape
@@ -511,39 +578,20 @@
         )
         y_first_sweep.append(step(phi + src, rea, kappa, sides))
 
-    def sweep(phis, x_phi, z_phi, y_phi):
-        results = []
-        for x in range(nx):
-            phi, kappa = phis[x], conduct[x]
-            sides = []
-            if x:
-                sides.append((phis[x - 1], conduct[x - 1], None))
-            else:
-                sides.append((x_phi[0], xf[KAP1][0], flags_x[0]))
-            if x < nx - 1:
-                sides.append((phis[x + 1], conduct[x + 1], None))
-            else:
-                sides.append((x_phi[1], xf[KAP1][1], flags_x[1]))
-            sides += along_rows(
-                phi,
-                kappa,
-                (z_phi[0][x : x + 1], zf[KAP1][0][x : x + 1]),
-                (z_phi[1][x : x + 1], zf[KAP1][1][x : x + 1]),
-                flags_z,
+    def sweep(phis, x_phi, z_phi, y_phi, planes):
+        below = [(x_phi[0], xf[KAP1][0], flags_x[0])] + [(phis[x], conduct[x], None) for x in range(nx - 1)]
+        above = [(phis[x], conduct[x], None) for x in range(1, nx)] + [(x_phi[1], xf[KAP1][1], flags_x[1])]
+        return [
+            sweep_plane(
+                x, phis[x], conduct[x], start[x] + src_ref[x], rea_ref[x],
+                [below[x], above[x]], z_phi, zf[KAP1], y_phi, yf, flags_z, flags_y,
             )
-            spot = KAP1 * nx + x
-            sides += along_lanes(
-                phi,
-                kappa,
-                (roll_lanes(y_phi[0], -x), roll_lanes(yf[0], -spot)),
-                (roll_lanes(y_phi[1], LANES - 1 - x), roll_lanes(yf[1], LANES - 1 - spot)),
-                flags_y,
-            )
-            results.append(step(start[x] + src_ref[x], rea_ref[x], kappa, sides))
-        return results
-
-    first = sweep(start, xf[PHI1], (zhalo_ref[0, 0], zhalo_ref[1, 0]), yf)
-    second = sweep(first, x_first_sweep, z_first_sweep, y_first_sweep)
+            for x in planes
+        ]
+
+    ends = sweep(start, xf[PHI1], (zhalo_ref[0, 0], zhalo_ref[1, 0]), yf, (0, nx - 1))
+    first = [ends[0]] + [first_ref[x] for x in range(1, nx - 1)] + [ends[1]]
+    second = sweep(first, x_first_sweep, z_first_sweep, y_first_sweep, range(nx))
     for x in range(nx):
         out_ref[x] = second[x]
 
@@ -608,13 +656,15 @@
 
     (send,) = call(address, (parts, za, zb), [(line, part + 2, rows, ny)])
     recv = lax.all_to_all(send, "gy", 0, 0, tiled=True)
-    src, rea, sya, syb = call(
-        fold_kernel,
-        (home, old_field, conduct, source, reaction, coarse, za, zb),
-        [block, block, (nz + nx, ny), (nz + nx, ny)],
-        smem=1,
+
+    def columns(*refs):
+        columns_kernel(*refs, width=width)
+
+    sya, syb = call(
+        columns, (sza, old_field, conduct, source, reaction, coarse, za, zb), [(nz + nx, ny)] * 2
     )
     ya, yb = swap("gy", sya, syb)
+    src, rea = call(fold_kernel, (conduct, source, reaction, coarse, sya), [block, block])
     start, zhalo, yhalo, own = call(
         place_kernel,
         (home, recv, old_field, za, zb, ya, yb),
@@ -626,10 +676,13 @@
         (start, conduct, src, rea, zhalo, yhalo, za, zb),
         [(7 * nz + 8, ny)] * 2,
     )
+    (first,) = call(
+        inner_kernel, (start, conduct, src, rea, zhalo, yhalo, za, zb, xa), [block]
+    )
     xa, xb = swap("gx", xa, xb)
     (relaxed,) = call(
         sweeps_kernel,
-        (start, conduct, src, rea, zhalo, yhalo, own, za, zb, sya, syb, xa, xb),
+        (start, conduct, src, rea, zhalo, yhalo, own, za, zb, sya, syb, xa, xb, first),
         [block],
     )
     return relaxed

time: 64.5 us -> 63.1 us (0.978)
  the two profiles are of different devices: /device:TPU:97 before, /device:TPU:65 now
where the time goes in v9:
time: 63.1 us; the launch traced here: 62.6 us
  starting transfers between devices  45.4 us (72%)
  waiting for transfers between devices  9.44 us (15%)
  Pallas kernels  7.52 us (12%)
    ppermute x6, starting transfers between devices, swap(): results.append(lax.ppermute(value, axis, pairs))  30.9 us
    all_to_all x1, starting transfers between devices, on_device(): recv = lax.all_to_all(send, 'gy', 0, 0, tiled=True)  9.42 us
    pallas_call x8, Pallas kernels, call(): pl.pallas_call(kernel, out_shape=[jax.ShapeDtypeStruct(shape, F32) for sh...  7.52 us
    all_to_all x1, waiting for transfers between devices, on_device(): recv = lax.all_to_all(send, 'gy', 0, 0, tiled=True)  5.99 us
    all_to_all x1, starting transfers between devices, on_device(): lax.all_to_all(parts, 'gy', 0, 0, tiled=True, axis_index_groups=groups)  5.04 us
    ppermute x6, waiting for transfers between devices, swap(): results.append(lax.ppermute(value, axis, pairs))  3.45 us
  transfers between devices with their start and end apart: 8, of which 3 were waited for; matrix products, arithmetic and copies ran while one was open for 0% of the time, Pallas kernels for 3%

profile of v9, /device:TPU:65, one launch (start us, length us, event | category | flops | bytes accessed | tf_op | source)
XLA Modules:
  0.0 62.6 jit_solution(4739826710623490869)
XLA Ops:
  0.0 2.2 %shard_map.64 = (f32[7,8,128]{2,1,0:T(8,128)S(1)}, f32[7,8,128]{2,1,0:T(8,128)S(1)}, f32[8,2,8,128]{3,2,1,0:T(8,128)}) custom-call(s32[1,1,4]{2,1,0:T(1,128)} %home_hbm.1, f32[8,32,128]{2,1,0:T(8,128)} %old_ref.1, f32[8,32,128]{2,1,0:T(8,128)} %conduct_ref.7, f32[8,32,128]{2,1,0:T(8,128)} %source_ref.1, f32[8,32,128]{2,1,0:T(8,128)} %reaction_ref.1, ...), custom_call_target="tpu_custom_call" | custom-call | tf_op jit(solution)/shard_map/pallas_call | solution.py:616
  2.2 5.0 %all-to-all-start = ((f32[8,2,8,128]{3,2,1,0:T(8,128)}), f32[8,2,8,128]{3,2,1,0:T(8,128)S(1)}, u32[]{:S(2)}, u32[]{:S(2)}) async-start(f32[8,2,8,128]{3,2,1,0:T(8,128)} %get-tuple-element.18), calls=%async_computation | async-start | bytes 131072 | tf_op jit(solution)/shard_map/all_to_all | solution.py:652
  7.3 2.9 %collective-permute-start = (f32[7,8,128]{2,1,0:T(8,128)S(1)}, f32[7,8,128]{2,1,0:T(8,128)S(1)}, u32[]{:S(2)}, u32[]{:S(2)}) collective-permute-start(f32[7,8,128]{2,1,0:T(8,128)S(1)} %get-tuple-element.19.refs_0_), channel_id=1, source_target_pairs={{0,1},{1,0},{2,3},{3,2},{4,5},{5,4},{6,7},{7,6},{8,9},{9,8},{10,11... | collective-permute-start | bytes 86024 | tf_op jit(solution)/shard_map/ppermute | solution.py:606
  10.1 18.1 %collective-permute-start.1 = (f32[7,8,128]{2,1,0:T(8,128)S(1)}, f32[7,8,128]{2,1,0:T(8,128)S(1)}, u32[]{:S(2)}, u32[]{:S(2)}) collective-permute-start(f32[7,8,128]{2,1,0:T(8,128)S(1)} %get-tuple-element.20), channel_id=1, source_target_pairs={{1,2},{2,1},{5,6},{6,5},{9,10},{10,9},{13,14},{14,13},{17,18},{18,... | collective-permute-start | bytes 86024 | tf_op jit(solution)/shard_map/ppermute | solution.py:606
  28.2 0.0 collective-permute-done.refs_1_.refs_6_.za_ref
  28.2 1.5 %collective-permute-done.1.refs_2_.refs_7_.zb_ref = f32[7,8,128]{2,1,0:T(8,128)S(1)} collective-permute-done((f32[7,8,128]{2,1,0:T(8,128)S(1)}, f32[7,8,128]{2,1,0:T(8,128)S(1)}, u32[]{:S(2)}, u32[]{:S(2)}) %collective-permute-start.1) | collective-permute-done | bytes 28704 | tf_op jit(solution)/shard_map/ppermute | solution.py:606
  29.7 0.0 all-to-all-done.refs_0_
  29.8 1.0 %shard_map.65 = f32[32,3,8,128]{3,2,1,0:T(8,128)} custom-call(f32[8,2,8,128]{3,2,1,0:T(8,128)S(1)} %all-to-all-done.refs_0_, f32[7,8,128]{2,1,0:T(8,128)S(1)} %collective-permute-done.refs_1_.refs_6_.za_ref, f32[7,8,128]{2,1,0:T(8,128)S(1)} %collective-permute-done.1.refs_2_.refs_7_.zb_ref), custom_call_target="tpu_custom_call" | custom-call | tf_op jit(solution)/shard_map/pallas_call | solution.py:616
  30.7 0.0 copy-start
  30.7 0.0 copy-start.1
  30.7 0.0 copy-start.2
  30.7 0.0 copy-start.3
  30.8 0.0 copy-start.4
  30.8 9.4 %all-to-all-start.1 = ((f32[32,3,8,128]{3,2,1,0:T(8,128)}), f32[32,3,8,128]{3,2,1,0:T(8,128)S(1)}, u32[]{:S(2)}, u32[]{:S(2)}) async-start(f32[32,3,8,128]{3,2,1,0:T(8,128)} %shard_map.65), calls=%async_computation.1 | async-start | bytes 786432 | tf_op jit(solution)/shard_map/all_to_all | solution.py:658
  40.2 0.0 copy-done
  40.2 0.0 copy-done.1
  40.2 0.0 copy-done.2
  40.2 0.0 copy-done.3
  40.2 0.0 copy-done.4
  40.2 0.6 shard_map.66
  40.9 3.1 %collective-permute-start.2 = (f32[40,128]{1,0:T(8,128)S(1)}, f32[40,128]{1,0:T(8,128)S(1)}, u32[]{:S(2)}, u32[]{:S(2)}) collective-permute-start(f32[40,128]{1,0:T(8,128)S(1)} %get-tuple-element.21.after_ref.sya_ref), channel_id=1, source_target_pairs={{0,4},{4,0},{8,12},{12,8},{16,20},{20,16},{24,28},{28,24},{32,36},... | collective-permute-start | bytes 61448 | tf_op jit(solution)/shard_map/ppermute | solution.py:606
  44.0 0.7 %collective-permute-start.3 = (f32[40,128]{1,0:T(8,128)S(1)}, f32[40,128]{1,0:T(8,128)S(1)}, u32[]{:S(2)}, u32[]{:S(2)}) collective-permute-start(f32[40,128]{1,0:T(8,128)S(1)} %get-tuple-element.22.syb_ref), channel_id=1, source_target_pairs={{4,8},{8,4},{12,16},{16,12},{20,24},{24,20},{28,32},{32,28},{36,40... | collective-permute-start | bytes 61448 | tf_op jit(solution)/shard_map/ppermute | solution.py:606
  44.7 0.9 %shard_map.68 = (f32[8,32,128]{2,1,0:T(8,128)S(1)}, f32[8,32,128]{2,1,0:T(8,128)S(1)}) custom-call(f32[8,32,128]{2,1,0:T(8,128)S(1)} %copy-done, f32[8,32,128]{2,1,0:T(8,128)S(1)} %copy-done.1, f32[8,32,128]{2,1,0:T(8,128)S(1)} %copy-done.2, f32[4,16,64]{2,1,0:T(8,128)S(1)} %copy-done.4, f32[40,128]{1,0:T(8,128)S(1)} %get-tuple-element.21.after_ref.sya_ref), custom_call_target="tpu_custom_call" | custom-call | tf_op jit(solution)/shard_map/pallas_call | solution.py:616
  45.6 0.0 copy-start.5
  45.6 0.0 collective-permute-done.2.ya_ref
  45.6 0.0 collective-permute-done.3.yb_ref
  45.7 6.0 %all-to-all-done.1.recv_ref = f32[32,3,8,128]{3,2,1,0:T(8,128)S(1)} async-done(((f32[32,3,8,128]{3,2,1,0:T(8,128)}), f32[32,3,8,128]{3,2,1,0:T(8,128)S(1)}, u32[]{:S(2)}, u32[]{:S(2)}) %all-to-all-start.1) | async-done | bytes 393248 | tf_op jit(solution)/shard_map/all_to_all | solution.py:658
  51.6 0.0 copy-done.5
  51.6 1.0 %shard_map.67 = (f32[8,32,128]{2,1,0:T(8,128)S(1)}, f32[2,2,8,128]{3,2,1,0:T(8,128)S(1)}, f32[2,40,128]{2,1,0:T(8,128)S(1)}, f32[2,32,128]{2,1,0:T(8,128)S(1)}) custom-call(s32[4]{0:T(128)S(1)} %bitcast.1, f32[32,3,8,128]{3,2,1,0:T(8,128)S(1)} %all-to-all-done.1.recv_ref, f32[8,32,128]{2,1,0:T(8,128)S(1)} %copy-done.3, ...), custom_call_target="tpu_custom_call" | custom-call | tf_op jit(solution)/shard_map/pallas_call | solution.py:616
  52.7 0.1 shard_map.69
  52.8 2.7 %collective-permute-start.4 = (f32[232,128]{1,0:T(8,128)S(1)}, f32[232,128]{1,0:T(8,128)S(1)}, u32[]{:S(2)}, u32[]{:S(2)}) collective-permute-start(f32[232,128]{1,0:T(8,128)S(1)} %get-tuple-element.29.after_ref), channel_id=1, source_target_pairs={{0,128},{128,0},{256,384},{384,256},{512,640},{640,512},{768,896},... | collective-permute-start | bytes 356360 | tf_op jit(solution)/shard_map/ppermute | solution.py:606
  55.5 3.5 %collective-permute-start.5 = (f32[232,128]{1,0:T(8,128)S(1)}, f32[232,128]{1,0:T(8,128)S(1)}, u32[]{:S(2)}, u32[]{:S(2)}) collective-permute-start(f32[232,128]{1,0:T(8,128)S(1)} %get-tuple-element.30), channel_id=1, source_target_pairs={{128,256},{256,128},{384,512},{512,384},{640,768},{768,640},{129,2... | collective-permute-start | bytes 356360 | tf_op jit(solution)/shard_map/ppermute | solution.py:606
  59.0 0.3 shard_map.70.first_ref
  59.3 0.0 collective-permute-done.4.xa_ref
  59.3 1.9 %collective-permute-done.5.xb_ref = f32[232,128]{1,0:T(8,128)S(1)} collective-permute-done((f32[232,128]{1,0:T(8,128)S(1)}, f32[232,128]{1,0:T(8,128)S(1)}, u32[]{:S(2)}, u32[]{:S(2)}) %collective-permute-start.5) | collective-permute-done | bytes 118816 | tf_op jit(solution)/shard_map/ppermute | solution.py:606
  61.2 1.3 %shard_map.71 = f32[8,32,128]{2,1,0:T(8,128)} custom-call(f32[8,32,128]{2,1,0:T(8,128)S(1)} %get-tuple-element.23.start_ref, f32[8,32,128]{2,1,0:T(8,128)S(1)} %copy-done, f32[8,32,128]{2,1,0:T(8,128)S(1)} %get-tuple-element.24.src_ref, f32[8,32,128]{2,1,0:T(8,128)S(1)} %get-tuple-element.25.rea_ref, f32[2,2,8,128]{3,2,1,0:T(8,128)S(1)} %get-tuple-element.26.zhalo_ref, ...), custom_call_target="tpu_custom_call" | custom-call | tf_op jit(solution)/shard_map/pallas_call | solution.py:616
Async XLA Ops:
  2.2 27.5 %all-to-all-start = ((f32[8,2,8,128]{3,2,1,0:T(8,128)}), f32[8,2,8,128]{3,2,1,0:T(8,128)S(1)}, u32[]{:S(2)}, u32[]{:S(2)}) async-start(f32[8,2,8,128]{3,2,1,0:T(8,128)} %get-tuple-element.18), calls=%async_computation | async-start | bytes 131072 | tf_op jit(solution)/shard_map/all_to_all | solution.py:652
  7.3 20.9 %collective-permute-start = (f32[7,8,128]{2,1,0:T(8,128)S(1)}, f32[7,8,128]{2,1,0:T(8,128)S(1)}, u32[]{:S(2)}, u32[]{:S(2)}) collective-permute-start(f32[7,8,128]{2,1,0:T(8,128)S(1)} %get-tuple-element.19.refs_0_), channel_id=1, source_target_pairs={{0,1},{1,0},{2,3},{3,2},{4,5},{5,4},{6,7},{7,6},{8,9},{9,8},{10,11... | collective-permute-start | bytes 86024 | tf_op jit(solution)/shard_map/ppermute | solution.py:606
  10.1 19.6 %collective-permute-start.1 = (f32[7,8,128]{2,1,0:T(8,128)S(1)}, f32[7,8,128]{2,1,0:T(8,128)S(1)}, u32[]{:S(2)}, u32[]{:S(2)}) collective-permute-start(f32[7,8,128]{2,1,0:T(8,128)S(1)} %get-tuple-element.20), channel_id=1, source_target_pairs={{1,2},{2,1},{5,6},{6,5},{9,10},{10,9},{13,14},{14,13},{17,18},{18,... | collective-permute-start | bytes 86024 | tf_op jit(solution)/shard_map/ppermute | solution.py:606
  30.7 9.5 %copy-start = (f32[8,32,128]{2,1,0:T(8,128)S(1)}, f32[8,32,128]{2,1,0:T(8,128)}, u32[]{:S(2)}) copy-start(f32[8,32,128]{2,1,0:T(8,128)} %conduct_ref.7) | copy-start | bytes 393220
  30.7 9.5 %copy-start.1 = (f32[8,32,128]{2,1,0:T(8,128)S(1)}, f32[8,32,128]{2,1,0:T(8,128)}, u32[]{:S(2)}) copy-start(f32[8,32,128]{2,1,0:T(8,128)} %source_ref.1) | copy-start | bytes 393220
  30.7 9.5 %copy-start.2 = (f32[8,32,128]{2,1,0:T(8,128)S(1)}, f32[8,32,128]{2,1,0:T(8,128)}, u32[]{:S(2)}) copy-start(f32[8,32,128]{2,1,0:T(8,128)} %reaction_ref.1) | copy-start | bytes 393220
  30.7 9.5 %copy-start.3 = (f32[8,32,128]{2,1,0:T(8,128)S(1)}, f32[8,32,128]{2,1,0:T(8,128)}, u32[]{:S(2)}) copy-start(f32[8,32,128]{2,1,0:T(8,128)} %old_ref.1) | copy-start | bytes 393220
  30.8 9.5 %copy-start.4 = (f32[4,16,64]{2,1,0:T(8,128)S(1)}, f32[4,16,64]{2,1,0:T(8,128)}, u32[]{:S(2)}) copy-start(f32[4,16,64]{2,1,0:T(8,128)} %coarse_ref.1) | copy-start | bytes 49156
  30.8 20.9 %all-to-all-start.1 = ((f32[32,3,8,128]{3,2,1,0:T(8,128)}), f32[32,3,8,128]{3,2,1,0:T(8,128)S(1)}, u32[]{:S(2)}, u32[]{:S(2)}) async-start(f32[32,3,8,128]{3,2,1,0:T(8,128)} %shard_map.65), calls=%async_computation.1 | async-start | bytes 786432 | tf_op jit(solution)/shard_map/all_to_all | solution.py:658
  40.9 4.8 %collective-permute-start.2 = (f32[40,128]{1,0:T(8,128)S(1)}, f32[40,128]{1,0:T(8,128)S(1)}, u32[]{:S(2)}, u32[]{:S(2)}) collective-permute-start(f32[40,128]{1,0:T(8,128)S(1)} %get-tuple-element.21.after_ref.sya_ref), channel_id=1, source_target_pairs={{0,4},{4,0},{8,12},{12,8},{16,20},{20,16},{24,28},{28,24},{32,36},... | collective-permute-start | bytes 61448 | tf_op jit(solution)/shard_map/ppermute | solution.py:606
  44.0 1.6 %collective-permute-start.3 = (f32[40,128]{1,0:T(8,128)S(1)}, f32[40,128]{1,0:T(8,128)S(1)}, u32[]{:S(2)}, u32[]{:S(2)}) collective-permute-start(f32[40,128]{1,0:T(8,128)S(1)} %get-tuple-element.22.syb_ref), channel_id=1, source_target_pairs={{4,8},{8,4},{12,16},{16,12},{20,24},{24,20},{28,32},{32,28},{36,40... | collective-permute-start | bytes 61448 | tf_op jit(solution)/shard_map/ppermute | solution.py:606
  45.6 6.0 %copy-start.5 = (s32[1,1,4]{2,1,0:T(1,128)S(1)}, s32[1,1,4]{2,1,0:T(1,128)}, u32[]{:S(2)}) copy-start(s32[1,1,4]{2,1,0:T(1,128)} %home_hbm.1) | copy-start | bytes 52
  52.8 6.5 %collective-permute-start.4 = (f32[232,128]{1,0:T(8,128)S(1)}, f32[232,128]{1,0:T(8,128)S(1)}, u32[]{:S(2)}, u32[]{:S(2)}) collective-permute-start(f32[232,128]{1,0:T(8,128)S(1)} %get-tuple-element.29.after_ref), channel_id=1, source_target_pairs={{0,128},{128,0},{256,384},{384,256},{512,640},{640,512},{768,896},... | collective-permute-start | bytes 356360 | tf_op jit(solution)/shard_map/ppermute | solution.py:606
  55.5 5.7 %collective-permute-start.5 = (f32[232,128]{1,0:T(8,128)S(1)}, f32[232,128]{1,0:T(8,128)S(1)}, u32[]{:S(2)}, u32[]{:S(2)}) collective-permute-start(f32[232,128]{1,0:T(8,128)S(1)} %get-tuple-element.30), channel_id=1, source_target_pairs={{128,256},{256,128},{384,512},{512,384},{640,768},{768,640},{129,2... | collective-permute-start | bytes 356360 | tf_op jit(solution)/shard_map/ppermute | solution.py:606

commit v10 on v9

--- a/solution.py
+++ b/solution.py
@@ -6,7 +6,7 @@
 from jax.sharding import PartitionSpec as P
 
 LANES = 128
-RUN = 8
+RUN = 4
 VMEM = pl.BlockSpec(memory_space=pltpu.VMEM)
 SMEM = pl.BlockSpec(memory_space=pltpu.SMEM)
 HBM = pl.BlockSpec(memory_space=pltpu.HBM)
@@ -287,7 +287,7 @@
 
 def place_kernel(
     home_ref, recv_ref, old_ref, za_ref, zb_ref, ya_ref, yb_ref,
-    start_ref, zhalo_ref, yhalo_ref, own_ref,
+    start_ref, zhalo_ref, yhalo_ref,
 ):
     slots = home_ref.shape[0]
     width = LANES // slots
@@ -361,14 +361,6 @@
             )
         yhalo_ref[side, nz : nz + nx] = corner
 
-    lane = lane_of((nz, LANES))
-    low = high = jnp.zeros((nz, LANES), F32)
-    for x in range(nx):
-        low = jnp.where(lane == x, roll_lanes(start_ref[x], x), low)
-        high = jnp.where(lane == x, roll_lanes(start_ref[x], x + 1), high)
-    own_ref[0] = low
-    own_ref[1] = high
-
 
 def edge_kernel(
     start_ref, conduct_ref, src_ref, rea_ref, zhalo_ref, yhalo_ref, za_ref, zb_ref,
@@ -475,7 +467,7 @@
 
 def inner_kernel(
     start_ref, conduct_ref, src_ref, rea_ref, zhalo_ref, yhalo_ref, za_ref, zb_ref, after_ref,
-    first_ref,
+    first_ref, own_ref,
 ):
     del after_ref
     nx, nz, _ = start_ref.shape
@@ -491,6 +483,14 @@
             x, start_ref[x], conduct_ref[x], start_ref[x] + src_ref[x], rea_ref[x],
             sides, z_phi, z_kappa, yf, yf, flags_z, flags_y,
         )
+
+    lane = lane_of((nz, LANES))
+    low = high = jnp.zeros((nz, LANES), F32)
+    for x in range(nx):
+        low = jnp.where(lane == x, roll_lanes(start_ref[x], x), low)
+        high = jnp.where(lane == x, roll_lanes(start_ref[x], x + 1), high)
+    own_ref[0] = low
+    own_ref[1] = high
 
 
 def sweeps_kernel(
@@ -665,10 +665,10 @@
     )
     ya, yb = swap("gy", sya, syb)
     src, rea = call(fold_kernel, (conduct, source, reaction, coarse, sya), [block, block])
-    start, zhalo, yhalo, own = call(
+    start, zhalo, yhalo = call(
         place_kernel,
         (home, recv, old_field, za, zb, ya, yb),
-        [block, (2, 2, nx, ny), (2, nz + nx, ny), (2, nz, ny)],
+        [block, (2, 2, nx, ny), (2, nz + nx, ny)],
         smem=1,
     )
     xa, xb = call(
@@ -676,8 +676,10 @@
         (start, conduct, src, rea, zhalo, yhalo, za, zb),
         [(7 * nz + 8, ny)] * 2,
     )
-    (first,) = call(
-        inner_kernel, (start, conduct, src, rea, zhalo, yhalo, za, zb, xa), [block]
+    first, own = call(
+        inner_kernel,
+        (start, conduct, src, rea, zhalo, yhalo, za, zb, xa),
+        [block, (2, nz, ny)],
     )
     xa, xb = swap("gx", xa, xb)
     (relaxed,) = call(

time: 63.1 us -> 64.2 us (1.017)
  waiting for transfers between devices: 9.44 us -> 10.7 us
    all_to_all x1, waiting for transfers between devices: 5.99 us -> 7.32 us  [on_device(): recv = lax.all_to_all(send, 'gy', 0, 0, tiled=True)]
    all_to_all x1, starting transfers between devices: 5.04 us -> 4.02 us  [on_device(): lax.all_to_all(parts, 'gy', 0, 0, tiled=True, axis_index_groups=groups)]
    all_to_all x1, starting transfers between devices: 9.42 us -> 10.3 us  [on_device(): recv = lax.all_to_all(send, 'gy', 0, 0, tiled=True)]
where the time goes in v10:
time: 64.2 us; the launch traced here: 63.6 us
  starting transfers between devices  45.3 us (71%)
  waiting for transfers between devices  10.7 us (17%)
  Pallas kernels  7.45 us (12%)
    ppermute x6, starting transfers between devices, swap(): results.append(lax.ppermute(value, axis, pairs))  30.9 us
    all_to_all x1, starting transfers between devices, on_device(): recv = lax.all_to_all(send, 'gy', 0, 0, tiled=True)  10.3 us
    pallas_call x8, Pallas kernels, call(): pl.pallas_call(kernel, out_shape=[jax.ShapeDtypeStruct(shape, F32) for sh...  7.45 us
    all_to_all x1, waiting for transfers between devices, on_device(): recv = lax.all_to_all(send, 'gy', 0, 0, tiled=True)  7.32 us
    all_to_all x1, starting transfers between devices, on_device(): lax.all_to_all(parts, 'gy', 0, 0, tiled=True, axis_index_groups=groups)  4.02 us
    ppermute x6, waiting for transfers between devices, swap(): results.append(lax.ppermute(value, axis, pairs))  3.4 us
  transfers between devices with their start and end apart: 8, of which 3 were waited for; matrix products, arithmetic and copies ran while one was open for 0% of the time, Pallas kernels for 3%

profile of v10, /device:TPU:65, one launch (start us, length us, event | category | flops | bytes accessed | tf_op | source)
XLA Modules:
  0.0 63.6 jit_solution(16559064161863148445)
XLA Ops:
  0.0 2.2 %shard_map.64 = (f32[7,8,128]{2,1,0:T(8,128)S(1)}, f32[7,8,128]{2,1,0:T(8,128)S(1)}, f32[4,3,8,128]{3,2,1,0:T(8,128)}) custom-call(s32[1,1,4]{2,1,0:T(1,128)} %home_hbm.1, f32[8,32,128]{2,1,0:T(8,128)} %old_ref.1, f32[8,32,128]{2,1,0:T(8,128)} %conduct_ref.7, f32[8,32,128]{2,1,0:T(8,128)} %source_ref.1, f32[8,32,128]{2,1,0:T(8,128)} %reaction_ref.1, ...), custom_call_target="tpu_custom_call" | custom-call | tf_op jit(solution)/shard_map/pallas_call | solution.py:616
  2.2 4.0 %all-to-all-start = ((f32[4,3,8,128]{3,2,1,0:T(8,128)}), f32[4,3,8,128]{3,2,1,0:T(8,128)S(1)}, u32[]{:S(2)}, u32[]{:S(2)}) async-start(f32[4,3,8,128]{3,2,1,0:T(8,128)} %get-tuple-element.19), calls=%async_computation | async-start | bytes 98304 | tf_op jit(solution)/shard_map/all_to_all | solution.py:652
  6.2 2.9 %collective-permute-start = (f32[7,8,128]{2,1,0:T(8,128)S(1)}, f32[7,8,128]{2,1,0:T(8,128)S(1)}, u32[]{:S(2)}, u32[]{:S(2)}) collective-permute-start(f32[7,8,128]{2,1,0:T(8,128)S(1)} %get-tuple-element.20.refs_0_), channel_id=1, source_target_pairs={{0,1},{1,0},{2,3},{3,2},{4,5},{5,4},{6,7},{7,6},{8,9},{9,8},{10,11... | collective-permute-start | bytes 86024 | tf_op jit(solution)/shard_map/ppermute | solution.py:606
  9.1 18.1 %collective-permute-start.1 = (f32[7,8,128]{2,1,0:T(8,128)S(1)}, f32[7,8,128]{2,1,0:T(8,128)S(1)}, u32[]{:S(2)}, u32[]{:S(2)}) collective-permute-start(f32[7,8,128]{2,1,0:T(8,128)S(1)} %get-tuple-element.21), channel_id=1, source_target_pairs={{1,2},{2,1},{5,6},{6,5},{9,10},{10,9},{13,14},{14,13},{17,18},{18,... | collective-permute-start | bytes 86024 | tf_op jit(solution)/shard_map/ppermute | solution.py:606
  27.2 0.0 collective-permute-done.refs_1_.refs_6_.za_ref
  27.2 1.5 %collective-permute-done.1.refs_2_.refs_7_.zb_ref = f32[7,8,128]{2,1,0:T(8,128)S(1)} collective-permute-done((f32[7,8,128]{2,1,0:T(8,128)S(1)}, f32[7,8,128]{2,1,0:T(8,128)S(1)}, u32[]{:S(2)}, u32[]{:S(2)}) %collective-permute-start.1) | collective-permute-done | bytes 28704 | tf_op jit(solution)/shard_map/ppermute | solution.py:606
  28.7 0.0 all-to-all-done.refs_0_
  28.7 1.0 %shard_map.65 = f32[32,4,8,128]{3,2,1,0:T(8,128)} custom-call(f32[4,3,8,128]{3,2,1,0:T(8,128)S(1)} %all-to-all-done.refs_0_, f32[7,8,128]{2,1,0:T(8,128)S(1)} %collective-permute-done.refs_1_.refs_6_.za_ref, f32[7,8,128]{2,1,0:T(8,128)S(1)} %collective-permute-done.1.refs_2_.refs_7_.zb_ref), custom_call_target="tpu_custom_call" | custom-call | tf_op jit(solution)/shard_map/pallas_call | solution.py:616
  29.7 0.0 copy-start
  29.8 0.0 copy-start.1
  29.8 0.0 copy-start.2
  29.8 0.0 copy-start.3
  29.8 0.0 copy-start.4
  29.8 10.3 %all-to-all-start.1 = ((f32[32,4,8,128]{3,2,1,0:T(8,128)}), f32[32,4,8,128]{3,2,1,0:T(8,128)S(1)}, u32[]{:S(2)}, u32[]{:S(2)}) async-start(f32[32,4,8,128]{3,2,1,0:T(8,128)} %shard_map.65), calls=%async_computation.1 | async-start | bytes 1048576 | tf_op jit(solution)/shard_map/all_to_all | solution.py:658
  40.1 0.0 copy-done
  40.1 0.0 copy-done.1
  40.1 0.0 copy-done.2
  40.1 0.0 copy-done.3
  40.1 0.0 copy-done.4
  40.1 0.6 shard_map.66
  40.8 3.1 %collective-permute-start.2 = (f32[40,128]{1,0:T(8,128)S(1)}, f32[40,128]{1,0:T(8,128)S(1)}, u32[]{:S(2)}, u32[]{:S(2)}) collective-permute-start(f32[40,128]{1,0:T(8,128)S(1)} %get-tuple-element.22.after_ref.sya_ref), channel_id=1, source_target_pairs={{0,4},{4,0},{8,12},{12,8},{16,20},{20,16},{24,28},{28,24},{32,36},... | collective-permute-start | bytes 61448 | tf_op jit(solution)/shard_map/ppermute | solution.py:606
  43.9 0.7 %collective-permute-start.3 = (f32[40,128]{1,0:T(8,128)S(1)}, f32[40,128]{1,0:T(8,128)S(1)}, u32[]{:S(2)}, u32[]{:S(2)}) collective-permute-start(f32[40,128]{1,0:T(8,128)S(1)} %get-tuple-element.23.syb_ref), channel_id=1, source_target_pairs={{4,8},{8,4},{12,16},{16,12},{20,24},{24,20},{28,32},{32,28},{36,40... | collective-permute-start | bytes 61448 | tf_op jit(solution)/shard_map/ppermute | solution.py:606
  44.6 0.9 %shard_map.68 = (f32[8,32,128]{2,1,0:T(8,128)S(1)}, f32[8,32,128]{2,1,0:T(8,128)S(1)}) custom-call(f32[8,32,128]{2,1,0:T(8,128)S(1)} %copy-done, f32[8,32,128]{2,1,0:T(8,128)S(1)} %copy-done.1, f32[8,32,128]{2,1,0:T(8,128)S(1)} %copy-done.2, f32[4,16,64]{2,1,0:T(8,128)S(1)} %copy-done.4, f32[40,128]{1,0:T(8,128)S(1)} %get-tuple-element.22.after_ref.sya_ref), custom_call_target="tpu_custom_call" | custom-call | tf_op jit(solution)/shard_map/pallas_call | solution.py:616
  45.5 0.0 copy-start.5
  45.5 0.0 collective-permute-done.2.ya_ref
  45.6 0.0 collective-permute-done.3.yb_ref
  45.6 7.3 %all-to-all-done.1.recv_ref = f32[32,4,8,128]{3,2,1,0:T(8,128)S(1)} async-done(((f32[32,4,8,128]{3,2,1,0:T(8,128)}), f32[32,4,8,128]{3,2,1,0:T(8,128)S(1)}, u32[]{:S(2)}, u32[]{:S(2)}) %all-to-all-start.1) | async-done | bytes 524320 | tf_op jit(solution)/shard_map/all_to_all | solution.py:658
  52.9 0.0 copy-done.5
  52.9 0.9 %shard_map.67 = (f32[8,32,128]{2,1,0:T(8,128)S(1)}, f32[2,2,8,128]{3,2,1,0:T(8,128)S(1)}, f32[2,40,128]{2,1,0:T(8,128)S(1)}) custom-call(s32[4]{0:T(128)S(1)} %bitcast.1, f32[32,4,8,128]{3,2,1,0:T(8,128)S(1)} %all-to-all-done.1.recv_ref, f32[8,32,128]{2,1,0:T(8,128)S(1)} %copy-done.3, f32[7,8,128]{2,1,0:T(8,128)S(1)} %collective-permute-done.refs_1_.refs_6_.za_ref, ...), custom_call_target="tpu_custom_call" | custom-call | tf_op jit(solution)/shard_map/pallas_call | solution.py:616
  53.8 0.1 shard_map.69
  53.9 2.2 %collective-permute-start.4 = (f32[232,128]{1,0:T(8,128)S(1)}, f32[232,128]{1,0:T(8,128)S(1)}, u32[]{:S(2)}, u32[]{:S(2)}) collective-permute-start(f32[232,128]{1,0:T(8,128)S(1)} %get-tuple-element.29.after_ref), channel_id=1, source_target_pairs={{0,128},{128,0},{256,384},{384,256},{512,640},{640,512},{768,896},... | collective-permute-start | bytes 356360 | tf_op jit(solution)/shard_map/ppermute | solution.py:606
  56.1 4.0 %collective-permute-start.5 = (f32[232,128]{1,0:T(8,128)S(1)}, f32[232,128]{1,0:T(8,128)S(1)}, u32[]{:S(2)}, u32[]{:S(2)}) collective-permute-start(f32[232,128]{1,0:T(8,128)S(1)} %get-tuple-element.31), channel_id=1, source_target_pairs={{128,256},{256,128},{384,512},{512,384},{640,768},{768,640},{129,2... | collective-permute-start | bytes 356360 | tf_op jit(solution)/shard_map/ppermute | solution.py:606
  60.1 0.3 shard_map.70
  60.4 0.0 collective-permute-done.4.xa_ref
  60.5 1.9 %collective-permute-done.5.xb_ref = f32[232,128]{1,0:T(8,128)S(1)} collective-permute-done((f32[232,128]{1,0:T(8,128)S(1)}, f32[232,128]{1,0:T(8,128)S(1)}, u32[]{:S(2)}, u32[]{:S(2)}) %collective-permute-start.5) | collective-permute-done | bytes 118816 | tf_op jit(solution)/shard_map/ppermute | solution.py:606
  62.3 1.3 %shard_map.71 = f32[8,32,128]{2,1,0:T(8,128)} custom-call(f32[8,32,128]{2,1,0:T(8,128)S(1)} %get-tuple-element.24.start_ref, f32[8,32,128]{2,1,0:T(8,128)S(1)} %copy-done, f32[8,32,128]{2,1,0:T(8,128)S(1)} %get-tuple-element.25.src_ref, f32[8,32,128]{2,1,0:T(8,128)S(1)} %get-tuple-element.26.rea_ref, f32[2,2,8,128]{3,2,1,0:T(8,128)S(1)} %get-tuple-element.27.zhalo_ref, ...), custom_call_target="tpu_custom_call" | custom-call | tf_op jit(solution)/shard_map/pallas_call | solution.py:616
Async XLA Ops:
  2.2 26.5 %all-to-all-start = ((f32[4,3,8,128]{3,2,1,0:T(8,128)}), f32[4,3,8,128]{3,2,1,0:T(8,128)S(1)}, u32[]{:S(2)}, u32[]{:S(2)}) async-start(f32[4,3,8,128]{3,2,1,0:T(8,128)} %get-tuple-element.19), calls=%async_computation | async-start | bytes 98304 | tf_op jit(solution)/shard_map/all_to_all | solution.py:652
  6.2 20.9 %collective-permute-start = (f32[7,8,128]{2,1,0:T(8,128)S(1)}, f32[7,8,128]{2,1,0:T(8,128)S(1)}, u32[]{:S(2)}, u32[]{:S(2)}) collective-permute-start(f32[7,8,128]{2,1,0:T(8,128)S(1)} %get-tuple-element.20.refs_0_), channel_id=1, source_target_pairs={{0,1},{1,0},{2,3},{3,2},{4,5},{5,4},{6,7},{7,6},{8,9},{9,8},{10,11... | collective-permute-start | bytes 86024 | tf_op jit(solution)/shard_map/ppermute | solution.py:606
  9.1 19.6 %collective-permute-start.1 = (f32[7,8,128]{2,1,0:T(8,128)S(1)}, f32[7,8,128]{2,1,0:T(8,128)S(1)}, u32[]{:S(2)}, u32[]{:S(2)}) collective-permute-start(f32[7,8,128]{2,1,0:T(8,128)S(1)} %get-tuple-element.21), channel_id=1, source_target_pairs={{1,2},{2,1},{5,6},{6,5},{9,10},{10,9},{13,14},{14,13},{17,18},{18,... | collective-permute-start | bytes 86024 | tf_op jit(solution)/shard_map/ppermute | solution.py:606
  29.7 10.4 %copy-start = (f32[8,32,128]{2,1,0:T(8,128)S(1)}, f32[8,32,128]{2,1,0:T(8,128)}, u32[]{:S(2)}) copy-start(f32[8,32,128]{2,1,0:T(8,128)} %conduct_ref.7) | copy-start | bytes 393220
  29.8 10.4 %copy-start.1 = (f32[8,32,128]{2,1,0:T(8,128)S(1)}, f32[8,32,128]{2,1,0:T(8,128)}, u32[]{:S(2)}) copy-start(f32[8,32,128]{2,1,0:T(8,128)} %source_ref.1) | copy-start | bytes 393220
  29.8 10.4 %copy-start.2 = (f32[8,32,128]{2,1,0:T(8,128)S(1)}, f32[8,32,128]{2,1,0:T(8,128)}, u32[]{:S(2)}) copy-start(f32[8,32,128]{2,1,0:T(8,128)} %reaction_ref.1) | copy-start | bytes 393220
  29.8 10.4 %copy-start.3 = (f32[8,32,128]{2,1,0:T(8,128)S(1)}, f32[8,32,128]{2,1,0:T(8,128)}, u32[]{:S(2)}) copy-start(f32[8,32,128]{2,1,0:T(8,128)} %old_ref.1) | copy-start | bytes 393220
  29.8 10.4 %copy-start.4 = (f32[4,16,64]{2,1,0:T(8,128)S(1)}, f32[4,16,64]{2,1,0:T(8,128)}, u32[]{:S(2)}) copy-start(f32[4,16,64]{2,1,0:T(8,128)} %coarse_ref.1) | copy-start | bytes 49156
  29.8 23.1 %all-to-all-start.1 = ((f32[32,4,8,128]{3,2,1,0:T(8,128)}), f32[32,4,8,128]{3,2,1,0:T(8,128)S(1)}, u32[]{:S(2)}, u32[]{:S(2)}) async-start(f32[32,4,8,128]{3,2,1,0:T(8,128)} %shard_map.65), calls=%async_computation.1 | async-start | bytes 1048576 | tf_op jit(solution)/shard_map/all_to_all | solution.py:658
  40.8 4.8 %collective-permute-start.2 = (f32[40,128]{1,0:T(8,128)S(1)}, f32[40,128]{1,0:T(8,128)S(1)}, u32[]{:S(2)}, u32[]{:S(2)}) collective-permute-start(f32[40,128]{1,0:T(8,128)S(1)} %get-tuple-element.22.after_ref.sya_ref), channel_id=1, source_target_pairs={{0,4},{4,0},{8,12},{12,8},{16,20},{20,16},{24,28},{28,24},{32,36},... | collective-permute-start | bytes 61448 | tf_op jit(solution)/shard_map/ppermute | solution.py:606
  43.9 1.6 %collective-permute-start.3 = (f32[40,128]{1,0:T(8,128)S(1)}, f32[40,128]{1,0:T(8,128)S(1)}, u32[]{:S(2)}, u32[]{:S(2)}) collective-permute-start(f32[40,128]{1,0:T(8,128)S(1)} %get-tuple-element.23.syb_ref), channel_id=1, source_target_pairs={{4,8},{8,4},{12,16},{16,12},{20,24},{24,20},{28,32},{32,28},{36,40... | collective-permute-start | bytes 61448 | tf_op jit(solution)/shard_map/ppermute | solution.py:606
  45.5 7.4 %copy-start.5 = (s32[1,1,4]{2,1,0:T(1,128)S(1)}, s32[1,1,4]{2,1,0:T(1,128)}, u32[]{:S(2)}) copy-start(s32[1,1,4]{2,1,0:T(1,128)} %home_hbm.1) | copy-start | bytes 52
  53.9 6.6 %collective-permute-start.4 = (f32[232,128]{1,0:T(8,128)S(1)}, f32[232,128]{1,0:T(8,128)S(1)}, u32[]{:S(2)}, u32[]{:S(2)}) collective-permute-start(f32[232,128]{1,0:T(8,128)S(1)} %get-tuple-element.29.after_ref), channel_id=1, source_target_pairs={{0,128},{128,0},{256,384},{384,256},{512,640},{640,512},{768,896},... | collective-permute-start | bytes 356360 | tf_op jit(solution)/shard_map/ppermute | solution.py:606
  56.1 6.2 %collective-permute-start.5 = (f32[232,128]{1,0:T(8,128)S(1)}, f32[232,128]{1,0:T(8,128)S(1)}, u32[]{:S(2)}, u32[]{:S(2)}) collective-permute-start(f32[232,128]{1,0:T(8,128)S(1)} %get-tuple-element.31), channel_id=1, source_target_pairs={{128,256},{256,128},{384,512},{512,384},{640,768},{768,640},{129,2... | collective-permute-start | bytes 356360 | tf_op jit(solution)/shard_map/ppermute | solution.py:606

commit v11 on v10

--- a/solution.py
+++ b/solution.py
@@ -6,7 +6,7 @@
 from jax.sharding import PartitionSpec as P
 
 LANES = 128
-RUN = 4
+RUN = 8
 VMEM = pl.BlockSpec(memory_space=pltpu.VMEM)
 SMEM = pl.BlockSpec(memory_space=pltpu.SMEM)
 HBM = pl.BlockSpec(memory_space=pltpu.HBM)
@@ -90,8 +90,8 @@
 
 def first_kernel(
     home_hbm, old_hbm, conduct_hbm, source_hbm, reaction_hbm, coarse_hbm,
-    za_ref, zb_ref, parts_ref, home_ref, old_ref, rows_ref, coarse_ref,
-    home_sem, old_sems, sems, coarse_sem,
+    za_ref, zb_ref, parts_hbm, parts_ref, home_ref, old_ref, rows_ref, coarse_ref,
+    home_sem, old_sems, sems, coarse_sem, part_sems,
 ):
     slots = home_ref.shape[2]
     width = LANES // slots
@@ -124,7 +124,8 @@
         + ((lane == LANES - 1) & y_last).astype(F32)
     )
     rows = nz // slots
-    count, planes = parts_ref.shape[0], parts_ref.shape[1] - 1
+    planes = parts_ref.shape[1] - 1
+    stores = []
     group = lax.div(lane_of((rows, LANES)), width)
     for x in range(nx):
         loads[x].wait()
@@ -133,9 +134,12 @@
             shift = lax.rem(width * (g - slot) + LANES, LANES)
             rolled = pltpu.roll(old_ref[x, g * rows : (g + 1) * rows, :], shift, 1)
             box = jnp.where(group == g, rolled, box)
-        parts_ref[x // planes, x % planes] = box
-    for k in range(count):
-        parts_ref[k, planes] = jnp.full((rows, LANES), device, jnp.int32).astype(F32)
+        k = x // planes
+        parts_ref[k, x % planes] = box
+        if x % planes == planes - 1:
+            parts_ref[k, planes] = jnp.full((rows, LANES), device, jnp.int32).astype(F32)
+            stores.append(pltpu.make_async_copy(parts_ref.at[k], parts_hbm.at[k], part_sems.at[k]))
+            stores[k].start()
     for copy in copies:
         copy.wait()
     cx, cz, cy = coarse_ref.shape
@@ -161,6 +165,8 @@
         faces.append([old, old2, kappa, kappa2, src, rea, rims(old, old2)])
     for i in range(7):
         write_pair("gz", za_ref, zb_ref, i, faces[0][i], faces[1][i])
+    for store in stores:
+        store.wait()
 
 
 def columns_kernel(
@@ -607,7 +613,7 @@
     return results[::-1]
 
 
-def call(kernel, operands, outs, smem=0, hbm=(), scratch=()):
+def call(kernel, operands, outs, smem=0, hbm=(), hbm_outs=(), scratch=()):
     specs = [SMEM] * smem + [VMEM] * (len(operands) - smem)
     operands = list(operands)
     for i in hbm:
@@ -617,7 +623,7 @@
         kernel,
         out_shape=[jax.ShapeDtypeStruct(shape, F32) for shape in outs],
         in_specs=specs,
-        out_specs=[VMEM] * len(outs),
+        out_specs=[HBM if i in hbm_outs else VMEM for i in range(len(outs))],
         scratch_shapes=scratch,
         compiler_params=PARAMS,
     )(*operands)
@@ -636,7 +642,9 @@
         (new_home, old_field, conduct, source, reaction, coarse),
         [(7, nx, ny), (7, nx, ny), (RUN, part + 1, rows, ny)],
         hbm=(0, 1, 2, 3, 4, 5),
+        hbm_outs=(2,),
         scratch=[
+            pltpu.VMEM((RUN, part + 1, rows, ny), F32),
             pltpu.SMEM(new_home.shape, jnp.int32),
             pltpu.VMEM(block, F32),
             pltpu.VMEM((3, 2, nx, 8, ny), F32),
@@ -645,6 +653,7 @@
             pltpu.SemaphoreType.DMA((nx,)),
             pltpu.SemaphoreType.DMA((3, 2)),
             pltpu.SemaphoreType.DMA,
+            pltpu.SemaphoreType.DMA((RUN,)),
         ],
     )
     za, zb = swap("gz", sza, szb)

time: 64.2 us -> 62.9 us (0.980)
  waiting for transfers between devices: 10.7 us -> 9.39 us
    all_to_all x1, waiting for transfers between devices: 7.32 us -> 5.99 us  [on_device(): recv = lax.all_to_all(send, 'gy', 0, 0, tiled=True)]
    all_to_all x1, starting transfers between devices: 4.02 us -> 5.04 us  [on_device(): lax.all_to_all(parts, 'gy', 0, 0, tiled=True, axis_index_groups=groups)]
    all_to_all x1, starting transfers between devices: 10.3 us -> 9.42 us  [on_device(): recv = lax.all_to_all(send, 'gy', 0, 0, tiled=True)]
where the time goes in v11:
time: 62.9 us; the launch traced here: 62.5 us
  starting transfers between devices  45.4 us (72%)
  waiting for transfers between devices  9.39 us (15%)
  Pallas kernels  7.48 us (12%)
    ppermute x6, starting transfers between devices, swap(): results.append(lax.ppermute(value, axis, pairs))  30.9 us
    all_to_all x1, starting transfers between devices, on_device(): recv = lax.all_to_all(send, 'gy', 0, 0, tiled=True)  9.42 us
    pallas_call x8, Pallas kernels, call(): pl.pallas_call(kernel, out_shape=[jax.ShapeDtypeStruct(shape, F32) for sh...  7.48 us
    all_to_all x1, waiting for transfers between devices, on_device(): recv = lax.all_to_all(send, 'gy', 0, 0, tiled=True)  5.99 us
    all_to_all x1, starting transfers between devices, on_device(): lax.all_to_all(parts, 'gy', 0, 0, tiled=True, axis_index_groups=groups)  5.04 us
    ppermute x6, waiting for transfers between devices, swap(): results.append(lax.ppermute(value, axis, pairs))  3.4 us
  transfers between devices with their start and end apart: 8, of which 3 were waited for; matrix products, arithmetic and copies ran while one was open for 0% of the time, Pallas kernels for 3%

profile of v11, /device:TPU:65, one launch (start us, length us, event | category | flops | bytes accessed | tf_op | source)
XLA Modules:
  0.0 62.5 jit_solution(976900694043747463)
XLA Ops:
  0.0 2.2 %shard_map.64 = (f32[7,8,128]{2,1,0:T(8,128)S(1)}, f32[7,8,128]{2,1,0:T(8,128)S(1)}, f32[8,2,8,128]{3,2,1,0:T(8,128)}) custom-call(s32[1,1,4]{2,1,0:T(1,128)} %home_hbm.1, f32[8,32,128]{2,1,0:T(8,128)} %old_ref.1, f32[8,32,128]{2,1,0:T(8,128)} %conduct_ref.7, f32[8,32,128]{2,1,0:T(8,128)} %source_ref.1, f32[8,32,128]{2,1,0:T(8,128)} %reaction_ref.1, ...), custom_call_target="tpu_custom_call" | custom-call | tf_op jit(solution)/shard_map/pallas_call | solution.py:622
  2.2 5.0 %all-to-all-start = ((f32[8,2,8,128]{3,2,1,0:T(8,128)}), f32[8,2,8,128]{3,2,1,0:T(8,128)S(1)}, u32[]{:S(2)}, u32[]{:S(2)}) async-start(f32[8,2,8,128]{3,2,1,0:T(8,128)} %get-tuple-element.19), calls=%async_computation | async-start | bytes 131072 | tf_op jit(solution)/shard_map/all_to_all | solution.py:661
  7.3 2.9 %collective-permute-start = (f32[7,8,128]{2,1,0:T(8,128)S(1)}, f32[7,8,128]{2,1,0:T(8,128)S(1)}, u32[]{:S(2)}, u32[]{:S(2)}) collective-permute-start(f32[7,8,128]{2,1,0:T(8,128)S(1)} %get-tuple-element.20.refs_0_), channel_id=1, source_target_pairs={{0,1},{1,0},{2,3},{3,2},{4,5},{5,4},{6,7},{7,6},{8,9},{9,8},{10,11... | collective-permute-start | bytes 86024 | tf_op jit(solution)/shard_map/ppermute | solution.py:612
  10.1 18.1 %collective-permute-start.1 = (f32[7,8,128]{2,1,0:T(8,128)S(1)}, f32[7,8,128]{2,1,0:T(8,128)S(1)}, u32[]{:S(2)}, u32[]{:S(2)}) collective-permute-start(f32[7,8,128]{2,1,0:T(8,128)S(1)} %get-tuple-element.21), channel_id=1, source_target_pairs={{1,2},{2,1},{5,6},{6,5},{9,10},{10,9},{13,14},{14,13},{17,18},{18,... | collective-permute-start | bytes 86024 | tf_op jit(solution)/shard_map/ppermute | solution.py:612
  28.2 0.0 collective-permute-done.refs_1_.refs_6_.za_ref
  28.2 1.5 %collective-permute-done.1.refs_2_.refs_7_.zb_ref = f32[7,8,128]{2,1,0:T(8,128)S(1)} collective-permute-done((f32[7,8,128]{2,1,0:T(8,128)S(1)}, f32[7,8,128]{2,1,0:T(8,128)S(1)}, u32[]{:S(2)}, u32[]{:S(2)}) %collective-permute-start.1) | collective-permute-done | bytes 28704 | tf_op jit(solution)/shard_map/ppermute | solution.py:612
  29.8 0.0 all-to-all-done.refs_0_
  29.8 1.0 %shard_map.65 = f32[32,3,8,128]{3,2,1,0:T(8,128)} custom-call(f32[8,2,8,128]{3,2,1,0:T(8,128)S(1)} %all-to-all-done.refs_0_, f32[7,8,128]{2,1,0:T(8,128)S(1)} %collective-permute-done.refs_1_.refs_6_.za_ref, f32[7,8,128]{2,1,0:T(8,128)S(1)} %collective-permute-done.1.refs_2_.refs_7_.zb_ref), custom_call_target="tpu_custom_call" | custom-call | tf_op jit(solution)/shard_map/pallas_call | solution.py:622
  30.8 0.0 copy-start
  30.8 0.0 copy-start.1
  30.8 0.0 copy-start.2
  30.8 0.0 copy-start.3
  30.8 0.0 copy-start.4
  30.8 9.4 %all-to-all-start.1 = ((f32[32,3,8,128]{3,2,1,0:T(8,128)}), f32[32,3,8,128]{3,2,1,0:T(8,128)S(1)}, u32[]{:S(2)}, u32[]{:S(2)}) async-start(f32[32,3,8,128]{3,2,1,0:T(8,128)} %shard_map.65), calls=%async_computation.1 | async-start | bytes 786432 | tf_op jit(solution)/shard_map/all_to_all | solution.py:667
  40.2 0.0 copy-done
  40.2 0.0 copy-done.1
  40.2 0.0 copy-done.2
  40.2 0.0 copy-done.3
  40.2 0.0 copy-done.4
  40.3 0.6 shard_map.66
  40.9 3.1 %collective-permute-start.2 = (f32[40,128]{1,0:T(8,128)S(1)}, f32[40,128]{1,0:T(8,128)S(1)}, u32[]{:S(2)}, u32[]{:S(2)}) collective-permute-start(f32[40,128]{1,0:T(8,128)S(1)} %get-tuple-element.22.after_ref.sya_ref), channel_id=1, source_target_pairs={{0,4},{4,0},{8,12},{12,8},{16,20},{20,16},{24,28},{28,24},{32,36},... | collective-permute-start | bytes 61448 | tf_op jit(solution)/shard_map/ppermute | solution.py:612
  44.0 0.7 %collective-permute-start.3 = (f32[40,128]{1,0:T(8,128)S(1)}, f32[40,128]{1,0:T(8,128)S(1)}, u32[]{:S(2)}, u32[]{:S(2)}) collective-permute-start(f32[40,128]{1,0:T(8,128)S(1)} %get-tuple-element.23.syb_ref), channel_id=1, source_target_pairs={{4,8},{8,4},{12,16},{16,12},{20,24},{24,20},{28,32},{32,28},{36,40... | collective-permute-start | bytes 61448 | tf_op jit(solution)/shard_map/ppermute | solution.py:612
  44.7 0.9 %shard_map.68 = (f32[8,32,128]{2,1,0:T(8,128)S(1)}, f32[8,32,128]{2,1,0:T(8,128)S(1)}) custom-call(f32[8,32,128]{2,1,0:T(8,128)S(1)} %copy-done, f32[8,32,128]{2,1,0:T(8,128)S(1)} %copy-done.1, f32[8,32,128]{2,1,0:T(8,128)S(1)} %copy-done.2, f32[4,16,64]{2,1,0:T(8,128)S(1)} %copy-done.4, f32[40,128]{1,0:T(8,128)S(1)} %get-tuple-element.22.after_ref.sya_ref), custom_call_target="tpu_custom_call" | custom-call | tf_op jit(solution)/shard_map/pallas_call | solution.py:622
  45.6 0.0 copy-start.5
  45.6 0.0 collective-permute-done.2.ya_ref
  45.7 0.0 collective-permute-done.3.yb_ref
  45.7 6.0 %all-to-all-done.1.recv_ref = f32[32,3,8,128]{3,2,1,0:T(8,128)S(1)} async-done(((f32[32,3,8,128]{3,2,1,0:T(8,128)}), f32[32,3,8,128]{3,2,1,0:T(8,128)S(1)}, u32[]{:S(2)}, u32[]{:S(2)}) %all-to-all-start.1) | async-done | bytes 393248 | tf_op jit(solution)/shard_map/all_to_all | solution.py:667
  51.7 0.0 copy-done.5
  51.7 0.9 %shard_map.67 = (f32[8,32,128]{2,1,0:T(8,128)S(1)}, f32[2,2,8,128]{3,2,1,0:T(8,128)S(1)}, f32[2,40,128]{2,1,0:T(8,128)S(1)}) custom-call(s32[4]{0:T(128)S(1)} %bitcast.1, f32[32,3,8,128]{3,2,1,0:T(8,128)S(1)} %all-to-all-done.1.recv_ref, f32[8,32,128]{2,1,0:T(8,128)S(1)} %copy-done.3, f32[7,8,128]{2,1,0:T(8,128)S(1)} %collective-permute-done.refs_1_.refs_6_.za_ref, ...), custom_call_target="tpu_custom_call" | custom-call | tf_op jit(solution)/shard_map/pallas_call | solution.py:622
  52.6 0.1 shard_map.69
  52.7 2.7 %collective-permute-start.4 = (f32[232,128]{1,0:T(8,128)S(1)}, f32[232,128]{1,0:T(8,128)S(1)}, u32[]{:S(2)}, u32[]{:S(2)}) collective-permute-start(f32[232,128]{1,0:T(8,128)S(1)} %get-tuple-element.29.after_ref), channel_id=1, source_target_pairs={{0,128},{128,0},{256,384},{384,256},{512,640},{640,512},{768,896},... | collective-permute-start | bytes 356360 | tf_op jit(solution)/shard_map/ppermute | solution.py:612
  55.4 3.5 %collective-permute-start.5 = (f32[232,128]{1,0:T(8,128)S(1)}, f32[232,128]{1,0:T(8,128)S(1)}, u32[]{:S(2)}, u32[]{:S(2)}) collective-permute-start(f32[232,128]{1,0:T(8,128)S(1)} %get-tuple-element.31), channel_id=1, source_target_pairs={{128,256},{256,128},{384,512},{512,384},{640,768},{768,640},{129,2... | collective-permute-start | bytes 356360 | tf_op jit(solution)/shard_map/ppermute | solution.py:612
  58.9 0.3 shard_map.70
  59.3 0.0 collective-permute-done.4.xa_ref
  59.3 1.9 %collective-permute-done.5.xb_ref = f32[232,128]{1,0:T(8,128)S(1)} collective-permute-done((f32[232,128]{1,0:T(8,128)S(1)}, f32[232,128]{1,0:T(8,128)S(1)}, u32[]{:S(2)}, u32[]{:S(2)}) %collective-permute-start.5) | collective-permute-done | bytes 118816 | tf_op jit(solution)/shard_map/ppermute | solution.py:612
  61.1 1.3 %shard_map.71 = f32[8,32,128]{2,1,0:T(8,128)} custom-call(f32[8,32,128]{2,1,0:T(8,128)S(1)} %get-tuple-element.24.start_ref, f32[8,32,128]{2,1,0:T(8,128)S(1)} %copy-done, f32[8,32,128]{2,1,0:T(8,128)S(1)} %get-tuple-element.25.src_ref, f32[8,32,128]{2,1,0:T(8,128)S(1)} %get-tuple-element.26.rea_ref, f32[2,2,8,128]{3,2,1,0:T(8,128)S(1)} %get-tuple-element.27.zhalo_ref, ...), custom_call_target="tpu_custom_call" | custom-call | tf_op jit(solution)/shard_map/pallas_call | solution.py:622
Async XLA Ops:
  2.2 27.5 %all-to-all-start = ((f32[8,2,8,128]{3,2,1,0:T(8,128)}), f32[8,2,8,128]{3,2,1,0:T(8,128)S(1)}, u32[]{:S(2)}, u32[]{:S(2)}) async-start(f32[8,2,8,128]{3,2,1,0:T(8,128)} %get-tuple-element.19), calls=%async_computation | async-start | bytes 131072 | tf_op jit(solution)/shard_map/all_to_all | solution.py:661
  7.3 20.9 %collective-permute-start = (f32[7,8,128]{2,1,0:T(8,128)S(1)}, f32[7,8,128]{2,1,0:T(8,128)S(1)}, u32[]{:S(2)}, u32[]{:S(2)}) collective-permute-start(f32[7,8,128]{2,1,0:T(8,128)S(1)} %get-tuple-element.20.refs_0_), channel_id=1, source_target_pairs={{0,1},{1,0},{2,3},{3,2},{4,5},{5,4},{6,7},{7,6},{8,9},{9,8},{10,11... | collective-permute-start | bytes 86024 | tf_op jit(solution)/shard_map/ppermute | solution.py:612
  10.1 19.6 %collective-permute-start.1 = (f32[7,8,128]{2,1,0:T(8,128)S(1)}, f32[7,8,128]{2,1,0:T(8,128)S(1)}, u32[]{:S(2)}, u32[]{:S(2)}) collective-permute-start(f32[7,8,128]{2,1,0:T(8,128)S(1)} %get-tuple-element.21), channel_id=1, source_target_pairs={{1,2},{2,1},{5,6},{6,5},{9,10},{10,9},{13,14},{14,13},{17,18},{18,... | collective-permute-start | bytes 86024 | tf_op jit(solution)/shard_map/ppermute | solution.py:612
  30.8 9.5 %copy-start = (f32[8,32,128]{2,1,0:T(8,128)S(1)}, f32[8,32,128]{2,1,0:T(8,128)}, u32[]{:S(2)}) copy-start(f32[8,32,128]{2,1,0:T(8,128)} %conduct_ref.7) | copy-start | bytes 393220
  30.8 9.5 %copy-start.1 = (f32[8,32,128]{2,1,0:T(8,128)S(1)}, f32[8,32,128]{2,1,0:T(8,128)}, u32[]{:S(2)}) copy-start(f32[8,32,128]{2,1,0:T(8,128)} %source_ref.1) | copy-start | bytes 393220
  30.8 9.5 %copy-start.2 = (f32[8,32,128]{2,1,0:T(8,128)S(1)}, f32[8,32,128]{2,1,0:T(8,128)}, u32[]{:S(2)}) copy-start(f32[8,32,128]{2,1,0:T(8,128)} %reaction_ref.1) | copy-start | bytes 393220
  30.8 9.5 %copy-start.3 = (f32[8,32,128]{2,1,0:T(8,128)S(1)}, f32[8,32,128]{2,1,0:T(8,128)}, u32[]{:S(2)}) copy-start(f32[8,32,128]{2,1,0:T(8,128)} %old_ref.1) | copy-start | bytes 393220
  30.8 9.5 %copy-start.4 = (f32[4,16,64]{2,1,0:T(8,128)S(1)}, f32[4,16,64]{2,1,0:T(8,128)}, u32[]{:S(2)}) copy-start(f32[4,16,64]{2,1,0:T(8,128)} %coarse_ref.1) | copy-start | bytes 49156
  30.8 20.9 %all-to-all-start.1 = ((f32[32,3,8,128]{3,2,1,0:T(8,128)}), f32[32,3,8,128]{3,2,1,0:T(8,128)S(1)}, u32[]{:S(2)}, u32[]{:S(2)}) async-start(f32[32,3,8,128]{3,2,1,0:T(8,128)} %shard_map.65), calls=%async_computation.1 | async-start | bytes 786432 | tf_op jit(solution)/shard_map/all_to_all | solution.py:667
  40.9 4.8 %collective-permute-start.2 = (f32[40,128]{1,0:T(8,128)S(1)}, f32[40,128]{1,0:T(8,128)S(1)}, u32[]{:S(2)}, u32[]{:S(2)}) collective-permute-start(f32[40,128]{1,0:T(8,128)S(1)} %get-tuple-element.22.after_ref.sya_ref), channel_id=1, source_target_pairs={{0,4},{4,0},{8,12},{12,8},{16,20},{20,16},{24,28},{28,24},{32,36},... | collective-permute-start | bytes 61448 | tf_op jit(solution)/shard_map/ppermute | solution.py:612
  44.0 1.6 %collective-permute-start.3 = (f32[40,128]{1,0:T(8,128)S(1)}, f32[40,128]{1,0:T(8,128)S(1)}, u32[]{:S(2)}, u32[]{:S(2)}) collective-permute-start(f32[40,128]{1,0:T(8,128)S(1)} %get-tuple-element.23.syb_ref), channel_id=1, source_target_pairs={{4,8},{8,4},{12,16},{16,12},{20,24},{24,20},{28,32},{32,28},{36,40... | collective-permute-start | bytes 61448 | tf_op jit(solution)/shard_map/ppermute | solution.py:612
  45.6 6.0 %copy-start.5 = (s32[1,1,4]{2,1,0:T(1,128)S(1)}, s32[1,1,4]{2,1,0:T(1,128)}, u32[]{:S(2)}) copy-start(s32[1,1,4]{2,1,0:T(1,128)} %home_hbm.1) | copy-start | bytes 52
  52.7 6.6 %collective-permute-start.4 = (f32[232,128]{1,0:T(8,128)S(1)}, f32[232,128]{1,0:T(8,128)S(1)}, u32[]{:S(2)}, u32[]{:S(2)}) collective-permute-start(f32[232,128]{1,0:T(8,128)S(1)} %get-tuple-element.29.after_ref), channel_id=1, source_target_pairs={{0,128},{128,0},{256,384},{384,256},{512,640},{640,512},{768,896},... | collective-permute-start | bytes 356360 | tf_op jit(solution)/shard_map/ppermute | solution.py:612
  55.4 5.7 %collective-permute-start.5 = (f32[232,128]{1,0:T(8,128)S(1)}, f32[232,128]{1,0:T(8,128)S(1)}, u32[]{:S(2)}, u32[]{:S(2)}) collective-permute-start(f32[232,128]{1,0:T(8,128)S(1)} %get-tuple-element.31), channel_id=1, source_target_pairs={{128,256},{256,128},{384,512},{512,384},{640,768},{768,640},{129,2... | collective-permute-start | bytes 356360 | tf_op jit(solution)/shard_map/ppermute | solution.py:612

commit v12 on v11

--- a/solution.py
+++ b/solution.py
@@ -14,6 +14,7 @@
 F32 = jnp.float32
 
 PHI1, PHI2, KAP1, KAP2, SRC, REA, RIM = range(7)
+XPHI, XKAP, XNUM, XDEN = range(4)
 
 
 def lane_of(shape):
@@ -373,13 +374,21 @@
     xa_ref, xb_ref,
 ):
     nx, nz, _ = start_ref.shape
-    for f, (ref, depth) in enumerate(
-        ((start_ref, 0), (start_ref, 1), (conduct_ref, 0), (conduct_ref, 1), (src_ref, 0), (rea_ref, 0))
-    ):
-        write_pair(
-            "gx", xa_ref, xb_ref, slice(f * nz, (f + 1) * nz), ref[depth], ref[nx - 1 - depth]
+    _, flags_z, flags_y = edges()
+    z_kappa = received("gz", za_ref[KAP1], zb_ref[KAP1])
+    z_phi = (zhalo_ref[0, 0], zhalo_ref[1, 0])
+    yf = [yhalo_ref[side, :nz] for side in range(2)]
+    faces = []
+    for me, inner in ((0, 1), (nx - 1, nx - 2)):
+        sides = plane_sides(
+            me, start_ref[me], conduct_ref[me], [(start_ref[inner], conduct_ref[inner], None)],
+            z_phi, z_kappa, yf, yf, flags_z, flags_y,
         )
-    base = 6 * nz
+        sums = gather(start_ref[me] + src_ref[me], rea_ref[me], conduct_ref[me], sides)
+        faces.append((start_ref[me], conduct_ref[me], *sums))
+    for f in range(4):
+        write_pair("gx", xa_ref, xb_ref, slice(f * nz, (f + 1) * nz), faces[0][f], faces[1][f])
+    base = 4 * nz
     kappas = received("gz", za_ref[KAP1], zb_ref[KAP1])
     xa_ref[base : base + 8] = jnp.zeros((8, LANES), F32)
     xb_ref[base : base + 8] = jnp.zeros((8, LANES), F32)
@@ -400,13 +409,18 @@
     write_pair("gx", xa_ref, xb_ref, slice(base + 8, base + 8 + nz), low, high)
 
 
-def step(numerator, denominator, kappa, sides):
+def gather(numerator, denominator, kappa, sides):
     for phi, beside, outside in sides:
         weight = 0.5 * (kappa + beside)
         if outside is not None:
             weight = jnp.where(outside, 0.0, weight)
         numerator = numerator + weight * phi
         denominator = denominator + weight
+    return numerator, denominator
+
+
+def step(numerator, denominator, kappa, sides):
+    numerator, denominator = gather(numerator, denominator, kappa, sides)
     return numerator / denominator
 
 
@@ -452,7 +466,7 @@
     )
 
 
-def sweep_plane(x, phi, kappa, numerator, denominator, sides, z_phi, z_kappa, y_phi, y_kappa, flags_z, flags_y):
+def plane_sides(x, phi, kappa, sides, z_phi, z_kappa, y_phi, y_kappa, flags_z, flags_y):
     sides = sides + along_rows(
         phi,
         kappa,
@@ -468,7 +482,7 @@
         (roll_lanes(y_phi[1], LANES - 1 - x), roll_lanes(y_kappa[1], LANES - 1 - spot)),
         flags_y,
     )
-    return step(numerator, denominator, kappa, sides)
+    return sides
 
 
 def inner_kernel(
@@ -485,10 +499,10 @@
     first_ref[nx - 1] = start_ref[nx - 1]
     for x in range(1, nx - 1):
         sides = [(start_ref[i], conduct_ref[i], None) for i in (x - 1, x + 1)]
-        first_ref[x] = sweep_plane(
-            x, start_ref[x], conduct_ref[x], start_ref[x] + src_ref[x], rea_ref[x],
-            sides, z_phi, z_kappa, yf, yf, flags_z, flags_y,
+        sides = plane_sides(
+            x, start_ref[x], conduct_ref[x], sides, z_phi, z_kappa, yf, yf, flags_z, flags_y
         )
+        first_ref[x] = step(start_ref[x] + src_ref[x], rea_ref[x], conduct_ref[x], sides)
 
     lane = lane_of((nz, LANES))
     low = high = jnp.zeros((nz, LANES), F32)
@@ -501,19 +515,22 @@
 
 def sweeps_kernel(
     start_ref, conduct_ref, src_ref, rea_ref, zhalo_ref, yhalo_ref, own_ref,
-    za_ref, zb_ref, sya_ref, syb_ref, xa_ref, xb_ref, first_ref,
+    za_ref, zb_ref, sya_ref, syb_ref, sxa_ref, sxb_ref, xa_ref, xb_ref, first_ref,
     out_ref,
 ):
     nx, nz, _ = start_ref.shape
     flags_x, flags_z, flags_y = edges()
     start = [start_ref[x] for x in range(nx)]
     conduct = [conduct_ref[x] for x in range(nx)]
-    base = 6 * nz
+    base = 4 * nz
 
     def part(axis, a_ref, b_ref, begin, size):
         return received(axis, a_ref[begin : begin + size], b_ref[begin : begin + size])
 
-    xf = [part("gx", xa_ref, xb_ref, f * nz, nz) for f in range(6)]
+    xf = [part("gx", xa_ref, xb_ref, f * nz, nz) for f in range(4)]
+    num, den = [
+        sent("gx", sxa_ref[f * nz : (f + 1) * nz], sxb_ref[f * nz : (f + 1) * nz]) for f in (XNUM, XDEN)
+    ]
     xrows = part("gx", xa_ref, xb_ref, base, 8)
     xcols = part("gx", xa_ref, xb_ref, base + 8, nz)
     zf = [received("gz", za_ref[i], zb_ref[i]) for i in range(6)]
@@ -524,18 +541,13 @@
     def columns(tile, phi_spot, kappa_spot, lane):
         return roll_lanes(tile, lane - phi_spot), roll_lanes(tile, lane - kappa_spot)
 
-    x_first_sweep = []
-    for side in range(2):
-        phi, kappa = xf[PHI1][side], xf[KAP1][side]
-        me = 0 if side == 0 else nx - 1
-        rows = xrows[side]
-        sides = [(xf[PHI2][side], xf[KAP2][side], None), (start[me], conduct[me], None)]
-        sides += along_rows(phi, kappa, (rows[0:1], rows[1:2]), (rows[2:3], rows[3:4]), flags_z)
-        tile = xcols[side]
-        sides += along_lanes(
-            phi, kappa, columns(tile, 0, 1, 0), columns(tile, 2, 3, LANES - 1), flags_y
-        )
-        x_first_sweep.append(step(phi + xf[SRC][side], xf[REA][side], kappa, sides))
+    x_first_sweep, ends = [], []
+    for side, me in ((0, 0), (1, nx - 1)):
+        kappa = xf[XKAP][side]
+        sides = [(start[me], conduct[me], None)]
+        x_first_sweep.append(step(xf[XNUM][side], xf[XDEN][side], kappa, sides))
+        sides = [(xf[XPHI][side], kappa, flags_x[side])]
+        ends.append(step(num[side], den[side], conduct[me], sides))
 
     z_first_sweep = []
     for side in range(2):
@@ -584,22 +596,20 @@
         )
         y_first_sweep.append(step(phi + src, rea, kappa, sides))
 
-    def sweep(phis, x_phi, z_phi, y_phi, planes):
-        below = [(x_phi[0], xf[KAP1][0], flags_x[0])] + [(phis[x], conduct[x], None) for x in range(nx - 1)]
-        above = [(phis[x], conduct[x], None) for x in range(1, nx)] + [(x_phi[1], xf[KAP1][1], flags_x[1])]
-        return [
-            sweep_plane(
-                x, phis[x], conduct[x], start[x] + src_ref[x], rea_ref[x],
-                [below[x], above[x]], z_phi, zf[KAP1], y_phi, yf, flags_z, flags_y,
-            )
-            for x in planes
-        ]
-
-    ends = sweep(start, xf[PHI1], (zhalo_ref[0, 0], zhalo_ref[1, 0]), yf, (0, nx - 1))
     first = [ends[0]] + [first_ref[x] for x in range(1, nx - 1)] + [ends[1]]
-    second = sweep(first, x_first_sweep, z_first_sweep, y_first_sweep, range(nx))
     for x in range(nx):
-        out_ref[x] = second[x]
+        below = (first[x - 1], conduct[x - 1], None)
+        if x == 0:
+            below = (x_first_sweep[0], xf[XKAP][0], flags_x[0])
+        if x == nx - 1:
+            above = (x_first_sweep[1], xf[XKAP][1], flags_x[1])
+        else:
+            above = (first[x + 1], conduct[x + 1], None)
+        sides = plane_sides(
+            x, first[x], conduct[x], [below, above],
+            z_first_sweep, zf[KAP1], y_first_sweep, yf, flags_z, flags_y,
+        )
+        out_ref[x] = step(start[x] + src_ref[x], rea_ref[x], conduct[x], sides)
 
 
 def swap(axis, first, second):
@@ -680,20 +690,20 @@
         [block, (2, 2, nx, ny), (2, nz + nx, ny)],
         smem=1,
     )
-    xa, xb = call(
+    sxa, sxb = call(
         edge_kernel,
         (start, conduct, src, rea, zhalo, yhalo, za, zb),
-        [(7 * nz + 8, ny)] * 2,
+        [(5 * nz + 8, ny)] * 2,
     )
     first, own = call(
         inner_kernel,
-        (start, conduct, src, rea, zhalo, yhalo, za, zb, xa),
+        (start, conduct, src, rea, zhalo, yhalo, za, zb, sxa),
         [block, (2, nz, ny)],
     )
-    xa, xb = swap("gx", xa, xb)
+    xa, xb = swap("gx", sxa, sxb)
     (relaxed,) = call(
         sweeps_kernel,
-        (start, conduct, src, rea, zhalo, yhalo, own, za, zb, sya, syb, xa, xb, first),
+        (start, conduct, src, rea, zhalo, yhalo, own, za, zb, sya, syb, sxa, sxb, xa, xb, first),
         [block],
     )
     return relaxed

time: 62.9 us -> 62.6 us (level)
  no operation moved by 1% of the time
where the time goes in v12:
time: 62.6 us; the launch traced here: 62.1 us
  starting transfers between devices  45.4 us (73%)
  waiting for transfers between devices  9.04 us (14%)
  Pallas kernels  7.47 us (12%)
    ppermute x6, starting transfers between devices, swap(): results.append(lax.ppermute(value, axis, pairs))  30.9 us
    all_to_all x1, starting transfers between devices, on_device(): recv = lax.all_to_all(send, 'gy', 0, 0, tiled=True)  9.42 us
    pallas_call x8, Pallas kernels, call(): pl.pallas_call(kernel, out_shape=[jax.ShapeDtypeStruct(shape, F32) for sh...  7.47 us
    all_to_all x1, waiting for transfers between devices, on_device(): recv = lax.all_to_all(send, 'gy', 0, 0, tiled=True)  5.99 us
    all_to_all x1, starting transfers between devices, on_device(): lax.all_to_all(parts, 'gy', 0, 0, tiled=True, axis_index_groups=groups)  5.04 us
    ppermute x6, waiting for transfers between devices, swap(): results.append(lax.ppermute(value, axis, pairs))  3.05 us
  transfers between devices with their start and end apart: 8, of which 3 were waited for; matrix products, arithmetic and copies ran while one was open for 0% of the time, Pallas kernels for 3%

profile of v12, /device:TPU:65, one launch (start us, length us, event | category | flops | bytes accessed | tf_op | source)
XLA Modules:
  0.0 62.1 jit_solution(13596148779981911251)
XLA Ops:
  0.0 2.2 %shard_map.64 = (f32[7,8,128]{2,1,0:T(8,128)S(1)}, f32[7,8,128]{2,1,0:T(8,128)S(1)}, f32[8,2,8,128]{3,2,1,0:T(8,128)}) custom-call(s32[1,1,4]{2,1,0:T(1,128)} %home_hbm.1, f32[8,32,128]{2,1,0:T(8,128)} %old_ref.1, f32[8,32,128]{2,1,0:T(8,128)} %conduct_ref.7, f32[8,32,128]{2,1,0:T(8,128)} %source_ref.1, f32[8,32,128]{2,1,0:T(8,128)} %reaction_ref.1, ...), custom_call_target="tpu_custom_call" | custom-call | tf_op jit(solution)/shard_map/pallas_call | solution.py:632
  2.2 5.0 %all-to-all-start = ((f32[8,2,8,128]{3,2,1,0:T(8,128)}), f32[8,2,8,128]{3,2,1,0:T(8,128)S(1)}, u32[]{:S(2)}, u32[]{:S(2)}) async-start(f32[8,2,8,128]{3,2,1,0:T(8,128)} %get-tuple-element.19), calls=%async_computation | async-start | bytes 131072 | tf_op jit(solution)/shard_map/all_to_all | solution.py:671
  7.3 2.9 %collective-permute-start = (f32[7,8,128]{2,1,0:T(8,128)S(1)}, f32[7,8,128]{2,1,0:T(8,128)S(1)}, u32[]{:S(2)}, u32[]{:S(2)}) collective-permute-start(f32[7,8,128]{2,1,0:T(8,128)S(1)} %get-tuple-element.20.refs_0_), channel_id=1, source_target_pairs={{0,1},{1,0},{2,3},{3,2},{4,5},{5,4},{6,7},{7,6},{8,9},{9,8},{10,11... | collective-permute-start | bytes 86024 | tf_op jit(solution)/shard_map/ppermute | solution.py:622
  10.1 18.1 %collective-permute-start.1 = (f32[7,8,128]{2,1,0:T(8,128)S(1)}, f32[7,8,128]{2,1,0:T(8,128)S(1)}, u32[]{:S(2)}, u32[]{:S(2)}) collective-permute-start(f32[7,8,128]{2,1,0:T(8,128)S(1)} %get-tuple-element.21), channel_id=1, source_target_pairs={{1,2},{2,1},{5,6},{6,5},{9,10},{10,9},{13,14},{14,13},{17,18},{18,... | collective-permute-start | bytes 86024 | tf_op jit(solution)/shard_map/ppermute | solution.py:622
  28.2 0.0 collective-permute-done.refs_1_.refs_6_.za_ref
  28.2 1.5 %collective-permute-done.1.refs_2_.refs_7_.zb_ref = f32[7,8,128]{2,1,0:T(8,128)S(1)} collective-permute-done((f32[7,8,128]{2,1,0:T(8,128)S(1)}, f32[7,8,128]{2,1,0:T(8,128)S(1)}, u32[]{:S(2)}, u32[]{:S(2)}) %collective-permute-start.1) | collective-permute-done | bytes 28704 | tf_op jit(solution)/shard_map/ppermute | solution.py:622
  29.8 0.0 all-to-all-done.refs_0_
  29.8 1.0 %shard_map.65 = f32[32,3,8,128]{3,2,1,0:T(8,128)} custom-call(f32[8,2,8,128]{3,2,1,0:T(8,128)S(1)} %all-to-all-done.refs_0_, f32[7,8,128]{2,1,0:T(8,128)S(1)} %collective-permute-done.refs_1_.refs_6_.za_ref, f32[7,8,128]{2,1,0:T(8,128)S(1)} %collective-permute-done.1.refs_2_.refs_7_.zb_ref), custom_call_target="tpu_custom_call" | custom-call | tf_op jit(solution)/shard_map/pallas_call | solution.py:632
  30.8 0.0 copy-start
  30.8 0.0 copy-start.1
  30.8 0.0 copy-start.2
  30.8 0.0 copy-start.3
  30.8 0.0 copy-start.4
  30.8 9.4 %all-to-all-start.1 = ((f32[32,3,8,128]{3,2,1,0:T(8,128)}), f32[32,3,8,128]{3,2,1,0:T(8,128)S(1)}, u32[]{:S(2)}, u32[]{:S(2)}) async-start(f32[32,3,8,128]{3,2,1,0:T(8,128)} %shard_map.65), calls=%async_computation.1 | async-start | bytes 786432 | tf_op jit(solution)/shard_map/all_to_all | solution.py:677
  40.2 0.0 copy-done
  40.2 0.0 copy-done.1
  40.2 0.0 copy-done.2
  40.2 0.0 copy-done.3
  40.2 0.0 copy-done.4
  40.3 0.6 shard_map.66
  40.9 3.1 %collective-permute-start.2 = (f32[40,128]{1,0:T(8,128)S(1)}, f32[40,128]{1,0:T(8,128)S(1)}, u32[]{:S(2)}, u32[]{:S(2)}) collective-permute-start(f32[40,128]{1,0:T(8,128)S(1)} %get-tuple-element.22.after_ref.sya_ref), channel_id=1, source_target_pairs={{0,4},{4,0},{8,12},{12,8},{16,20},{20,16},{24,28},{28,24},{32,36},... | collective-permute-start | bytes 61448 | tf_op jit(solution)/shard_map/ppermute | solution.py:622
  44.0 0.7 %collective-permute-start.3 = (f32[40,128]{1,0:T(8,128)S(1)}, f32[40,128]{1,0:T(8,128)S(1)}, u32[]{:S(2)}, u32[]{:S(2)}) collective-permute-start(f32[40,128]{1,0:T(8,128)S(1)} %get-tuple-element.23.syb_ref), channel_id=1, source_target_pairs={{4,8},{8,4},{12,16},{16,12},{20,24},{24,20},{28,32},{32,28},{36,40... | collective-permute-start | bytes 61448 | tf_op jit(solution)/shard_map/ppermute | solution.py:622
  44.7 0.9 %shard_map.68 = (f32[8,32,128]{2,1,0:T(8,128)S(1)}, f32[8,32,128]{2,1,0:T(8,128)S(1)}) custom-call(f32[8,32,128]{2,1,0:T(8,128)S(1)} %copy-done, f32[8,32,128]{2,1,0:T(8,128)S(1)} %copy-done.1, f32[8,32,128]{2,1,0:T(8,128)S(1)} %copy-done.2, f32[4,16,64]{2,1,0:T(8,128)S(1)} %copy-done.4, f32[40,128]{1,0:T(8,128)S(1)} %get-tuple-element.22.after_ref.sya_ref), custom_call_target="tpu_custom_call" | custom-call | tf_op jit(solution)/shard_map/pallas_call | solution.py:632
  45.6 0.0 copy-start.5
  45.6 0.0 collective-permute-done.2.ya_ref
  45.7 0.0 collective-permute-done.3.yb_ref
  45.7 6.0 %all-to-all-done.1.recv_ref = f32[32,3,8,128]{3,2,1,0:T(8,128)S(1)} async-done(((f32[32,3,8,128]{3,2,1,0:T(8,128)}), f32[32,3,8,128]{3,2,1,0:T(8,128)S(1)}, u32[]{:S(2)}, u32[]{:S(2)}) %all-to-all-start.1) | async-done | bytes 393248 | tf_op jit(solution)/shard_map/all_to_all | solution.py:677
  51.7 0.0 copy-done.5
  51.7 0.9 %shard_map.67 = (f32[8,32,128]{2,1,0:T(8,128)S(1)}, f32[2,2,8,128]{3,2,1,0:T(8,128)S(1)}, f32[2,40,128]{2,1,0:T(8,128)S(1)}) custom-call(s32[4]{0:T(128)S(1)} %bitcast.1, f32[32,3,8,128]{3,2,1,0:T(8,128)S(1)} %all-to-all-done.1.recv_ref, f32[8,32,128]{2,1,0:T(8,128)S(1)} %copy-done.3, f32[7,8,128]{2,1,0:T(8,128)S(1)} %collective-permute-done.refs_1_.refs_6_.za_ref, ...), custom_call_target="tpu_custom_call" | custom-call | tf_op jit(solution)/shard_map/pallas_call | solution.py:632
  52.6 0.2 shard_map.69
  52.8 2.7 %collective-permute-start.4 = (f32[168,128]{1,0:T(8,128)S(1)}, f32[168,128]{1,0:T(8,128)S(1)}, u32[]{:S(2)}, u32[]{:S(2)}) collective-permute-start(f32[168,128]{1,0:T(8,128)S(1)} %get-tuple-element.29.after_ref.sxa_ref), channel_id=1, source_target_pairs={{0,128},{128,0},{256,384},{384,256},{512,640},{640,512},{768,896},... | collective-permute-start | bytes 258056 | tf_op jit(solution)/shard_map/ppermute | solution.py:622
  55.5 3.5 %collective-permute-start.5 = (f32[168,128]{1,0:T(8,128)S(1)}, f32[168,128]{1,0:T(8,128)S(1)}, u32[]{:S(2)}, u32[]{:S(2)}) collective-permute-start(f32[168,128]{1,0:T(8,128)S(1)} %get-tuple-element.31.sxb_ref), channel_id=1, source_target_pairs={{128,256},{256,128},{384,512},{512,384},{640,768},{768,640},{129,2... | collective-permute-start | bytes 258056 | tf_op jit(solution)/shard_map/ppermute | solution.py:622
  59.0 0.3 shard_map.70
  59.3 0.0 collective-permute-done.4.xa_ref
  59.3 1.5 %collective-permute-done.5.xb_ref = f32[168,128]{1,0:T(8,128)S(1)} collective-permute-done((f32[168,128]{1,0:T(8,128)S(1)}, f32[168,128]{1,0:T(8,128)S(1)}, u32[]{:S(2)}, u32[]{:S(2)}) %collective-permute-start.5) | collective-permute-done | bytes 86048 | tf_op jit(solution)/shard_map/ppermute | solution.py:622
  60.8 1.3 %shard_map.71 = f32[8,32,128]{2,1,0:T(8,128)} custom-call(f32[8,32,128]{2,1,0:T(8,128)S(1)} %get-tuple-element.24.start_ref, f32[8,32,128]{2,1,0:T(8,128)S(1)} %copy-done, f32[8,32,128]{2,1,0:T(8,128)S(1)} %get-tuple-element.25.src_ref, f32[8,32,128]{2,1,0:T(8,128)S(1)} %get-tuple-element.26.rea_ref, f32[2,2,8,128]{3,2,1,0:T(8,128)S(1)} %get-tuple-element.27.zhalo_ref, ...), custom_call_target="tpu_custom_call" | custom-call | tf_op jit(solution)/shard_map/pallas_call | solution.py:632
Async XLA Ops:
  2.2 27.5 %all-to-all-start = ((f32[8,2,8,128]{3,2,1,0:T(8,128)}), f32[8,2,8,128]{3,2,1,0:T(8,128)S(1)}, u32[]{:S(2)}, u32[]{:S(2)}) async-start(f32[8,2,8,128]{3,2,1,0:T(8,128)} %get-tuple-element.19), calls=%async_computation | async-start | bytes 131072 | tf_op jit(solution)/shard_map/all_to_all | solution.py:671
  7.3 20.9 %collective-permute-start = (f32[7,8,128]{2,1,0:T(8,128)S(1)}, f32[7,8,128]{2,1,0:T(8,128)S(1)}, u32[]{:S(2)}, u32[]{:S(2)}) collective-permute-start(f32[7,8,128]{2,1,0:T(8,128)S(1)} %get-tuple-element.20.refs_0_), channel_id=1, source_target_pairs={{0,1},{1,0},{2,3},{3,2},{4,5},{5,4},{6,7},{7,6},{8,9},{9,8},{10,11... | collective-permute-start | bytes 86024 | tf_op jit(solution)/shard_map/ppermute | solution.py:622
  10.1 19.6 %collective-permute-start.1 = (f32[7,8,128]{2,1,0:T(8,128)S(1)}, f32[7,8,128]{2,1,0:T(8,128)S(1)}, u32[]{:S(2)}, u32[]{:S(2)}) collective-permute-start(f32[7,8,128]{2,1,0:T(8,128)S(1)} %get-tuple-element.21), channel_id=1, source_target_pairs={{1,2},{2,1},{5,6},{6,5},{9,10},{10,9},{13,14},{14,13},{17,18},{18,... | collective-permute-start | bytes 86024 | tf_op jit(solution)/shard_map/ppermute | solution.py:622
  30.8 9.5 %copy-start = (f32[8,32,128]{2,1,0:T(8,128)S(1)}, f32[8,32,128]{2,1,0:T(8,128)}, u32[]{:S(2)}) copy-start(f32[8,32,128]{2,1,0:T(8,128)} %conduct_ref.7) | copy-start | bytes 393220
  30.8 9.5 %copy-start.1 = (f32[8,32,128]{2,1,0:T(8,128)S(1)}, f32[8,32,128]{2,1,0:T(8,128)}, u32[]{:S(2)}) copy-start(f32[8,32,128]{2,1,0:T(8,128)} %source_ref.1) | copy-start | bytes 393220
  30.8 9.5 %copy-start.2 = (f32[8,32,128]{2,1,0:T(8,128)S(1)}, f32[8,32,128]{2,1,0:T(8,128)}, u32[]{:S(2)}) copy-start(f32[8,32,128]{2,1,0:T(8,128)} %reaction_ref.1) | copy-start | bytes 393220
  30.8 9.5 %copy-start.3 = (f32[8,32,128]{2,1,0:T(8,128)S(1)}, f32[8,32,128]{2,1,0:T(8,128)}, u32[]{:S(2)}) copy-start(f32[8,32,128]{2,1,0:T(8,128)} %old_ref.1) | copy-start | bytes 393220
  30.8 9.5 %copy-start.4 = (f32[4,16,64]{2,1,0:T(8,128)S(1)}, f32[4,16,64]{2,1,0:T(8,128)}, u32[]{:S(2)}) copy-start(f32[4,16,64]{2,1,0:T(8,128)} %coarse_ref.1) | copy-start | bytes 49156
  30.8 20.9 %all-to-all-start.1 = ((f32[32,3,8,128]{3,2,1,0:T(8,128)}), f32[32,3,8,128]{3,2,1,0:T(8,128)S(1)}, u32[]{:S(2)}, u32[]{:S(2)}) async-start(f32[32,3,8,128]{3,2,1,0:T(8,128)} %shard_map.65), calls=%async_computation.1 | async-start | bytes 786432 | tf_op jit(solution)/shard_map/all_to_all | solution.py:677
  40.9 4.8 %collective-permute-start.2 = (f32[40,128]{1,0:T(8,128)S(1)}, f32[40,128]{1,0:T(8,128)S(1)}, u32[]{:S(2)}, u32[]{:S(2)}) collective-permute-start(f32[40,128]{1,0:T(8,128)S(1)} %get-tuple-element.22.after_ref.sya_ref), channel_id=1, source_target_pairs={{0,4},{4,0},{8,12},{12,8},{16,20},{20,16},{24,28},{28,24},{32,36},... | collective-permute-start | bytes 61448 | tf_op jit(solution)/shard_map/ppermute | solution.py:622
  44.0 1.6 %collective-permute-start.3 = (f32[40,128]{1,0:T(8,128)S(1)}, f32[40,128]{1,0:T(8,128)S(1)}, u32[]{:S(2)}, u32[]{:S(2)}) collective-permute-start(f32[40,128]{1,0:T(8,128)S(1)} %get-tuple-element.23.syb_ref), channel_id=1, source_target_pairs={{4,8},{8,4},{12,16},{16,12},{20,24},{24,20},{28,32},{32,28},{36,40... | collective-permute-start | bytes 61448 | tf_op jit(solution)/shard_map/ppermute | solution.py:622
  45.6 6.0 %copy-start.5 = (s32[1,1,4]{2,1,0:T(1,128)S(1)}, s32[1,1,4]{2,1,0:T(1,128)}, u32[]{:S(2)}) copy-start(s32[1,1,4]{2,1,0:T(1,128)} %home_hbm.1) | copy-start | bytes 52
  52.8 6.6 %collective-permute-start.4 = (f32[168,128]{1,0:T(8,128)S(1)}, f32[168,128]{1,0:T(8,128)S(1)}, u32[]{:S(2)}, u32[]{:S(2)}) collective-permute-start(f32[168,128]{1,0:T(8,128)S(1)} %get-tuple-element.29.after_ref.sxa_ref), channel_id=1, source_target_pairs={{0,128},{128,0},{256,384},{384,256},{512,640},{640,512},{768,896},... | collective-permute-start | bytes 258056 | tf_op jit(solution)/shard_map/ppermute | solution.py:622
  55.5 5.3 %collective-permute-start.5 = (f32[168,128]{1,0:T(8,128)S(1)}, f32[168,128]{1,0:T(8,128)S(1)}, u32[]{:S(2)}, u32[]{:S(2)}) collective-permute-start(f32[168,128]{1,0:T(8,128)S(1)} %get-tuple-element.31.sxb_ref), channel_id=1, source_target_pairs={{128,256},{256,128},{384,512},{512,384},{640,768},{768,640},{129,2... | collective-permute-start | bytes 258056 | tf_op jit(solution)/shard_map/ppermute | solution.py:622

commit v13 on v12

--- a/solution.py
+++ b/solution.py
@@ -657,7 +657,7 @@
             pltpu.VMEM((RUN, part + 1, rows, ny), F32),
             pltpu.SMEM(new_home.shape, jnp.int32),
             pltpu.VMEM(block, F32),
-            pltpu.VMEM((3, 2, nx, 8, ny), F32),
+            pltpu.VMEM((3, 2, nx, 2, ny), F32),
             pltpu.VMEM(coarse.shape, F32),
             pltpu.SemaphoreType.DMA,
             pltpu.SemaphoreType.DMA((nx,)),

time: 62.6 us -> 62.6 us (level)
  no operation moved by 1% of the time
where the time goes in v13:
time: 62.6 us; the launch traced here: 62.1 us
  starting transfers between devices  45.4 us (73%)
  waiting for transfers between devices  9.04 us (14%)
  Pallas kernels  7.47 us (12%)
    ppermute x6, starting transfers between devices, swap(): results.append(lax.ppermute(value, axis, pairs))  30.9 us
    all_to_all x1, starting transfers between devices, on_device(): recv = lax.all_to_all(send, 'gy', 0, 0, tiled=True)  9.42 us
    pallas_call x8, Pallas kernels, call(): pl.pallas_call(kernel, out_shape=[jax.ShapeDtypeStruct(shape, F32) for sh...  7.47 us
    all_to_all x1, waiting for transfers between devices, on_device(): recv = lax.all_to_all(send, 'gy', 0, 0, tiled=True)  5.99 us
    all_to_all x1, starting transfers between devices, on_device(): lax.all_to_all(parts, 'gy', 0, 0, tiled=True, axis_index_groups=groups)  5.04 us
    ppermute x6, waiting for transfers between devices, swap(): results.append(lax.ppermute(value, axis, pairs))  3.05 us
  transfers between devices with their start and end apart: 8, of which 3 were waited for; matrix products, arithmetic and copies ran while one was open for 0% of the time, Pallas kernels for 3%

profile of v13, /device:TPU:65, one launch (start us, length us, event | category | flops | bytes accessed | tf_op | source)
XLA Modules:
  0.0 62.1 jit_solution(12386290525438441807)
XLA Ops:
  0.0 2.2 %shard_map.64 = (f32[7,8,128]{2,1,0:T(8,128)S(1)}, f32[7,8,128]{2,1,0:T(8,128)S(1)}, f32[8,2,8,128]{3,2,1,0:T(8,128)}) custom-call(s32[1,1,4]{2,1,0:T(1,128)} %home_hbm.1, f32[8,32,128]{2,1,0:T(8,128)} %old_ref.1, f32[8,32,128]{2,1,0:T(8,128)} %conduct_ref.7, f32[8,32,128]{2,1,0:T(8,128)} %source_ref.1, f32[8,32,128]{2,1,0:T(8,128)} %reaction_ref.1, ...), custom_call_target="tpu_custom_call" | custom-call | tf_op jit(solution)/shard_map/pallas_call | solution.py:632
  2.2 5.0 %all-to-all-start = ((f32[8,2,8,128]{3,2,1,0:T(8,128)}), f32[8,2,8,128]{3,2,1,0:T(8,128)S(1)}, u32[]{:S(2)}, u32[]{:S(2)}) async-start(f32[8,2,8,128]{3,2,1,0:T(8,128)} %get-tuple-element.19), calls=%async_computation | async-start | bytes 131072 | tf_op jit(solution)/shard_map/all_to_all | solution.py:671
  7.3 2.9 %collective-permute-start = (f32[7,8,128]{2,1,0:T(8,128)S(1)}, f32[7,8,128]{2,1,0:T(8,128)S(1)}, u32[]{:S(2)}, u32[]{:S(2)}) collective-permute-start(f32[7,8,128]{2,1,0:T(8,128)S(1)} %get-tuple-element.20.refs_0_), channel_id=1, source_target_pairs={{0,1},{1,0},{2,3},{3,2},{4,5},{5,4},{6,7},{7,6},{8,9},{9,8},{10,11... | collective-permute-start | bytes 86024 | tf_op jit(solution)/shard_map/ppermute | solution.py:622
  10.1 18.1 %collective-permute-start.1 = (f32[7,8,128]{2,1,0:T(8,128)S(1)}, f32[7,8,128]{2,1,0:T(8,128)S(1)}, u32[]{:S(2)}, u32[]{:S(2)}) collective-permute-start(f32[7,8,128]{2,1,0:T(8,128)S(1)} %get-tuple-element.21), channel_id=1, source_target_pairs={{1,2},{2,1},{5,6},{6,5},{9,10},{10,9},{13,14},{14,13},{17,18},{18,... | collective-permute-start | bytes 86024 | tf_op jit(solution)/shard_map/ppermute | solution.py:622
  28.2 0.0 collective-permute-done.refs_1_.refs_6_.za_ref
  28.2 1.5 %collective-permute-done.1.refs_2_.refs_7_.zb_ref = f32[7,8,128]{2,1,0:T(8,128)S(1)} collective-permute-done((f32[7,8,128]{2,1,0:T(8,128)S(1)}, f32[7,8,128]{2,1,0:T(8,128)S(1)}, u32[]{:S(2)}, u32[]{:S(2)}) %collective-permute-start.1) | collective-permute-done | bytes 28704 | tf_op jit(solution)/shard_map/ppermute | solution.py:622
  29.8 0.0 all-to-all-done.refs_0_
  29.8 1.0 %shard_map.65 = f32[32,3,8,128]{3,2,1,0:T(8,128)} custom-call(f32[8,2,8,128]{3,2,1,0:T(8,128)S(1)} %all-to-all-done.refs_0_, f32[7,8,128]{2,1,0:T(8,128)S(1)} %collective-permute-done.refs_1_.refs_6_.za_ref, f32[7,8,128]{2,1,0:T(8,128)S(1)} %collective-permute-done.1.refs_2_.refs_7_.zb_ref), custom_call_target="tpu_custom_call" | custom-call | tf_op jit(solution)/shard_map/pallas_call | solution.py:632
  30.8 0.0 copy-start
  30.8 0.0 copy-start.1
  30.8 0.0 copy-start.2
  30.8 0.0 copy-start.3
  30.8 0.0 copy-start.4
  30.8 9.4 %all-to-all-start.1 = ((f32[32,3,8,128]{3,2,1,0:T(8,128)}), f32[32,3,8,128]{3,2,1,0:T(8,128)S(1)}, u32[]{:S(2)}, u32[]{:S(2)}) async-start(f32[32,3,8,128]{3,2,1,0:T(8,128)} %shard_map.65), calls=%async_computation.1 | async-start | bytes 786432 | tf_op jit(solution)/shard_map/all_to_all | solution.py:677
  40.2 0.0 copy-done
  40.2 0.0 copy-done.1
  40.2 0.0 copy-done.2
  40.2 0.0 copy-done.3
  40.2 0.0 copy-done.4
  40.3 0.6 shard_map.66
  40.9 3.1 %collective-permute-start.2 = (f32[40,128]{1,0:T(8,128)S(1)}, f32[40,128]{1,0:T(8,128)S(1)}, u32[]{:S(2)}, u32[]{:S(2)}) collective-permute-start(f32[40,128]{1,0:T(8,128)S(1)} %get-tuple-element.22.after_ref.sya_ref), channel_id=1, source_target_pairs={{0,4},{4,0},{8,12},{12,8},{16,20},{20,16},{24,28},{28,24},{32,36},... | collective-permute-start | bytes 61448 | tf_op jit(solution)/shard_map/ppermute | solution.py:622
  44.0 0.7 %collective-permute-start.3 = (f32[40,128]{1,0:T(8,128)S(1)}, f32[40,128]{1,0:T(8,128)S(1)}, u32[]{:S(2)}, u32[]{:S(2)}) collective-permute-start(f32[40,128]{1,0:T(8,128)S(1)} %get-tuple-element.23.syb_ref), channel_id=1, source_target_pairs={{4,8},{8,4},{12,16},{16,12},{20,24},{24,20},{28,32},{32,28},{36,40... | collective-permute-start | bytes 61448 | tf_op jit(solution)/shard_map/ppermute | solution.py:622
  44.7 0.9 %shard_map.68 = (f32[8,32,128]{2,1,0:T(8,128)S(1)}, f32[8,32,128]{2,1,0:T(8,128)S(1)}) custom-call(f32[8,32,128]{2,1,0:T(8,128)S(1)} %copy-done, f32[8,32,128]{2,1,0:T(8,128)S(1)} %copy-done.1, f32[8,32,128]{2,1,0:T(8,128)S(1)} %copy-done.2, f32[4,16,64]{2,1,0:T(8,128)S(1)} %copy-done.4, f32[40,128]{1,0:T(8,128)S(1)} %get-tuple-element.22.after_ref.sya_ref), custom_call_target="tpu_custom_call" | custom-call | tf_op jit(solution)/shard_map/pallas_call | solution.py:632
  45.6 0.0 copy-start.5
  45.6 0.0 collective-permute-done.2.ya_ref
  45.7 0.0 collective-permute-done.3.yb_ref
  45.7 6.0 %all-to-all-done.1.recv_ref = f32[32,3,8,128]{3,2,1,0:T(8,128)S(1)} async-done(((f32[32,3,8,128]{3,2,1,0:T(8,128)}), f32[32,3,8,128]{3,2,1,0:T(8,128)S(1)}, u32[]{:S(2)}, u32[]{:S(2)}) %all-to-all-start.1) | async-done | bytes 393248 | tf_op jit(solution)/shard_map/all_to_all | solution.py:677
  51.7 0.0 copy-done.5
  51.7 0.9 %shard_map.67 = (f32[8,32,128]{2,1,0:T(8,128)S(1)}, f32[2,2,8,128]{3,2,1,0:T(8,128)S(1)}, f32[2,40,128]{2,1,0:T(8,128)S(1)}) custom-call(s32[4]{0:T(128)S(1)} %bitcast.1, f32[32,3,8,128]{3,2,1,0:T(8,128)S(1)} %all-to-all-done.1.recv_ref, f32[8,32,128]{2,1,0:T(8,128)S(1)} %copy-done.3, f32[7,8,128]{2,1,0:T(8,128)S(1)} %collective-permute-done.refs_1_.refs_6_.za_ref, ...), custom_call_target="tpu_custom_call" | custom-call | tf_op jit(solution)/shard_map/pallas_call | solution.py:632
  52.6 0.2 shard_map.69
  52.8 2.7 %collective-permute-start.4 = (f32[168,128]{1,0:T(8,128)S(1)}, f32[168,128]{1,0:T(8,128)S(1)}, u32[]{:S(2)}, u32[]{:S(2)}) collective-permute-start(f32[168,128]{1,0:T(8,128)S(1)} %get-tuple-element.29.after_ref.sxa_ref), channel_id=1, source_target_pairs={{0,128},{128,0},{256,384},{384,256},{512,640},{640,512},{768,896},... | collective-permute-start | bytes 258056 | tf_op jit(solution)/shard_map/ppermute | solution.py:622
  55.5 3.5 %collective-permute-start.5 = (f32[168,128]{1,0:T(8,128)S(1)}, f32[168,128]{1,0:T(8,128)S(1)}, u32[]{:S(2)}, u32[]{:S(2)}) collective-permute-start(f32[168,128]{1,0:T(8,128)S(1)} %get-tuple-element.31.sxb_ref), channel_id=1, source_target_pairs={{128,256},{256,128},{384,512},{512,384},{640,768},{768,640},{129,2... | collective-permute-start | bytes 258056 | tf_op jit(solution)/shard_map/ppermute | solution.py:622
  59.0 0.3 shard_map.70
  59.3 0.0 collective-permute-done.4.xa_ref
  59.3 1.5 %collective-permute-done.5.xb_ref = f32[168,128]{1,0:T(8,128)S(1)} collective-permute-done((f32[168,128]{1,0:T(8,128)S(1)}, f32[168,128]{1,0:T(8,128)S(1)}, u32[]{:S(2)}, u32[]{:S(2)}) %collective-permute-start.5) | collective-permute-done | bytes 86048 | tf_op jit(solution)/shard_map/ppermute | solution.py:622
  60.8 1.3 %shard_map.71 = f32[8,32,128]{2,1,0:T(8,128)} custom-call(f32[8,32,128]{2,1,0:T(8,128)S(1)} %get-tuple-element.24.start_ref, f32[8,32,128]{2,1,0:T(8,128)S(1)} %copy-done, f32[8,32,128]{2,1,0:T(8,128)S(1)} %get-tuple-element.25.src_ref, f32[8,32,128]{2,1,0:T(8,128)S(1)} %get-tuple-element.26.rea_ref, f32[2,2,8,128]{3,2,1,0:T(8,128)S(1)} %get-tuple-element.27.zhalo_ref, ...), custom_call_target="tpu_custom_call" | custom-call | tf_op jit(solution)/shard_map/pallas_call | solution.py:632
Async XLA Ops:
  2.2 27.5 %all-to-all-start = ((f32[8,2,8,128]{3,2,1,0:T(8,128)}), f32[8,2,8,128]{3,2,1,0:T(8,128)S(1)}, u32[]{:S(2)}, u32[]{:S(2)}) async-start(f32[8,2,8,128]{3,2,1,0:T(8,128)} %get-tuple-element.19), calls=%async_computation | async-start | bytes 131072 | tf_op jit(solution)/shard_map/all_to_all | solution.py:671
  7.3 20.9 %collective-permute-start = (f32[7,8,128]{2,1,0:T(8,128)S(1)}, f32[7,8,128]{2,1,0:T(8,128)S(1)}, u32[]{:S(2)}, u32[]{:S(2)}) collective-permute-start(f32[7,8,128]{2,1,0:T(8,128)S(1)} %get-tuple-element.20.refs_0_), channel_id=1, source_target_pairs={{0,1},{1,0},{2,3},{3,2},{4,5},{5,4},{6,7},{7,6},{8,9},{9,8},{10,11... | collective-permute-start | bytes 86024 | tf_op jit(solution)/shard_map/ppermute | solution.py:622
  10.1 19.6 %collective-permute-start.1 = (f32[7,8,128]{2,1,0:T(8,128)S(1)}, f32[7,8,128]{2,1,0:T(8,128)S(1)}, u32[]{:S(2)}, u32[]{:S(2)}) collective-permute-start(f32[7,8,128]{2,1,0:T(8,128)S(1)} %get-tuple-element.21), channel_id=1, source_target_pairs={{1,2},{2,1},{5,6},{6,5},{9,10},{10,9},{13,14},{14,13},{17,18},{18,... | collective-permute-start | bytes 86024 | tf_op jit(solution)/shard_map/ppermute | solution.py:622
  30.8 9.5 %copy-start = (f32[8,32,128]{2,1,0:T(8,128)S(1)}, f32[8,32,128]{2,1,0:T(8,128)}, u32[]{:S(2)}) copy-start(f32[8,32,128]{2,1,0:T(8,128)} %conduct_ref.7) | copy-start | bytes 393220
  30.8 9.5 %copy-start.1 = (f32[8,32,128]{2,1,0:T(8,128)S(1)}, f32[8,32,128]{2,1,0:T(8,128)}, u32[]{:S(2)}) copy-start(f32[8,32,128]{2,1,0:T(8,128)} %source_ref.1) | copy-start | bytes 393220
  30.8 9.5 %copy-start.2 = (f32[8,32,128]{2,1,0:T(8,128)S(1)}, f32[8,32,128]{2,1,0:T(8,128)}, u32[]{:S(2)}) copy-start(f32[8,32,128]{2,1,0:T(8,128)} %reaction_ref.1) | copy-start | bytes 393220
  30.8 9.5 %copy-start.3 = (f32[8,32,128]{2,1,0:T(8,128)S(1)}, f32[8,32,128]{2,1,0:T(8,128)}, u32[]{:S(2)}) copy-start(f32[8,32,128]{2,1,0:T(8,128)} %old_ref.1) | copy-start | bytes 393220
  30.8 9.5 %copy-start.4 = (f32[4,16,64]{2,1,0:T(8,128)S(1)}, f32[4,16,64]{2,1,0:T(8,128)}, u32[]{:S(2)}) copy-start(f32[4,16,64]{2,1,0:T(8,128)} %coarse_ref.1) | copy-start | bytes 49156
  30.8 20.9 %all-to-all-start.1 = ((f32[32,3,8,128]{3,2,1,0:T(8,128)}), f32[32,3,8,128]{3,2,1,0:T(8,128)S(1)}, u32[]{:S(2)}, u32[]{:S(2)}) async-start(f32[32,3,8,128]{3,2,1,0:T(8,128)} %shard_map.65), calls=%async_computation.1 | async-start | bytes 786432 | tf_op jit(solution)/shard_map/all_to_all | solution.py:677
  40.9 4.8 %collective-permute-start.2 = (f32[40,128]{1,0:T(8,128)S(1)}, f32[40,128]{1,0:T(8,128)S(1)}, u32[]{:S(2)}, u32[]{:S(2)}) collective-permute-start(f32[40,128]{1,0:T(8,128)S(1)} %get-tuple-element.22.after_ref.sya_ref), channel_id=1, source_target_pairs={{0,4},{4,0},{8,12},{12,8},{16,20},{20,16},{24,28},{28,24},{32,36},... | collective-permute-start | bytes 61448 | tf_op jit(solution)/shard_map/ppermute | solution.py:622
  44.0 1.6 %collective-permute-start.3 = (f32[40,128]{1,0:T(8,128)S(1)}, f32[40,128]{1,0:T(8,128)S(1)}, u32[]{:S(2)}, u32[]{:S(2)}) collective-permute-start(f32[40,128]{1,0:T(8,128)S(1)} %get-tuple-element.23.syb_ref), channel_id=1, source_target_pairs={{4,8},{8,4},{12,16},{16,12},{20,24},{24,20},{28,32},{32,28},{36,40... | collective-permute-start | bytes 61448 | tf_op jit(solution)/shard_map/ppermute | solution.py:622
  45.6 6.0 %copy-start.5 = (s32[1,1,4]{2,1,0:T(1,128)S(1)}, s32[1,1,4]{2,1,0:T(1,128)}, u32[]{:S(2)}) copy-start(s32[1,1,4]{2,1,0:T(1,128)} %home_hbm.1) | copy-start | bytes 52
  52.8 6.6 %collective-permute-start.4 = (f32[168,128]{1,0:T(8,128)S(1)}, f32[168,128]{1,0:T(8,128)S(1)}, u32[]{:S(2)}, u32[]{:S(2)}) collective-permute-start(f32[168,128]{1,0:T(8,128)S(1)} %get-tuple-element.29.after_ref.sxa_ref), channel_id=1, source_target_pairs={{0,128},{128,0},{256,384},{384,256},{512,640},{640,512},{768,896},... | collective-permute-start | bytes 258056 | tf_op jit(solution)/shard_map/ppermute | solution.py:622
  55.5 5.3 %collective-permute-start.5 = (f32[168,128]{1,0:T(8,128)S(1)}, f32[168,128]{1,0:T(8,128)S(1)}, u32[]{:S(2)}, u32[]{:S(2)}) collective-permute-start(f32[168,128]{1,0:T(8,128)S(1)} %get-tuple-element.31.sxb_ref), channel_id=1, source_target_pairs={{128,256},{256,128},{384,512},{512,384},{640,768},{768,640},{129,2... | collective-permute-start | bytes 258056 | tf_op jit(solution)/shard_map/ppermute | solution.py:622
